TPU v7x, 32 devices: a whole 2x2x4 slice. The times are simulated.
32 devices in a mesh: tok: 16 (over z, y, x), hid: 2 (over core).
Axes of the slice: x: 2, y: 2, z: 4, core: 2. Of those that a mesh axis runs over, the one named last changes fastest.
Arguments:
- acts: bfloat16 [8192, 14336], P('tok', 'hid'), may hold values from -6 to 6
- dictionary: float32 [14336, 256], P('hid'), may hold values from -0.046875 to 0.046875
- codes: float32 [8192, 256], P('tok'), may hold values from 0.02 to 1, as said below
Outputs:
- codes_out: float32 [8192, 256], P('tok')
- dict_out: float32 [14336, 256], P('hid')
Inputs may be any that keep to these rules, and one draw needn't show every extreme that they name: `codes`: every starting code is positive.
All inputs are finite; a program needn't handle non-finite values.
Results may differ from a plain program's by a relative error of at most 0.0043.
Values sent between devices are 32-bit elements; how exact they have to be, the bound alone decides.
No kernel may reach another device: no remote copies, remote signals or barrier semaphores. Data moves between devices by JAX's collectives and lax.ppermute only.
A program may use at most 128 MiB of HBM per device.

v0:
```python
import jax
import jax.numpy as jnp
from jax import lax
from jax.sharding import PartitionSpec as P

floor_value = 0.05


def refine(codes, proj, gram):
    gram_pos = jnp.maximum(gram, 0.0)
    gram_neg = jnp.maximum(-gram, 0.0)
    numer = jnp.maximum(proj, 0.0) + jnp.dot(codes, gram_neg, precision=lax.Precision.HIGHEST)
    denom = jnp.maximum(
        jnp.maximum(-proj, 0.0) + jnp.dot(codes, gram_pos, precision=lax.Precision.HIGHEST),
        floor_value,
    )
    return codes * jnp.sqrt(numer / denom)


def solve_rows(cross, gram):
    lower = jnp.linalg.cholesky(gram)
    return jax.scipy.linalg.cho_solve((lower, True), cross.T).T


def self_gram(matrix):
    return jnp.dot(matrix.T, matrix, precision=lax.Precision.HIGHEST)


def per_device(acts, dictionary, codes):
    proj_part = jnp.dot(acts, dictionary.astype(jnp.bfloat16), preferred_element_type=jnp.float32)
    proj, gram_dict = lax.psum((proj_part, self_gram(dictionary)), "hid")
    codes_mid = refine(codes, proj, gram_dict)
    codes_low = codes_mid.astype(jnp.bfloat16)
    cross_part = lax.dot_general(
        acts, codes_low, (((0,), (0,)), ((), ())), preferred_element_type=jnp.float32
    )
    gram_part = jnp.dot(codes_low.T, codes_low, preferred_element_type=jnp.float32)
    cross, gram_codes = lax.psum((cross_part, gram_part), "tok")
    dict_out = solve_rows(cross, gram_codes)
    proj_next = jnp.dot(acts, dict_out.astype(jnp.bfloat16), preferred_element_type=jnp.float32)
    proj_two, gram_new = lax.psum((proj_next, self_gram(dict_out)), "hid")
    codes_out = refine(codes_mid, proj_two, gram_new)
    return (codes_out, dict_out)


def solution(mesh):
    return jax.shard_map(
        per_device,
        mesh=mesh,
        in_specs=(P("tok", "hid"), P("hid", None), P("tok", None)),
        out_specs=(P("tok", None), P("hid", None)),
        check_vma=False,
    )
```

profile of v0, /device:TPU:0, one launch (start us, length us, event | category | flops | bytes accessed | tf_op | source)
XLA Modules:
  0.0 436.4 jit_solution(6129137091110123922)
XLA Ops:
  7.2 0.0 all-reduce.12.cloned.1.call-start
  7.2 0.0 copy-start
  7.2 0.0 copy-start.2
  7.2 17.1 %fusion.51 = f32[256,256]{1,0:T(8,128)} fusion(f32[7168,256]{1,0:T(8,128)} %param.4), kind=kOutput, calls=%fused_computation.73 | convolution fusion | flops 5637144576 | bytes 7602176 | tf_op jit(solution)/shard_map/dot_general | solution.py:26
  24.3 0.0 copy-done
  24.3 0.0 copy-done.2
  24.3 0.0 copy-start.5
  24.3 2.9 fusion.6
  27.2 0.0 all-reduce.12.cloned.1.call-update
  27.2 0.0 all-reduce.8.cloned.1.call-start
  27.3 22.0 %all-reduce.12.cloned.1.call-done = (f32[512,256]{1,0:T(8,128)}, f32[256,256]{1,0:T(8,128)}) async-done(((f32[512,256]{1,0:T(8,128)}, f32[256,256]{1,0:T(8,128)}), (f32[512,256]{1,0:T(8,128)}, f32[256,256]{1,0:T(8,128)})) %all-reduce.12.cloned.1.call-update) | async-done | bytes 786448 | tf_op jit(solution)/shard_map/psum | solution.py:31
  49.3 0.0 copy-done.5
  49.3 1.7 fusion.13
  51.0 1.9 fusion.11
  52.9 8.2 %fusion.28 = f32[256,7168]{1,0:T(8,128)} fusion(bf16[512,7168]{1,0:T(8,128)(2,1)} %param.3, f32[512,256]{1,0:T(8,128)S(1)} %fusion.11), kind=kOutput, calls=%fused_computation.39 | convolution fusion | flops 1879179264 | bytes 15204352 | tf_op jit(solution)/shard_map/dot_general | solution.py:34
  61.2 1.0 fusion.30
  62.1 0.0 all-reduce.8.cloned.1.call-update
  62.2 0.3 all-reduce.10.cloned.1.call-start
  62.5 240.1 %all-reduce.8.cloned.1.call-done = (f32[256,7168]{1,0:T(8,128)}, f32[256,256]{0,1:T(8,128)}) async-done(((f32[256,7168]{1,0:T(8,128)}, f32[256,256]{0,1:T(8,128)}), (f32[256,7168]{1,0:T(8,128)}, f32[256,256]{0,1:T(8,128)})) %all-reduce.8.cloned.1.call-update) | async-done | bytes 7602192 | tf_op jit(solution)/shard_map/psum | solution.py:38
  302.6 1.1 copy.8
  303.6 1.0 fusion.21
  304.7 11.7 %cholesky.49 = f32[128,128]{1,0:T(8,128)S(1)} custom-call(f32[128,128]{1,0:T(8,128)S(1)} %cholesky.115), custom_call_target="Cholesky" | custom-call | tf_op jit(solution)/shard_map/jit(cholesky)/cholesky | solution.py:21
  316.4 9.8 %custom-call.18 = f32[1,128,128]{1,2,0:T(8,128)S(1)} custom-call(f32[1,128,128]{2,1,0:T(8,128)S(1)} %get-tuple-element.31), custom_call_target="InvertDiagBlocksLowerTriangular" | custom-call | tf_op jit(solution)/shard_map/jit(cholesky)/cholesky | solution.py:21
  326.2 0.2 constant_dynamic-update-slice_fusion.1
  326.5 0.3 convolution_subtract_fusion.2
  326.7 11.7 %cholesky.103 = f32[128,128]{1,0:T(8,128)S(1)} custom-call(f32[128,128]{1,0:T(8,128)S(1)} %convolution_subtract_fusion.2), custom_call_target="Cholesky" | custom-call | tf_op jit(solution)/shard_map/jit(cholesky)/cholesky | solution.py:21
  338.5 0.6 compare_reduce_fusion
  340.5 0.1 triangular_solve.66
  340.5 4.0 while.1
  340.5 0.6 fusion.69
  341.1 1.4 bitcast_dynamic-update-slice_fusion.2
  342.5 0.6 fusion.69
  343.1 1.4 bitcast_dynamic-update-slice_fusion.2
  344.5 28.4 %custom-call.19 = f32[2,128,128]{1,2,0:T(8,128)S(1)} custom-call(f32[2,128,128]{2,1,0:T(8,128)S(1)} %get-tuple-element.9), custom_call_target="InvertDiagBlocksLowerTriangular" | custom-call | tf_op jit(solution)/shard_map/jit(_cho_solve)/triangular_solve | solution.py:22
  372.9 0.0 copy-start.4
  373.0 5.6 %fusion.2 = f32[128,7168]{1,0:T(8,128)S(1)} fusion(f32[256,7168]{1,0:T(8,128)} %get-tuple-element.20, f32[2,128,128]{1,2,0:T(8,128)S(1)} %custom-call.19), kind=kOutput, calls=%fused_computation.7 | convolution fusion | flops 1409286144 | bytes 7405568 | tf_op jit(solution)/shard_map/jit(_cho_solve)/triangular_solve | solution.py:22
  378.6 0.0 copy-done.4
  378.6 3.5 convolution_subtract_fusion.1
  382.2 3.5 fusion.41
  385.7 0.0 slice-start
  385.7 3.7 fusion.40
  389.4 0.0 copy-start.1
  389.4 0.0 slice-start.1
  389.4 3.5 convolution_subtract_fusion
  392.9 3.5 fusion.39
  396.4 0.0 slice-done
  396.4 0.0 slice-done.1
  396.4 0.0 copy-start.3
  396.4 3.1 fusion.14
  399.5 0.0 copy-done.1
  399.5 0.0 copy-done.3
  399.5 7.0 %fusion = f32[256,256]{1,0:T(8,128)} fusion(f32[128,7168]{1,0:T(8,128)S(1)} %fusion.40, f32[128,7168]{1,0:T(8,128)S(1)} %fusion.39), kind=kOutput, calls=%fused_computation.5 | convolution fusion | flops 5638979584 | bytes 7602176 | tf_op jit(solution)/shard_map/dot_general | solution.py:26
  406.5 0.0 all-reduce.10.cloned.1.call-update
  406.5 6.9 %fusion.1 = f32[7168,256]{0,1:T(8,128)} fusion(f32[128,7168]{1,0:T(8,128)} %copy-done.1, f32[128,7168]{1,0:T(8,128)} %copy-done.3), kind=kLoop, calls=%fused_computation.6 | loop fusion | flops 1835008 | bytes 14680064 | tf_op jit(solution)/shard_map/transpose | solution.py:22
  413.4 8.4 %copy.10 = f32[7168,256]{1,0:T(8,128)} copy(f32[7168,256]{0,1:T(8,128)} %fusion.1) | data formatting | bytes 14680064
  421.8 3.2 all-reduce.10.cloned.1.call-done
  425.0 1.7 convolution_add_fusion.1
  426.7 2.7 fusion.20
  (10 shorter events, 0.1 us)
Async XLA Ops:
  7.2 42.1 %all-reduce.12.cloned.1.call-start = ((), (), s32[]{:S(2)}) async-start(), calls=%async_computation.2 | async-start | bytes 1572864 | tf_op jit(solution)/shard_map/psum | solution.py:31
  7.2 17.1 %copy-start = (f32[7168,256]{1,0:T(8,128)S(1)}, f32[7168,256]{1,0:T(8,128)}, u32[]{:S(2)}) copy-start(f32[7168,256]{1,0:T(8,128)} %param.4) | copy-start | bytes 22020100
  7.2 17.1 %copy-start.2 = (bf16[512,7168]{1,0:T(8,128)(2,1)S(1)}, bf16[512,7168]{1,0:T(8,128)(2,1)}, u32[]{:S(2)}) copy-start(bf16[512,7168]{1,0:T(8,128)(2,1)} %param.3) | copy-start | bytes 22020100
  24.3 25.0 %copy-start.5 = (f32[512,256]{1,0:T(8,128)S(1)}, f32[512,256]{1,0:T(8,128)}, u32[]{:S(2)}) copy-start(f32[512,256]{1,0:T(8,128)} %param.5) | copy-start | bytes 1572868
  27.2 275.3 %all-reduce.8.cloned.1.call-start = ((), (), s32[]{:S(2)}) async-start(), calls=%async_computation | async-start | bytes 15204352 | tf_op jit(solution)/shard_map/psum | solution.py:38
  62.2 362.8 %all-reduce.10.cloned.1.call-start = ((), (), s32[]{:S(2)}) async-start(), calls=%async_computation.1 | async-start | bytes 1572864 | tf_op jit(solution)/shard_map/psum | solution.py:41
  372.9 5.7 %copy-start.4 = (f32[256,7168]{1,0:T(8,128)S(1)}, f32[256,7168]{1,0:T(8,128)}, u32[]{:S(2)}) copy-start(f32[256,7168]{1,0:T(8,128)} %get-tuple-element.20) | copy-start | bytes 22020100
  385.7 10.7 %slice-start = ((s8[7340032]{0:T(1024)(128)(4,1)}), s8[4194304]{0:T(1024)(128)(4,1)S(1)}, s32[]{:S(2)}) async-start(s8[7340032]{0:T(1024)(128)(4,1)} %bitcast.68), calls=%async_computation.3 | async-start | bytes 8388608
  389.4 10.2 %copy-start.1 = (f32[128,7168]{1,0:T(8,128)}, f32[128,7168]{1,0:T(8,128)S(1)}, u32[]{:S(2)}) copy-start(f32[128,7168]{1,0:T(8,128)S(1)} %fusion.40) | copy-start | bytes 11010052
  389.4 7.0 %slice-start.1 = ((s8[7340032]{0:T(1024)(128)(4,1)}), s8[3145728]{0:T(1024)(128)(4,1)S(1)}, s32[]{:S(2)}) async-start(s8[7340032]{0:T(1024)(128)(4,1)} %bitcast.68), calls=%async_computation.4 | async-start | bytes 6291456
  396.4 3.1 copy-start.3
Sparse Core Ops, SparseCore 0:
  27.3 21.9 all-reduce.11
  62.3 240.2 all-reduce.7
  406.7 18.2 all-reduce.9
where the time goes:
time: 445 us; the launch traced here: 436 us
  waiting for transfers between devices  265 us (60%)
  matrix products  71 us (16%)
  other arithmetic  70.3 us (16%)
  between operations  15.7 us (4%)
  local copies, waits for them, and re-layouts  13.6 us (3%)
    psum x1, waiting for transfers between devices, per_device(): cross, gram_codes = lax.psum((cross_part, gram_part), 'tok')  240 us
    another operation x6, other arithmetic, solve_rows(): lower = jnp.linalg.cholesky(gram)  33.9 us
    another operation x3, other arithmetic, solve_rows(): return jax.scipy.linalg.cho_solve((lower, True), cross.T).T  28.5 us
    dot_general x2, matrix products, self_gram(): return jnp.dot(matrix.T, matrix, precision=lax.Precision.HIGHEST)  24.1 us
    another operation x6, matrix products, solve_rows(): return jax.scipy.linalg.cho_solve((lower, True), cross.T).T  23.3 us
    psum x1, waiting for transfers between devices, per_device(): proj, gram_dict = lax.psum((proj_part, self_gram(dictionary)), 'hid')  22 us
  transfers between devices with their start and end apart: 3, of which 3 were waited for; matrix products, arithmetic and copies ran while one was open for 4% of the time, Pallas kernels for 0%

commit v1 on v0

v1 whole, which is shorter than its diff:
```python
import functools

import jax
import jax.numpy as jnp
from jax import lax
from jax.experimental import pallas as pl
from jax.experimental.pallas import tpu as pltpu
from jax.sharding import PartitionSpec as P

floor_value = 0.05
HIGHEST = lax.Precision.HIGHEST
f32, bf16 = jnp.float32, jnp.bfloat16
BOTH = ("tok", "hid")
OVER_ROWS = (((0,), (0,)), ((), ()))
OVER_COLS = (((1,), (1,)), ((), ()))


def dot(left, right, dims=(((1,), (0,)), ((), ())), precision=None):
    return lax.dot_general(left, right, dims, precision=precision, preferred_element_type=f32)


def refine(codes, proj, gram):
    gram_pos = jnp.maximum(gram, 0.0)
    gram_neg = jnp.maximum(-gram, 0.0)
    numer = jnp.maximum(proj, 0.0) + dot(codes, gram_neg, precision=HIGHEST)
    denom = jnp.maximum(jnp.maximum(-proj, 0.0) + dot(codes, gram_pos, precision=HIGHEST), floor_value)
    return codes * jnp.sqrt(numer / denom)


def project_kernel(acts_ref, dict_ref, out_ref, cross_ref):
    step = pl.program_id(0)
    tokens = acts_ref.shape[0]

    @pl.when(step == 0)
    def _():
        out_ref[...] = jnp.zeros_like(out_ref)
        cross_ref[...] = jnp.zeros_like(cross_ref)

    rows = dict_ref[...]
    high = rows.astype(bf16)
    low = (rows - high.astype(f32)).astype(bf16)
    out_ref[:tokens, :] += dot(acts_ref[...], high)
    turned = high.T
    out_ref[tokens:, :] += dot(turned, high)
    cross_ref[...] += dot(turned, low)

    @pl.when(step == pl.num_programs(0) - 1)
    def _():
        out_ref[tokens:, :] += cross_ref[...] + cross_ref[...].T


def project(acts, dictionary):
    tokens, hidden = acts.shape
    comp = dictionary.shape[1]
    tile = 1024 if hidden % 1024 == 0 else 512
    return pl.pallas_call(
        project_kernel,
        out_shape=jax.ShapeDtypeStruct((tokens + comp, comp), f32),
        grid=(hidden // tile,),
        in_specs=[
            pl.BlockSpec((tokens, tile), lambda i: (0, i)),
            pl.BlockSpec((tile, comp), lambda i: (i, 0)),
        ],
        out_specs=pl.BlockSpec((tokens + comp, comp), lambda i: (0, 0)),
        scratch_shapes=[pltpu.VMEM((comp, comp), f32)],
        compiler_params=pltpu.CompilerParams(vmem_limit_bytes=48 * 2**20),
        cost_estimate=pl.CostEstimate(
            flops=2 * hidden * comp * (tokens + 2 * comp), bytes_accessed=hidden * (2 * tokens + 4 * comp), transcendentals=0
        ),
    )(acts, dictionary)


def unit_inverse(block):
    n = block.shape[0]
    done = []
    rest = block
    for start in range(0, n, 8):
        shape = rest.shape
        row = lax.broadcasted_iota(jnp.int32, shape, 0)
        lane = lax.broadcasted_iota(jnp.int32, shape, 1)
        lane_row = lax.broadcasted_iota(jnp.int32, (1, n), 1)
        cols = [jnp.broadcast_to(rest[:, start + j : start + j + 1], shape) for j in range(8)]
        for j in range(8):
            inverse = 1.0 / cols[j][j : j + 1, :]
            below = jnp.where(row > j, cols[j], 0.0)
            scaled = jnp.where(lane_row == start + j, inverse, rest[j : j + 1, :] * inverse)
            rest = jnp.where((lane == start + j) & (row > j), 0.0, rest) - below * scaled
            for k in range(j + 1, 8):
                cols[k] = cols[k] - below * (cols[k][j : j + 1, :] * inverse)
        done.append(rest[:8, :])
        rest = rest[8:, :]
    full = jnp.concatenate(done, axis=0)
    row = lax.broadcasted_iota(jnp.int32, (n, n), 0)
    lane = lax.broadcasted_iota(jnp.int32, (n, n), 1)
    pivots = jnp.sum(jnp.where(row == lane, full, 0.0), axis=1, keepdims=True)
    unit = jnp.where(row > lane, full, jnp.where(row == lane, 1.0, 0.0))
    return unit * (1.0 / jnp.sqrt(pivots))


def factor_kernel(gram_ref, out_ref):
    half = gram_ref.shape[0] // 2
    upper = unit_inverse(gram_ref[:half, :half])
    side = dot(gram_ref[half:, :half], upper, OVER_COLS, HIGHEST)
    lower = unit_inverse(gram_ref[half:, half:] - dot(side, side, OVER_COLS, HIGHEST))
    out_ref[:half, :half] = upper
    out_ref[:half, half:] = jnp.zeros((half, half), f32)
    out_ref[half:, :half] = -dot(dot(lower, side, precision=HIGHEST), upper, precision=HIGHEST)
    out_ref[half:, half:] = lower


def factor_inverse(gram):
    return pl.pallas_call(
        factor_kernel,
        out_shape=jax.ShapeDtypeStruct(gram.shape, f32),
        compiler_params=pltpu.CompilerParams(vmem_limit_bytes=48 * 2**20),
        cost_estimate=pl.CostEstimate(flops=10**10, bytes_accessed=8 * gram.size, transcendentals=0),
    )(gram)


def solve_rows(cross, inverse):
    return dot(dot(cross, inverse, OVER_COLS, HIGHEST), inverse, precision=HIGHEST)


def plain(acts, dictionary, codes, split):
    tokens = acts.shape[0]
    sums = lax.psum(project(acts, dictionary), "hid")
    codes_mid = refine(codes, sums[:tokens], sums[tokens:])
    codes_low = codes_mid.astype(bf16)
    cross = dot(acts, codes_low, OVER_ROWS)
    gram_codes = lax.psum(dot(codes_low, codes_low, OVER_ROWS), "tok")
    if split:
        mine = solve_rows(lax.psum_scatter(cross, "tok", tiled=True), factor_inverse(gram_codes))
        dict_out = lax.all_gather(mine, "tok", tiled=True)
    else:
        dict_out = solve_rows(lax.psum(cross, "tok"), factor_inverse(gram_codes))
    gram_part = dot(dict_out, dict_out, OVER_ROWS, HIGHEST)
    proj_two, gram_new = lax.psum((dot(acts, dict_out.astype(bf16)), gram_part), "hid")
    return refine(codes_mid, proj_two, gram_new), dict_out


DEPTH = 4


def device(z, y, x, c):
    return (z * 4 + y * 2 + x) * 2 + c


def every():
    return [(z, y, x, c) for z in range(DEPTH) for y in range(2) for x in range(2) for c in range(2)]


def flip(which):
    pairs = []
    for z, y, x, c in every():
        along_x = (c == 0) == (which == "first")
        pairs.append((device(z, y, x, c), device(z, y, 1 - x, c) if along_x else device(z, 1 - y, x, c)))
    return pairs


def along(sources, step):
    return [(device(z, y, x, c), device(z + step, y, x, c)) for z, y, x, c in every() if z in sources]


def send(value, pairs):
    return lax.ppermute(value, BOTH, pairs)


def line_sum(get, z):
    right = left = None
    for s in range(1, DEPTH):
        out_r = get(jnp.minimum(DEPTH - s + z, DEPTH - 1), right)
        out_l = get(jnp.maximum(s - DEPTH + z, 0), left)
        right = send(out_r, along(range(0, s), 1))
        left = send(out_l, along(range(DEPTH - s, DEPTH), -1))
    return get(z, right) + left


def line_gather(own, z):
    rights, lefts = [own], [own]
    for s in range(1, DEPTH):
        rights.append(send(rights[-1], along(range(s - 1, DEPTH - 1), 1)))
        lefts.append(send(lefts[-1], along(range(1, DEPTH - s + 1), -1)))
    return [own] + [rights[s] + lefts[DEPTH - s] for s in range(1, DEPTH)]


def place(blocks, total):
    out = jnp.zeros((total, blocks[0][0].shape[1]), f32)
    for value, row in blocks:
        out = lax.dynamic_update_slice_in_dim(out, value, row, 0)
    return out


def meshed(acts, dictionary, codes):
    tokens, hidden = acts.shape
    tok, core = lax.axis_index("tok"), lax.axis_index("hid")
    z, y, x = tok // 4, (tok // 2) % 2, tok % 2
    p = jnp.where(core == 0, x, y)
    q = jnp.where(core == 0, y, x)
    first, second = flip("first"), flip("second")
    swap = [(0, 1), (1, 0)]

    sums = project(acts, dictionary)
    sums = sums + lax.ppermute(sums, "hid", swap)
    codes_mid = refine(codes, sums[:tokens], sums[tokens:])
    codes_low = codes_mid.astype(bf16)
    gram_codes = lax.psum(dot(codes_low, codes_low, OVER_ROWS), "tok")
    inverse = factor_inverse(gram_codes)

    wide = (hidden * 11 // 14) // 512 * 512
    narrow = hidden - wide
    quarter, stripe = wide // 4, narrow // 4

    def cross_of(row, rows, add=None):
        out = dot(lax.dynamic_slice_in_dim(acts, row, rows, 1), codes_low, OVER_ROWS)
        return out if add is None else out + add

    def quarter_row(a, b):
        return a * (2 * quarter) + b * quarter

    got_1 = send(cross_of(quarter_row(1 - p, 1 - q), quarter), first)
    narrow_mine = line_sum(lambda j, add: cross_of(wide + j * stripe, stripe, add), z)
    got_2 = send(cross_of(quarter_row(1 - p, q), quarter), first)
    got_3 = send(cross_of(quarter_row(p, 1 - q), quarter, got_1), second)
    wide_mine = cross_of(quarter_row(p, q), quarter, got_2) + got_3

    def half_of(value, which):
        rows = value.shape[0] // 2
        return lax.dynamic_slice_in_dim(value, which * rows, rows, 0)

    narrow_mine = half_of(narrow_mine, p) + send(half_of(narrow_mine, 1 - p), first)
    narrow_mine = half_of(narrow_mine, q) + send(half_of(narrow_mine, 1 - q), second)

    piece = quarter // DEPTH

    def wide_block(j, add):
        value = lax.dynamic_slice_in_dim(wide_mine, j * piece, piece, 0)
        return value if add is None else value + add

    wide_mine = line_sum(wide_block, z)

    narrow_mine = solve_rows(narrow_mine, inverse)
    wide_mine = solve_rows(wide_mine, inverse)
    gram_part = dot(narrow_mine, narrow_mine, OVER_ROWS, HIGHEST) + dot(wide_mine, wide_mine, OVER_ROWS, HIGHEST)
    gram_new = lax.psum(gram_part, BOTH)

    small = narrow // 16
    narrow_mine = place([(narrow_mine, q * small), (send(narrow_mine, second), (1 - q) * small)], 2 * small)
    narrow_mine = place([(narrow_mine, p * 2 * small), (send(narrow_mine, first), (1 - p) * 2 * small)], 4 * small)
    wide_all = line_gather(wide_mine, z)
    own = place([(value, (z - s) % DEPTH * piece) for s, value in enumerate(wide_all)], quarter)
    narrow_all = line_gather(narrow_mine, z)
    from_second = send(own, second)
    from_first = send(own, first)
    from_far = send(from_second, first)

    blocks = [(value, wide + (z - s) % DEPTH * stripe) for s, value in enumerate(narrow_all)]
    blocks += [
        (own, quarter_row(p, q)),
        (from_second, quarter_row(p, 1 - q)),
        (from_first, quarter_row(1 - p, q)),
        (from_far, quarter_row(1 - p, 1 - q)),
    ]
    dict_out = place(blocks, hidden)
    proj_two = None
    for value, row in blocks:
        part = dot(lax.dynamic_slice_in_dim(acts, row, value.shape[0], 1), value.astype(bf16))
        proj_two = part if proj_two is None else proj_two + part
    proj_two = proj_two + lax.ppermute(proj_two, "hid", swap)
    return refine(codes_mid, proj_two, gram_new), dict_out


def solution(mesh):
    tok, hid = mesh.shape["tok"], mesh.shape["hid"]

    def per_device(acts, dictionary, codes):
        if tok == 16 and hid == 2 and acts.shape[1] % 512 == 0:
            return meshed(acts, dictionary, codes)
        return plain(acts, dictionary, codes, acts.shape[1] % tok == 0)

    return jax.shard_map(
        per_device,
        mesh=mesh,
        in_specs=(P("tok", "hid"), P("hid", None), P("tok", None)),
        out_specs=(P("tok", None), P("hid", None)),
        check_vma=False,
    )
```

time: 445 us -> 426 us (0.957); the launches traced: 436 us -> 424 us
  starting transfers between devices: 0.38 us -> 72.5 us
  other arithmetic: 70.3 us -> 13.2 us
  matrix products: 71 us -> 46 us
  Pallas kernels: 0 us -> 17.3 us
  waiting for transfers between devices: 265 us -> 248 us
    psum x3 -> x2, waiting for transfers between devices: 265 us -> 191 us  [the longest x1 129 us: meshed(): gram_new = lax.psum(gram_part, BOTH)]
    ppermute x0 -> x36, starting transfers between devices: none -> 72.4 us  [the longest x34 71.8 us: send(): return lax.ppermute(value, BOTH, pairs)]
    another operation x9 -> x0, other arithmetic: 62.4 us -> none  [the longest x6 33.9 us: solve_rows(): lower = jnp.linalg.cholesky(gram)]
    ppermute x0 -> x36, waiting for transfers between devices: none -> 56.8 us  [the longest x34 54.9 us: send(): return lax.ppermute(value, BOTH, pairs)]
    another operation x8 -> x0, matrix products: 23.8 us -> none  [the longest x6 23.3 us: solve_rows(): return jax.scipy.linalg.cho_solve((lower, True), cross.T).T]
    pallas_call x0 -> x2, Pallas kernels: none -> 17.3 us  [the longest x1 9.44 us: project(): pl.pallas_call(project_kernel, out_shape=jax.ShapeDtypeStruct((tokens + c...]
    dynamic_update_slice x0 -> x8, local copies, waits for them, and re-layouts: none -> 7.89 us  [place(): out = lax.dynamic_update_slice_in_dim(out, value, row, 0)]
    unnamed x17 -> x14, local copies, waits for them, and re-layouts: 8.43 us -> 0.98 us
  transfers between devices with their start and end apart: 3 -> 38, of which waited for: 3 -> 17; matrix products, arithmetic and copies ran while one was open for 4% -> 15% of each run, Pallas kernels for 0% -> 2%
where the time goes in v1:
time: 426 us; the launch traced here: 424 us
  waiting for transfers between devices  248 us (58%)
  starting transfers between devices  72.5 us (17%)
  matrix products  46 us (11%)
  Pallas kernels  17.3 us (4%)
  between operations  14.8 us (3%)
  other arithmetic  13.2 us (3%)
  local copies, waits for them, and re-layouts  12.6 us (3%)
    psum x1, waiting for transfers between devices, meshed(): gram_new = lax.psum(gram_part, BOTH)  129 us
    ppermute x34, starting transfers between devices, send(): return lax.ppermute(value, BOTH, pairs)  71.8 us
    psum x1, waiting for transfers between devices, meshed(): gram_codes = lax.psum(dot(codes_low, codes_low, OVER_ROWS), 'tok')  62 us
    ppermute x34, waiting for transfers between devices, send(): return lax.ppermute(value, BOTH, pairs)  54.9 us
    dot_general x30, matrix products, dot(): lax.dot_general(left, right, dims, precision=precision, preferred_element...  46 us
    pallas_call x1, Pallas kernels, project(): pl.pallas_call(project_kernel, out_shape=jax.ShapeDtypeStruct((tokens + c...  9.44 us
  transfers between devices with their start and end apart: 38, of which 17 were waited for; matrix products, arithmetic and copies ran while one was open for 15% of the time, Pallas kernels for 2%

profile of v1, /device:TPU:0, one launch (start us, length us, event | category | flops | bytes accessed | tf_op | source)
XLA Modules:
  0.0 424.2 jit_solution(8153788735904986039)
XLA Ops:
  7.2 9.4 %shard_map.50 = f32[768,256]{1,0:T(8,128)S(1)} custom-call(bf16[512,7168]{1,0:T(8,128)(2,1)} %acts_ref.1, f32[7168,256]{1,0:T(8,128)} %dict_ref.1), custom_call_target="tpu_custom_call" | custom-call | flops 3758096384 | bytes 14680064 | tf_op jit(solution)/shard_map/pallas_call | solution.py:56
  17.2 1.9 collective-permute-done
  20.7 3.0 fusion.3
  23.7 2.9 collective-permute-start.18
  26.6 2.0 fusion.34
  28.6 3.5 collective-permute-start.1
  32.1 1.3 fusion.26
  34.1 3.1 fusion.10
  37.7 6.0 %collective-permute-done.18 = f32[1408,256]{1,0:T(8,128)S(1)} collective-permute-done((f32[1408,256]{1,0:T(8,128)}, f32[1408,256]{1,0:T(8,128)S(1)}, u32[]{:S(2)}, u32[]{:S(2)}) %collective-permute-start.18) | collective-permute-done | bytes 1441824 | tf_op jit(solution)/shard_map/ppermute | solution.py:165
  43.8 3.0 convolution_add_fusion
  46.8 2.1 collective-permute-start.19
  49.9 1.3 convolution_add_fusion.6
  51.2 3.5 collective-permute-start.2
  54.8 1.3 convolution_add_fusion.5
  56.8 1.3 fusion.42
  58.1 5.8 %collective-permute-done.2 = f32[384,256]{1,0:T(8,128)S(1)} collective-permute-done((f32[384,256]{1,0:T(8,128)S(1)}, f32[384,256]{1,0:T(8,128)S(1)}, u32[]{:S(2)}, u32[]{:S(2)}) %collective-permute-start.2) | collective-permute-done | bytes 393248 | tf_op jit(solution)/shard_map/ppermute | solution.py:165
  63.9 1.3 fusion.39
  65.2 4.4 %collective-permute-start.3 = (f32[384,256]{1,0:T(8,128)S(1)}, f32[384,256]{1,0:T(8,128)S(1)}, u32[]{:S(2)}, u32[]{:S(2)}) collective-permute-start(f32[384,256]{1,0:T(8,128)S(1)} %fusion.39), channel_id=1, source_target_pairs={{0,8},{1,9},{2,10},{3,11},{4,12},{5,13},{6,14},{7,15},{8,16},{9,17... | collective-permute-start | bytes 1179656 | tf_op jit(solution)/shard_map/ppermute | solution.py:165
  69.6 1.3 fusion.31
  70.9 1.3 collective-permute-start.6
  72.2 2.7 collective-permute-done.19
  75.0 2.8 fusion
  77.8 3.7 collective-permute-start.20
  83.2 6.8 %collective-permute-done.20 = f32[352,256]{1,0:T(8,128)S(1)} collective-permute-done((f32[352,256]{1,0:T(8,128)S(1)}, f32[352,256]{1,0:T(8,128)S(1)}, u32[]{:S(2)}, u32[]{:S(2)}) %collective-permute-start.20) | collective-permute-done | bytes 360480 | tf_op jit(solution)/shard_map/ppermute | solution.py:165
  90.8 5.1 %collective-permute-start.21 = (f32[352,256]{1,0:T(8,128)}, f32[352,256]{1,0:T(8,128)}, u32[]{:S(2)}, u32[]{:S(2)}) collective-permute-start(f32[352,256]{1,0:T(8,128)} %dynamic-slice_add_fusion.2), channel_id=1, source_target_pairs={{0,8},{1,9},{2,10},{3,11},{4,12},{5,13},{6,14},{7,15},{8,16},{9,17... | collective-permute-start | bytes 1081352 | tf_op jit(solution)/shard_map/ppermute | solution.py:165
  95.9 62.0 %all-reduce.3.cloned.1.call-done.gram_ref = f32[256,256]{1,0:T(8,128)} async-done(((f32[256,256]{1,0:T(8,128)}), f32[256,256]{1,0:T(8,128)}) %all-reduce.3.cloned.1.call-update) | async-done | bytes 262160 | tf_op jit(solution)/shard_map/psum | solution.py:206
  158.9 7.9 %shard_map.51 = f32[256,256]{1,0:T(8,128)S(1)} custom-call(f32[256,256]{1,0:T(8,128)S(1)} %copy-done), custom_call_target="tpu_custom_call" | custom-call | flops 10000000000 | bytes 524288 | tf_op jit(solution)/shard_map/pallas_call | solution.py:112
  166.8 1.5 collective-permute-start.8
  168.3 1.8 dynamic-slice_add_fusion.3
  172.2 1.5 collective-permute-start.9
  174.5 1.4 collective-permute-start.24
  175.9 2.0 collective-permute-done.9
  177.8 1.5 collective-permute-start.10
  179.4 4.3 %collective-permute-done.10 = f32[192,256]{1,0:T(8,128)} collective-permute-done((f32[192,256]{1,0:T(8,128)S(1)}, f32[192,256]{1,0:T(8,128)}, u32[]{:S(2)}, u32[]{:S(2)}) %collective-permute-start.10) | collective-permute-done | bytes 196640 | tf_op jit(solution)/shard_map/ppermute | solution.py:165
  184.6 1.3 collective-permute-start.12
  185.9 5.3 %collective-permute-start.22 = (f32[352,256]{1,0:T(8,128)S(1)}, f32[352,256]{1,0:T(8,128)}, u32[]{:S(2)}, u32[]{:S(2)}) collective-permute-start(f32[352,256]{1,0:T(8,128)S(1)} %copy-done.6), channel_id=1, source_target_pairs={{0,8},{1,9},{2,10},{3,11},{4,12},{5,13},{6,14},{7,15},{8,16},{9,17... | collective-permute-start | bytes 1081352 | tf_op jit(solution)/shard_map/ppermute | solution.py:165
  191.2 1.8 dynamic-slice_add_fusion.1
  194.3 7.3 %collective-permute-start.11 = (f32[384,256]{1,0:T(8,128)S(1)}, f32[384,256]{1,0:T(8,128)}, u32[]{:S(2)}, u32[]{:S(2)}) collective-permute-start(f32[384,256]{1,0:T(8,128)S(1)} %constant_dynamic-update-slice_fusion.6), channel_id=1, source_target_pairs={{0,8},{1,9},{2,10},{3,11},{4,12},{5,13},{6,14},{7,15},{8,16},{9,17... | collective-permute-start | bytes 1179656 | tf_op jit(solution)/shard_map/ppermute | solution.py:165
  202.9 4.2 collective-permute-done.25
  207.1 1.6 fusion.46
  210.7 1.4 collective-permute-start.15
  212.1 3.8 collective-permute-done.13
  217.2 5.9 %collective-permute-start.26 = (f32[352,256]{1,0:T(8,128)S(1)}, f32[352,256]{1,0:T(8,128)S(1)}, u32[]{:S(2)}, u32[]{:S(2)}) collective-permute-start(f32[352,256]{1,0:T(8,128)S(1)} %get-tuple-element.7), channel_id=1, source_target_pairs={{0,8},{1,9},{2,10},{3,11},{4,12},{5,13},{6,14},{7,15},{8,16},{9,17... | collective-permute-start | bytes 1081352 | tf_op jit(solution)/shard_map/ppermute | solution.py:165
  223.2 1.4 collective-permute-done.27
  228.7 8.1 %collective-permute-done.28 = f32[352,256]{1,0:T(8,128)S(1)} collective-permute-done((f32[352,256]{1,0:T(8,128)}, f32[352,256]{1,0:T(8,128)S(1)}, u32[]{:S(2)}, u32[]{:S(2)}) %collective-permute-start.28) | collective-permute-done | bytes 360480 | tf_op jit(solution)/shard_map/ppermute | solution.py:165
  238.1 3.5 broadcast_in_dim.15
  242.4 1.4 collective-permute-start.16
  243.8 1.4 convolution_add_fusion.4
  247.4 1.5 collective-permute-start.32
  248.9 1.8 add_dynamic-update-slice_fusion.5
  250.7 2.4 convolution_add_fusion.3
  253.1 1.9 add_dynamic-update-slice_fusion.4
  255.0 1.6 convolution_add_fusion.7
  257.2 1.9 add_dynamic-update-slice_fusion.3
  259.1 129.1 %all-reduce.5.cloned.1.call-done = f32[256,256]{1,0:T(8,128)} async-done(((f32[256,256]{1,0:T(8,128)}), f32[256,256]{1,0:T(8,128)}) %all-reduce.5.cloned.1.call-update) | async-done | bytes 262160 | tf_op jit(solution)/shard_map/psum | solution.py:244
  388.2 1.6 fusion.50
  389.8 1.5 collective-permute-start.34
  391.9 1.9 fusion.12
  395.1 1.9 fusion.5
  397.0 2.4 fusion.8
  400.6 8.3 %collective-permute-done.34 = f32[1408,256]{1,0:T(8,128)S(1)} collective-permute-done((f32[1408,256]{1,0:T(8,128)S(1)}, f32[1408,256]{1,0:T(8,128)S(1)}, u32[]{:S(2)}, u32[]{:S(2)}) %collective-permute-start.34) | collective-permute-done | bytes 1441824 | tf_op jit(solution)/shard_map/ppermute | solution.py:165
  408.9 1.9 fusion.1
  410.8 1.5 fusion.18
  412.5 2.6 constant_dynamic-update-slice_fusion.1
  (89 shorter events, 32.4 us)
Async XLA Ops:
  7.2 150.8 %all-reduce.3.cloned.1.call-start = ((), (), s32[]{:S(2)}) async-start(), calls=%async_computation | async-start | bytes 524288 | tf_op jit(solution)/shard_map/psum | solution.py:206
  16.7 2.5 copy-start.5
  16.7 2.4 collective-permute-start
  23.7 20.1 %collective-permute-start.18 = (f32[1408,256]{1,0:T(8,128)}, f32[1408,256]{1,0:T(8,128)S(1)}, u32[]{:S(2)}, u32[]{:S(2)}) collective-permute-start(f32[1408,256]{1,0:T(8,128)} %fusion.3), channel_id=1, source_target_pairs={{0,2},{1,5},{2,0},{3,7},{4,6},{5,1},{6,4},{7,3},{8,10},{9,13},{10,... | collective-permute-start | bytes 4325384 | tf_op jit(solution)/shard_map/ppermute | solution.py:165
  28.6 21.3 %collective-permute-start.1 = (f32[384,256]{1,0:T(8,128)}, f32[384,256]{1,0:T(8,128)S(1)}, u32[]{:S(2)}, u32[]{:S(2)}) collective-permute-start(f32[384,256]{1,0:T(8,128)} %fusion.34), channel_id=1, source_target_pairs={{0,8},{1,9},{2,10},{3,11},{4,12},{5,13},{6,14},{7,15}} | collective-permute-start | bytes 1179656 | tf_op jit(solution)/shard_map/ppermute | solution.py:165
  33.4 21.3 %collective-permute-start.4 = (f32[384,256]{1,0:T(8,128)S(1)}, f32[384,256]{1,0:T(8,128)S(1)}, u32[]{:S(2)}, u32[]{:S(2)}) collective-permute-start(f32[384,256]{1,0:T(8,128)S(1)} %fusion.26), channel_id=1, source_target_pairs={{24,16},{25,17},{26,18},{27,19},{28,20},{29,21},{30,22},{31,23}} | collective-permute-start | bytes 1179656 | tf_op jit(solution)/shard_map/ppermute | solution.py:165
  37.2 35.1 %collective-permute-start.17 = (f32[1408,256]{1,0:T(8,128)}, f32[1408,256]{1,0:T(8,128)}, u32[]{:S(2)}, u32[]{:S(2)}) collective-permute-start(f32[1408,256]{1,0:T(8,128)} %fusion.10), channel_id=1, source_target_pairs={{0,2},{1,5},{2,0},{3,7},{4,6},{5,1},{6,4},{7,3},{8,10},{9,13},{10,... | collective-permute-start | bytes 4325384 | tf_op jit(solution)/shard_map/ppermute | solution.py:165
  46.8 28.1 %collective-permute-start.19 = (f32[1408,256]{1,0:T(8,128)}, f32[1408,256]{1,0:T(8,128)}, u32[]{:S(2)}, u32[]{:S(2)}) collective-permute-start(f32[1408,256]{1,0:T(8,128)} %convolution_add_fusion), channel_id=1, source_target_pairs={{0,4},{1,3},{2,6},{3,1},{4,0},{5,7},{6,2},{7,5},{8,12},{9,11},{10,... | collective-permute-start | bytes 4325384 | tf_op jit(solution)/shard_map/ppermute | solution.py:165
  49.9 338.3 %all-reduce.5.cloned.1.call-start = ((), (), s32[]{:S(2)}) async-start(), calls=%async_computation.1 | async-start | bytes 524288 | tf_op jit(solution)/shard_map/psum | solution.py:244
  51.2 12.6 %collective-permute-start.2 = (f32[384,256]{1,0:T(8,128)S(1)}, f32[384,256]{1,0:T(8,128)S(1)}, u32[]{:S(2)}, u32[]{:S(2)}) collective-permute-start(f32[384,256]{1,0:T(8,128)S(1)} %convolution_add_fusion.6), channel_id=1, source_target_pairs={{0,8},{1,9},{2,10},{3,11},{4,12},{5,13},{6,14},{7,15},{8,16},{9,17... | collective-permute-start | bytes 1179656 | tf_op jit(solution)/shard_map/ppermute | solution.py:165
  56.1 13.5 %collective-permute-start.5 = (f32[384,256]{1,0:T(8,128)S(1)}, f32[384,256]{1,0:T(8,128)S(1)}, u32[]{:S(2)}, u32[]{:S(2)}) collective-permute-start(f32[384,256]{1,0:T(8,128)S(1)} %convolution_add_fusion.5), channel_id=1, source_target_pairs={{16,8},{17,9},{18,10},{19,11},{20,12},{21,13},{22,14},{23,15},{24,... | collective-permute-start | bytes 1179656 | tf_op jit(solution)/shard_map/ppermute | solution.py:165
  65.2 16.4 %collective-permute-start.3 = (f32[384,256]{1,0:T(8,128)S(1)}, f32[384,256]{1,0:T(8,128)S(1)}, u32[]{:S(2)}, u32[]{:S(2)}) collective-permute-start(f32[384,256]{1,0:T(8,128)S(1)} %fusion.39), channel_id=1, source_target_pairs={{0,8},{1,9},{2,10},{3,11},{4,12},{5,13},{6,14},{7,15},{8,16},{9,17... | collective-permute-start | bytes 1179656 | tf_op jit(solution)/shard_map/ppermute | solution.py:165
  70.9 10.9 %collective-permute-start.6 = (f32[384,256]{1,0:T(8,128)S(1)}, f32[384,256]{1,0:T(8,128)S(1)}, u32[]{:S(2)}, u32[]{:S(2)}) collective-permute-start(f32[384,256]{1,0:T(8,128)S(1)} %fusion.31), channel_id=1, source_target_pairs={{8,0},{9,1},{10,2},{11,3},{12,4},{13,5},{14,6},{15,7},{16,8},{17,9... | collective-permute-start | bytes 1179656 | tf_op jit(solution)/shard_map/ppermute | solution.py:165
  77.8 12.2 %collective-permute-start.20 = (f32[352,256]{1,0:T(8,128)S(1)}, f32[352,256]{1,0:T(8,128)S(1)}, u32[]{:S(2)}, u32[]{:S(2)}) collective-permute-start(f32[352,256]{1,0:T(8,128)S(1)} %constant_dynamic-slice_fusion.1), channel_id=1, source_target_pairs={{0,8},{1,9},{2,10},{3,11},{4,12},{5,13},{6,14},{7,15}} | collective-permute-start | bytes 1081352 | tf_op jit(solution)/shard_map/ppermute | solution.py:165
  82.0 84.7 %collective-permute-start.7 = (f32[192,256]{1,0:T(8,128)S(1)}, f32[192,256]{1,0:T(8,128)S(1)}, u32[]{:S(2)}, u32[]{:S(2)}) collective-permute-start(f32[192,256]{1,0:T(8,128)S(1)} %constant_dynamic-slice_fusion.3), channel_id=1, source_target_pairs={{0,2},{1,5},{2,0},{3,7},{4,6},{5,1},{6,4},{7,3},{8,10},{9,13},{10,... | collective-permute-start | bytes 589832 | tf_op jit(solution)/shard_map/ppermute | solution.py:165
  90.8 77.5 %collective-permute-start.21 = (f32[352,256]{1,0:T(8,128)}, f32[352,256]{1,0:T(8,128)}, u32[]{:S(2)}, u32[]{:S(2)}) collective-permute-start(f32[352,256]{1,0:T(8,128)} %dynamic-slice_add_fusion.2), channel_id=1, source_target_pairs={{0,8},{1,9},{2,10},{3,11},{4,12},{5,13},{6,14},{7,15},{8,16},{9,17... | collective-permute-start | bytes 1081352 | tf_op jit(solution)/shard_map/ppermute | solution.py:165
  157.9 0.9 copy-start
  166.8 4.7 %collective-permute-start.8 = (f32[96,256]{1,0:T(8,128)S(1)}, f32[96,256]{1,0:T(8,128)S(1)}, u32[]{:S(2)}, u32[]{:S(2)}) collective-permute-start(f32[96,256]{1,0:T(8,128)S(1)} %constant_dynamic-slice_fusion.2), channel_id=1, source_target_pairs={{0,4},{1,3},{2,6},{3,1},{4,0},{5,7},{6,2},{7,5},{8,12},{9,11},{10,... | collective-permute-start | bytes 294920 | tf_op jit(solution)/shard_map/ppermute | solution.py:165
  170.1 3.6 collective-permute-start.23
  171.9 14.0 %copy-start.6 = (f32[352,256]{1,0:T(8,128)S(1)}, f32[352,256]{1,0:T(8,128)}, u32[]{:S(2)}) copy-start(f32[352,256]{1,0:T(8,128)} %get-tuple-element.2) | copy-start | bytes 1081348
  172.2 5.6 %collective-permute-start.9 = (f32[96,256]{1,0:T(8,128)S(1)}, f32[96,256]{1,0:T(8,128)S(1)}, u32[]{:S(2)}, u32[]{:S(2)}) collective-permute-start(f32[96,256]{1,0:T(8,128)S(1)} %get-tuple-element.9), channel_id=1, source_target_pairs={{0,4},{1,3},{2,6},{3,1},{4,0},{5,7},{6,2},{7,5},{8,12},{9,11},{10,... | collective-permute-start | bytes 294920 | tf_op jit(solution)/shard_map/ppermute | solution.py:165
  174.5 16.8 %collective-permute-start.24 = (f32[352,256]{1,0:T(8,128)}, f32[352,256]{1,0:T(8,128)}, u32[]{:S(2)}, u32[]{:S(2)}) collective-permute-start(f32[352,256]{1,0:T(8,128)} %dynamic-slice_add_fusion), channel_id=1, source_target_pairs={{16,8},{17,9},{18,10},{19,11},{20,12},{21,13},{22,14},{23,15},{24,... | collective-permute-start | bytes 1081352 | tf_op jit(solution)/shard_map/ppermute | solution.py:165
  177.8 5.8 %collective-permute-start.10 = (f32[192,256]{1,0:T(8,128)S(1)}, f32[192,256]{1,0:T(8,128)}, u32[]{:S(2)}, u32[]{:S(2)}) collective-permute-start(f32[192,256]{1,0:T(8,128)S(1)} %constant_dynamic-update-slice_fusion.8), channel_id=1, source_target_pairs={{0,2},{1,5},{2,0},{3,7},{4,6},{5,1},{6,4},{7,3},{8,10},{9,13},{10,... | collective-permute-start | bytes 589832 | tf_op jit(solution)/shard_map/ppermute | solution.py:165
  184.6 17.0 %collective-permute-start.12 = (f32[384,256]{1,0:T(8,128)S(1)}, f32[384,256]{1,0:T(8,128)}, u32[]{:S(2)}, u32[]{:S(2)}) collective-permute-start(f32[384,256]{1,0:T(8,128)S(1)} %constant_dynamic-update-slice_fusion.6), channel_id=1, source_target_pairs={{8,0},{9,1},{10,2},{11,3},{12,4},{13,5},{14,6},{15,7},{16,8},{17,9... | collective-permute-start | bytes 1179656 | tf_op jit(solution)/shard_map/ppermute | solution.py:165
  185.9 17.0 %collective-permute-start.22 = (f32[352,256]{1,0:T(8,128)S(1)}, f32[352,256]{1,0:T(8,128)}, u32[]{:S(2)}, u32[]{:S(2)}) collective-permute-start(f32[352,256]{1,0:T(8,128)S(1)} %copy-done.6), channel_id=1, source_target_pairs={{0,8},{1,9},{2,10},{3,11},{4,12},{5,13},{6,14},{7,15},{8,16},{9,17... | collective-permute-start | bytes 1081352 | tf_op jit(solution)/shard_map/ppermute | solution.py:165
  193.0 14.2 %collective-permute-start.25 = (f32[352,256]{1,0:T(8,128)}, f32[352,256]{1,0:T(8,128)}, u32[]{:S(2)}, u32[]{:S(2)}) collective-permute-start(f32[352,256]{1,0:T(8,128)} %dynamic-slice_add_fusion.1), channel_id=1, source_target_pairs={{8,0},{9,1},{10,2},{11,3},{12,4},{13,5},{14,6},{15,7},{16,8},{17,9... | collective-permute-start | bytes 1081352 | tf_op jit(solution)/shard_map/ppermute | solution.py:165
  194.3 16.4 %collective-permute-start.11 = (f32[384,256]{1,0:T(8,128)S(1)}, f32[384,256]{1,0:T(8,128)}, u32[]{:S(2)}, u32[]{:S(2)}) collective-permute-start(f32[384,256]{1,0:T(8,128)S(1)} %constant_dynamic-update-slice_fusion.6), channel_id=1, source_target_pairs={{0,8},{1,9},{2,10},{3,11},{4,12},{5,13},{6,14},{7,15},{8,16},{9,17... | collective-permute-start | bytes 1179656 | tf_op jit(solution)/shard_map/ppermute | solution.py:165
  201.6 14.3 %collective-permute-start.13 = (f32[384,256]{1,0:T(8,128)}, f32[384,256]{1,0:T(8,128)}, u32[]{:S(2)}, u32[]{:S(2)}) collective-permute-start(f32[384,256]{1,0:T(8,128)} %collective-permute-done.12), channel_id=1, source_target_pairs={{8,0},{9,1},{10,2},{11,3},{12,4},{13,5},{14,6},{15,7},{16,8},{17,9... | collective-permute-start | bytes 1179656 | tf_op jit(solution)/shard_map/ppermute | solution.py:165
  209.3 32.3 %copy-start.1 = (f32[352,256]{1,0:T(8,128)}, f32[352,256]{1,0:T(8,128)S(1)}, u32[]{:S(2)}) copy-start(f32[352,256]{1,0:T(8,128)S(1)} %get-tuple-element.7) | copy-start | bytes 1081348
  209.3 15.2 %collective-permute-start.27 = (f32[352,256]{1,0:T(8,128)S(1)}, f32[352,256]{1,0:T(8,128)}, u32[]{:S(2)}, u32[]{:S(2)}) collective-permute-start(f32[352,256]{1,0:T(8,128)S(1)} %get-tuple-element.7), channel_id=1, source_target_pairs={{8,0},{9,1},{10,2},{11,3},{12,4},{13,5},{14,6},{15,7},{16,8},{17,9... | collective-permute-start | bytes 1081352 | tf_op jit(solution)/shard_map/ppermute | solution.py:165
  210.7 31.7 %collective-permute-start.15 = (f32[384,256]{1,0:T(8,128)}, f32[384,256]{1,0:T(8,128)}, u32[]{:S(2)}, u32[]{:S(2)}) collective-permute-start(f32[384,256]{1,0:T(8,128)} %collective-permute-done.11), channel_id=1, source_target_pairs={{8,16},{9,17},{10,18},{11,19},{12,20},{13,21},{14,22},{15,23},{16,... | collective-permute-start | bytes 1179656 | tf_op jit(solution)/shard_map/ppermute | solution.py:165
  215.9 27.9 %collective-permute-start.14 = (f32[384,256]{1,0:T(8,128)}, f32[384,256]{1,0:T(8,128)S(1)}, u32[]{:S(2)}, u32[]{:S(2)}) collective-permute-start(f32[384,256]{1,0:T(8,128)} %collective-permute-done.13), channel_id=1, source_target_pairs={{8,0},{9,1},{10,2},{11,3},{12,4},{13,5},{14,6},{15,7}} | collective-permute-start | bytes 1179656 | tf_op jit(solution)/shard_map/ppermute | solution.py:165
  217.2 10.8 %collective-permute-start.26 = (f32[352,256]{1,0:T(8,128)S(1)}, f32[352,256]{1,0:T(8,128)S(1)}, u32[]{:S(2)}, u32[]{:S(2)}) collective-permute-start(f32[352,256]{1,0:T(8,128)S(1)} %get-tuple-element.7), channel_id=1, source_target_pairs={{0,8},{1,9},{2,10},{3,11},{4,12},{5,13},{6,14},{7,15},{8,16},{9,17... | collective-permute-start | bytes 1081352 | tf_op jit(solution)/shard_map/ppermute | solution.py:165
  224.5 12.3 %collective-permute-start.28 = (f32[352,256]{1,0:T(8,128)}, f32[352,256]{1,0:T(8,128)S(1)}, u32[]{:S(2)}, u32[]{:S(2)}) collective-permute-start(f32[352,256]{1,0:T(8,128)} %collective-permute-done.27), channel_id=1, source_target_pairs={{8,0},{9,1},{10,2},{11,3},{12,4},{13,5},{14,6},{15,7},{16,8},{17,9... | collective-permute-start | bytes 1081352 | tf_op jit(solution)/shard_map/ppermute | solution.py:165
  228.1 17.2 %collective-permute-start.30 = (f32[352,256]{1,0:T(8,128)S(1)}, f32[352,256]{1,0:T(8,128)S(1)}, u32[]{:S(2)}, u32[]{:S(2)}) collective-permute-start(f32[352,256]{1,0:T(8,128)S(1)} %collective-permute-done.26), channel_id=1, source_target_pairs={{8,16},{9,17},{10,18},{11,19},{12,20},{13,21},{14,22},{15,23},{16,... | collective-permute-start | bytes 1081352 | tf_op jit(solution)/shard_map/ppermute | solution.py:165
  236.8 9.4 %collective-permute-start.29 = (f32[352,256]{1,0:T(8,128)S(1)}, f32[352,256]{1,0:T(8,128)S(1)}, u32[]{:S(2)}, u32[]{:S(2)}) collective-permute-start(f32[352,256]{1,0:T(8,128)S(1)} %collective-permute-done.28), channel_id=1, source_target_pairs={{8,0},{9,1},{10,2},{11,3},{12,4},{13,5},{14,6},{15,7}} | collective-permute-start | bytes 1081352 | tf_op jit(solution)/shard_map/ppermute | solution.py:165
  242.4 14.8 %collective-permute-start.16 = (f32[384,256]{1,0:T(8,128)}, f32[384,256]{1,0:T(8,128)}, u32[]{:S(2)}, u32[]{:S(2)}) collective-permute-start(f32[384,256]{1,0:T(8,128)} %collective-permute-done.15), channel_id=1, source_target_pairs={{16,24},{17,25},{18,26},{19,27},{20,28},{21,29},{22,30},{23,31}} | collective-permute-start | bytes 1179656 | tf_op jit(solution)/shard_map/ppermute | solution.py:165
  245.3 1.0 collective-permute-start.31
  247.4 142.4 %collective-permute-start.32 = (f32[1408,256]{1,0:T(8,128)S(1)}, f32[1408,256]{1,0:T(8,128)S(1)}, u32[]{:S(2)}, u32[]{:S(2)}) collective-permute-start(f32[1408,256]{1,0:T(8,128)S(1)} %add_dynamic-update-slice_fusion), channel_id=1, source_target_pairs={{0,4},{1,3},{2,6},{3,1},{4,0},{5,7},{6,2},{7,5},{8,12},{9,11},{10,... | collective-permute-start | bytes 4325384 | tf_op jit(solution)/shard_map/ppermute | solution.py:165
  250.7 4.3 %copy-start.2 = (f32[352,256]{1,0:T(8,128)S(1)}, f32[352,256]{1,0:T(8,128)}, u32[]{:S(2)}) copy-start(f32[352,256]{1,0:T(8,128)} %copy-done.1) | copy-start | bytes 1081348
  256.6 140.5 %collective-permute-start.33 = (f32[1408,256]{1,0:T(8,128)S(1)}, f32[1408,256]{1,0:T(8,128)}, u32[]{:S(2)}, u32[]{:S(2)}) collective-permute-start(f32[1408,256]{1,0:T(8,128)S(1)} %add_dynamic-update-slice_fusion), channel_id=1, source_target_pairs={{0,2},{1,5},{2,0},{3,7},{4,6},{5,1},{6,4},{7,3},{8,10},{9,13},{10,... | collective-permute-start | bytes 4325384 | tf_op jit(solution)/shard_map/ppermute | solution.py:165
  388.2 3.1 copy-start.4
  389.8 19.1 %collective-permute-start.34 = (f32[1408,256]{1,0:T(8,128)S(1)}, f32[1408,256]{1,0:T(8,128)S(1)}, u32[]{:S(2)}, u32[]{:S(2)}) collective-permute-start(f32[1408,256]{1,0:T(8,128)S(1)} %collective-permute-done.32), channel_id=1, source_target_pairs={{0,2},{1,5},{2,0},{3,7},{4,6},{5,1},{6,4},{7,3},{8,10},{9,13},{10,... | collective-permute-start | bytes 4325384 | tf_op jit(solution)/shard_map/ppermute | solution.py:165
  400.6 10.2 %copy-start.3 = (f32[512,256]{1,0:T(8,128)S(1)}, f32[512,256]{1,0:T(8,128)}, u32[]{:S(2)}) copy-start(f32[512,256]{1,0:T(8,128)} %convolution_add_fusion.3) | copy-start | bytes 1572868
  412.4 3.8 collective-permute-start.35
Sparse Core Ops, SparseCore 0:
  50.0 107.8 all-reduce.2
  256.7 131.4 all-reduce.4

commit v2 on v1

--- a/solution.py
+++ b/solution.py
@@ -138,142 +138,199 @@
     return refine(codes_mid, proj_two, gram_new), dict_out
 
 
-DEPTH = 4
-
-
-def device(z, y, x, c):
-    return (z * 4 + y * 2 + x) * 2 + c
-
-
-def every():
-    return [(z, y, x, c) for z in range(DEPTH) for y in range(2) for x in range(2) for c in range(2)]
-
-
-def flip(which):
-    pairs = []
-    for z, y, x, c in every():
-        along_x = (c == 0) == (which == "first")
-        pairs.append((device(z, y, x, c), device(z, y, 1 - x, c) if along_x else device(z, 1 - y, x, c)))
-    return pairs
-
-
-def along(sources, step):
-    return [(device(z, y, x, c), device(z + step, y, x, c)) for z, y, x, c in every() if z in sources]
-
-
-def send(value, pairs):
-    return lax.ppermute(value, BOTH, pairs)
-
-
-def line_sum(get, z):
-    right = left = None
-    for s in range(1, DEPTH):
-        out_r = get(jnp.minimum(DEPTH - s + z, DEPTH - 1), right)
-        out_l = get(jnp.maximum(s - DEPTH + z, 0), left)
-        right = send(out_r, along(range(0, s), 1))
-        left = send(out_l, along(range(DEPTH - s, DEPTH), -1))
-    return get(z, right) + left
-
-
-def line_gather(own, z):
-    rights, lefts = [own], [own]
-    for s in range(1, DEPTH):
-        rights.append(send(rights[-1], along(range(s - 1, DEPTH - 1), 1)))
-        lefts.append(send(lefts[-1], along(range(1, DEPTH - s + 1), -1)))
-    return [own] + [rights[s] + lefts[DEPTH - s] for s in range(1, DEPTH)]
-
-
-def place(blocks, total):
-    out = jnp.zeros((total, blocks[0][0].shape[1]), f32)
-    for value, row in blocks:
-        out = lax.dynamic_update_slice_in_dim(out, value, row, 0)
-    return out
+def update(codes, sums, tokens, precision=HIGHEST):
+    proj, gram = sums[:tokens], sums[tokens:]
+    numer = jnp.maximum(proj, 0.0) + dot(codes, jnp.maximum(-gram, 0.0), precision=precision)
+    denom = jnp.maximum(-proj, 0.0) + dot(codes, jnp.maximum(gram, 0.0), precision=precision)
+    return codes * jnp.sqrt(numer / jnp.maximum(denom, floor_value))
+
+
+def first_kernel(core_ref, codes_ref, mine_ref, theirs_ref, mid_ref, low_ref, gram_ref):
+    mid = update(codes_ref[...], mine_ref[...] + theirs_ref[...], codes_ref.shape[0])
+    low = mid.astype(bf16)
+    mid_ref[...] = mid
+    low_ref[...] = low
+    half = low.shape[1] // 2
+    side = jnp.where(core_ref[0] == 0, mid[:, :half], mid[:, half:]).astype(bf16)
+    gram_ref[...] = dot(side.T, low)
+
+
+def first_update(core, codes, mine, theirs):
+    tokens, comp = codes.shape
+    whole = pl.BlockSpec(memory_space=pltpu.VMEM)
+    return pl.pallas_call(
+        first_kernel,
+        out_shape=[
+            jax.ShapeDtypeStruct((tokens, comp), f32),
+            jax.ShapeDtypeStruct((tokens, comp), bf16),
+            jax.ShapeDtypeStruct((comp // 2, comp), f32),
+        ],
+        in_specs=[pl.BlockSpec(memory_space=pltpu.SMEM), whole, whole, whole],
+        out_specs=[whole, whole, whole],
+        compiler_params=pltpu.CompilerParams(vmem_limit_bytes=48 * 2**20),
+    )(core, codes, mine, theirs)
+
+
+def second_kernel(codes_ref, mine_ref, theirs_ref, out_ref):
+    out_ref[...] = update(codes_ref[...], mine_ref[...] + theirs_ref[...], codes_ref.shape[0])
+
+
+def second_update(codes, mine, theirs):
+    return pl.pallas_call(
+        second_kernel,
+        out_shape=jax.ShapeDtypeStruct(codes.shape, f32),
+        compiler_params=pltpu.CompilerParams(vmem_limit_bytes=48 * 2**20),
+    )(codes, mine, theirs)
+
+
+def rows_kernel(mine_ref, theirs_ref, inverse_ref, out_ref):
+    inverse = inverse_ref[...]
+    out_ref[...] = dot(dot(mine_ref[...] + theirs_ref[...], inverse, OVER_COLS, HIGHEST), inverse, precision=HIGHEST)
+
+
+def solve_sum(mine, theirs, inverse):
+    return pl.pallas_call(
+        rows_kernel,
+        out_shape=jax.ShapeDtypeStruct(mine.shape, f32),
+        compiler_params=pltpu.CompilerParams(vmem_limit_bytes=48 * 2**20),
+    )(mine, theirs, inverse)
+
+
+def absorb_kernel(count, fresh, *refs):
+    row_ref, acts_ref = refs[:2]
+    values = refs[2 : 2 + count]
+    refs = refs[2 + count :]
+    if not fresh:
+        sums_ref, refs = refs[0], refs[2:]
+    out_ref, dict_ref = refs[:2]
+    buffers, in_sem, out_sem = refs[2 : 2 + count], refs[2 + count], refs[3 + count]
+    tokens = acts_ref.shape[0]
+    ins, outs = [], []
+    for k, value in enumerate(values):
+        row = pl.multiple_of(row_ref[k], 128)
+        rows = value.shape[0]
+        ins.append(pltpu.make_async_copy(acts_ref.at[:, pl.ds(row, rows)], buffers[k], in_sem.at[k]))
+        outs.append(pltpu.make_async_copy(value, dict_ref.at[pl.ds(row, rows), :], out_sem.at[k]))
+        ins[k].start()
+        outs[k].start()
+    proj, gram = (0.0, 0.0) if fresh else (sums_ref[:tokens, :], sums_ref[tokens:, :])
+    for k, value in enumerate(values):
+        block = value[...]
+        high = block.astype(bf16)
+        low = (block - high.astype(f32)).astype(bf16)
+        turned = high.T
+        cross = dot(turned, low)
+        gram = gram + (dot(turned, high) + (cross + cross.T))
+        ins[k].wait()
+        proj = proj + dot(buffers[k][...], high)
+    out_ref[:tokens, :] = proj
+    out_ref[tokens:, :] = gram
+    for copy in outs:
+        copy.wait()
+
+
+def absorb(state, acts, blocks):
+    tokens, hidden = acts.shape
+    comp = blocks[0][0].shape[1]
+    count = len(blocks)
+    values = [value for value, _ in blocks]
+    rows = jnp.stack([row for _, row in blocks]).astype(jnp.int32)
+    whole, anywhere = pl.BlockSpec(memory_space=pltpu.VMEM), pl.BlockSpec(memory_space=pl.ANY)
+    held = [] if state is None else list(state)
+    total = sum(value.shape[0] for value in values)
+    return pl.pallas_call(
+        functools.partial(absorb_kernel, count, state is None),
+        out_shape=[jax.ShapeDtypeStruct((tokens + comp, comp), f32), jax.ShapeDtypeStruct((hidden, comp), f32)],
+        in_specs=[pl.BlockSpec(memory_space=pltpu.SMEM), anywhere] + [whole] * count + ([whole, anywhere] if held else []),
+        out_specs=[whole, anywhere],
+        scratch_shapes=[pltpu.VMEM((tokens, value.shape[0]), bf16) for value in values]
+        + [pltpu.SemaphoreType.DMA((count,)), pltpu.SemaphoreType.DMA((count,))],
+        input_output_aliases={2 + count: 0, 3 + count: 1} if held else {},
+        compiler_params=pltpu.CompilerParams(vmem_limit_bytes=48 * 2**20),
+        cost_estimate=pl.CostEstimate(
+            flops=2 * total * comp * (tokens + 2 * comp), bytes_accessed=total * (2 * tokens + 8 * comp), transcendentals=0
+        ),
+    )(rows, acts, *values, *held)
+
+
+def flips(bits):
+    return [(t * 2 + c, (t ^ bits[c]) * 2 + c) for t in range(16) for c in range(2)]
+
+
+X, Y, ZL, ZH = 1, 2, 4, 8
+ALONG = {"first": (X, Y), "second": (Y, X), "near": (ZL, ZL), "far": (ZH, ZH), "x": (X, X), "y": (Y, Y)}
+
+
+def swap(value, along):
+    return lax.ppermute(value, BOTH, flips(ALONG[along]))
 
 
 def meshed(acts, dictionary, codes):
     tokens, hidden = acts.shape
     tok, core = lax.axis_index("tok"), lax.axis_index("hid")
-    z, y, x = tok // 4, (tok // 2) % 2, tok % 2
-    p = jnp.where(core == 0, x, y)
-    q = jnp.where(core == 0, y, x)
-    first, second = flip("first"), flip("second")
-    swap = [(0, 1), (1, 0)]
+
+    def other_core(value):
+        return lax.ppermute(value, "hid", [(0, 1), (1, 0)])
+
+    def bit(along):
+        on_0, on_1 = ALONG[along]
+        return jnp.where(core == 0, tok & on_0, tok & on_1) // jnp.where(core == 0, on_0, on_1)
 
     sums = project(acts, dictionary)
-    sums = sums + lax.ppermute(sums, "hid", swap)
-    codes_mid = refine(codes, sums[:tokens], sums[tokens:])
-    codes_low = codes_mid.astype(bf16)
-    gram_codes = lax.psum(dot(codes_low, codes_low, OVER_ROWS), "tok")
-    inverse = factor_inverse(gram_codes)
-
-    wide = (hidden * 11 // 14) // 512 * 512
-    narrow = hidden - wide
-    quarter, stripe = wide // 4, narrow // 4
-
-    def cross_of(row, rows, add=None):
-        out = dot(lax.dynamic_slice_in_dim(acts, row, rows, 1), codes_low, OVER_ROWS)
-        return out if add is None else out + add
-
-    def quarter_row(a, b):
-        return a * (2 * quarter) + b * quarter
-
-    got_1 = send(cross_of(quarter_row(1 - p, 1 - q), quarter), first)
-    narrow_mine = line_sum(lambda j, add: cross_of(wide + j * stripe, stripe, add), z)
-    got_2 = send(cross_of(quarter_row(1 - p, q), quarter), first)
-    got_3 = send(cross_of(quarter_row(p, 1 - q), quarter, got_1), second)
-    wide_mine = cross_of(quarter_row(p, q), quarter, got_2) + got_3
-
-    def half_of(value, which):
-        rows = value.shape[0] // 2
+    codes_mid, codes_low, gram = first_update(jnp.reshape(core, (1,)).astype(jnp.int32), codes, sums, other_core(sums))
+    for along in ("x", "y", "near", "far"):
+        gram = gram + swap(gram, along)
+    other = other_core(gram)
+    inverse = factor_inverse(jnp.where(core == 0, jnp.concatenate([gram, other]), jnp.concatenate([other, gram])))
+
+    def cross_of(row, rows):
+        return dot(lax.dynamic_slice_in_dim(acts, row, rows, 1), codes_low, OVER_ROWS)
+
+    def part_of(value, which, parts=2):
+        rows = value.shape[0] // parts
         return lax.dynamic_slice_in_dim(value, which * rows, rows, 0)
 
-    narrow_mine = half_of(narrow_mine, p) + send(half_of(narrow_mine, 1 - p), first)
-    narrow_mine = half_of(narrow_mine, q) + send(half_of(narrow_mine, 1 - q), second)
-
-    piece = quarter // DEPTH
-
-    def wide_block(j, add):
-        value = lax.dynamic_slice_in_dim(wide_mine, j * piece, piece, 0)
-        return value if add is None else value + add
-
-    wide_mine = line_sum(wide_block, z)
-
-    narrow_mine = solve_rows(narrow_mine, inverse)
-    wide_mine = solve_rows(wide_mine, inverse)
-    gram_part = dot(narrow_mine, narrow_mine, OVER_ROWS, HIGHEST) + dot(wide_mine, wide_mine, OVER_ROWS, HIGHEST)
-    gram_new = lax.psum(gram_part, BOTH)
-
-    small = narrow // 16
-    narrow_mine = place([(narrow_mine, q * small), (send(narrow_mine, second), (1 - q) * small)], 2 * small)
-    narrow_mine = place([(narrow_mine, p * 2 * small), (send(narrow_mine, first), (1 - p) * 2 * small)], 4 * small)
-    wide_all = line_gather(wide_mine, z)
-    own = place([(value, (z - s) % DEPTH * piece) for s, value in enumerate(wide_all)], quarter)
-    narrow_all = line_gather(narrow_mine, z)
-    from_second = send(own, second)
-    from_first = send(own, first)
-    from_far = send(from_second, first)
-
-    blocks = [(value, wide + (z - s) % DEPTH * stripe) for s, value in enumerate(narrow_all)]
-    blocks += [
-        (own, quarter_row(p, q)),
-        (from_second, quarter_row(p, 1 - q)),
-        (from_first, quarter_row(1 - p, q)),
-        (from_far, quarter_row(1 - p, 1 - q)),
+    def joined(mine, theirs, which):
+        return jnp.where(which == 0, jnp.concatenate([mine, theirs]), jnp.concatenate([theirs, mine]))
+
+    unit = hidden // 7
+    parts = [
+        (0, 3 * unit, ("first", "second", "near", "far")),
+        (3 * unit, 2 * unit, ("first", "second", "near", "far")),
+        (5 * unit, 2 * unit, ("near", "first", "second", "far")),
     ]
-    dict_out = place(blocks, hidden)
-    proj_two = None
-    for value, row in blocks:
-        part = dot(lax.dynamic_slice_in_dim(acts, row, value.shape[0], 1), value.astype(bf16))
-        proj_two = part if proj_two is None else proj_two + part
-    proj_two = proj_two + lax.ppermute(proj_two, "hid", swap)
-    return refine(codes_mid, proj_two, gram_new), dict_out
+
+    solved = []
+    for start, rows, order in parts:
+        a, b, c, d = (bit(along) for along in order)
+        quarter = rows // 4
+        got = swap(cross_of(start + (1 - a) * 2 * quarter, 2 * quarter), order[0])
+        out = cross_of(start + a * 2 * quarter + (1 - b) * quarter, quarter) + part_of(got, 1 - b)
+        held = cross_of(start + a * 2 * quarter + b * quarter, quarter) + part_of(got, b)
+        held = held + swap(out, order[1])
+        held = part_of(held, c) + swap(part_of(held, 1 - c), order[2])
+        solved.append(solve_sum(part_of(held, d), swap(part_of(held, 1 - d), order[3]), inverse))
+
+    state = None
+    for (start, rows, order), mine in zip(parts, solved):
+        a, b, c, d = (bit(along) for along in order)
+        quarter = rows // 4
+        mine = joined(mine, swap(mine, order[3]), d)
+        mine = joined(mine, swap(mine, order[2]), c)
+        theirs = swap(mine, order[1])
+        here, there = start + a * 2 * quarter, start + (1 - a) * 2 * quarter
+        state = absorb(state, acts, [(mine, here + b * quarter), (theirs, here + (1 - b) * quarter)])
+        far = [(swap(mine, order[0]), there + b * quarter), (swap(theirs, order[0]), there + (1 - b) * quarter)]
+        state = absorb(state, acts, far)
+    sums, dict_out = state
+    return second_update(codes_mid, sums, other_core(sums)), dict_out
 
 
 def solution(mesh):
     tok, hid = mesh.shape["tok"], mesh.shape["hid"]
 
     def per_device(acts, dictionary, codes):
-        if tok == 16 and hid == 2 and acts.shape[1] % 512 == 0:
+        if tok == 16 and hid == 2 and acts.shape[1] % (7 * 1024) == 0:
             return meshed(acts, dictionary, codes)
         return plain(acts, dictionary, codes, acts.shape[1] % tok == 0)
 

time: 426 us -> 207 us (0.49)
  waiting for transfers between devices: 248 us -> 97.3 us
  matrix products: 46 us -> 14.2 us
  Pallas kernels: 17.3 us -> 43.9 us
  starting transfers between devices: 72.5 us -> 46.6 us
  between operations: 14.8 us -> 1.04 us
  local copies, waits for them, and re-layouts: 12.6 us -> 0.98 us
  other arithmetic: 13.2 us -> 1.77 us
    psum x2 -> x0, waiting for transfers between devices: 191 us -> none  [the longest x1 129 us: meshed(): gram_new = lax.psum(gram_part, BOTH)]
    ppermute x36 -> x34, waiting for transfers between devices: 56.8 us -> 97.3 us  [the longest x31 93.5 us: swap(): return lax.ppermute(value, BOTH, flips(ALONG[along]))]
    dot_general x30 -> x9, matrix products: 46 us -> 14.2 us  [dot(): lax.dot_general(left, right, dims, precision=precision, preferred_element...]
    pallas_call x0 -> x11, Pallas kernels: none -> 26.6 us  [the longest x6 20.6 us: absorb(): pl.pallas_call(functools.partial(absorb_kernel, count, state is None), ou...]
    ppermute x36 -> x34, starting transfers between devices: 72.4 us -> 46.6 us  [the longest x31 45.1 us: swap(): return lax.ppermute(value, BOTH, flips(ALONG[along]))]
    dynamic_update_slice x8 -> x0, local copies, waits for them, and re-layouts: 7.89 us -> none  [place(): out = lax.dynamic_update_slice_in_dim(out, value, row, 0)]
    dynamic_update_slice x6 -> x0, other arithmetic: 6.75 us -> none  [place(): out = lax.dynamic_update_slice_in_dim(out, value, row, 0)]
  transfers between devices with their start and end apart: 38 -> 34, of which waited for: 17 -> 20; matrix products, arithmetic and copies ran while one was open for 15% -> 7% of each run, Pallas kernels for 2% -> 14%
where the time goes in v2:
time: 207 us; the launch traced here: 206 us
  waiting for transfers between devices  97.3 us (47%)
  starting transfers between devices  46.6 us (23%)
  Pallas kernels  43.9 us (21%)
  matrix products  14.2 us (7%)
    ppermute x31, waiting for transfers between devices, swap(): return lax.ppermute(value, BOTH, flips(ALONG[along]))  93.5 us
    ppermute x31, starting transfers between devices, swap(): return lax.ppermute(value, BOTH, flips(ALONG[along]))  45.1 us
    pallas_call x6, Pallas kernels, absorb(): pl.pallas_call(functools.partial(absorb_kernel, count, state is None), ou...  20.6 us
    dot_general x9, matrix products, dot(): lax.dot_general(left, right, dims, precision=precision, preferred_element...  14.2 us
    pallas_call x1, Pallas kernels, project(): pl.pallas_call(project_kernel, out_shape=jax.ShapeDtypeStruct((tokens + c...  9.5 us
    pallas_call x1, Pallas kernels, factor_inverse(): pl.pallas_call(factor_kernel, out_shape=jax.ShapeDtypeStruct(gram.shape,...  7.87 us
  transfers between devices with their start and end apart: 34, of which 20 were waited for; matrix products, arithmetic and copies ran while one was open for 7% of the time, Pallas kernels for 14%

profile of v2, /device:TPU:0, one launch (start us, length us, event | category | flops | bytes accessed | tf_op | source)
XLA Modules:
  0.0 205.8 jit_solution(11629312471327968070)
XLA Ops:
  0.6 9.5 %shard_map.50.mine_ref = f32[768,256]{1,0:T(8,128)S(1)} custom-call(bf16[512,7168]{1,0:T(8,128)(2,1)} %refs_1_.11, f32[7168,256]{1,0:T(8,128)} %dict_ref.1), custom_call_target="tpu_custom_call" | custom-call | flops 3758096384 | bytes 14680064 | tf_op jit(solution)/shard_map/pallas_call | solution.py:56
  10.7 1.9 collective-permute-done.theirs_ref
  12.6 1.4 shard_map.51
  14.8 2.0 fusion
  16.9 2.9 %collective-permute-start.24 = (f32[1536,256]{1,0:T(8,128)S(1)}, f32[1536,256]{1,0:T(8,128)S(1)}, u32[]{:S(2)}, u32[]{:S(2)}) collective-permute-start(f32[1536,256]{1,0:T(8,128)S(1)} %fusion), channel_id=1, source_target_pairs={{0,2},{1,5},{2,0},{3,7},{4,6},{5,1},{6,4},{7,3},{8,10},{9,13},{10,... | collective-permute-start | bytes 4718600 | tf_op jit(solution)/shard_map/ppermute | solution.py:265
  19.8 21.1 %collective-permute-done.5 = f32[128,256]{1,0:T(8,128)S(1)} collective-permute-done((f32[128,256]{1,0:T(8,128)S(1)}, f32[128,256]{1,0:T(8,128)S(1)}, u32[]{:S(2)}, u32[]{:S(2)}) %collective-permute-start.5) | collective-permute-done | bytes 131104 | tf_op jit(solution)/shard_map/ppermute | solution.py:265
  41.0 1.4 collective-permute-start.6
  42.3 3.7 %collective-permute-done.6 = f32[128,256]{1,0:T(8,128)S(1)} collective-permute-done((f32[128,256]{1,0:T(8,128)S(1)}, f32[128,256]{1,0:T(8,128)S(1)}, u32[]{:S(2)}, u32[]{:S(2)}) %collective-permute-start.6) | collective-permute-done | bytes 131104 | tf_op jit(solution)/shard_map/ppermute | solution.py:265
  46.0 2.2 %collective-permute-start.7 = (f32[128,256]{1,0:T(8,128)S(1)}, f32[128,256]{1,0:T(8,128)}, u32[]{:S(2)}, u32[]{:S(2)}) collective-permute-start(f32[128,256]{1,0:T(8,128)S(1)} %add.213), channel_id=1, source_target_pairs={{0,8},{1,9},{2,10},{3,11},{4,12},{5,13},{6,14},{7,15},{8,0},{9,1},... | collective-permute-start | bytes 393224 | tf_op jit(solution)/shard_map/ppermute | solution.py:265
  48.2 3.3 %collective-permute-done.7 = f32[128,256]{1,0:T(8,128)} collective-permute-done((f32[128,256]{1,0:T(8,128)S(1)}, f32[128,256]{1,0:T(8,128)}, u32[]{:S(2)}, u32[]{:S(2)}) %collective-permute-start.7) | collective-permute-done | bytes 131104 | tf_op jit(solution)/shard_map/ppermute | solution.py:265
  51.5 0.9 add.214
  52.4 2.9 %collective-permute-start.8 = (f32[128,256]{1,0:T(8,128)S(1)}, f32[128,256]{1,0:T(8,128)S(1)}, u32[]{:S(2)}, u32[]{:S(2)}) collective-permute-start(f32[128,256]{1,0:T(8,128)S(1)} %add.214), channel_id=1, source_target_pairs={{0,16},{1,17},{2,18},{3,19},{4,20},{5,21},{6,22},{7,23},{8,24},{9,... | collective-permute-start | bytes 393224 | tf_op jit(solution)/shard_map/ppermute | solution.py:265
  55.3 1.7 fusion.5
  57.0 1.5 collective-permute-start.15
  58.5 1.2 collective-permute-done.8
  59.9 1.7 fusion.7
  61.6 0.9 collective-permute-start.1
  62.6 1.5 convolution_add_fusion
  64.1 1.4 collective-permute-start.25
  65.5 7.9 %shard_map.52.inverse_ref = f32[256,256]{1,0:T(8,128)S(1)} custom-call(f32[256,256]{1,0:T(8,128)S(1)} %maximum_select_fusion.4.gram_ref), custom_call_target="tpu_custom_call" | custom-call | flops 10000000000 | bytes 524288 | tf_op jit(solution)/shard_map/pallas_call | solution.py:112
  73.4 3.3 %collective-permute-done.15 = f32[1024,256]{1,0:T(8,128)S(1)} collective-permute-done((f32[1024,256]{1,0:T(8,128)S(1)}, f32[1024,256]{1,0:T(8,128)S(1)}, u32[]{:S(2)}, u32[]{:S(2)}) %collective-permute-start.15) | collective-permute-done | bytes 1048608 | tf_op jit(solution)/shard_map/ppermute | solution.py:265
  76.7 1.4 convolution_add_fusion.2
  78.6 1.5 fusion.2
  80.2 4.8 %collective-permute-start.26 = (f32[384,256]{1,0:T(8,128)S(1)}, f32[384,256]{1,0:T(8,128)S(1)}, u32[]{:S(2)}, u32[]{:S(2)}) collective-permute-start(f32[384,256]{1,0:T(8,128)S(1)} %constant_dynamic-slice_fusion.2), channel_id=1, source_target_pairs={{0,8},{1,9},{2,10},{3,11},{4,12},{5,13},{6,14},{7,15},{8,0},{9,1},... | collective-permute-start | bytes 1179656 | tf_op jit(solution)/shard_map/ppermute | solution.py:265
  85.0 2.6 %collective-permute-done.1 = f32[1024,256]{1,0:T(8,128)S(1)} collective-permute-done((f32[1024,256]{1,0:T(8,128)S(1)}, f32[1024,256]{1,0:T(8,128)S(1)}, u32[]{:S(2)}, u32[]{:S(2)}) %collective-permute-start.1) | collective-permute-done | bytes 1048608 | tf_op jit(solution)/shard_map/ppermute | solution.py:265
  87.6 1.4 convolution_add_fusion.4
  89.0 2.0 collective-permute-start.2
  91.0 1.6 fusion.3
  93.1 3.0 %collective-permute-done.26 = f32[384,256]{1,0:T(8,128)S(1)} collective-permute-done((f32[384,256]{1,0:T(8,128)S(1)}, f32[384,256]{1,0:T(8,128)S(1)}, u32[]{:S(2)}, u32[]{:S(2)}) %collective-permute-start.26) | collective-permute-done | bytes 393248 | tf_op jit(solution)/shard_map/ppermute | solution.py:265
  96.1 2.4 %collective-permute-start.27 = (f32[192,256]{1,0:T(8,128)S(1)}, f32[192,256]{1,0:T(8,128)S(1)}, u32[]{:S(2)}, u32[]{:S(2)}) collective-permute-start(f32[192,256]{1,0:T(8,128)S(1)} %get-tuple-element.32), channel_id=1, source_target_pairs={{0,16},{1,17},{2,18},{3,19},{4,20},{5,21},{6,22},{7,23},{8,24},{9,... | collective-permute-start | bytes 589832 | tf_op jit(solution)/shard_map/ppermute | solution.py:265
  98.5 1.4 fusion.4
  99.9 1.0 collective-permute-start.3
  100.9 6.6 %collective-permute-done.27.theirs_ref = f32[192,256]{1,0:T(8,128)S(1)} collective-permute-done((f32[192,256]{1,0:T(8,128)S(1)}, f32[192,256]{1,0:T(8,128)S(1)}, u32[]{:S(2)}, u32[]{:S(2)}) %collective-permute-start.27) | collective-permute-done | bytes 196640 | tf_op jit(solution)/shard_map/ppermute | solution.py:265
  107.5 1.0 shard_map.55
  108.6 9.6 %collective-permute-done.28 = f32[192,256]{1,0:T(8,128)S(1)} collective-permute-done((f32[192,256]{1,0:T(8,128)S(1)}, f32[192,256]{1,0:T(8,128)S(1)}, u32[]{:S(2)}, u32[]{:S(2)}) %collective-permute-start.28) | collective-permute-done | bytes 196640 | tf_op jit(solution)/shard_map/ppermute | solution.py:265
  118.4 3.1 %collective-permute-start.18 = (f32[128,256]{1,0:T(8,128)S(1)}, f32[128,256]{1,0:T(8,128)S(1)}, u32[]{:S(2)}, u32[]{:S(2)}) collective-permute-start(f32[128,256]{1,0:T(8,128)S(1)} %get-tuple-element.34), channel_id=1, source_target_pairs={{0,16},{1,17},{2,18},{3,19},{4,20},{5,21},{6,22},{7,23},{8,24},{9,... | collective-permute-start | bytes 393224 | tf_op jit(solution)/shard_map/ppermute | solution.py:265
  121.6 9.1 %collective-permute-done.18.theirs_ref = f32[128,256]{1,0:T(8,128)S(1)} collective-permute-done((f32[128,256]{1,0:T(8,128)S(1)}, f32[128,256]{1,0:T(8,128)S(1)}, u32[]{:S(2)}, u32[]{:S(2)}) %collective-permute-start.18) | collective-permute-done | bytes 131104 | tf_op jit(solution)/shard_map/ppermute | solution.py:265
  131.5 3.4 %collective-permute-start.19 = (f32[128,256]{1,0:T(8,128)S(1)}, f32[128,256]{1,0:T(8,128)S(1)}, u32[]{:S(2)}, u32[]{:S(2)}) collective-permute-start(f32[128,256]{1,0:T(8,128)S(1)} %shard_map.54), channel_id=1, source_target_pairs={{0,16},{1,17},{2,18},{3,19},{4,20},{5,21},{6,22},{7,23},{8,24},{9,... | collective-permute-start | bytes 393224 | tf_op jit(solution)/shard_map/ppermute | solution.py:265
  135.0 1.2 collective-permute-start.31
  136.9 1.3 collective-permute-start.10
  138.3 6.7 %collective-permute-done.19 = f32[128,256]{1,0:T(8,128)S(1)} collective-permute-done((f32[128,256]{1,0:T(8,128)S(1)}, f32[128,256]{1,0:T(8,128)S(1)}, u32[]{:S(2)}, u32[]{:S(2)}) %collective-permute-start.19) | collective-permute-done | bytes 131104 | tf_op jit(solution)/shard_map/ppermute | solution.py:265
  145.1 2.0 collective-permute-done.10
  147.1 1.5 collective-permute-start.11
  148.6 1.2 collective-permute-start.30
  149.8 2.8 %collective-permute-done.20 = f32[256,256]{1,0:T(8,128)S(1)} collective-permute-done((f32[256,256]{1,0:T(8,128)S(1)}, f32[256,256]{1,0:T(8,128)S(1)}, u32[]{:S(2)}, u32[]{:S(2)}) %collective-permute-start.20) | collective-permute-done | bytes 262176 | tf_op jit(solution)/shard_map/ppermute | solution.py:265
  152.6 1.6 collective-permute-start.22
  154.2 2.1 %collective-permute-done.11 = f32[256,256]{1,0:T(8,128)S(1)} collective-permute-done((f32[256,256]{1,0:T(8,128)S(1)}, f32[256,256]{1,0:T(8,128)S(1)}, u32[]{:S(2)}, u32[]{:S(2)}) %collective-permute-start.11) | collective-permute-done | bytes 262176 | tf_op jit(solution)/shard_map/ppermute | solution.py:265
  156.3 1.6 collective-permute-start.13
  158.6 1.5 collective-permute-start.21
  160.1 7.5 %collective-permute-done.22.refs_3_ = f32[512,256]{1,0:T(8,128)} collective-permute-done((f32[512,256]{1,0:T(8,128)S(1)}, f32[512,256]{1,0:T(8,128)}, u32[]{:S(2)}, u32[]{:S(2)}) %collective-permute-start.22) | collective-permute-done | bytes 524320 | tf_op jit(solution)/shard_map/ppermute | solution.py:265
  167.6 1.5 collective-permute-start.23
  169.2 2.8 %collective-permute-done.13.refs_3_ = f32[512,256]{1,0:T(8,128)} collective-permute-done((f32[512,256]{1,0:T(8,128)S(1)}, f32[512,256]{1,0:T(8,128)}, u32[]{:S(2)}, u32[]{:S(2)}) %collective-permute-start.13) | collective-permute-done | bytes 524320 | tf_op jit(solution)/shard_map/ppermute | solution.py:265
  171.9 2.0 collective-permute-start.14
  174.1 4.0 %shard_map.56 = (f32[768,256]{1,0:T(8,128)S(1)}, f32[7168,256]{1,0:T(8,128)}) custom-call(s32[2]{0:T(128)S(1)} %pad_add_fusion.5.refs_0_, bf16[512,7168]{1,0:T(8,128)(2,1)} %refs_1_.11, f32[768,256]{1,0:T(8,128)S(1)} %maximum_select_fusion.refs_2_, f32[768,256]{1,0:T(8,128)} %collective-permute-done.31.refs_3_), custom_call_target="tpu_custom_call" | custom-call | flops 805306368 | bytes 4718592 | tf_op jit(solution)/shard_map/pallas_call | solution.py:241
  178.1 2.1 %collective-permute-done.32.refs_3_ = f32[768,256]{1,0:T(8,128)S(1)} collective-permute-done((f32[768,256]{1,0:T(8,128)}, f32[768,256]{1,0:T(8,128)S(1)}, u32[]{:S(2)}, u32[]{:S(2)}) %collective-permute-start.32) | collective-permute-done | bytes 786464 | tf_op jit(solution)/shard_map/ppermute | solution.py:265
  180.2 3.6 %shard_map.57 = (f32[768,256]{1,0:T(8,128)S(1)}, f32[7168,256]{1,0:T(8,128)}) custom-call(s32[2]{0:T(128)S(1)} %pad_add_fusion.4.refs_0_, bf16[512,7168]{1,0:T(8,128)(2,1)} %refs_1_.11, f32[768,256]{1,0:T(8,128)S(1)} %collective-permute-done.30.refs_2_, ...), custom_call_target="tpu_custom_call", output_to_operand_aliasing={{0}: (4, {}), {1}: (5, {})} | custom-call | flops 805306368 | bytes 4718592 | tf_op jit(solution)/shard_map/pallas_call | solution.py:241
  183.8 3.5 %shard_map.58 = (f32[768,256]{1,0:T(8,128)S(1)}, f32[7168,256]{1,0:T(8,128)}) custom-call(s32[2]{0:T(128)S(1)} %pad_add_fusion.3.refs_0_, bf16[512,7168]{1,0:T(8,128)(2,1)} %refs_1_.11, f32[512,256]{1,0:T(8,128)S(1)} %maximum_select_fusion.2.refs_2_, f32[512,256]{1,0:T(8,128)} %collective-permute-done.22.refs_3_, ...), custom_call_target="tpu_custom_call", output_to_operand_aliasing={{0}: (4, {}), {1}: (5, {})} | custom-call | flops 536870912 | bytes 3145728 | tf_op jit(solution)/shard_map/pallas_call | solution.py:241
  187.3 4.1 %collective-permute-done.23.refs_3_ = f32[512,256]{1,0:T(8,128)S(1)} collective-permute-done((f32[512,256]{1,0:T(8,128)}, f32[512,256]{1,0:T(8,128)S(1)}, u32[]{:S(2)}, u32[]{:S(2)}) %collective-permute-start.23) | collective-permute-done | bytes 524320 | tf_op jit(solution)/shard_map/ppermute | solution.py:265
  191.5 3.0 %shard_map.59 = (f32[768,256]{1,0:T(8,128)S(1)}, f32[7168,256]{1,0:T(8,128)}) custom-call(s32[2]{0:T(128)S(1)} %pad_add_fusion.2.refs_0_, bf16[512,7168]{1,0:T(8,128)(2,1)} %refs_1_.11, f32[512,256]{1,0:T(8,128)S(1)} %collective-permute-done.21.refs_2_, ...), custom_call_target="tpu_custom_call", output_to_operand_aliasing={{0}: (4, {}), {1}: (5, {})} | custom-call | flops 536870912 | bytes 3145728 | tf_op jit(solution)/shard_map/pallas_call | solution.py:241
  194.5 3.5 %shard_map.60 = (f32[768,256]{1,0:T(8,128)S(1)}, f32[7168,256]{1,0:T(8,128)}) custom-call(s32[2]{0:T(128)S(1)} %pad_add_fusion.1.refs_0_, bf16[512,7168]{1,0:T(8,128)(2,1)} %refs_1_.11, f32[512,256]{1,0:T(8,128)S(1)} %maximum_select_fusion.1.refs_2_, f32[512,256]{1,0:T(8,128)} %collective-permute-done.13.refs_3_, ...), custom_call_target="tpu_custom_call", output_to_operand_aliasing={{0}: (4, {}), {1}: (5, {})} | custom-call | flops 536870912 | bytes 3145728 | tf_op jit(solution)/shard_map/pallas_call | solution.py:241
  198.1 3.0 %shard_map.61 = (f32[768,256]{1,0:T(8,128)S(1)}, f32[7168,256]{1,0:T(8,128)}) custom-call(s32[2]{0:T(128)S(1)} %pad_add_fusion.refs_0_, bf16[512,7168]{1,0:T(8,128)(2,1)} %refs_1_.11, f32[512,256]{1,0:T(8,128)S(1)} %collective-permute-done.12.refs_2_, f32[512,256]{1,0:T(8,128)S(1)} %collective-permute-done.14.refs_3_, ...), custom_call_target="tpu_custom_call", output_to_operand_aliasing={{0}: (4, {}), {1}: (5, {})} | custom-call | flops 536870912 | bytes 3145728 | tf_op jit(solution)/shard_map/pallas_call | solution.py:241
  201.1 0.8 collective-permute-start.33
  201.9 1.9 collective-permute-done.33.theirs_ref
  203.8 2.0 shard_map.62
  (58 shorter events, 5.9 us)
Async XLA Ops:
  0.6 12.0 %copy-start = (f32[512,256]{1,0:T(8,128)S(1)}, f32[512,256]{1,0:T(8,128)}, u32[]{:S(2)}) copy-start(f32[512,256]{1,0:T(8,128)} %codes_ref.1) | copy-start | bytes 1572868
  10.1 2.4 %collective-permute-start = (f32[768,256]{1,0:T(8,128)S(1)}, f32[768,256]{1,0:T(8,128)S(1)}, u32[]{:S(2)}, u32[]{:S(2)}) collective-permute-start(f32[768,256]{1,0:T(8,128)S(1)} %shard_map.50.mine_ref), channel_id=1, source_target_pairs={{0,1},{1,0},{2,3},{3,2},{4,5},{5,4},{6,7},{7,6},{8,9},{9,8},{10,11... | collective-permute-start | bytes 2359304 | tf_op jit(solution)/shard_map/ppermute | solution.py:273
  14.0 0.8 copy-start.1
  16.9 45.7 %collective-permute-start.24 = (f32[1536,256]{1,0:T(8,128)S(1)}, f32[1536,256]{1,0:T(8,128)S(1)}, u32[]{:S(2)}, u32[]{:S(2)}) collective-permute-start(f32[1536,256]{1,0:T(8,128)S(1)} %fusion), channel_id=1, source_target_pairs={{0,2},{1,5},{2,0},{3,7},{4,6},{5,1},{6,4},{7,3},{8,10},{9,13},{10,... | collective-permute-start | bytes 4718600 | tf_op jit(solution)/shard_map/ppermute | solution.py:265
  19.7 21.2 %collective-permute-start.5 = (f32[128,256]{1,0:T(8,128)S(1)}, f32[128,256]{1,0:T(8,128)S(1)}, u32[]{:S(2)}, u32[]{:S(2)}) collective-permute-start(f32[128,256]{1,0:T(8,128)S(1)} %get-tuple-element.19), channel_id=1, source_target_pairs={{0,2},{1,3},{2,0},{3,1},{4,6},{5,7},{6,4},{7,5},{8,10},{9,11},{10,... | collective-permute-start | bytes 393224 | tf_op jit(solution)/shard_map/ppermute | solution.py:265
  41.0 5.0 %collective-permute-start.6 = (f32[128,256]{1,0:T(8,128)S(1)}, f32[128,256]{1,0:T(8,128)S(1)}, u32[]{:S(2)}, u32[]{:S(2)}) collective-permute-start(f32[128,256]{1,0:T(8,128)S(1)} %add.212), channel_id=1, source_target_pairs={{0,4},{1,5},{2,6},{3,7},{4,0},{5,1},{6,2},{7,3},{8,12},{9,13},{10,... | collective-permute-start | bytes 393224 | tf_op jit(solution)/shard_map/ppermute | solution.py:265
  46.0 5.5 %collective-permute-start.7 = (f32[128,256]{1,0:T(8,128)S(1)}, f32[128,256]{1,0:T(8,128)}, u32[]{:S(2)}, u32[]{:S(2)}) collective-permute-start(f32[128,256]{1,0:T(8,128)S(1)} %add.213), channel_id=1, source_target_pairs={{0,8},{1,9},{2,10},{3,11},{4,12},{5,13},{6,14},{7,15},{8,0},{9,1},... | collective-permute-start | bytes 393224 | tf_op jit(solution)/shard_map/ppermute | solution.py:265
  52.4 7.3 %collective-permute-start.8 = (f32[128,256]{1,0:T(8,128)S(1)}, f32[128,256]{1,0:T(8,128)S(1)}, u32[]{:S(2)}, u32[]{:S(2)}) collective-permute-start(f32[128,256]{1,0:T(8,128)S(1)} %add.214), channel_id=1, source_target_pairs={{0,16},{1,17},{2,18},{3,19},{4,20},{5,21},{6,22},{7,23},{8,24},{9,... | collective-permute-start | bytes 393224 | tf_op jit(solution)/shard_map/ppermute | solution.py:265
  57.0 19.7 %collective-permute-start.15 = (f32[1024,256]{1,0:T(8,128)S(1)}, f32[1024,256]{1,0:T(8,128)S(1)}, u32[]{:S(2)}, u32[]{:S(2)}) collective-permute-start(f32[1024,256]{1,0:T(8,128)S(1)} %fusion.5), channel_id=1, source_target_pairs={{0,2},{1,5},{2,0},{3,7},{4,6},{5,1},{6,4},{7,3},{8,10},{9,13},{10,... | collective-permute-start | bytes 3145736 | tf_op jit(solution)/shard_map/ppermute | solution.py:265
  59.8 2.7 %collective-permute-start.9 = (f32[128,256]{1,0:T(8,128)S(1)}, f32[128,256]{1,0:T(8,128)S(1)}, u32[]{:S(2)}, u32[]{:S(2)}) collective-permute-start(f32[128,256]{1,0:T(8,128)S(1)} %add.215), channel_id=1, source_target_pairs={{0,1},{1,0},{2,3},{3,2},{4,5},{5,4},{6,7},{7,6},{8,9},{9,8},{10,11... | collective-permute-start | bytes 393224 | tf_op jit(solution)/shard_map/ppermute | solution.py:273
  61.6 26.0 %collective-permute-start.1 = (f32[1024,256]{1,0:T(8,128)S(1)}, f32[1024,256]{1,0:T(8,128)S(1)}, u32[]{:S(2)}, u32[]{:S(2)}) collective-permute-start(f32[1024,256]{1,0:T(8,128)S(1)} %fusion.7), channel_id=1, source_target_pairs={{0,8},{1,9},{2,10},{3,11},{4,12},{5,13},{6,14},{7,15},{8,0},{9,1},... | collective-permute-start | bytes 3145736 | tf_op jit(solution)/shard_map/ppermute | solution.py:265
  64.1 14.5 %collective-permute-start.25 = (f32[768,256]{1,0:T(8,128)S(1)}, f32[768,256]{1,0:T(8,128)S(1)}, u32[]{:S(2)}, u32[]{:S(2)}) collective-permute-start(f32[768,256]{1,0:T(8,128)S(1)} %convolution_add_fusion), channel_id=1, source_target_pairs={{0,4},{1,3},{2,6},{3,1},{4,0},{5,7},{6,2},{7,5},{8,12},{9,11},{10,... | collective-permute-start | bytes 2359304 | tf_op jit(solution)/shard_map/ppermute | solution.py:265
  78.1 13.0 %collective-permute-start.16 = (f32[512,256]{1,0:T(8,128)S(1)}, f32[512,256]{1,0:T(8,128)S(1)}, u32[]{:S(2)}, u32[]{:S(2)}) collective-permute-start(f32[512,256]{1,0:T(8,128)S(1)} %convolution_add_fusion.2), channel_id=1, source_target_pairs={{0,4},{1,3},{2,6},{3,1},{4,0},{5,7},{6,2},{7,5},{8,12},{9,11},{10,... | collective-permute-start | bytes 1572872 | tf_op jit(solution)/shard_map/ppermute | solution.py:265
  80.2 15.8 %collective-permute-start.26 = (f32[384,256]{1,0:T(8,128)S(1)}, f32[384,256]{1,0:T(8,128)S(1)}, u32[]{:S(2)}, u32[]{:S(2)}) collective-permute-start(f32[384,256]{1,0:T(8,128)S(1)} %constant_dynamic-slice_fusion.2), channel_id=1, source_target_pairs={{0,8},{1,9},{2,10},{3,11},{4,12},{5,13},{6,14},{7,15},{8,0},{9,1},... | collective-permute-start | bytes 1179656 | tf_op jit(solution)/shard_map/ppermute | solution.py:265
  89.0 9.5 %collective-permute-start.2 = (f32[512,256]{1,0:T(8,128)S(1)}, f32[512,256]{1,0:T(8,128)S(1)}, u32[]{:S(2)}, u32[]{:S(2)}) collective-permute-start(f32[512,256]{1,0:T(8,128)S(1)} %convolution_add_fusion.4), channel_id=1, source_target_pairs={{0,2},{1,5},{2,0},{3,7},{4,6},{5,1},{6,4},{7,3},{8,10},{9,13},{10,... | collective-permute-start | bytes 1572872 | tf_op jit(solution)/shard_map/ppermute | solution.py:265
  92.6 16.0 %collective-permute-start.17 = (f32[256,256]{1,0:T(8,128)S(1)}, f32[256,256]{1,0:T(8,128)S(1)}, u32[]{:S(2)}, u32[]{:S(2)}) collective-permute-start(f32[256,256]{1,0:T(8,128)S(1)} %constant_dynamic-slice_fusion.5), channel_id=1, source_target_pairs={{0,8},{1,9},{2,10},{3,11},{4,12},{5,13},{6,14},{7,15},{8,0},{9,1},... | collective-permute-start | bytes 786440 | tf_op jit(solution)/shard_map/ppermute | solution.py:265
  96.1 11.4 %collective-permute-start.27 = (f32[192,256]{1,0:T(8,128)S(1)}, f32[192,256]{1,0:T(8,128)S(1)}, u32[]{:S(2)}, u32[]{:S(2)}) collective-permute-start(f32[192,256]{1,0:T(8,128)S(1)} %get-tuple-element.32), channel_id=1, source_target_pairs={{0,16},{1,17},{2,18},{3,19},{4,20},{5,21},{6,22},{7,23},{8,24},{9,... | collective-permute-start | bytes 589832 | tf_op jit(solution)/shard_map/ppermute | solution.py:265
  99.9 21.5 %collective-permute-start.3 = (f32[256,256]{1,0:T(8,128)S(1)}, f32[256,256]{1,0:T(8,128)S(1)}, u32[]{:S(2)}, u32[]{:S(2)}) collective-permute-start(f32[256,256]{1,0:T(8,128)S(1)} %constant_dynamic-slice_fusion.8), channel_id=1, source_target_pairs={{0,4},{1,3},{2,6},{3,1},{4,0},{5,7},{6,2},{7,5},{8,12},{9,11},{10,... | collective-permute-start | bytes 786440 | tf_op jit(solution)/shard_map/ppermute | solution.py:265
  108.5 9.7 %collective-permute-start.28 = (f32[192,256]{1,0:T(8,128)S(1)}, f32[192,256]{1,0:T(8,128)S(1)}, u32[]{:S(2)}, u32[]{:S(2)}) collective-permute-start(f32[192,256]{1,0:T(8,128)S(1)} %shard_map.55), channel_id=1, source_target_pairs={{0,16},{1,17},{2,18},{3,19},{4,20},{5,21},{6,22},{7,23},{8,24},{9,... | collective-permute-start | bytes 589832 | tf_op jit(solution)/shard_map/ppermute | solution.py:265
  118.2 16.7 %collective-permute-start.29 = (f32[384,256]{1,0:T(8,128)S(1)}, f32[384,256]{1,0:T(8,128)S(1)}, u32[]{:S(2)}, u32[]{:S(2)}) collective-permute-start(f32[384,256]{1,0:T(8,128)S(1)} %maximum_select_fusion.3), channel_id=1, source_target_pairs={{0,8},{1,9},{2,10},{3,11},{4,12},{5,13},{6,14},{7,15},{8,0},{9,1},... | collective-permute-start | bytes 1179656 | tf_op jit(solution)/shard_map/ppermute | solution.py:265
  118.4 12.3 %collective-permute-start.18 = (f32[128,256]{1,0:T(8,128)S(1)}, f32[128,256]{1,0:T(8,128)S(1)}, u32[]{:S(2)}, u32[]{:S(2)}) collective-permute-start(f32[128,256]{1,0:T(8,128)S(1)} %get-tuple-element.34), channel_id=1, source_target_pairs={{0,16},{1,17},{2,18},{3,19},{4,20},{5,21},{6,22},{7,23},{8,24},{9,... | collective-permute-start | bytes 393224 | tf_op jit(solution)/shard_map/ppermute | solution.py:265
  121.5 14.6 %collective-permute-start.4 = (f32[128,256]{1,0:T(8,128)S(1)}, f32[128,256]{1,0:T(8,128)S(1)}, u32[]{:S(2)}, u32[]{:S(2)}) collective-permute-start(f32[128,256]{1,0:T(8,128)S(1)} %get-tuple-element.36), channel_id=1, source_target_pairs={{0,16},{1,17},{2,18},{3,19},{4,20},{5,21},{6,22},{7,23},{8,24},{9,... | collective-permute-start | bytes 393224 | tf_op jit(solution)/shard_map/ppermute | solution.py:265
  131.5 13.5 %collective-permute-start.19 = (f32[128,256]{1,0:T(8,128)S(1)}, f32[128,256]{1,0:T(8,128)S(1)}, u32[]{:S(2)}, u32[]{:S(2)}) collective-permute-start(f32[128,256]{1,0:T(8,128)S(1)} %shard_map.54), channel_id=1, source_target_pairs={{0,16},{1,17},{2,18},{3,19},{4,20},{5,21},{6,22},{7,23},{8,24},{9,... | collective-permute-start | bytes 393224 | tf_op jit(solution)/shard_map/ppermute | solution.py:265
  135.0 22.9 %collective-permute-start.31 = (f32[768,256]{1,0:T(8,128)S(1)}, f32[768,256]{1,0:T(8,128)}, u32[]{:S(2)}, u32[]{:S(2)}) collective-permute-start(f32[768,256]{1,0:T(8,128)S(1)} %maximum_select_fusion.refs_2_), channel_id=1, source_target_pairs={{0,4},{1,3},{2,6},{3,1},{4,0},{5,7},{6,2},{7,5},{8,12},{9,11},{10,... | collective-permute-start | bytes 2359304 | tf_op jit(solution)/shard_map/ppermute | solution.py:265
  136.9 10.1 %collective-permute-start.10 = (f32[128,256]{1,0:T(8,128)S(1)}, f32[128,256]{1,0:T(8,128)S(1)}, u32[]{:S(2)}, u32[]{:S(2)}) collective-permute-start(f32[128,256]{1,0:T(8,128)S(1)} %shard_map.53), channel_id=1, source_target_pairs={{0,16},{1,17},{2,18},{3,19},{4,20},{5,21},{6,22},{7,23},{8,24},{9,... | collective-permute-start | bytes 393224 | tf_op jit(solution)/shard_map/ppermute | solution.py:265
  145.0 7.6 %collective-permute-start.20 = (f32[256,256]{1,0:T(8,128)S(1)}, f32[256,256]{1,0:T(8,128)S(1)}, u32[]{:S(2)}, u32[]{:S(2)}) collective-permute-start(f32[256,256]{1,0:T(8,128)S(1)} %maximum_select_fusion.6), channel_id=1, source_target_pairs={{0,8},{1,9},{2,10},{3,11},{4,12},{5,13},{6,14},{7,15},{8,0},{9,1},... | collective-permute-start | bytes 786440 | tf_op jit(solution)/shard_map/ppermute | solution.py:265
  147.1 9.2 %collective-permute-start.11 = (f32[256,256]{1,0:T(8,128)S(1)}, f32[256,256]{1,0:T(8,128)S(1)}, u32[]{:S(2)}, u32[]{:S(2)}) collective-permute-start(f32[256,256]{1,0:T(8,128)S(1)} %maximum_select_fusion.5), channel_id=1, source_target_pairs={{0,4},{1,3},{2,6},{3,1},{4,0},{5,7},{6,2},{7,5},{8,12},{9,11},{10,... | collective-permute-start | bytes 786440 | tf_op jit(solution)/shard_map/ppermute | solution.py:265
  148.6 23.3 %collective-permute-start.30 = (f32[768,256]{1,0:T(8,128)S(1)}, f32[768,256]{1,0:T(8,128)S(1)}, u32[]{:S(2)}, u32[]{:S(2)}) collective-permute-start(f32[768,256]{1,0:T(8,128)S(1)} %maximum_select_fusion.refs_2_), channel_id=1, source_target_pairs={{0,2},{1,5},{2,0},{3,7},{4,6},{5,1},{6,4},{7,3},{8,10},{9,13},{10,... | collective-permute-start | bytes 2359304 | tf_op jit(solution)/shard_map/ppermute | solution.py:265
  152.6 15.0 %collective-permute-start.22 = (f32[512,256]{1,0:T(8,128)S(1)}, f32[512,256]{1,0:T(8,128)}, u32[]{:S(2)}, u32[]{:S(2)}) collective-permute-start(f32[512,256]{1,0:T(8,128)S(1)} %maximum_select_fusion.2.refs_2_), channel_id=1, source_target_pairs={{0,4},{1,3},{2,6},{3,1},{4,0},{5,7},{6,2},{7,5},{8,12},{9,11},{10,... | collective-permute-start | bytes 1572872 | tf_op jit(solution)/shard_map/ppermute | solution.py:265
  156.3 15.6 %collective-permute-start.13 = (f32[512,256]{1,0:T(8,128)S(1)}, f32[512,256]{1,0:T(8,128)}, u32[]{:S(2)}, u32[]{:S(2)}) collective-permute-start(f32[512,256]{1,0:T(8,128)S(1)} %maximum_select_fusion.1.refs_2_), channel_id=1, source_target_pairs={{0,2},{1,5},{2,0},{3,7},{4,6},{5,1},{6,4},{7,3},{8,10},{9,13},{10,... | collective-permute-start | bytes 1572872 | tf_op jit(solution)/shard_map/ppermute | solution.py:265
  157.9 22.4 %collective-permute-start.32 = (f32[768,256]{1,0:T(8,128)}, f32[768,256]{1,0:T(8,128)S(1)}, u32[]{:S(2)}, u32[]{:S(2)}) collective-permute-start(f32[768,256]{1,0:T(8,128)} %collective-permute-done.31.refs_3_), channel_id=1, source_target_pairs={{0,2},{1,5},{2,0},{3,7},{4,6},{5,1},{6,4},{7,3},{8,10},{9,13},{10,... | collective-permute-start | bytes 2359304 | tf_op jit(solution)/shard_map/ppermute | solution.py:265
  158.6 28.7 %collective-permute-start.21 = (f32[512,256]{1,0:T(8,128)S(1)}, f32[512,256]{1,0:T(8,128)S(1)}, u32[]{:S(2)}, u32[]{:S(2)}) collective-permute-start(f32[512,256]{1,0:T(8,128)S(1)} %maximum_select_fusion.2.refs_2_), channel_id=1, source_target_pairs={{0,2},{1,5},{2,0},{3,7},{4,6},{5,1},{6,4},{7,3},{8,10},{9,13},{10,... | collective-permute-start | bytes 1572872 | tf_op jit(solution)/shard_map/ppermute | solution.py:265
  167.6 23.9 %collective-permute-start.23 = (f32[512,256]{1,0:T(8,128)}, f32[512,256]{1,0:T(8,128)S(1)}, u32[]{:S(2)}, u32[]{:S(2)}) collective-permute-start(f32[512,256]{1,0:T(8,128)} %collective-permute-done.22.refs_3_), channel_id=1, source_target_pairs={{0,2},{1,5},{2,0},{3,7},{4,6},{5,1},{6,4},{7,3},{8,10},{9,13},{10,... | collective-permute-start | bytes 1572872 | tf_op jit(solution)/shard_map/ppermute | solution.py:265
  171.9 26.1 %collective-permute-start.12 = (f32[512,256]{1,0:T(8,128)S(1)}, f32[512,256]{1,0:T(8,128)S(1)}, u32[]{:S(2)}, u32[]{:S(2)}) collective-permute-start(f32[512,256]{1,0:T(8,128)S(1)} %maximum_select_fusion.1.refs_2_), channel_id=1, source_target_pairs={{0,8},{1,9},{2,10},{3,11},{4,12},{5,13},{6,14},{7,15},{8,0},{9,1},... | collective-permute-start | bytes 1572872 | tf_op jit(solution)/shard_map/ppermute | solution.py:265
  171.9 26.1 %collective-permute-start.14 = (f32[512,256]{1,0:T(8,128)}, f32[512,256]{1,0:T(8,128)S(1)}, u32[]{:S(2)}, u32[]{:S(2)}) collective-permute-start(f32[512,256]{1,0:T(8,128)} %collective-permute-done.13.refs_3_), channel_id=1, source_target_pairs={{0,8},{1,9},{2,10},{3,11},{4,12},{5,13},{6,14},{7,15},{8,0},{9,1},... | collective-permute-start | bytes 1572872 | tf_op jit(solution)/shard_map/ppermute | solution.py:265
  198.0 5.8 %copy-start.2 = (f32[512,256]{1,0:T(8,128)S(1)}, f32[512,256]{1,0:T(8,128)}, u32[]{:S(2)}) copy-start(f32[512,256]{1,0:T(8,128)} %copy-done.1) | copy-start | bytes 1572868
  201.1 2.8 %collective-permute-start.33 = (f32[768,256]{1,0:T(8,128)S(1)}, f32[768,256]{1,0:T(8,128)S(1)}, u32[]{:S(2)}, u32[]{:S(2)}) collective-permute-start(f32[768,256]{1,0:T(8,128)S(1)} %get-tuple-element.30.mine_ref), channel_id=1, source_target_pairs={{0,1},{1,0},{2,3},{3,2},{4,5},{5,4},{6,7},{7,6},{8,9},{9,8},{10,11... | collective-permute-start | bytes 2359304 | tf_op jit(solution)/shard_map/ppermute | solution.py:273

commit v3 on v2

v3 whole, which is shorter than its diff:
```python
import functools

import jax
import jax.numpy as jnp
import numpy as np
from jax import lax
from jax.experimental import pallas as pl
from jax.experimental.pallas import tpu as pltpu
from jax.sharding import PartitionSpec as P

floor_value = 0.05
HIGHEST = lax.Precision.HIGHEST
f32, bf16 = jnp.float32, jnp.bfloat16
BOTH = ("tok", "hid")
OVER_ROWS = (((0,), (0,)), ((), ()))
OVER_COLS = (((1,), (1,)), ((), ()))
LIMIT = pltpu.CompilerParams(vmem_limit_bytes=48 * 2**20)


def dot(left, right, dims=(((1,), (0,)), ((), ())), precision=None):
    return lax.dot_general(left, right, dims, precision=precision, preferred_element_type=f32)


def refine(codes, proj, gram):
    gram_pos = jnp.maximum(gram, 0.0)
    gram_neg = jnp.maximum(-gram, 0.0)
    numer = jnp.maximum(proj, 0.0) + dot(codes, gram_neg, precision=HIGHEST)
    denom = jnp.maximum(jnp.maximum(-proj, 0.0) + dot(codes, gram_pos, precision=HIGHEST), floor_value)
    return codes * jnp.sqrt(numer / denom)


def project_kernel(acts_ref, dict_ref, out_ref, cross_ref):
    step = pl.program_id(0)
    tokens = acts_ref.shape[0]

    @pl.when(step == 0)
    def _():
        out_ref[...] = jnp.zeros_like(out_ref)
        cross_ref[...] = jnp.zeros_like(cross_ref)

    rows = dict_ref[...]
    high = rows.astype(bf16)
    low = (rows - high.astype(f32)).astype(bf16)
    out_ref[:tokens, :] += dot(acts_ref[...], high)
    turned = high.T
    out_ref[tokens:, :] += dot(turned, high)
    cross_ref[...] += dot(turned, low)

    @pl.when(step == pl.num_programs(0) - 1)
    def _():
        out_ref[tokens:, :] += cross_ref[...] + cross_ref[...].T


def project(acts, dictionary):
    tokens, hidden = acts.shape
    comp = dictionary.shape[1]
    tile = 1024 if hidden % 1024 == 0 else 512
    return pl.pallas_call(
        project_kernel,
        out_shape=jax.ShapeDtypeStruct((tokens + comp, comp), f32),
        grid=(hidden // tile,),
        in_specs=[
            pl.BlockSpec((tokens, tile), lambda i: (0, i)),
            pl.BlockSpec((tile, comp), lambda i: (i, 0)),
        ],
        out_specs=pl.BlockSpec((tokens + comp, comp), lambda i: (0, 0)),
        scratch_shapes=[pltpu.VMEM((comp, comp), f32)],
        compiler_params=LIMIT,
        cost_estimate=pl.CostEstimate(
            flops=2 * hidden * comp * (tokens + 2 * comp), bytes_accessed=hidden * (2 * tokens + 4 * comp), transcendentals=0
        ),
    )(acts, dictionary)


def unit_inverse(block):
    n = block.shape[0]
    done = []
    rest = block
    for start in range(0, n, 8):
        shape = rest.shape
        row = lax.broadcasted_iota(jnp.int32, shape, 0)
        lane = lax.broadcasted_iota(jnp.int32, shape, 1)
        lane_row = lax.broadcasted_iota(jnp.int32, (1, n), 1)
        cols = [jnp.broadcast_to(rest[:, start + j : start + j + 1], shape) for j in range(8)]
        for j in range(8):
            inverse = 1.0 / cols[j][j : j + 1, :]
            below = jnp.where(row > j, cols[j], 0.0)
            scaled = jnp.where(lane_row == start + j, inverse, rest[j : j + 1, :] * inverse)
            rest = jnp.where((lane == start + j) & (row > j), 0.0, rest) - below * scaled
            for k in range(j + 1, 8):
                cols[k] = cols[k] - below * (cols[k][j : j + 1, :] * inverse)
        done.append(rest[:8, :])
        rest = rest[8:, :]
    full = jnp.concatenate(done, axis=0)
    row = lax.broadcasted_iota(jnp.int32, (n, n), 0)
    lane = lax.broadcasted_iota(jnp.int32, (n, n), 1)
    pivots = jnp.sum(jnp.where(row == lane, full, 0.0), axis=1, keepdims=True)
    unit = jnp.where(row > lane, full, jnp.where(row == lane, 1.0, 0.0))
    return unit * (1.0 / jnp.sqrt(pivots))


def factor(gram_ref, out_ref):
    half = gram_ref.shape[0] // 2
    upper = unit_inverse(gram_ref[:half, :half])
    side = dot(gram_ref[half:, :half], upper, OVER_COLS, HIGHEST)
    lower = unit_inverse(gram_ref[half:, half:] - dot(side, side, OVER_COLS, HIGHEST))
    out_ref[:half, :half] = upper
    out_ref[:half, half:] = jnp.zeros((half, half), f32)
    out_ref[half:, :half] = -dot(dot(lower, side, precision=HIGHEST), upper, precision=HIGHEST)
    out_ref[half:, half:] = lower


def halves_kernel(table_ref, mine_ref, theirs_ref, *refs):
    half = mine_ref.shape[0]
    out_ref, gram_ref = refs[-2:]
    gram_ref[pl.ds(pl.multiple_of(table_ref[0] * half, half), half), :] = mine_ref[...]
    gram_ref[pl.ds(pl.multiple_of((1 - table_ref[0]) * half, half), half), :] = theirs_ref[...]
    factor(gram_ref, out_ref)


def factor_inverse(table, mine, theirs, after=()):
    comp = mine.shape[1]
    return pl.pallas_call(
        halves_kernel,
        out_shape=jax.ShapeDtypeStruct((comp, comp), f32),
        in_specs=[pl.BlockSpec(memory_space=pltpu.SMEM)]
        + [pl.BlockSpec(memory_space=pltpu.VMEM)] * 2
        + [pl.BlockSpec(memory_space=pl.ANY)] * len(after),
        scratch_shapes=[pltpu.VMEM((comp, comp), f32)],
        compiler_params=LIMIT,
        cost_estimate=pl.CostEstimate(flops=10**10, bytes_accessed=8 * comp * comp, transcendentals=0),
    )(table, mine, theirs, *after)


def solve_rows(cross, inverse):
    return dot(dot(cross, inverse, OVER_COLS, HIGHEST), inverse, precision=HIGHEST)


def plain(acts, dictionary, codes, split):
    tokens = acts.shape[0]
    sums = lax.psum(project(acts, dictionary), "hid")
    codes_mid = refine(codes, sums[:tokens], sums[tokens:])
    codes_low = codes_mid.astype(bf16)
    cross = dot(acts, codes_low, OVER_ROWS)
    gram_codes = lax.psum(dot(codes_low, codes_low, OVER_ROWS), "tok")
    half = gram_codes.shape[0] // 2
    if split:
        mine = solve_rows(lax.psum_scatter(cross, "tok", tiled=True), factor_inverse(jnp.zeros((1,), jnp.int32), gram_codes[:half], gram_codes[half:]))
        dict_out = lax.all_gather(mine, "tok", tiled=True)
    else:
        dict_out = solve_rows(lax.psum(cross, "tok"), factor_inverse(jnp.zeros((1,), jnp.int32), gram_codes[:half], gram_codes[half:]))
    gram_part = dot(dict_out, dict_out, OVER_ROWS, HIGHEST)
    proj_two, gram_new = lax.psum((dot(acts, dict_out.astype(bf16)), gram_part), "hid")
    return refine(codes_mid, proj_two, gram_new), dict_out


def update(codes, sums, tokens, precision=HIGHEST):
    proj, gram = sums[:tokens], sums[tokens:]
    numer = jnp.maximum(proj, 0.0) + dot(codes, jnp.maximum(-gram, 0.0), precision=precision)
    denom = jnp.maximum(-proj, 0.0) + dot(codes, jnp.maximum(gram, 0.0), precision=precision)
    return codes * jnp.sqrt(numer / jnp.maximum(denom, floor_value))


def first_kernel(core_ref, codes_ref, mine_ref, theirs_ref, mid_ref, low_ref, gram_ref):
    mid = update(codes_ref[...], mine_ref[...] + theirs_ref[...], codes_ref.shape[0])
    low = mid.astype(bf16)
    mid_ref[...] = mid
    low_ref[...] = low
    half = low.shape[1] // 2
    side = jnp.where(core_ref[0] == 0, mid[:, :half], mid[:, half:]).astype(bf16)
    gram_ref[...] = dot(side.T, low)


def first_update(core, codes, mine, theirs):
    tokens, comp = codes.shape
    whole = pl.BlockSpec(memory_space=pltpu.VMEM)
    return pl.pallas_call(
        first_kernel,
        out_shape=[
            jax.ShapeDtypeStruct((tokens, comp), f32),
            jax.ShapeDtypeStruct((tokens, comp), bf16),
            jax.ShapeDtypeStruct((comp // 2, comp), f32),
        ],
        in_specs=[pl.BlockSpec(memory_space=pltpu.SMEM), whole, whole, whole],
        out_specs=[whole, whole, whole],
        compiler_params=LIMIT,
    )(core, codes, mine, theirs)


def second_kernel(codes_ref, mine_ref, theirs_ref, out_ref):
    out_ref[...] = update(codes_ref[...], mine_ref[...] + theirs_ref[...], codes_ref.shape[0])


def second_update(codes, mine, theirs):
    return pl.pallas_call(
        second_kernel,
        out_shape=jax.ShapeDtypeStruct(codes.shape, f32),
        compiler_params=LIMIT,
    )(codes, mine, theirs)


WHOLE = pl.BlockSpec(memory_space=pltpu.VMEM)
SCALARS = pl.BlockSpec(memory_space=pltpu.SMEM)
ANYWHERE = pl.BlockSpec(memory_space=pl.ANY)
TILE = 256


def call(kernel, out_shapes, table, values, after):
    return pl.pallas_call(
        kernel,
        out_shape=out_shapes,
        in_specs=[SCALARS] + [WHOLE] * len(values) + [ANYWHERE] * len(after),
        out_specs=[WHOLE] * len(out_shapes),
        compiler_params=LIMIT,
    )(table, *values, *after)


def shape(rows, comp):
    return jax.ShapeDtypeStruct((rows, comp), f32)


def first_fold_kernel(at, table_ref, mine_ref, theirs_ref, gram_ref, *refs):
    whole = mine_ref.shape[0]
    rows = whole // 2
    keep = pl.ds(pl.multiple_of(table_ref[at] * rows, rows), rows)
    give = pl.ds(pl.multiple_of((1 - table_ref[at]) * rows, rows), rows)
    gram = gram_ref[...] + theirs_ref[whole:, :]
    refs[-2][:rows, :] = mine_ref[give, :] + theirs_ref[give, :]
    refs[-2][rows:, :] = gram
    refs[-1][:rows, :] = mine_ref[keep, :] + theirs_ref[keep, :]
    refs[-1][rows:, :] = gram


def first_fold(table, at, mine, theirs, gram):
    half = shape(mine.shape[0] // 2 + gram.shape[0], mine.shape[1])
    return call(functools.partial(first_fold_kernel, at), [half, half], table, [mine, theirs, gram], [])


def mixed_fold_kernel(at, extra, table_ref, mine_ref, theirs_ref, *refs):
    whole = mine_ref.shape[0] - extra
    rows = whole // 2
    keep = pl.ds(pl.multiple_of(table_ref[at] * rows, 8), rows)
    give = pl.ds(pl.multiple_of((1 - table_ref[at]) * rows, 8), rows)
    gram = mine_ref[whole:, :] + theirs_ref[whole:, :]
    refs[-2][:rows, :] = mine_ref[give, :] + theirs_ref[give, :]
    refs[-2][rows:, :] = gram
    refs[-1][:rows, :] = mine_ref[keep, :] + theirs_ref[keep, :]
    refs[-1][rows:, :] = gram


def mixed_fold(table, at, extra, mine, theirs, after):
    half = shape((mine.shape[0] - extra) // 2 + extra, mine.shape[1])
    return call(functools.partial(mixed_fold_kernel, at, extra), [half, half], table, [mine, theirs], after)


def part_kernel(rows, table_ref, mine_ref, theirs_ref, *refs):
    refs[-2][...] = mine_ref[:rows, :] + theirs_ref[:rows, :]
    refs[-1][...] = mine_ref[rows:, :] + theirs_ref[rows:, :]


def part(table, rows, mine, theirs, after):
    shapes = [shape(rows, mine.shape[1]), shape(mine.shape[0] - rows, mine.shape[1])]
    return call(functools.partial(part_kernel, rows), shapes, table, [mine, theirs], after)


def rows_kernel(table_ref, inverse_ref, mine_ref, *refs):
    inverse = inverse_ref[...]
    cross = mine_ref[...] + refs[0][...] if len(refs) > 1 else mine_ref[...]
    refs[-1][...] = dot(dot(cross, inverse, OVER_COLS, HIGHEST), inverse, precision=HIGHEST)


def solve_sum(table, inverse, parts):
    return call(rows_kernel, [shape(*parts[0].shape)], table, [inverse, *parts], [])[0]


def absorb_kernel(ats, fresh, table_ref, acts_ref, *refs):
    count = len(ats)
    values, refs = refs[:count], refs[count:]
    if not fresh:
        sums_ref, refs = refs[0], refs[2:]
    out_ref, dict_ref = refs[:2]
    buffers, in_sem, out_sem = refs[2 : 2 + count], refs[2 + count], refs[3 + count]
    tokens = acts_ref.shape[0]
    ins, outs = [], []
    for k, value in enumerate(values):
        row = pl.multiple_of(table_ref[ats[k]] * TILE, TILE)
        rows = value.shape[0]
        ins.append(pltpu.make_async_copy(acts_ref.at[:, pl.ds(row, rows)], buffers[k], in_sem.at[k]))
        outs.append(pltpu.make_async_copy(value, dict_ref.at[pl.ds(row, rows), :], out_sem.at[k]))
        ins[k].start()
        outs[k].start()
    proj, gram = (0.0, 0.0) if fresh else (sums_ref[:tokens, :], sums_ref[tokens:, :])
    for k, value in enumerate(values):
        high = value[...].astype(bf16)
        gram = gram + dot(high.T, high)
        ins[k].wait()
        proj = proj + dot(buffers[k][...], high)
    out_ref[:tokens, :] = proj
    out_ref[tokens:, :] = gram
    for copy in outs:
        copy.wait()


def absorb(table, state, acts, blocks):
    tokens, hidden = acts.shape
    comp = blocks[0][0].shape[1]
    count = len(blocks)
    values = [value for value, _ in blocks]
    held = [] if state is None else list(state)
    total = sum(value.shape[0] for value in values)
    return pl.pallas_call(
        functools.partial(absorb_kernel, [at for _, at in blocks], state is None),
        out_shape=[shape(tokens + comp, comp), shape(hidden, comp)],
        in_specs=[SCALARS, ANYWHERE] + [WHOLE] * count + ([WHOLE, ANYWHERE] if held else []),
        out_specs=[WHOLE, ANYWHERE],
        scratch_shapes=[pltpu.VMEM((tokens, value.shape[0]), bf16) for value in values]
        + [pltpu.SemaphoreType.DMA((count,)), pltpu.SemaphoreType.DMA((count,))],
        input_output_aliases={2 + count: 0, 3 + count: 1} if held else {},
        compiler_params=LIMIT,
        cost_estimate=pl.CostEstimate(
            flops=2 * total * comp * (tokens + comp), bytes_accessed=total * (2 * tokens + 8 * comp), transcendentals=0
        ),
    )(table, acts, *values, *held)


def flips(bits):
    return [(t * 2 + c, (t ^ bits[c]) * 2 + c) for t in range(16) for c in range(2)]


X, Y, ZL, ZH = 1, 2, 4, 8
ALONG = {"first": (X, Y), "second": (Y, X), "near": (ZL, ZL), "far": (ZH, ZH)}
ORDERS = {
    "A": ("first", "second", "near", "far"),
    "B": ("first", "second", "near", "far"),
    "N": ("near", "first", "second", "far"),
}
SHARES = {"A": 2, "B": 3, "N": 2}
FIELDS = ("c", "d", "mine", "theirs", "far_mine", "far_theirs")


def swap(value, along):
    return lax.ppermute(value, BOTH, flips(ALONG[along]))


def layout(hidden):
    unit = hidden // sum(SHARES.values())
    rows = {name: share * unit for name, share in SHARES.items()}
    table = np.zeros((32, 1 + len(FIELDS) * len(rows)), np.int32)
    where = {"core": 0}
    start, column = 0, 1
    for name, order in ORDERS.items():
        half, quarter = rows[name] // 2 // TILE, rows[name] // 4 // TILE
        for t in range(16):
            for core in range(2):
                a, b, c, d = (int(t & ALONG[along][core] != 0) for along in order)
                here, there = start + a * half, start + (1 - a) * half
                table[t * 2 + core, 0] = core
                table[t * 2 + core, column : column + len(FIELDS)] = (
                    c, d,
                    here + b * quarter, here + (1 - b) * quarter, there + b * quarter, there + (1 - b) * quarter,
                )
        for k, field in enumerate(FIELDS):
            where[name, field] = column + k
        start, column = start + 2 * half, column + len(FIELDS)
    return rows, table, where


def meshed(acts, dictionary, codes):
    hidden = acts.shape[1]
    tok, core = lax.axis_index("tok"), lax.axis_index("hid")
    rows, places, where = layout(hidden)
    table = lax.dynamic_slice_in_dim(jnp.asarray(places), tok * 2 + core, 1, 0).reshape(-1)

    def other_core(value):
        return lax.ppermute(value, "hid", [(0, 1), (1, 0)])

    sums = project(acts, dictionary)
    codes_mid, low, gram = first_update(table, codes, sums, other_core(sums))

    def bit(along):
        on_0, on_1 = ALONG[along]
        return jnp.where(core == 0, (tok & on_0) // on_0, (tok & on_1) // on_1)

    bits = {along: bit(along) for along in ALONG}
    starts, start = {}, 0
    for name in ORDERS:
        starts[name], start = start, start + rows[name]

    def cross_of(row, count):
        return dot(lax.dynamic_slice_in_dim(acts, row, count, 1), low, OVER_ROWS)

    def give_1(name):
        half = rows[name] // 2
        return cross_of(starts[name] + (1 - bits[ORDERS[name][0]]) * half, half)

    def stage_2(name, got, keep):
        half, quarter = rows[name] // 2, rows[name] // 4
        a, b = (bits[along] for along in ORDERS[name][:2])
        which = b if keep else 1 - b
        out = cross_of(starts[name] + a * half + which * quarter, quarter)
        return out + lax.dynamic_slice_in_dim(got, which * quarter, quarter, 0)

    def part_of(value, which):
        half = value.shape[0] // 2
        return lax.dynamic_slice_in_dim(value, which * half, half, 0)

    def joined(one, other, which):
        return jnp.where(which == 0, jnp.concatenate([one, other]), jnp.concatenate([other, one]))

    extra = gram.shape[0]
    got = {
        "A": swap(jnp.concatenate([give_1("A"), gram]), ORDERS["A"][0]),
        "N": swap(give_1("N"), ORDERS["N"][0]),
        "B": swap(give_1("B"), ORDERS["B"][0]),
    }
    gram = gram + got["A"][rows["A"] // 2 :]
    held = {}
    for name in ("A", "N", "B"):
        give = stage_2(name, got[name], False)
        if name == "A":
            give = jnp.concatenate([give, gram])
        held[name] = stage_2(name, got[name], True), swap(give, ORDERS[name][1])
    for name, (keep, arrived) in held.items():
        along = ORDERS[name][2]
        if name == "A":
            give, keep = first_fold(table, where[name, "c"], keep, arrived, gram)
            held[name] = keep, swap(give, along)
        else:
            keep = keep + arrived
            held[name] = part_of(keep, bits[along]), swap(part_of(keep, 1 - bits[along]), along)
    for name, (keep, arrived) in held.items():
        along = ORDERS[name][3]
        if name == "A":
            give, keep = mixed_fold(table, where[name, "d"], extra, keep, arrived, [])
            held[name] = keep, swap(give, along)
        else:
            keep = keep + arrived
            held[name] = part_of(keep, bits[along]), swap(part_of(keep, 1 - bits[along]), along)

    a_mine, gram = part(table, rows["A"] // 16, *held["A"], [])
    inverse = factor_inverse(table, gram, other_core(gram), [held["N"][0], held["B"][0]])
    held["A"] = (a_mine,)
    mine = {name: solve_sum(table, inverse, held[name]) for name in held}

    for k in (3, 2):
        for name in mine:
            along = ORDERS[name][k]
            mine[name] = joined(mine[name], swap(mine[name], along), bits[along])
    near, far = [], []
    for name in mine:
        theirs = swap(mine[name], ORDERS[name][1])
        near += [(mine[name], where[name, "mine"]), (theirs, where[name, "theirs"])]
        far += [(swap(value, ORDERS[name][0]), where[name, field]) for value, field in ((mine[name], "far_mine"), (theirs, "far_theirs"))]
    sums, dict_out = absorb(table, absorb(table, None, acts, near), acts, far)
    return second_update(codes_mid, sums, other_core(sums)), dict_out


def solution(mesh):
    tok, hid = mesh.shape["tok"], mesh.shape["hid"]

    def per_device(acts, dictionary, codes):
        if tok == 16 and hid == 2 and acts.shape[1] % (7 * 1024) == 0:
            return meshed(acts, dictionary, codes)
        return plain(acts, dictionary, codes, acts.shape[1] % tok == 0)

    return jax.shard_map(
        per_device,
        mesh=mesh,
        in_specs=(P("tok", "hid"), P("hid", None), P("tok", None)),
        out_specs=(P("tok", None), P("hid", None)),
        check_vma=False,
    )
```

time: 207 us -> 216 us (1.043)
  waiting for transfers between devices: 97.3 us -> 117 us
  starting transfers between devices: 46.6 us -> 35.4 us
  Pallas kernels: 43.9 us -> 37.8 us
  other arithmetic: 1.77 us -> 5.21 us
  matrix products: 14.2 us -> 17.6 us
    ppermute x31 -> x27, waiting for transfers between devices: 93.5 us -> 113 us  [swap(): return lax.ppermute(value, BOTH, flips(ALONG[along]))]
    ppermute x31 -> x27, starting transfers between devices: 45.1 us -> 32.7 us  [swap(): return lax.ppermute(value, BOTH, flips(ALONG[along]))]
    pallas_call x10 -> x9, Pallas kernels: 31 us -> 24.3 us  [the longest x2 9.92 us: absorb(): pl.pallas_call(functools.partial(absorb_kernel, [at for _, at in blocks],...]
    dot_general x9, matrix products: 14.2 us -> 17.6 us  [dot(): lax.dot_general(left, right, dims, precision=precision, preferred_element...]
  transfers between devices with their start and end apart: 34 -> 30, of which waited for: 20 -> 17; matrix products, arithmetic and copies ran while one was open for 7% -> 10% of each run, Pallas kernels for 14% -> 8%
where the time goes in v3:
time: 216 us; the launch traced here: 215 us
  waiting for transfers between devices  117 us (54%)
  Pallas kernels  37.8 us (17%)
  starting transfers between devices  35.4 us (16%)
  matrix products  17.6 us (8%)
  other arithmetic  5.21 us (2%)
    ppermute x27, waiting for transfers between devices, swap(): return lax.ppermute(value, BOTH, flips(ALONG[along]))  113 us
    ppermute x27, starting transfers between devices, swap(): return lax.ppermute(value, BOTH, flips(ALONG[along]))  32.7 us
    dot_general x9, matrix products, dot(): lax.dot_general(left, right, dims, precision=precision, preferred_element...  17.6 us
    pallas_call x2, Pallas kernels, absorb(): pl.pallas_call(functools.partial(absorb_kernel, [at for _, at in blocks],...  9.92 us
    pallas_call x1, Pallas kernels, project(): pl.pallas_call(project_kernel, out_shape=jax.ShapeDtypeStruct((tokens + c...  9.55 us
    pallas_call x1, Pallas kernels, factor_inverse(): pl.pallas_call(halves_kernel, out_shape=jax.ShapeDtypeStruct((comp, comp)...  8.42 us
    pallas_call x6, Pallas kernels, call(): pl.pallas_call(kernel, out_shape=out_shapes, in_specs=[SCALARS] + [WHOLE]...  5.93 us
  transfers between devices with their start and end apart: 30, of which 17 were waited for; matrix products, arithmetic and copies ran while one was open for 10% of the time, Pallas kernels for 8%

profile of v3, /device:TPU:0, one launch (start us, length us, event | category | flops | bytes accessed | tf_op | source)
XLA Modules:
  0.0 215.0 jit_solution(3565707174016169346)
XLA Ops:
  0.6 9.6 %shard_map.59.mine_ref = f32[768,256]{1,0:T(8,128)S(1)} custom-call(bf16[512,7168]{1,0:T(8,128)(2,1)} %acts_ref.5, f32[7168,256]{1,0:T(8,128)} %dict_ref.1), custom_call_target="tpu_custom_call" | custom-call | flops 3758096384 | bytes 14680064 | tf_op jit(solution)/shard_map/pallas_call | solution.py:58
  10.7 0.7 fusion.23.core_ref.table_ref
  11.4 1.2 collective-permute-done.theirs_ref
  12.6 2.0 shard_map.60
  14.6 1.7 fusion.4
  16.3 1.7 fusion.6
  18.0 3.0 %collective-permute-start.6 = (f32[1024,256]{1,0:T(8,128)S(1)}, f32[1024,256]{1,0:T(8,128)}, u32[]{:S(2)}, u32[]{:S(2)}) collective-permute-start(f32[1024,256]{1,0:T(8,128)S(1)} %fusion.4), channel_id=1, source_target_pairs={{0,8},{1,9},{2,10},{3,11},{4,12},{5,13},{6,14},{7,15},{8,0},{9,1},... | collective-permute-start | bytes 3145736 | tf_op jit(solution)/shard_map/ppermute | solution.py:342
  21.0 3.2 %fusion = f32[1536,256]{1,0:T(8,128)} fusion(bf16[512,256]{1,0:T(8,128)(2,1)S(1)} %get-tuple-element.16, bf16[512,7168]{1,0:T(8,128)(2,1)} %acts_ref.5, s32[]{:T(128)S(6)} %select_n.160), kind=kOutput, calls=%fused_computation | convolution fusion | flops 402653184 | bytes 3407876 | tf_op jit(solution)/shard_map/dot_general | solution.py:21
  24.2 1.5 collective-permute-start.9
  25.7 1.1 pad_maximum_fusion
  27.3 17.3 %collective-permute-done.6 = f32[1024,256]{1,0:T(8,128)} collective-permute-done((f32[1024,256]{1,0:T(8,128)S(1)}, f32[1024,256]{1,0:T(8,128)}, u32[]{:S(2)}, u32[]{:S(2)}) %collective-permute-start.6) | collective-permute-done | bytes 1048608 | tf_op jit(solution)/shard_map/ppermute | solution.py:342
  44.6 1.5 convolution_add_fusion.2
  46.2 1.7 collective-permute-start.7
  47.9 9.7 %collective-permute-done.1 = f32[1152,256]{1,0:T(8,128)} collective-permute-done((f32[1152,256]{1,0:T(8,128)}, f32[1152,256]{1,0:T(8,128)}, u32[]{:S(2)}, u32[]{:S(2)}) %collective-permute-start.1) | collective-permute-done | bytes 1179680 | tf_op jit(solution)/shard_map/ppermute | solution.py:342
  57.6 1.5 convolution_add_fusion.4
  59.1 2.7 %convolution_add_fusion = f32[768,256]{1,0:T(8,128)} fusion(bf16[512,256]{1,0:T(8,128)(2,1)S(1)} %get-tuple-element.16, f32[1536,256]{1,0:T(8,128)} %collective-permute-done.9, s32[]{:T(128)S(6)} %select_n.163, bf16[512,7168]{1,0:T(8,128)(2,1)} %acts_ref.5, s32[]{:T(128)S(6)} %select_n.162), kind=kOutput, calls=%fused_computation.2 | convolution fusion | flops 201523200 | bytes 2621448 | tf_op jit(solution)/shard_map/dot_general | solution.py:21
  61.8 1.5 collective-permute-start.10
  63.3 0.9 slice_add_fusion.gram_ref
  64.3 0.9 pad_maximum_fusion.1
  65.7 1.5 convolution_add_fusion.5.mine_ref
  67.2 1.7 fusion.3
  69.0 1.6 collective-permute-start.8
  70.6 10.5 %collective-permute-done.2.theirs_ref = f32[640,256]{1,0:T(8,128)S(1)} collective-permute-done((f32[640,256]{1,0:T(8,128)}, f32[640,256]{1,0:T(8,128)S(1)}, u32[]{:S(2)}, u32[]{:S(2)}) %collective-permute-start.2) | collective-permute-done | bytes 655392 | tf_op jit(solution)/shard_map/ppermute | solution.py:342
  81.0 0.6 shard_map.61
  81.8 2.0 fusion.2
  83.8 0.8 constant_dynamic-slice_fusion
  84.6 2.0 collective-permute-start.11
  86.6 10.0 %collective-permute-done.3.theirs_ref = f32[384,256]{1,0:T(8,128)S(1)} collective-permute-done((f32[384,256]{1,0:T(8,128)S(1)}, f32[384,256]{1,0:T(8,128)S(1)}, u32[]{:S(2)}, u32[]{:S(2)}) %collective-permute-start.3) | collective-permute-done | bytes 393248 | tf_op jit(solution)/shard_map/ppermute | solution.py:342
  96.6 0.6 shard_map.62
  97.2 0.6 collective-permute-start.4
  97.8 1.0 dynamic-slice_add_fusion.1
  98.8 9.7 %collective-permute-done.4.theirs_ref = f32[256,256]{1,0:T(8,128)S(1)} collective-permute-done((f32[256,256]{1,0:T(8,128)S(1)}, f32[256,256]{1,0:T(8,128)S(1)}, u32[]{:S(2)}, u32[]{:S(2)}) %collective-permute-start.4) | collective-permute-done | bytes 262176 | tf_op jit(solution)/shard_map/ppermute | solution.py:342
  108.5 0.6 shard_map.63
  109.2 1.1 dynamic-slice_add_fusion
  110.5 8.4 %shard_map.64.inverse_ref = f32[256,256]{1,0:T(8,128)S(1)} custom-call(s32[19]{0:T(128)S(1)} %fusion.23.core_ref.table_ref, f32[128,256]{1,0:T(8,128)S(1)} %get-tuple-element.22.mine_ref, f32[128,256]{1,0:T(8,128)S(1)} %collective-permute-done.5.theirs_ref, f32[128,256]{1,0:T(8,128)S(1)} %get-tuple-element.31.refs_0_.mine_ref, ...), custom_call_target="tpu_custom_call" | custom-call | flops 10000000000 | bytes 524288 | tf_op jit(solution)/shard_map/pallas_call | solution.py:123
  118.9 2.5 %collective-permute-done.23.refs_0_ = f32[192,256]{1,0:T(8,128)S(1)} collective-permute-done((f32[192,256]{1,0:T(8,128)S(1)}, f32[192,256]{1,0:T(8,128)S(1)}, u32[]{:S(2)}, u32[]{:S(2)}) %collective-permute-start.23) | collective-permute-done | bytes 196640 | tf_op jit(solution)/shard_map/ppermute | solution.py:342
  121.5 1.5 shard_map.67
  123.3 11.6 %collective-permute-done.24 = f32[192,256]{1,0:T(8,128)S(1)} collective-permute-done((f32[192,256]{1,0:T(8,128)S(1)}, f32[192,256]{1,0:T(8,128)S(1)}, u32[]{:S(2)}, u32[]{:S(2)}) %collective-permute-start.24) | collective-permute-done | bytes 196640 | tf_op jit(solution)/shard_map/ppermute | solution.py:342
  135.0 2.0 collective-permute-start.17
  137.0 1.3 shard_map.65
  138.3 1.1 collective-permute-start.12
  139.4 7.9 %collective-permute-done.17.refs_0_ = f32[128,256]{1,0:T(8,128)S(1)} collective-permute-done((f32[128,256]{1,0:T(8,128)S(1)}, f32[128,256]{1,0:T(8,128)S(1)}, u32[]{:S(2)}, u32[]{:S(2)}) %collective-permute-start.17) | collective-permute-done | bytes 131104 | tf_op jit(solution)/shard_map/ppermute | solution.py:342
  147.2 1.3 shard_map.66
  148.6 3.4 %collective-permute-start.18 = (f32[128,256]{1,0:T(8,128)S(1)}, f32[128,256]{1,0:T(8,128)S(1)}, u32[]{:S(2)}, u32[]{:S(2)}) collective-permute-start(f32[128,256]{1,0:T(8,128)S(1)} %shard_map.66), channel_id=1, source_target_pairs={{0,16},{1,17},{2,18},{3,19},{4,20},{5,21},{6,22},{7,23},{8,24},{9,... | collective-permute-start | bytes 393224 | tf_op jit(solution)/shard_map/ppermute | solution.py:342
  152.1 1.6 collective-permute-start.27
  153.8 3.2 %collective-permute-done.18 = f32[128,256]{1,0:T(8,128)S(1)} collective-permute-done((f32[128,256]{1,0:T(8,128)S(1)}, f32[128,256]{1,0:T(8,128)S(1)}, u32[]{:S(2)}, u32[]{:S(2)}) %collective-permute-start.18) | collective-permute-done | bytes 131104 | tf_op jit(solution)/shard_map/ppermute | solution.py:342
  157.1 1.6 collective-permute-start.19
  158.6 3.0 %collective-permute-done.13 = f32[256,256]{1,0:T(8,128)S(1)} collective-permute-done((f32[256,256]{1,0:T(8,128)S(1)}, f32[256,256]{1,0:T(8,128)S(1)}, u32[]{:S(2)}, u32[]{:S(2)}) %collective-permute-start.13) | collective-permute-done | bytes 262176 | tf_op jit(solution)/shard_map/ppermute | solution.py:342
  161.6 1.6 collective-permute-start.15
  163.2 1.0 collective-permute-start.14
  164.2 6.1 %collective-permute-done.19 = f32[256,256]{1,0:T(8,128)S(1)} collective-permute-done((f32[256,256]{1,0:T(8,128)S(1)}, f32[256,256]{1,0:T(8,128)S(1)}, u32[]{:S(2)}, u32[]{:S(2)}) %collective-permute-start.19) | collective-permute-done | bytes 262176 | tf_op jit(solution)/shard_map/ppermute | solution.py:342
  170.3 1.5 collective-permute-start.21
  171.8 0.6 collective-permute-start.26
  172.4 1.4 collective-permute-start.28
  173.8 7.7 %collective-permute-done.15.refs_1_ = f32[512,256]{1,0:T(8,128)S(1)} collective-permute-done((f32[512,256]{1,0:T(8,128)S(1)}, f32[512,256]{1,0:T(8,128)S(1)}, u32[]{:S(2)}, u32[]{:S(2)}) %collective-permute-start.15) | collective-permute-done | bytes 524320 | tf_op jit(solution)/shard_map/ppermute | solution.py:342
  181.5 1.4 collective-permute-start.16
  182.9 2.0 collective-permute-start.22
  184.9 5.0 %shard_map.68 = (f32[768,256]{1,0:T(8,128)S(1)}, f32[7168,256]{1,0:T(8,128)}) custom-call(s32[19]{0:T(128)S(1)} %fusion.23.core_ref.table_ref, bf16[512,7168]{1,0:T(8,128)(2,1)} %acts_ref.5, f32[512,256]{1,0:T(8,128)S(1)} %maximum_select_fusion.1.refs_0_, f32[512,256]{1,0:T(8,128)S(1)} %collective-permute-done.15.refs_1_, ...), custom_call_target="tpu_custom_call" | custom-call | flops 1409286144 | bytes 11010048 | tf_op jit(solution)/shard_map/pallas_call | solution.py:311
  189.9 4.9 %collective-permute-done.20.refs_2_ = f32[512,256]{1,0:T(8,128)S(1)} collective-permute-done((f32[512,256]{1,0:T(8,128)S(1)}, f32[512,256]{1,0:T(8,128)S(1)}, u32[]{:S(2)}, u32[]{:S(2)}) %collective-permute-start.20) | collective-permute-done | bytes 524320 | tf_op jit(solution)/shard_map/ppermute | solution.py:342
  194.8 9.3 %collective-permute-done.16.refs_1_ = f32[512,256]{1,0:T(8,128)S(1)} collective-permute-done((f32[512,256]{1,0:T(8,128)S(1)}, f32[512,256]{1,0:T(8,128)S(1)}, u32[]{:S(2)}, u32[]{:S(2)}) %collective-permute-start.16) | collective-permute-done | bytes 524320 | tf_op jit(solution)/shard_map/ppermute | solution.py:342
  204.1 4.9 %shard_map.69 = (f32[768,256]{1,0:T(8,128)S(1)}, f32[7168,256]{1,0:T(8,128)}) custom-call(s32[19]{0:T(128)S(1)} %fusion.23.core_ref.table_ref, bf16[512,7168]{1,0:T(8,128)(2,1)} %acts_ref.5, f32[512,256]{1,0:T(8,128)S(1)} %collective-permute-done.14.refs_0_, ...), custom_call_target="tpu_custom_call", output_to_operand_aliasing={{0}: (8, {}), {1}: (9, {})} | custom-call | flops 1409286144 | bytes 11010048 | tf_op jit(solution)/shard_map/pallas_call | solution.py:311
  209.1 2.1 collective-permute-start.29
  211.1 1.9 collective-permute-done.29.theirs_ref
  213.1 2.0 shard_map.70
  (35 shorter events, 2.7 us)
Async XLA Ops:
  0.6 12.0 %copy-start = (f32[512,256]{1,0:T(8,128)S(1)}, f32[512,256]{1,0:T(8,128)}, u32[]{:S(2)}) copy-start(f32[512,256]{1,0:T(8,128)} %codes_ref.1) | copy-start | bytes 1572868
  10.2 2.4 %collective-permute-start = (f32[768,256]{1,0:T(8,128)S(1)}, f32[768,256]{1,0:T(8,128)S(1)}, u32[]{:S(2)}, u32[]{:S(2)}) collective-permute-start(f32[768,256]{1,0:T(8,128)S(1)} %shard_map.59.mine_ref), channel_id=1, source_target_pairs={{0,1},{1,0},{2,3},{3,2},{4,5},{5,4},{6,7},{7,6},{8,9},{9,8},{10,11... | collective-permute-start | bytes 2359304 | tf_op jit(solution)/shard_map/ppermute | solution.py:375
  18.0 26.6 %collective-permute-start.6 = (f32[1024,256]{1,0:T(8,128)S(1)}, f32[1024,256]{1,0:T(8,128)}, u32[]{:S(2)}, u32[]{:S(2)}) collective-permute-start(f32[1024,256]{1,0:T(8,128)S(1)} %fusion.4), channel_id=1, source_target_pairs={{0,8},{1,9},{2,10},{3,11},{4,12},{5,13},{6,14},{7,15},{8,0},{9,1},... | collective-permute-start | bytes 3145736 | tf_op jit(solution)/shard_map/ppermute | solution.py:342
  24.2 34.9 %collective-permute-start.9 = (f32[1536,256]{1,0:T(8,128)}, f32[1536,256]{1,0:T(8,128)}, u32[]{:S(2)}, u32[]{:S(2)}) collective-permute-start(f32[1536,256]{1,0:T(8,128)} %fusion), channel_id=1, source_target_pairs={{0,2},{1,5},{2,0},{3,7},{4,6},{5,1},{6,4},{7,3},{8,10},{9,13},{10,... | collective-permute-start | bytes 4718600 | tf_op jit(solution)/shard_map/ppermute | solution.py:342
  26.8 30.8 %collective-permute-start.1 = (f32[1152,256]{1,0:T(8,128)}, f32[1152,256]{1,0:T(8,128)}, u32[]{:S(2)}, u32[]{:S(2)}) collective-permute-start(f32[1152,256]{1,0:T(8,128)} %pad_maximum_fusion), channel_id=1, source_target_pairs={{0,2},{1,5},{2,0},{3,7},{4,6},{5,1},{6,4},{7,3},{8,10},{9,13},{10,... | collective-permute-start | bytes 3538952 | tf_op jit(solution)/shard_map/ppermute | solution.py:342
  46.2 21.1 %collective-permute-start.7 = (f32[512,256]{1,0:T(8,128)S(1)}, f32[512,256]{1,0:T(8,128)}, u32[]{:S(2)}, u32[]{:S(2)}) collective-permute-start(f32[512,256]{1,0:T(8,128)S(1)} %convolution_add_fusion.2), channel_id=1, source_target_pairs={{0,2},{1,5},{2,0},{3,7},{4,6},{5,1},{6,4},{7,3},{8,10},{9,13},{10,... | collective-permute-start | bytes 1572872 | tf_op jit(solution)/shard_map/ppermute | solution.py:342
  61.8 19.9 %collective-permute-start.10 = (f32[768,256]{1,0:T(8,128)}, f32[768,256]{1,0:T(8,128)}, u32[]{:S(2)}, u32[]{:S(2)}) collective-permute-start(f32[768,256]{1,0:T(8,128)} %convolution_add_fusion), channel_id=1, source_target_pairs={{0,4},{1,3},{2,6},{3,1},{4,0},{5,7},{6,2},{7,5},{8,12},{9,11},{10,... | collective-permute-start | bytes 2359304 | tf_op jit(solution)/shard_map/ppermute | solution.py:342
  65.2 15.9 %collective-permute-start.2 = (f32[640,256]{1,0:T(8,128)}, f32[640,256]{1,0:T(8,128)S(1)}, u32[]{:S(2)}, u32[]{:S(2)}) collective-permute-start(f32[640,256]{1,0:T(8,128)} %pad_maximum_fusion.1), channel_id=1, source_target_pairs={{0,4},{1,3},{2,6},{3,1},{4,0},{5,7},{6,2},{7,5},{8,12},{9,11},{10,... | collective-permute-start | bytes 1966088 | tf_op jit(solution)/shard_map/ppermute | solution.py:342
  69.0 28.8 %collective-permute-start.8 = (f32[256,256]{1,0:T(8,128)S(1)}, f32[256,256]{1,0:T(8,128)}, u32[]{:S(2)}, u32[]{:S(2)}) collective-permute-start(f32[256,256]{1,0:T(8,128)S(1)} %constant_dynamic-slice_fusion.3), channel_id=1, source_target_pairs={{0,4},{1,3},{2,6},{3,1},{4,0},{5,7},{6,2},{7,5},{8,12},{9,11},{10,... | collective-permute-start | bytes 786440 | tf_op jit(solution)/shard_map/ppermute | solution.py:342
  81.7 14.9 %collective-permute-start.3 = (f32[384,256]{1,0:T(8,128)S(1)}, f32[384,256]{1,0:T(8,128)S(1)}, u32[]{:S(2)}, u32[]{:S(2)}) collective-permute-start(f32[384,256]{1,0:T(8,128)S(1)} %get-tuple-element.19), channel_id=1, source_target_pairs={{0,8},{1,9},{2,10},{3,11},{4,12},{5,13},{6,14},{7,15},{8,0},{9,1},... | collective-permute-start | bytes 1179656 | tf_op jit(solution)/shard_map/ppermute | solution.py:342
  84.6 24.6 %collective-permute-start.11 = (f32[384,256]{1,0:T(8,128)}, f32[384,256]{1,0:T(8,128)}, u32[]{:S(2)}, u32[]{:S(2)}) collective-permute-start(f32[384,256]{1,0:T(8,128)} %constant_dynamic-slice_fusion), channel_id=1, source_target_pairs={{0,8},{1,9},{2,10},{3,11},{4,12},{5,13},{6,14},{7,15},{8,0},{9,1},... | collective-permute-start | bytes 1179656 | tf_op jit(solution)/shard_map/ppermute | solution.py:342
  97.2 11.3 %collective-permute-start.4 = (f32[256,256]{1,0:T(8,128)S(1)}, f32[256,256]{1,0:T(8,128)S(1)}, u32[]{:S(2)}, u32[]{:S(2)}) collective-permute-start(f32[256,256]{1,0:T(8,128)S(1)} %get-tuple-element.21), channel_id=1, source_target_pairs={{0,16},{1,17},{2,18},{3,19},{4,20},{5,21},{6,22},{7,23},{8,24},{9,... | collective-permute-start | bytes 786440 | tf_op jit(solution)/shard_map/ppermute | solution.py:342
  109.1 1.4 collective-permute-start.5
  110.3 11.2 %collective-permute-start.23 = (f32[192,256]{1,0:T(8,128)S(1)}, f32[192,256]{1,0:T(8,128)S(1)}, u32[]{:S(2)}, u32[]{:S(2)}) collective-permute-start(f32[192,256]{1,0:T(8,128)S(1)} %get-tuple-element.28), channel_id=1, source_target_pairs={{0,16},{1,17},{2,18},{3,19},{4,20},{5,21},{6,22},{7,23},{8,24},{9,... | collective-permute-start | bytes 589832 | tf_op jit(solution)/shard_map/ppermute | solution.py:342
  123.0 11.9 %collective-permute-start.24 = (f32[192,256]{1,0:T(8,128)S(1)}, f32[192,256]{1,0:T(8,128)S(1)}, u32[]{:S(2)}, u32[]{:S(2)}) collective-permute-start(f32[192,256]{1,0:T(8,128)S(1)} %shard_map.67), channel_id=1, source_target_pairs={{0,16},{1,17},{2,18},{3,19},{4,20},{5,21},{6,22},{7,23},{8,24},{9,... | collective-permute-start | bytes 589832 | tf_op jit(solution)/shard_map/ppermute | solution.py:342
  134.9 17.1 %collective-permute-start.25 = (f32[384,256]{1,0:T(8,128)S(1)}, f32[384,256]{1,0:T(8,128)S(1)}, u32[]{:S(2)}, u32[]{:S(2)}) collective-permute-start(f32[384,256]{1,0:T(8,128)S(1)} %maximum_select_fusion.3), channel_id=1, source_target_pairs={{0,8},{1,9},{2,10},{3,11},{4,12},{5,13},{6,14},{7,15},{8,0},{9,1},... | collective-permute-start | bytes 1179656 | tf_op jit(solution)/shard_map/ppermute | solution.py:342
  135.0 12.3 %collective-permute-start.17 = (f32[128,256]{1,0:T(8,128)S(1)}, f32[128,256]{1,0:T(8,128)S(1)}, u32[]{:S(2)}, u32[]{:S(2)}) collective-permute-start(f32[128,256]{1,0:T(8,128)S(1)} %get-tuple-element.30), channel_id=1, source_target_pairs={{0,16},{1,17},{2,18},{3,19},{4,20},{5,21},{6,22},{7,23},{8,24},{9,... | collective-permute-start | bytes 393224 | tf_op jit(solution)/shard_map/ppermute | solution.py:342
  138.3 15.4 %collective-permute-start.12 = (f32[128,256]{1,0:T(8,128)S(1)}, f32[128,256]{1,0:T(8,128)S(1)}, u32[]{:S(2)}, u32[]{:S(2)}) collective-permute-start(f32[128,256]{1,0:T(8,128)S(1)} %shard_map.65), channel_id=1, source_target_pairs={{0,16},{1,17},{2,18},{3,19},{4,20},{5,21},{6,22},{7,23},{8,24},{9,... | collective-permute-start | bytes 393224 | tf_op jit(solution)/shard_map/ppermute | solution.py:342
  148.6 8.5 %collective-permute-start.18 = (f32[128,256]{1,0:T(8,128)S(1)}, f32[128,256]{1,0:T(8,128)S(1)}, u32[]{:S(2)}, u32[]{:S(2)}) collective-permute-start(f32[128,256]{1,0:T(8,128)S(1)} %shard_map.66), channel_id=1, source_target_pairs={{0,16},{1,17},{2,18},{3,19},{4,20},{5,21},{6,22},{7,23},{8,24},{9,... | collective-permute-start | bytes 393224 | tf_op jit(solution)/shard_map/ppermute | solution.py:342
  152.1 20.3 %collective-permute-start.27 = (f32[768,256]{1,0:T(8,128)S(1)}, f32[768,256]{1,0:T(8,128)S(1)}, u32[]{:S(2)}, u32[]{:S(2)}) collective-permute-start(f32[768,256]{1,0:T(8,128)S(1)} %maximum_select_fusion.refs_4_), channel_id=1, source_target_pairs={{0,4},{1,3},{2,6},{3,1},{4,0},{5,7},{6,2},{7,5},{8,12},{9,11},{10,... | collective-permute-start | bytes 2359304 | tf_op jit(solution)/shard_map/ppermute | solution.py:342
  153.7 7.9 %collective-permute-start.13 = (f32[256,256]{1,0:T(8,128)S(1)}, f32[256,256]{1,0:T(8,128)S(1)}, u32[]{:S(2)}, u32[]{:S(2)}) collective-permute-start(f32[256,256]{1,0:T(8,128)S(1)} %maximum_select_fusion.4), channel_id=1, source_target_pairs={{0,8},{1,9},{2,10},{3,11},{4,12},{5,13},{6,14},{7,15},{8,0},{9,1},... | collective-permute-start | bytes 786440 | tf_op jit(solution)/shard_map/ppermute | solution.py:342
  157.1 13.2 %collective-permute-start.19 = (f32[256,256]{1,0:T(8,128)S(1)}, f32[256,256]{1,0:T(8,128)S(1)}, u32[]{:S(2)}, u32[]{:S(2)}) collective-permute-start(f32[256,256]{1,0:T(8,128)S(1)} %maximum_select_fusion.5), channel_id=1, source_target_pairs={{0,4},{1,3},{2,6},{3,1},{4,0},{5,7},{6,2},{7,5},{8,12},{9,11},{10,... | collective-permute-start | bytes 786440 | tf_op jit(solution)/shard_map/ppermute | solution.py:342
  161.6 19.9 %collective-permute-start.15 = (f32[512,256]{1,0:T(8,128)S(1)}, f32[512,256]{1,0:T(8,128)S(1)}, u32[]{:S(2)}, u32[]{:S(2)}) collective-permute-start(f32[512,256]{1,0:T(8,128)S(1)} %maximum_select_fusion.1.refs_0_), channel_id=1, source_target_pairs={{0,4},{1,3},{2,6},{3,1},{4,0},{5,7},{6,2},{7,5},{8,12},{9,11},{10,... | collective-permute-start | bytes 1572872 | tf_op jit(solution)/shard_map/ppermute | solution.py:342
  163.2 18.3 %collective-permute-start.14 = (f32[512,256]{1,0:T(8,128)S(1)}, f32[512,256]{1,0:T(8,128)S(1)}, u32[]{:S(2)}, u32[]{:S(2)}) collective-permute-start(f32[512,256]{1,0:T(8,128)S(1)} %maximum_select_fusion.1.refs_0_), channel_id=1, source_target_pairs={{0,2},{1,5},{2,0},{3,7},{4,6},{5,1},{6,4},{7,3},{8,10},{9,13},{10,... | collective-permute-start | bytes 1572872 | tf_op jit(solution)/shard_map/ppermute | solution.py:342
  170.3 12.6 %collective-permute-start.21 = (f32[512,256]{1,0:T(8,128)S(1)}, f32[512,256]{1,0:T(8,128)S(1)}, u32[]{:S(2)}, u32[]{:S(2)}) collective-permute-start(f32[512,256]{1,0:T(8,128)S(1)} %maximum_select_fusion.2.refs_2_), channel_id=1, source_target_pairs={{0,2},{1,5},{2,0},{3,7},{4,6},{5,1},{6,4},{7,3},{8,10},{9,13},{10,... | collective-permute-start | bytes 1572872 | tf_op jit(solution)/shard_map/ppermute | solution.py:342
  171.8 32.3 %collective-permute-start.26 = (f32[768,256]{1,0:T(8,128)S(1)}, f32[768,256]{1,0:T(8,128)S(1)}, u32[]{:S(2)}, u32[]{:S(2)}) collective-permute-start(f32[768,256]{1,0:T(8,128)S(1)} %maximum_select_fusion.refs_4_), channel_id=1, source_target_pairs={{0,2},{1,5},{2,0},{3,7},{4,6},{5,1},{6,4},{7,3},{8,10},{9,13},{10,... | collective-permute-start | bytes 2359304 | tf_op jit(solution)/shard_map/ppermute | solution.py:342
  172.4 31.7 %collective-permute-start.28 = (f32[768,256]{1,0:T(8,128)S(1)}, f32[768,256]{1,0:T(8,128)S(1)}, u32[]{:S(2)}, u32[]{:S(2)}) collective-permute-start(f32[768,256]{1,0:T(8,128)S(1)} %collective-permute-done.27.refs_5_), channel_id=1, source_target_pairs={{0,2},{1,5},{2,0},{3,7},{4,6},{5,1},{6,4},{7,3},{8,10},{9,13},{10,... | collective-permute-start | bytes 2359304 | tf_op jit(solution)/shard_map/ppermute | solution.py:342
  181.5 13.3 %collective-permute-start.20 = (f32[512,256]{1,0:T(8,128)S(1)}, f32[512,256]{1,0:T(8,128)S(1)}, u32[]{:S(2)}, u32[]{:S(2)}) collective-permute-start(f32[512,256]{1,0:T(8,128)S(1)} %maximum_select_fusion.2.refs_2_), channel_id=1, source_target_pairs={{0,8},{1,9},{2,10},{3,11},{4,12},{5,13},{6,14},{7,15},{8,0},{9,1},... | collective-permute-start | bytes 1572872 | tf_op jit(solution)/shard_map/ppermute | solution.py:342
  181.5 22.6 %collective-permute-start.16 = (f32[512,256]{1,0:T(8,128)S(1)}, f32[512,256]{1,0:T(8,128)S(1)}, u32[]{:S(2)}, u32[]{:S(2)}) collective-permute-start(f32[512,256]{1,0:T(8,128)S(1)} %collective-permute-done.15.refs_1_), channel_id=1, source_target_pairs={{0,2},{1,5},{2,0},{3,7},{4,6},{5,1},{6,4},{7,3},{8,10},{9,13},{10,... | collective-permute-start | bytes 1572872 | tf_op jit(solution)/shard_map/ppermute | solution.py:342
  182.9 21.2 %collective-permute-start.22 = (f32[512,256]{1,0:T(8,128)S(1)}, f32[512,256]{1,0:T(8,128)S(1)}, u32[]{:S(2)}, u32[]{:S(2)}) collective-permute-start(f32[512,256]{1,0:T(8,128)S(1)} %collective-permute-done.21.refs_3_), channel_id=1, source_target_pairs={{0,8},{1,9},{2,10},{3,11},{4,12},{5,13},{6,14},{7,15},{8,0},{9,1},... | collective-permute-start | bytes 1572872 | tf_op jit(solution)/shard_map/ppermute | solution.py:342
  209.1 4.0 %collective-permute-start.29 = (f32[768,256]{1,0:T(8,128)S(1)}, f32[768,256]{1,0:T(8,128)S(1)}, u32[]{:S(2)}, u32[]{:S(2)}) collective-permute-start(f32[768,256]{1,0:T(8,128)S(1)} %get-tuple-element.26.mine_ref), channel_id=1, source_target_pairs={{0,1},{1,0},{2,3},{3,2},{4,5},{5,4},{6,7},{7,6},{8,9},{9,8},{10,11... | collective-permute-start | bytes 2359304 | tf_op jit(solution)/shard_map/ppermute | solution.py:375

commit v4 on v3

--- a/solution.py
+++ b/solution.py
@@ -202,7 +202,7 @@
 WHOLE = pl.BlockSpec(memory_space=pltpu.VMEM)
 SCALARS = pl.BlockSpec(memory_space=pltpu.SMEM)
 ANYWHERE = pl.BlockSpec(memory_space=pl.ANY)
-TILE = 256
+TILE = 128
 
 
 def call(kernel, out_shapes, table, values, after):
@@ -236,41 +236,29 @@
     return call(functools.partial(first_fold_kernel, at), [half, half], table, [mine, theirs, gram], [])
 
 
-def mixed_fold_kernel(at, extra, table_ref, mine_ref, theirs_ref, *refs):
-    whole = mine_ref.shape[0] - extra
-    rows = whole // 2
-    keep = pl.ds(pl.multiple_of(table_ref[at] * rows, 8), rows)
-    give = pl.ds(pl.multiple_of((1 - table_ref[at]) * rows, 8), rows)
-    gram = mine_ref[whole:, :] + theirs_ref[whole:, :]
-    refs[-2][:rows, :] = mine_ref[give, :] + theirs_ref[give, :]
-    refs[-2][rows:, :] = gram
-    refs[-1][:rows, :] = mine_ref[keep, :] + theirs_ref[keep, :]
-    refs[-1][rows:, :] = gram
-
-
-def mixed_fold(table, at, extra, mine, theirs, after):
-    half = shape((mine.shape[0] - extra) // 2 + extra, mine.shape[1])
-    return call(functools.partial(mixed_fold_kernel, at, extra), [half, half], table, [mine, theirs], after)
-
-
-def part_kernel(rows, table_ref, mine_ref, theirs_ref, *refs):
-    refs[-2][...] = mine_ref[:rows, :] + theirs_ref[:rows, :]
-    refs[-1][...] = mine_ref[rows:, :] + theirs_ref[rows:, :]
-
-
-def part(table, rows, mine, theirs, after):
-    shapes = [shape(rows, mine.shape[1]), shape(mine.shape[0] - rows, mine.shape[1])]
-    return call(functools.partial(part_kernel, rows), shapes, table, [mine, theirs], after)
+def split_fold_kernel(at, table_ref, mine_ref, theirs_ref, give_ref, keep_ref, gram_ref):
+    rows = give_ref.shape[0]
+    keep = pl.ds(pl.multiple_of(table_ref[at] * rows, rows), rows)
+    give = pl.ds(pl.multiple_of((1 - table_ref[at]) * rows, rows), rows)
+    give_ref[...] = mine_ref[give, :] + theirs_ref[give, :]
+    keep_ref[...] = mine_ref[keep, :] + theirs_ref[keep, :]
+    gram_ref[...] = mine_ref[2 * rows :, :] + theirs_ref[2 * rows :, :]
+
+
+def split_fold(table, at, extra, mine, theirs):
+    comp = mine.shape[1]
+    half = shape((mine.shape[0] - extra) // 2, comp)
+    return call(functools.partial(split_fold_kernel, at), [half, half, shape(extra, comp)], table, [mine, theirs], [])
 
 
 def rows_kernel(table_ref, inverse_ref, mine_ref, *refs):
     inverse = inverse_ref[...]
-    cross = mine_ref[...] + refs[0][...] if len(refs) > 1 else mine_ref[...]
+    cross = mine_ref[...] + refs[0][...]
     refs[-1][...] = dot(dot(cross, inverse, OVER_COLS, HIGHEST), inverse, precision=HIGHEST)
 
 
-def solve_sum(table, inverse, parts):
-    return call(rows_kernel, [shape(*parts[0].shape)], table, [inverse, *parts], [])[0]
+def solve_sum(table, inverse, parts, after):
+    return call(rows_kernel, [shape(*parts[0].shape)], table, [inverse, *parts], after)[0]
 
 
 def absorb_kernel(ats, fresh, table_ref, acts_ref, *refs):
@@ -331,10 +319,10 @@
 ALONG = {"first": (X, Y), "second": (Y, X), "near": (ZL, ZL), "far": (ZH, ZH)}
 ORDERS = {
     "A": ("first", "second", "near", "far"),
-    "B": ("first", "second", "near", "far"),
+    "B": ("first", "near", "second", "far"),
     "N": ("near", "first", "second", "far"),
 }
-SHARES = {"A": 2, "B": 3, "N": 2}
+SHARES = {"A": 4, "B": 5, "N": 5}
 FIELDS = ("c", "d", "mine", "theirs", "far_mine", "far_theirs")
 
 
@@ -407,19 +395,14 @@
     def joined(one, other, which):
         return jnp.where(which == 0, jnp.concatenate([one, other]), jnp.concatenate([other, one]))
 
-    extra = gram.shape[0]
-    got = {
-        "A": swap(jnp.concatenate([give_1("A"), gram]), ORDERS["A"][0]),
-        "N": swap(give_1("N"), ORDERS["N"][0]),
-        "B": swap(give_1("B"), ORDERS["B"][0]),
-    }
-    gram = gram + got["A"][rows["A"] // 2 :]
+    gram = gram + swap(gram, "far")
     held = {}
-    for name in ("A", "N", "B"):
-        give = stage_2(name, got[name], False)
+    for name, order in ORDERS.items():
+        got = swap(give_1(name), order[0])
+        give = stage_2(name, got, False)
         if name == "A":
             give = jnp.concatenate([give, gram])
-        held[name] = stage_2(name, got[name], True), swap(give, ORDERS[name][1])
+        held[name] = stage_2(name, got, True), swap(give, order[1])
     for name, (keep, arrived) in held.items():
         along = ORDERS[name][2]
         if name == "A":
@@ -431,27 +414,32 @@
     for name, (keep, arrived) in held.items():
         along = ORDERS[name][3]
         if name == "A":
-            give, keep = mixed_fold(table, where[name, "d"], extra, keep, arrived, [])
+            give, keep, gram = split_fold(table, where[name, "d"], gram.shape[0], keep, arrived)
+            gram = gram + swap(gram, "first")
             held[name] = keep, swap(give, along)
         else:
             keep = keep + arrived
             held[name] = part_of(keep, bits[along]), swap(part_of(keep, 1 - bits[along]), along)
 
-    a_mine, gram = part(table, rows["A"] // 16, *held["A"], [])
-    inverse = factor_inverse(table, gram, other_core(gram), [held["N"][0], held["B"][0]])
-    held["A"] = (a_mine,)
-    mine = {name: solve_sum(table, inverse, held[name]) for name in held}
+    inverse = factor_inverse(table, gram, other_core(gram))
+    mine = {}
+    for name in held:
+        mine[name] = solve_sum(table, inverse, held[name], list(mine.values()))
 
     for k in (3, 2):
         for name in mine:
             along = ORDERS[name][k]
             mine[name] = joined(mine[name], swap(mine[name], along), bits[along])
-    near, far = [], []
+    near, far, last = [], [], []
     for name in mine:
         theirs = swap(mine[name], ORDERS[name][1])
         near += [(mine[name], where[name, "mine"]), (theirs, where[name, "theirs"])]
-        far += [(swap(value, ORDERS[name][0]), where[name, field]) for value, field in ((mine[name], "far_mine"), (theirs, "far_theirs"))]
-    sums, dict_out = absorb(table, absorb(table, None, acts, near), acts, far)
+        far += [(swap(mine[name], ORDERS[name][0]), where[name, "far_mine"])]
+        last += [(swap(theirs, ORDERS[name][0]), where[name, "far_theirs"])]
+    state = None
+    for blocks in (near, far, last):
+        state = absorb(table, state, acts, blocks)
+    sums, dict_out = state
     return second_update(codes_mid, sums, other_core(sums)), dict_out
 
 
@@ -459,7 +447,7 @@
     tok, hid = mesh.shape["tok"], mesh.shape["hid"]
 
     def per_device(acts, dictionary, codes):
-        if tok == 16 and hid == 2 and acts.shape[1] % (7 * 1024) == 0:
+        if tok == 16 and hid == 2 and acts.shape[1] % (14 * 512) == 0:
             return meshed(acts, dictionary, codes)
         return plain(acts, dictionary, codes, acts.shape[1] % tok == 0)
 

time: 216 us -> 197 us (0.912)
  waiting for transfers between devices: 117 us -> 91.4 us
  starting transfers between devices: 35.4 us -> 43.7 us
  other arithmetic: 5.21 us -> 0.38 us
    ppermute x27 -> x29, waiting for transfers between devices: 113 us -> 87.9 us  [swap(): return lax.ppermute(value, BOTH, flips(ALONG[along]))]
    ppermute x27 -> x29, starting transfers between devices: 32.7 us -> 43.1 us  [swap(): return lax.ppermute(value, BOTH, flips(ALONG[along]))]
    pallas_call x2 -> x3, Pallas kernels: 9.92 us -> 12.7 us  [absorb(): pl.pallas_call(functools.partial(absorb_kernel, [at for _, at in blocks],...]
    pallas_call x6 -> x5, Pallas kernels: 5.93 us -> 5.29 us  [call(): pl.pallas_call(kernel, out_shape=out_shapes, in_specs=[SCALARS] + [WHOLE]...]
  transfers between devices with their start and end apart: 30 -> 32, of which waited for: 17 -> 17; matrix products, arithmetic and copies ran while one was open for 10% -> 10% of each run, Pallas kernels for 8% -> 12%
where the time goes in v4:
time: 197 us
  waiting for transfers between devices  91.4 us (46%)
  starting transfers between devices  43.7 us (22%)
  Pallas kernels  39.9 us (20%)
  matrix products  19.6 us (10%)
    ppermute x29, waiting for transfers between devices, swap(): return lax.ppermute(value, BOTH, flips(ALONG[along]))  87.9 us
    ppermute x29, starting transfers between devices, swap(): return lax.ppermute(value, BOTH, flips(ALONG[along]))  43.1 us
    dot_general x9, matrix products, dot(): lax.dot_general(left, right, dims, precision=precision, preferred_element...  19.6 us
    pallas_call x3, Pallas kernels, absorb(): pl.pallas_call(functools.partial(absorb_kernel, [at for _, at in blocks],...  12.7 us
    pallas_call x1, Pallas kernels, project(): pl.pallas_call(project_kernel, out_shape=jax.ShapeDtypeStruct((tokens + c...  9.55 us
    pallas_call x1, Pallas kernels, factor_inverse(): pl.pallas_call(halves_kernel, out_shape=jax.ShapeDtypeStruct((comp, comp)...  8.43 us
    pallas_call x5, Pallas kernels, call(): pl.pallas_call(kernel, out_shape=out_shapes, in_specs=[SCALARS] + [WHOLE]...  5.29 us
  transfers between devices with their start and end apart: 32, of which 17 were waited for; matrix products, arithmetic and copies ran while one was open for 10% of the time, Pallas kernels for 12%

profile of v4, /device:TPU:0, one launch (start us, length us, event | category | flops | bytes accessed | tf_op | source)
XLA Modules:
  0.0 196.9 jit_solution(17189443234962184408)
XLA Ops:
  0.6 9.6 %shard_map.59.mine_ref = f32[768,256]{1,0:T(8,128)S(1)} custom-call(bf16[512,7168]{1,0:T(8,128)(2,1)} %acts_ref.7, f32[7168,256]{1,0:T(8,128)} %dict_ref.1), custom_call_target="tpu_custom_call" | custom-call | flops 3758096384 | bytes 14680064 | tf_op jit(solution)/shard_map/pallas_call | solution.py:58
  10.2 0.5 collective-permute-start
  10.7 0.7 fusion.23.core_ref.table_ref
  11.4 1.2 collective-permute-done.theirs_ref
  12.6 2.0 %shard_map.60 = (f32[512,256]{1,0:T(8,128)S(1)}, bf16[512,256]{1,0:T(8,128)(2,1)S(1)}, f32[128,256]{1,0:T(8,128)S(1)}) custom-call(s32[19]{0:T(128)S(1)} %fusion.23.core_ref.table_ref, f32[512,256]{1,0:T(8,128)S(1)} %copy-done, f32[768,256]{1,0:T(8,128)S(1)} %shard_map.59.mine_ref, f32[768,256]{1,0:T(8,128)S(1)} %collective-permute-done.theirs_ref), custom_call_target="tpu_custom_call" | custom-call | tf_op jit(solution)/shard_map/pallas_call | solution.py:177
  14.6 1.7 fusion.6
  16.3 2.9 %collective-permute-start.1 = (f32[1024,256]{1,0:T(8,128)S(1)}, f32[1024,256]{1,0:T(8,128)S(1)}, u32[]{:S(2)}, u32[]{:S(2)}) collective-permute-start(f32[1024,256]{1,0:T(8,128)S(1)} %fusion.6), channel_id=1, source_target_pairs={{0,2},{1,5},{2,0},{3,7},{4,6},{5,1},{6,4},{7,3},{8,10},{9,13},{10,... | collective-permute-start | bytes 3145736 | tf_op jit(solution)/shard_map/ppermute | solution.py:330
  19.3 2.9 %fusion.2 = f32[1280,256]{1,0:T(8,128)} fusion(bf16[512,256]{1,0:T(8,128)(2,1)S(1)} %get-tuple-element.17, bf16[512,7168]{1,0:T(8,128)(2,1)} %acts_ref.7, s32[]{:T(128)S(6)} %select_n.146), kind=kOutput, calls=%fused_computation.2 | convolution fusion | flops 335544320 | bytes 2883588 | tf_op jit(solution)/shard_map/dot_general | solution.py:21
  22.2 2.9 %fusion = f32[1280,256]{1,0:T(8,128)} fusion(bf16[512,256]{1,0:T(8,128)(2,1)S(1)} %get-tuple-element.17, bf16[512,7168]{1,0:T(8,128)(2,1)} %acts_ref.7, s32[]{:T(128)S(6)} %select_n.157), kind=kOutput, calls=%fused_computation | convolution fusion | flops 335544320 | bytes 2883588 | tf_op jit(solution)/shard_map/dot_general | solution.py:21
  25.1 2.1 %collective-permute-start.20 = (f32[1280,256]{1,0:T(8,128)}, f32[1280,256]{1,0:T(8,128)}, u32[]{:S(2)}, u32[]{:S(2)}) collective-permute-start(f32[1280,256]{1,0:T(8,128)} %fusion), channel_id=1, source_target_pairs={{0,8},{1,9},{2,10},{3,11},{4,12},{5,13},{6,14},{7,15},{8,0},{9,1},... | collective-permute-start | bytes 3932168 | tf_op jit(solution)/shard_map/ppermute | solution.py:330
  27.2 2.6 %collective-permute-start.2 = (f32[128,256]{1,0:T(8,128)S(1)}, f32[128,256]{1,0:T(8,128)S(1)}, u32[]{:S(2)}, u32[]{:S(2)}) collective-permute-start(f32[128,256]{1,0:T(8,128)S(1)} %get-tuple-element.18), channel_id=1, source_target_pairs={{0,16},{1,17},{2,18},{3,19},{4,20},{5,21},{6,22},{7,23},{8,24},{9,... | collective-permute-start | bytes 393224 | tf_op jit(solution)/shard_map/ppermute | solution.py:330
  29.8 28.2 %collective-permute-done.2 = f32[128,256]{1,0:T(8,128)S(1)} collective-permute-done((f32[128,256]{1,0:T(8,128)S(1)}, f32[128,256]{1,0:T(8,128)S(1)}, u32[]{:S(2)}, u32[]{:S(2)}) %collective-permute-start.2) | collective-permute-done | bytes 131104 | tf_op jit(solution)/shard_map/ppermute | solution.py:330
  58.0 1.8 convolution_add_fusion.4
  59.9 1.6 collective-permute-start.3
  61.5 2.5 %convolution_add_fusion.2 = f32[640,256]{1,0:T(8,128)} fusion(bf16[512,256]{1,0:T(8,128)(2,1)S(1)} %get-tuple-element.17, f32[1280,256]{1,0:T(8,128)} %collective-permute-done.12, s32[]{:T(128)S(6)} %select_n.149, bf16[512,7168]{1,0:T(8,128)(2,1)} %acts_ref.7, s32[]{:T(128)S(6)} %select_n.148), kind=kOutput, calls=%fused_computation.6 | convolution fusion | flops 167936000 | bytes 2228232 | tf_op jit(solution)/shard_map/dot_general | solution.py:21
  64.0 3.5 %collective-permute-start.13 = (f32[640,256]{1,0:T(8,128)}, f32[640,256]{1,0:T(8,128)}, u32[]{:S(2)}, u32[]{:S(2)}) collective-permute-start(f32[640,256]{1,0:T(8,128)} %convolution_add_fusion.2), channel_id=1, source_target_pairs={{0,8},{1,9},{2,10},{3,11},{4,12},{5,13},{6,14},{7,15},{8,0},{9,1},... | collective-permute-start | bytes 1966088 | tf_op jit(solution)/shard_map/ppermute | solution.py:330
  67.5 2.5 %convolution_add_fusion = f32[640,256]{1,0:T(8,128)} fusion(bf16[512,256]{1,0:T(8,128)(2,1)S(1)} %get-tuple-element.17, f32[1280,256]{1,0:T(8,128)} %collective-permute-done.20, s32[]{:T(128)S(6)} %select_n.160, bf16[512,7168]{1,0:T(8,128)(2,1)} %acts_ref.7, s32[]{:T(128)S(6)} %select_n.159), kind=kOutput, calls=%fused_computation.4 | convolution fusion | flops 167936000 | bytes 2228232 | tf_op jit(solution)/shard_map/dot_general | solution.py:21
  70.0 1.5 collective-permute-start.21
  71.5 1.5 convolution_add_fusion.5.mine_ref
  73.0 0.6 shard_map.61
  73.6 4.2 %collective-permute-start.4 = (f32[384,256]{1,0:T(8,128)S(1)}, f32[384,256]{1,0:T(8,128)S(1)}, u32[]{:S(2)}, u32[]{:S(2)}) collective-permute-start(f32[384,256]{1,0:T(8,128)S(1)} %get-tuple-element.20), channel_id=1, source_target_pairs={{0,8},{1,9},{2,10},{3,11},{4,12},{5,13},{6,14},{7,15},{8,0},{9,1},... | collective-permute-start | bytes 1179656 | tf_op jit(solution)/shard_map/ppermute | solution.py:330
  77.8 5.6 %collective-permute-done.13 = f32[640,256]{1,0:T(8,128)} collective-permute-done((f32[640,256]{1,0:T(8,128)}, f32[640,256]{1,0:T(8,128)}, u32[]{:S(2)}, u32[]{:S(2)}) %collective-permute-start.13) | collective-permute-done | bytes 655392 | tf_op jit(solution)/shard_map/ppermute | solution.py:330
  83.4 1.9 fusion.4
  85.4 0.6 collective-permute-start.14
  85.9 3.1 %collective-permute-done.4.theirs_ref = f32[384,256]{1,0:T(8,128)S(1)} collective-permute-done((f32[384,256]{1,0:T(8,128)S(1)}, f32[384,256]{1,0:T(8,128)S(1)}, u32[]{:S(2)}, u32[]{:S(2)}) %collective-permute-start.4) | collective-permute-done | bytes 393248 | tf_op jit(solution)/shard_map/ppermute | solution.py:330
  89.1 0.6 shard_map.62
  89.7 0.6 collective-permute-start.5
  90.3 1.9 fusion.5
  92.2 1.6 collective-permute-start.22
  93.8 1.6 collective-permute-start.7
  95.5 0.1 collective-permute-start.6
  95.7 2.0 %collective-permute-start.15 = (f32[160,256]{1,0:T(8,128)S(1)}, f32[160,256]{1,0:T(8,128)S(1)}, u32[]{:S(2)}, u32[]{:S(2)}) collective-permute-start(f32[160,256]{1,0:T(8,128)S(1)} %get-tuple-element.32), channel_id=1, source_target_pairs={{0,16},{1,17},{2,18},{3,19},{4,20},{5,21},{6,22},{7,23},{8,24},{9,... | collective-permute-start | bytes 491528 | tf_op jit(solution)/shard_map/ppermute | solution.py:330
  97.7 1.6 collective-permute-done.22
  99.4 1.7 collective-permute-start.23
  101.1 8.4 %shard_map.63.inverse_ref = f32[256,256]{1,0:T(8,128)S(1)} custom-call(s32[19]{0:T(128)S(1)} %fusion.23.core_ref.table_ref, f32[128,256]{1,0:T(8,128)S(1)} %add.155.mine_ref, f32[128,256]{1,0:T(8,128)S(1)} %collective-permute-done.6.theirs_ref), custom_call_target="tpu_custom_call" | custom-call | flops 10000000000 | bytes 524288 | tf_op jit(solution)/shard_map/pallas_call | solution.py:123
  109.6 1.3 shard_map.64.refs_1_
  110.9 0.7 collective-permute-done.15.refs_0_
  111.6 1.4 shard_map.65.refs_2_
  113.0 0.6 collective-permute-start.16
  113.7 1.4 collective-permute-done.23.refs_0_
  115.1 1.4 shard_map.66
  116.5 1.0 collective-permute-start.24
  117.5 8.3 %collective-permute-done.16 = f32[160,256]{1,0:T(8,128)S(1)} collective-permute-done((f32[160,256]{1,0:T(8,128)S(1)}, f32[160,256]{1,0:T(8,128)S(1)}, u32[]{:S(2)}, u32[]{:S(2)}) %collective-permute-start.16) | collective-permute-done | bytes 163872 | tf_op jit(solution)/shard_map/ppermute | solution.py:330
  125.8 1.7 collective-permute-start.17
  127.5 1.7 collective-permute-done.24
  129.2 4.6 %collective-permute-start.25 = (f32[320,256]{1,0:T(8,128)S(1)}, f32[320,256]{1,0:T(8,128)S(1)}, u32[]{:S(2)}, u32[]{:S(2)}) collective-permute-start(f32[320,256]{1,0:T(8,128)S(1)} %maximum_select_fusion.4), channel_id=1, source_target_pairs={{0,4},{1,3},{2,6},{3,1},{4,0},{5,7},{6,2},{7,5},{8,12},{9,11},{10,... | collective-permute-start | bytes 983048 | tf_op jit(solution)/shard_map/ppermute | solution.py:330
  133.8 2.2 %collective-permute-done.8 = f32[128,256]{1,0:T(8,128)S(1)} collective-permute-done((f32[128,256]{1,0:T(8,128)S(1)}, f32[128,256]{1,0:T(8,128)S(1)}, u32[]{:S(2)}, u32[]{:S(2)}) %collective-permute-start.8) | collective-permute-done | bytes 131104 | tf_op jit(solution)/shard_map/ppermute | solution.py:330
  136.3 2.1 %collective-permute-start.18 = (f32[640,256]{1,0:T(8,128)S(1)}, f32[640,256]{1,0:T(8,128)S(1)}, u32[]{:S(2)}, u32[]{:S(2)}) collective-permute-start(f32[640,256]{1,0:T(8,128)S(1)} %maximum_select_fusion.refs_2_), channel_id=1, source_target_pairs={{0,8},{1,9},{2,10},{3,11},{4,12},{5,13},{6,14},{7,15},{8,0},{9,1},... | collective-permute-start | bytes 1966088 | tf_op jit(solution)/shard_map/ppermute | solution.py:330
  138.3 0.6 collective-permute-done.25
  139.0 6.3 %collective-permute-done.9 = f32[256,256]{1,0:T(8,128)S(1)} collective-permute-done((f32[256,256]{1,0:T(8,128)S(1)}, f32[256,256]{1,0:T(8,128)S(1)}, u32[]{:S(2)}, u32[]{:S(2)}) %collective-permute-start.9) | collective-permute-done | bytes 262176 | tf_op jit(solution)/shard_map/ppermute | solution.py:330
  145.4 0.6 collective-permute-start.28
  146.0 0.5 collective-permute-start.10
  146.5 1.4 collective-permute-start.29
  147.8 13.0 %collective-permute-done.28.refs_0_ = f32[512,256]{1,0:T(8,128)S(1)} collective-permute-done((f32[512,256]{1,0:T(8,128)S(1)}, f32[512,256]{1,0:T(8,128)S(1)}, u32[]{:S(2)}, u32[]{:S(2)}) %collective-permute-start.28) | collective-permute-done | bytes 524320 | tf_op jit(solution)/shard_map/ppermute | solution.py:330
  160.8 1.7 collective-permute-start.19
  162.5 0.4 collective-permute-start.27
  162.9 2.0 collective-permute-start.11
  164.9 5.4 %shard_map.67 = (f32[768,256]{1,0:T(8,128)S(1)}, f32[7168,256]{1,0:T(8,128)}) custom-call(s32[19]{0:T(128)S(1)} %fusion.23.core_ref.table_ref, bf16[512,7168]{1,0:T(8,128)(2,1)} %acts_ref.7, f32[512,256]{1,0:T(8,128)S(1)} %maximum_select_fusion.2.refs_0_, f32[512,256]{1,0:T(8,128)S(1)} %collective-permute-done.10.refs_1_, ...), custom_call_target="tpu_custom_call" | custom-call | flops 1409286144 | bytes 11010048 | tf_op jit(solution)/shard_map/pallas_call | solution.py:299
  170.3 8.2 %collective-permute-done.30.refs_2_ = f32[640,256]{1,0:T(8,128)S(1)} collective-permute-done((f32[640,256]{1,0:T(8,128)S(1)}, f32[640,256]{1,0:T(8,128)S(1)}, u32[]{:S(2)}, u32[]{:S(2)}) %collective-permute-start.30) | collective-permute-done | bytes 655392 | tf_op jit(solution)/shard_map/ppermute | solution.py:330
  178.5 3.7 %shard_map.68 = (f32[768,256]{1,0:T(8,128)S(1)}, f32[7168,256]{1,0:T(8,128)}) custom-call(s32[19]{0:T(128)S(1)} %fusion.23.core_ref.table_ref, bf16[512,7168]{1,0:T(8,128)(2,1)} %acts_ref.7, f32[512,256]{1,0:T(8,128)S(1)} %collective-permute-done.28.refs_0_, ...), custom_call_target="tpu_custom_call", output_to_operand_aliasing={{0}: (5, {}), {1}: (6, {})} | custom-call | flops 704643072 | bytes 5505024 | tf_op jit(solution)/shard_map/pallas_call | solution.py:299
  182.2 6.7 %collective-permute-done.27.refs_2_ = f32[640,256]{1,0:T(8,128)S(1)} collective-permute-done((f32[640,256]{1,0:T(8,128)S(1)}, f32[640,256]{1,0:T(8,128)S(1)}, u32[]{:S(2)}, u32[]{:S(2)}) %collective-permute-start.27) | collective-permute-done | bytes 655392 | tf_op jit(solution)/shard_map/ppermute | solution.py:330
  188.9 3.6 %shard_map.69 = (f32[768,256]{1,0:T(8,128)S(1)}, f32[7168,256]{1,0:T(8,128)}) custom-call(s32[19]{0:T(128)S(1)} %fusion.23.core_ref.table_ref, bf16[512,7168]{1,0:T(8,128)(2,1)} %acts_ref.7, f32[512,256]{1,0:T(8,128)S(1)} %collective-permute-done.11.refs_0_, ...), custom_call_target="tpu_custom_call", output_to_operand_aliasing={{0}: (5, {}), {1}: (6, {})} | custom-call | flops 704643072 | bytes 5505024 | tf_op jit(solution)/shard_map/pallas_call | solution.py:299
  192.6 2.3 %collective-permute-done.31.theirs_ref = f32[768,256]{1,0:T(8,128)S(1)} collective-permute-done((f32[768,256]{1,0:T(8,128)S(1)}, f32[768,256]{1,0:T(8,128)S(1)}, u32[]{:S(2)}, u32[]{:S(2)}) %collective-permute-start.31) | collective-permute-done | bytes 786464 | tf_op jit(solution)/shard_map/ppermute | solution.py:363
  194.9 2.0 %shard_map.70 = f32[512,256]{1,0:T(8,128)} custom-call(f32[512,256]{1,0:T(8,128)S(1)} %get-tuple-element.16.codes_ref, f32[768,256]{1,0:T(8,128)S(1)} %get-tuple-element.28.mine_ref, f32[768,256]{1,0:T(8,128)S(1)} %collective-permute-done.31.theirs_ref), custom_call_target="tpu_custom_call" | custom-call | tf_op jit(solution)/shard_map/pallas_call | solution.py:195
  (41 shorter events, 0.9 us)
Async XLA Ops:
  0.6 12.0 %copy-start = (f32[512,256]{1,0:T(8,128)S(1)}, f32[512,256]{1,0:T(8,128)}, u32[]{:S(2)}) copy-start(f32[512,256]{1,0:T(8,128)} %codes_ref.1) | copy-start | bytes 1572868
  10.2 2.4 %collective-permute-start = (f32[768,256]{1,0:T(8,128)S(1)}, f32[768,256]{1,0:T(8,128)S(1)}, u32[]{:S(2)}, u32[]{:S(2)}) collective-permute-start(f32[768,256]{1,0:T(8,128)S(1)} %shard_map.59.mine_ref), channel_id=1, source_target_pairs={{0,1},{1,0},{2,3},{3,2},{4,5},{5,4},{6,7},{7,6},{8,9},{9,8},{10,11... | collective-permute-start | bytes 2359304 | tf_op jit(solution)/shard_map/ppermute | solution.py:363
  16.3 41.7 %collective-permute-start.1 = (f32[1024,256]{1,0:T(8,128)S(1)}, f32[1024,256]{1,0:T(8,128)S(1)}, u32[]{:S(2)}, u32[]{:S(2)}) collective-permute-start(f32[1024,256]{1,0:T(8,128)S(1)} %fusion.6), channel_id=1, source_target_pairs={{0,2},{1,5},{2,0},{3,7},{4,6},{5,1},{6,4},{7,3},{8,10},{9,13},{10,... | collective-permute-start | bytes 3145736 | tf_op jit(solution)/shard_map/ppermute | solution.py:330
  22.2 39.3 %collective-permute-start.12 = (f32[1280,256]{1,0:T(8,128)}, f32[1280,256]{1,0:T(8,128)}, u32[]{:S(2)}, u32[]{:S(2)}) collective-permute-start(f32[1280,256]{1,0:T(8,128)} %fusion.2), channel_id=1, source_target_pairs={{0,2},{1,5},{2,0},{3,7},{4,6},{5,1},{6,4},{7,3},{8,10},{9,13},{10,... | collective-permute-start | bytes 3932168 | tf_op jit(solution)/shard_map/ppermute | solution.py:330
  25.1 42.4 %collective-permute-start.20 = (f32[1280,256]{1,0:T(8,128)}, f32[1280,256]{1,0:T(8,128)}, u32[]{:S(2)}, u32[]{:S(2)}) collective-permute-start(f32[1280,256]{1,0:T(8,128)} %fusion), channel_id=1, source_target_pairs={{0,8},{1,9},{2,10},{3,11},{4,12},{5,13},{6,14},{7,15},{8,0},{9,1},... | collective-permute-start | bytes 3932168 | tf_op jit(solution)/shard_map/ppermute | solution.py:330
  27.2 30.8 %collective-permute-start.2 = (f32[128,256]{1,0:T(8,128)S(1)}, f32[128,256]{1,0:T(8,128)S(1)}, u32[]{:S(2)}, u32[]{:S(2)}) collective-permute-start(f32[128,256]{1,0:T(8,128)S(1)} %get-tuple-element.18), channel_id=1, source_target_pairs={{0,16},{1,17},{2,18},{3,19},{4,20},{5,21},{6,22},{7,23},{8,24},{9,... | collective-permute-start | bytes 393224 | tf_op jit(solution)/shard_map/ppermute | solution.py:330
  58.0 1.8 copy-start.1
  59.9 13.1 %collective-permute-start.3 = (f32[640,256]{1,0:T(8,128)S(1)}, f32[640,256]{1,0:T(8,128)S(1)}, u32[]{:S(2)}, u32[]{:S(2)}) collective-permute-start(f32[640,256]{1,0:T(8,128)S(1)} %pad_maximum_fusion), channel_id=1, source_target_pairs={{0,4},{1,3},{2,6},{3,1},{4,0},{5,7},{6,2},{7,5},{8,12},{9,11},{10,... | collective-permute-start | bytes 1966088 | tf_op jit(solution)/shard_map/ppermute | solution.py:330
  64.0 19.5 %collective-permute-start.13 = (f32[640,256]{1,0:T(8,128)}, f32[640,256]{1,0:T(8,128)}, u32[]{:S(2)}, u32[]{:S(2)}) collective-permute-start(f32[640,256]{1,0:T(8,128)} %convolution_add_fusion.2), channel_id=1, source_target_pairs={{0,8},{1,9},{2,10},{3,11},{4,12},{5,13},{6,14},{7,15},{8,0},{9,1},... | collective-permute-start | bytes 1966088 | tf_op jit(solution)/shard_map/ppermute | solution.py:330
  70.0 20.3 %collective-permute-start.21 = (f32[640,256]{1,0:T(8,128)}, f32[640,256]{1,0:T(8,128)}, u32[]{:S(2)}, u32[]{:S(2)}) collective-permute-start(f32[640,256]{1,0:T(8,128)} %convolution_add_fusion), channel_id=1, source_target_pairs={{0,2},{1,5},{2,0},{3,7},{4,6},{5,1},{6,4},{7,3},{8,10},{9,13},{10,... | collective-permute-start | bytes 1966088 | tf_op jit(solution)/shard_map/ppermute | solution.py:330
  73.6 15.4 %collective-permute-start.4 = (f32[384,256]{1,0:T(8,128)S(1)}, f32[384,256]{1,0:T(8,128)S(1)}, u32[]{:S(2)}, u32[]{:S(2)}) collective-permute-start(f32[384,256]{1,0:T(8,128)S(1)} %get-tuple-element.20), channel_id=1, source_target_pairs={{0,8},{1,9},{2,10},{3,11},{4,12},{5,13},{6,14},{7,15},{8,0},{9,1},... | collective-permute-start | bytes 1179656 | tf_op jit(solution)/shard_map/ppermute | solution.py:330
  85.4 10.2 %collective-permute-start.14 = (f32[320,256]{1,0:T(8,128)S(1)}, f32[320,256]{1,0:T(8,128)S(1)}, u32[]{:S(2)}, u32[]{:S(2)}) collective-permute-start(f32[320,256]{1,0:T(8,128)S(1)} %constant_dynamic-slice_fusion.4), channel_id=1, source_target_pairs={{0,4},{1,3},{2,6},{3,1},{4,0},{5,7},{6,2},{7,5},{8,12},{9,11},{10,... | collective-permute-start | bytes 983048 | tf_op jit(solution)/shard_map/ppermute | solution.py:330
  89.7 5.8 %collective-permute-start.5 = (f32[128,256]{1,0:T(8,128)S(1)}, f32[128,256]{1,0:T(8,128)S(1)}, u32[]{:S(2)}, u32[]{:S(2)}) collective-permute-start(f32[128,256]{1,0:T(8,128)S(1)} %get-tuple-element.21), channel_id=1, source_target_pairs={{0,2},{1,5},{2,0},{3,7},{4,6},{5,1},{6,4},{7,3},{8,10},{9,13},{10,... | collective-permute-start | bytes 393224 | tf_op jit(solution)/shard_map/ppermute | solution.py:330
  92.2 7.1 %collective-permute-start.22 = (f32[320,256]{1,0:T(8,128)S(1)}, f32[320,256]{1,0:T(8,128)S(1)}, u32[]{:S(2)}, u32[]{:S(2)}) collective-permute-start(f32[320,256]{1,0:T(8,128)S(1)} %constant_dynamic-slice_fusion.5), channel_id=1, source_target_pairs={{0,4},{1,3},{2,6},{3,1},{4,0},{5,7},{6,2},{7,5},{8,12},{9,11},{10,... | collective-permute-start | bytes 983048 | tf_op jit(solution)/shard_map/ppermute | solution.py:330
  93.8 15.8 %collective-permute-start.7 = (f32[128,256]{1,0:T(8,128)S(1)}, f32[128,256]{1,0:T(8,128)S(1)}, u32[]{:S(2)}, u32[]{:S(2)}) collective-permute-start(f32[128,256]{1,0:T(8,128)S(1)} %get-tuple-element.23), channel_id=1, source_target_pairs={{0,16},{1,17},{2,18},{3,19},{4,20},{5,21},{6,22},{7,23},{8,24},{9,... | collective-permute-start | bytes 393224 | tf_op jit(solution)/shard_map/ppermute | solution.py:330
  95.5 5.6 %collective-permute-start.6 = (f32[128,256]{1,0:T(8,128)S(1)}, f32[128,256]{1,0:T(8,128)S(1)}, u32[]{:S(2)}, u32[]{:S(2)}) collective-permute-start(f32[128,256]{1,0:T(8,128)S(1)} %add.155.mine_ref), channel_id=1, source_target_pairs={{0,1},{1,0},{2,3},{3,2},{4,5},{5,4},{6,7},{7,6},{8,9},{9,8},{10,11... | collective-permute-start | bytes 393224 | tf_op jit(solution)/shard_map/ppermute | solution.py:363
  95.7 16.0 %collective-permute-start.15 = (f32[160,256]{1,0:T(8,128)S(1)}, f32[160,256]{1,0:T(8,128)S(1)}, u32[]{:S(2)}, u32[]{:S(2)}) collective-permute-start(f32[160,256]{1,0:T(8,128)S(1)} %get-tuple-element.32), channel_id=1, source_target_pairs={{0,16},{1,17},{2,18},{3,19},{4,20},{5,21},{6,22},{7,23},{8,24},{9,... | collective-permute-start | bytes 491528 | tf_op jit(solution)/shard_map/ppermute | solution.py:330
  99.4 15.7 %collective-permute-start.23 = (f32[160,256]{1,0:T(8,128)S(1)}, f32[160,256]{1,0:T(8,128)S(1)}, u32[]{:S(2)}, u32[]{:S(2)}) collective-permute-start(f32[160,256]{1,0:T(8,128)S(1)} %get-tuple-element.30), channel_id=1, source_target_pairs={{0,16},{1,17},{2,18},{3,19},{4,20},{5,21},{6,22},{7,23},{8,24},{9,... | collective-permute-start | bytes 491528 | tf_op jit(solution)/shard_map/ppermute | solution.py:330
  113.0 12.8 %collective-permute-start.16 = (f32[160,256]{1,0:T(8,128)S(1)}, f32[160,256]{1,0:T(8,128)S(1)}, u32[]{:S(2)}, u32[]{:S(2)}) collective-permute-start(f32[160,256]{1,0:T(8,128)S(1)} %shard_map.65.refs_2_), channel_id=1, source_target_pairs={{0,16},{1,17},{2,18},{3,19},{4,20},{5,21},{6,22},{7,23},{8,24},{9,... | collective-permute-start | bytes 491528 | tf_op jit(solution)/shard_map/ppermute | solution.py:330
  116.5 12.7 %collective-permute-start.24 = (f32[160,256]{1,0:T(8,128)S(1)}, f32[160,256]{1,0:T(8,128)S(1)}, u32[]{:S(2)}, u32[]{:S(2)}) collective-permute-start(f32[160,256]{1,0:T(8,128)S(1)} %shard_map.66), channel_id=1, source_target_pairs={{0,16},{1,17},{2,18},{3,19},{4,20},{5,21},{6,22},{7,23},{8,24},{9,... | collective-permute-start | bytes 491528 | tf_op jit(solution)/shard_map/ppermute | solution.py:330
  125.8 10.4 %collective-permute-start.17 = (f32[320,256]{1,0:T(8,128)S(1)}, f32[320,256]{1,0:T(8,128)S(1)}, u32[]{:S(2)}, u32[]{:S(2)}) collective-permute-start(f32[320,256]{1,0:T(8,128)S(1)} %maximum_select_fusion.3), channel_id=1, source_target_pairs={{0,4},{1,3},{2,6},{3,1},{4,0},{5,7},{6,2},{7,5},{8,12},{9,11},{10,... | collective-permute-start | bytes 983048 | tf_op jit(solution)/shard_map/ppermute | solution.py:330
  127.5 8.6 %collective-permute-start.8 = (f32[128,256]{1,0:T(8,128)S(1)}, f32[128,256]{1,0:T(8,128)S(1)}, u32[]{:S(2)}, u32[]{:S(2)}) collective-permute-start(f32[128,256]{1,0:T(8,128)S(1)} %shard_map.64.refs_1_), channel_id=1, source_target_pairs={{0,16},{1,17},{2,18},{3,19},{4,20},{5,21},{6,22},{7,23},{8,24},{9,... | collective-permute-start | bytes 393224 | tf_op jit(solution)/shard_map/ppermute | solution.py:330
  129.2 9.6 %collective-permute-start.25 = (f32[320,256]{1,0:T(8,128)S(1)}, f32[320,256]{1,0:T(8,128)S(1)}, u32[]{:S(2)}, u32[]{:S(2)}) collective-permute-start(f32[320,256]{1,0:T(8,128)S(1)} %maximum_select_fusion.4), channel_id=1, source_target_pairs={{0,4},{1,3},{2,6},{3,1},{4,0},{5,7},{6,2},{7,5},{8,12},{9,11},{10,... | collective-permute-start | bytes 983048 | tf_op jit(solution)/shard_map/ppermute | solution.py:330
  136.1 9.2 %collective-permute-start.9 = (f32[256,256]{1,0:T(8,128)S(1)}, f32[256,256]{1,0:T(8,128)S(1)}, u32[]{:S(2)}, u32[]{:S(2)}) collective-permute-start(f32[256,256]{1,0:T(8,128)S(1)} %maximum_select_fusion.5), channel_id=1, source_target_pairs={{0,8},{1,9},{2,10},{3,11},{4,12},{5,13},{6,14},{7,15},{8,0},{9,1},... | collective-permute-start | bytes 786440 | tf_op jit(solution)/shard_map/ppermute | solution.py:330
  136.3 24.6 %collective-permute-start.18 = (f32[640,256]{1,0:T(8,128)S(1)}, f32[640,256]{1,0:T(8,128)S(1)}, u32[]{:S(2)}, u32[]{:S(2)}) collective-permute-start(f32[640,256]{1,0:T(8,128)S(1)} %maximum_select_fusion.refs_2_), channel_id=1, source_target_pairs={{0,8},{1,9},{2,10},{3,11},{4,12},{5,13},{6,14},{7,15},{8,0},{9,1},... | collective-permute-start | bytes 1966088 | tf_op jit(solution)/shard_map/ppermute | solution.py:330
  138.9 23.6 %collective-permute-start.26 = (f32[640,256]{1,0:T(8,128)S(1)}, f32[640,256]{1,0:T(8,128)S(1)}, u32[]{:S(2)}, u32[]{:S(2)}) collective-permute-start(f32[640,256]{1,0:T(8,128)S(1)} %maximum_select_fusion.1.refs_4_), channel_id=1, source_target_pairs={{0,2},{1,5},{2,0},{3,7},{4,6},{5,1},{6,4},{7,3},{8,10},{9,13},{10,... | collective-permute-start | bytes 1966088 | tf_op jit(solution)/shard_map/ppermute | solution.py:330
  145.4 15.4 %collective-permute-start.28 = (f32[512,256]{1,0:T(8,128)S(1)}, f32[512,256]{1,0:T(8,128)S(1)}, u32[]{:S(2)}, u32[]{:S(2)}) collective-permute-start(f32[512,256]{1,0:T(8,128)S(1)} %maximum_select_fusion.2.refs_0_), channel_id=1, source_target_pairs={{0,2},{1,5},{2,0},{3,7},{4,6},{5,1},{6,4},{7,3},{8,10},{9,13},{10,... | collective-permute-start | bytes 1572872 | tf_op jit(solution)/shard_map/ppermute | solution.py:330
  146.0 16.9 %collective-permute-start.10 = (f32[512,256]{1,0:T(8,128)S(1)}, f32[512,256]{1,0:T(8,128)S(1)}, u32[]{:S(2)}, u32[]{:S(2)}) collective-permute-start(f32[512,256]{1,0:T(8,128)S(1)} %maximum_select_fusion.2.refs_0_), channel_id=1, source_target_pairs={{0,4},{1,3},{2,6},{3,1},{4,0},{5,7},{6,2},{7,5},{8,12},{9,11},{10,... | collective-permute-start | bytes 1572872 | tf_op jit(solution)/shard_map/ppermute | solution.py:330
  146.5 23.8 %collective-permute-start.29 = (f32[640,256]{1,0:T(8,128)S(1)}, f32[640,256]{1,0:T(8,128)S(1)}, u32[]{:S(2)}, u32[]{:S(2)}) collective-permute-start(f32[640,256]{1,0:T(8,128)S(1)} %maximum_select_fusion.refs_2_), channel_id=1, source_target_pairs={{0,2},{1,5},{2,0},{3,7},{4,6},{5,1},{6,4},{7,3},{8,10},{9,13},{10,... | collective-permute-start | bytes 1966088 | tf_op jit(solution)/shard_map/ppermute | solution.py:330
  160.8 17.7 %collective-permute-start.30 = (f32[640,256]{1,0:T(8,128)S(1)}, f32[640,256]{1,0:T(8,128)S(1)}, u32[]{:S(2)}, u32[]{:S(2)}) collective-permute-start(f32[640,256]{1,0:T(8,128)S(1)} %maximum_select_fusion.1.refs_4_), channel_id=1, source_target_pairs={{0,8},{1,9},{2,10},{3,11},{4,12},{5,13},{6,14},{7,15},{8,0},{9,1},... | collective-permute-start | bytes 1966088 | tf_op jit(solution)/shard_map/ppermute | solution.py:330
  160.8 21.3 %collective-permute-start.19 = (f32[640,256]{1,0:T(8,128)S(1)}, f32[640,256]{1,0:T(8,128)S(1)}, u32[]{:S(2)}, u32[]{:S(2)}) collective-permute-start(f32[640,256]{1,0:T(8,128)S(1)} %collective-permute-done.18.refs_3_), channel_id=1, source_target_pairs={{0,2},{1,5},{2,0},{3,7},{4,6},{5,1},{6,4},{7,3},{8,10},{9,13},{10,... | collective-permute-start | bytes 1966088 | tf_op jit(solution)/shard_map/ppermute | solution.py:330
  162.5 26.4 %collective-permute-start.27 = (f32[640,256]{1,0:T(8,128)S(1)}, f32[640,256]{1,0:T(8,128)S(1)}, u32[]{:S(2)}, u32[]{:S(2)}) collective-permute-start(f32[640,256]{1,0:T(8,128)S(1)} %collective-permute-done.26.refs_5_), channel_id=1, source_target_pairs={{0,8},{1,9},{2,10},{3,11},{4,12},{5,13},{6,14},{7,15},{8,0},{9,1},... | collective-permute-start | bytes 1966088 | tf_op jit(solution)/shard_map/ppermute | solution.py:330
  162.9 19.2 %collective-permute-start.11 = (f32[512,256]{1,0:T(8,128)S(1)}, f32[512,256]{1,0:T(8,128)S(1)}, u32[]{:S(2)}, u32[]{:S(2)}) collective-permute-start(f32[512,256]{1,0:T(8,128)S(1)} %collective-permute-done.10.refs_1_), channel_id=1, source_target_pairs={{0,2},{1,5},{2,0},{3,7},{4,6},{5,1},{6,4},{7,3},{8,10},{9,13},{10,... | collective-permute-start | bytes 1572872 | tf_op jit(solution)/shard_map/ppermute | solution.py:330
  192.5 2.4 %collective-permute-start.31 = (f32[768,256]{1,0:T(8,128)S(1)}, f32[768,256]{1,0:T(8,128)S(1)}, u32[]{:S(2)}, u32[]{:S(2)}) collective-permute-start(f32[768,256]{1,0:T(8,128)S(1)} %get-tuple-element.28.mine_ref), channel_id=1, source_target_pairs={{0,1},{1,0},{2,3},{3,2},{4,5},{5,4},{6,7},{7,6},{8,9},{9,8},{10,11... | collective-permute-start | bytes 2359304 | tf_op jit(solution)/shard_map/ppermute | solution.py:363

commit v5 on v4

--- a/solution.py
+++ b/solution.py
@@ -217,6 +217,52 @@
 
 def shape(rows, comp):
     return jax.ShapeDtypeStruct((rows, comp), f32)
+
+
+def relay_kernel(table_ref, mine_ref, theirs_ref, low_ref, out_ref, low_out_ref):
+    out_ref[...] = mine_ref[...] + theirs_ref[...]
+    low_out_ref[...] = low_ref[...]
+
+
+def relay(table, mine, theirs, low):
+    shapes = [shape(*mine.shape), jax.ShapeDtypeStruct(low.shape, low.dtype)]
+    return call(relay_kernel, shapes, table, [mine, theirs, low], [])
+
+
+def fold_kernel(at, table_ref, mine_ref, theirs_ref, *refs):
+    rows = mine_ref.shape[0] // 2
+    keep = pl.ds(pl.multiple_of(table_ref[at] * rows, rows), rows)
+    give = pl.ds(pl.multiple_of((1 - table_ref[at]) * rows, rows), rows)
+    refs[-2][...] = mine_ref[give, :] + theirs_ref[give, :]
+    refs[-1][...] = mine_ref[keep, :] + theirs_ref[keep, :]
+
+
+def fold(table, at, mine, theirs, after):
+    half = shape(mine.shape[0] // 2, mine.shape[1])
+    return call(functools.partial(fold_kernel, at), [half, half], table, [mine, theirs], after)
+
+
+def join_kernel(at, table_ref, mine_ref, theirs_ref, *refs):
+    rows = mine_ref.shape[0]
+    refs[-1][pl.ds(pl.multiple_of(table_ref[at] * rows, rows), rows), :] = mine_ref[...]
+    refs[-1][pl.ds(pl.multiple_of((1 - table_ref[at]) * rows, rows), rows), :] = theirs_ref[...]
+
+
+def join(table, at, mine, theirs, after):
+    return call(functools.partial(join_kernel, at), [shape(2 * mine.shape[0], mine.shape[1])], table, [mine, theirs], after)[0]
+
+
+def take_kernel(at, count, table_ref, mine_ref, theirs_ref, *refs):
+    which = 1 - table_ref[at]
+    refs[-1][:count, :] = mine_ref[...] + theirs_ref[pl.ds(pl.multiple_of(which * count, count), count), :]
+    if refs[-1].shape[0] > count:
+        refs[-1][count:, :] = refs[0][...]
+
+
+def take(table, at, mine, theirs, tail, after):
+    count = mine.shape[0]
+    rows = count + sum(value.shape[0] for value in tail)
+    return call(functools.partial(take_kernel, at, count), [shape(rows, mine.shape[1])], table, [mine, theirs, *tail], after)[0]
 
 
 def first_fold_kernel(at, table_ref, mine_ref, theirs_ref, gram_ref, *refs):
@@ -322,8 +368,8 @@
     "B": ("first", "near", "second", "far"),
     "N": ("near", "first", "second", "far"),
 }
-SHARES = {"A": 4, "B": 5, "N": 5}
-FIELDS = ("c", "d", "mine", "theirs", "far_mine", "far_theirs")
+SHARES = {"A": 5, "B": 5, "N": 4}
+FIELDS = ("b", "c", "d", "mine", "theirs", "far_mine", "far_theirs")
 
 
 def swap(value, along):
@@ -344,7 +390,7 @@
                 here, there = start + a * half, start + (1 - a) * half
                 table[t * 2 + core, 0] = core
                 table[t * 2 + core, column : column + len(FIELDS)] = (
-                    c, d,
+                    b, c, d,
                     here + b * quarter, here + (1 - b) * quarter, there + b * quarter, there + (1 - b) * quarter,
                 )
         for k, field in enumerate(FIELDS):
@@ -374,62 +420,53 @@
     for name in ORDERS:
         starts[name], start = start, start + rows[name]
 
-    def cross_of(row, count):
+    def cross_of(row, count, low):
         return dot(lax.dynamic_slice_in_dim(acts, row, count, 1), low, OVER_ROWS)
 
-    def give_1(name):
+    def give_1(name, low):
         half = rows[name] // 2
-        return cross_of(starts[name] + (1 - bits[ORDERS[name][0]]) * half, half)
-
-    def stage_2(name, got, keep):
+        return cross_of(starts[name] + (1 - bits[ORDERS[name][0]]) * half, half, low)
+
+    def own_2(name, keep):
         half, quarter = rows[name] // 2, rows[name] // 4
         a, b = (bits[along] for along in ORDERS[name][:2])
-        which = b if keep else 1 - b
-        out = cross_of(starts[name] + a * half + which * quarter, quarter)
-        return out + lax.dynamic_slice_in_dim(got, which * quarter, quarter, 0)
-
-    def part_of(value, which):
-        half = value.shape[0] // 2
-        return lax.dynamic_slice_in_dim(value, which * half, half, 0)
-
-    def joined(one, other, which):
-        return jnp.where(which == 0, jnp.concatenate([one, other]), jnp.concatenate([other, one]))
-
-    gram = gram + swap(gram, "far")
-    held = {}
+        return cross_of(starts[name] + a * half + (b if keep else 1 - b) * quarter, quarter, low)
+
+    gram, low_later = relay(table, gram, swap(gram, "far"), low)
+    got, keeps, held, last = {}, {}, {}, []
     for name, order in ORDERS.items():
-        got = swap(give_1(name), order[0])
-        give = stage_2(name, got, False)
+        got[name] = swap(give_1(name, low if name == "A" else low_later), order[0])
+    for name, order in ORDERS.items():
+        give = take(table, where[name, "b"], own_2(name, False), got[name], [gram] if name == "A" else [], last)
+        held[name], last = swap(give, order[1]), [give]
+        quarter = rows[name] // 4
+        keeps[name] = own_2(name, True) + lax.dynamic_slice_in_dim(got[name], bits[order[1]] * quarter, quarter, 0)
+    last = []
+    for name, order in ORDERS.items():
         if name == "A":
-            give = jnp.concatenate([give, gram])
-        held[name] = stage_2(name, got, True), swap(give, order[1])
-    for name, (keep, arrived) in held.items():
-        along = ORDERS[name][2]
+            give, keep = first_fold(table, where[name, "c"], keeps[name], held[name], gram)
+        else:
+            give, keep = fold(table, where[name, "c"], keeps[name], held[name], last)
+        keeps[name], held[name], last = keep, swap(give, order[2]), [keep]
+    last = []
+    for name, order in ORDERS.items():
         if name == "A":
-            give, keep = first_fold(table, where[name, "c"], keep, arrived, gram)
-            held[name] = keep, swap(give, along)
+            give, keep, gram = split_fold(table, where[name, "d"], gram.shape[0], keeps[name], held[name])
+            gram = gram + swap(gram, "first")
         else:
-            keep = keep + arrived
-            held[name] = part_of(keep, bits[along]), swap(part_of(keep, 1 - bits[along]), along)
-    for name, (keep, arrived) in held.items():
-        along = ORDERS[name][3]
-        if name == "A":
-            give, keep, gram = split_fold(table, where[name, "d"], gram.shape[0], keep, arrived)
-            gram = gram + swap(gram, "first")
-            held[name] = keep, swap(give, along)
-        else:
-            keep = keep + arrived
-            held[name] = part_of(keep, bits[along]), swap(part_of(keep, 1 - bits[along]), along)
-
-    inverse = factor_inverse(table, gram, other_core(gram))
+            give, keep = fold(table, where[name, "d"], keeps[name], held[name], last)
+        held[name], last = (keep, swap(give, order[3])), [keep]
+
+    inverse = factor_inverse(table, gram, other_core(gram), last)
     mine = {}
     for name in held:
         mine[name] = solve_sum(table, inverse, held[name], list(mine.values()))
 
-    for k in (3, 2):
-        for name in mine:
-            along = ORDERS[name][k]
-            mine[name] = joined(mine[name], swap(mine[name], along), bits[along])
+    for k, field in ((3, "d"), (2, "c")):
+        last = []
+        for name, order in ORDERS.items():
+            mine[name] = join(table, where[name, field], mine[name], swap(mine[name], order[k]), last)
+            last = [mine[name]]
     near, far, last = [], [], []
     for name in mine:
         theirs = swap(mine[name], ORDERS[name][1])
@@ -437,7 +474,7 @@
         far += [(swap(mine[name], ORDERS[name][0]), where[name, "far_mine"])]
         last += [(swap(theirs, ORDERS[name][0]), where[name, "far_theirs"])]
     state = None
-    for blocks in (near, far, last):
+    for blocks in (near, far, last[:2], last[2:]):
         state = absorb(table, state, acts, blocks)
     sums, dict_out = state
     return second_update(codes_mid, sums, other_core(sums)), dict_out

time: 197 us -> 212 us (1.076)
  Pallas kernels: 39.9 us -> 51.1 us
  waiting for transfers between devices: 91.4 us -> 102 us
  starting transfers between devices: 43.7 us -> 38.6 us
  matrix products: 19.6 us -> 17.3 us
    ppermute x29, waiting for transfers between devices: 87.9 us -> 98.2 us  [swap(): return lax.ppermute(value, BOTH, flips(ALONG[along]))]
    pallas_call x5 -> x19, Pallas kernels: 5.29 us -> 14.9 us  [call(): pl.pallas_call(kernel, out_shape=out_shapes, in_specs=[SCALARS] + [WHOLE]...]
    ppermute x29, starting transfers between devices: 43.1 us -> 37.9 us  [swap(): return lax.ppermute(value, BOTH, flips(ALONG[along]))]
    dot_general x9, matrix products: 19.6 us -> 17.3 us  [dot(): lax.dot_general(left, right, dims, precision=precision, preferred_element...]
    pallas_call x3 -> x4, Pallas kernels: 12.7 us -> 14.3 us  [absorb(): pl.pallas_call(functools.partial(absorb_kernel, [at for _, at in blocks],...]
  transfers between devices with their start and end apart: 32 -> 32, of which waited for: 17 -> 17; matrix products, arithmetic and copies ran while one was open for 10% -> 9% of each run, Pallas kernels for 12% -> 17%
where the time goes in v5:
time: 212 us; the launch traced here: 211 us
  waiting for transfers between devices  102 us (48%)
  Pallas kernels  51.1 us (24%)
  starting transfers between devices  38.6 us (18%)
  matrix products  17.3 us (8%)
    ppermute x29, waiting for transfers between devices, swap(): return lax.ppermute(value, BOTH, flips(ALONG[along]))  98.2 us
    ppermute x29, starting transfers between devices, swap(): return lax.ppermute(value, BOTH, flips(ALONG[along]))  37.9 us
    dot_general x9, matrix products, dot(): lax.dot_general(left, right, dims, precision=precision, preferred_element...  17.3 us
    pallas_call x19, Pallas kernels, call(): pl.pallas_call(kernel, out_shape=out_shapes, in_specs=[SCALARS] + [WHOLE]...  14.9 us
    pallas_call x4, Pallas kernels, absorb(): pl.pallas_call(functools.partial(absorb_kernel, [at for _, at in blocks],...  14.3 us
    pallas_call x1, Pallas kernels, project(): pl.pallas_call(project_kernel, out_shape=jax.ShapeDtypeStruct((tokens + c...  9.55 us
    pallas_call x1, Pallas kernels, factor_inverse(): pl.pallas_call(halves_kernel, out_shape=jax.ShapeDtypeStruct((comp, comp)...  8.43 us
  transfers between devices with their start and end apart: 32, of which 17 were waited for; matrix products, arithmetic and copies ran while one was open for 9% of the time, Pallas kernels for 17%

profile of v5, /device:TPU:0, one launch (start us, length us, event | category | flops | bytes accessed | tf_op | source)
XLA Modules:
  0.0 211.3 jit_solution(6852052744986360839)
XLA Ops:
  0.6 9.6 %shard_map.59.mine_ref = f32[768,256]{1,0:T(8,128)S(1)} custom-call(bf16[512,7168]{1,0:T(8,128)(2,1)} %acts_ref.9, f32[7168,256]{1,0:T(8,128)} %dict_ref.1), custom_call_target="tpu_custom_call" | custom-call | flops 3758096384 | bytes 14680064 | tf_op jit(solution)/shard_map/pallas_call | solution.py:58
  10.7 0.7 fusion.24.core_ref.table_ref
  11.4 1.2 collective-permute-done.theirs_ref
  12.6 2.0 shard_map.60
  14.6 0.8 copy-done.1
  15.4 4.0 %collective-permute-start.2 = (f32[128,256]{1,0:T(8,128)S(1)}, f32[128,256]{1,0:T(8,128)S(1)}, u32[]{:S(2)}, u32[]{:S(2)}) collective-permute-start(f32[128,256]{1,0:T(8,128)S(1)} %get-tuple-element.30.mine_ref), channel_id=1, source_target_pairs={{0,16},{1,17},{2,18},{3,19},{4,20},{5,21},{6,22},{7,23},{8,24},{9,... | collective-permute-start | bytes 393224 | tf_op jit(solution)/shard_map/ppermute | solution.py:376
  19.4 2.9 %fusion.2 = f32[1280,256]{1,0:T(8,128)} fusion(bf16[512,256]{1,0:T(8,128)(2,1)S(1)} %get-tuple-element.29.low_ref, bf16[512,7168]{1,0:T(8,128)(2,1)} %acts_ref.9, s32[]{:T(128)S(6)} %select_n.63), kind=kOutput, calls=%fused_computation.2 | convolution fusion | flops 335544320 | bytes 2883588 | tf_op jit(solution)/shard_map/dot_general | solution.py:21
  22.3 1.5 collective-permute-start.1
  23.8 2.2 %collective-permute-done.2.theirs_ref = f32[128,256]{1,0:T(8,128)S(1)} collective-permute-done((f32[128,256]{1,0:T(8,128)S(1)}, f32[128,256]{1,0:T(8,128)S(1)}, u32[]{:S(2)}, u32[]{:S(2)}) %collective-permute-start.2) | collective-permute-done | bytes 131104 | tf_op jit(solution)/shard_map/ppermute | solution.py:376
  26.6 2.9 %fusion = f32[1280,256]{1,0:T(8,128)} fusion(bf16[512,256]{1,0:T(8,128)(2,1)S(1)} %get-tuple-element.35, bf16[512,7168]{1,0:T(8,128)(2,1)} %acts_ref.9, s32[]{:T(128)S(6)} %select_n.72), kind=kOutput, calls=%fused_computation | convolution fusion | flops 335544320 | bytes 2883588 | tf_op jit(solution)/shard_map/dot_general | solution.py:21
  29.5 1.5 collective-permute-start.8
  31.0 2.7 %fusion.4 = f32[1024,256]{1,0:T(8,128)} fusion(bf16[512,256]{1,0:T(8,128)(2,1)S(1)} %get-tuple-element.35, bf16[512,7168]{1,0:T(8,128)(2,1)} %acts_ref.9, s32[]{:T(128)S(6)} %select_n.68), kind=kOutput, calls=%fused_computation.7 | convolution fusion | flops 268435456 | bytes 2359300 | tf_op jit(solution)/shard_map/dot_general | solution.py:21
  33.7 0.7 collective-permute-start.7
  34.4 1.5 fusion.9.mine_ref
  35.9 4.3 %collective-permute-done.1.theirs_ref = f32[1280,256]{1,0:T(8,128)S(1)} collective-permute-done((f32[1280,256]{1,0:T(8,128)}, f32[1280,256]{1,0:T(8,128)S(1)}, u32[]{:S(2)}, u32[]{:S(2)}) %collective-permute-start.1) | collective-permute-done | bytes 1310752 | tf_op jit(solution)/shard_map/ppermute | solution.py:376
  40.1 0.6 shard_map.62.refs_0_
  40.7 1.6 collective-permute-start.3
  42.3 1.5 fusion.7.mine_ref
  43.8 18.9 %collective-permute-done.8.theirs_ref = f32[1280,256]{1,0:T(8,128)} collective-permute-done((f32[1280,256]{1,0:T(8,128)}, f32[1280,256]{1,0:T(8,128)}, u32[]{:S(2)}, u32[]{:S(2)}) %collective-permute-start.8) | collective-permute-done | bytes 1310752 | tf_op jit(solution)/shard_map/ppermute | solution.py:376
  62.7 1.4 shard_map.65.refs_0_
  64.1 1.6 collective-permute-start.10
  65.7 1.4 fusion.12.mine_ref
  67.7 1.6 collective-permute-start.9
  69.3 1.5 convolution_add_fusion.1.mine_ref
  70.8 1.2 shard_map.63
  72.5 1.7 convolution_add_fusion.mine_ref
  74.2 7.6 %collective-permute-done.10.theirs_ref = f32[640,256]{1,0:T(8,128)S(1)} collective-permute-done((f32[640,256]{1,0:T(8,128)S(1)}, f32[640,256]{1,0:T(8,128)S(1)}, u32[]{:S(2)}, u32[]{:S(2)}) %collective-permute-start.10) | collective-permute-done | bytes 655392 | tf_op jit(solution)/shard_map/ppermute | solution.py:376
  81.8 0.6 shard_map.67
  82.5 1.6 collective-permute-start.12
  84.0 1.4 convolution_add_fusion.2.mine_ref
  85.4 0.6 shard_map.68
  86.6 3.0 %collective-permute-done.4.theirs_ref = f32[448,256]{1,0:T(8,128)S(1)} collective-permute-done((f32[448,256]{1,0:T(8,128)S(1)}, f32[448,256]{1,0:T(8,128)S(1)}, u32[]{:S(2)}, u32[]{:S(2)}) %collective-permute-start.4) | collective-permute-done | bytes 458784 | tf_op jit(solution)/shard_map/ppermute | solution.py:376
  90.2 1.6 collective-permute-start.5
  91.8 3.5 %collective-permute-done.5 = f32[128,256]{1,0:T(8,128)S(1)} collective-permute-done((f32[128,256]{1,0:T(8,128)S(1)}, f32[128,256]{1,0:T(8,128)S(1)}, u32[]{:S(2)}, u32[]{:S(2)}) %collective-permute-start.5) | collective-permute-done | bytes 131104 | tf_op jit(solution)/shard_map/ppermute | solution.py:376
  96.3 2.7 %collective-permute-start.15 = (f32[160,256]{1,0:T(8,128)S(1)}, f32[160,256]{1,0:T(8,128)S(1)}, u32[]{:S(2)}, u32[]{:S(2)}) collective-permute-start(f32[160,256]{1,0:T(8,128)S(1)} %get-tuple-element.45), channel_id=1, source_target_pairs={{0,16},{1,17},{2,18},{3,19},{4,20},{5,21},{6,22},{7,23},{8,24},{9,... | collective-permute-start | bytes 491528 | tf_op jit(solution)/shard_map/ppermute | solution.py:376
  99.6 8.4 %shard_map.71.inverse_ref = f32[256,256]{1,0:T(8,128)S(1)} custom-call(s32[22]{0:T(128)S(1)} %fusion.24.core_ref.table_ref, f32[128,256]{1,0:T(8,128)S(1)} %add.102.mine_ref, f32[128,256]{1,0:T(8,128)S(1)} %collective-permute-done.6.theirs_ref, f32[128,256]{1,0:T(8,128)S(1)} %get-tuple-element.42.refs_0_.mine_ref), custom_call_target="tpu_custom_call" | custom-call | flops 10000000000 | bytes 524288 | tf_op jit(solution)/shard_map/pallas_call | solution.py:123
  108.0 2.3 %collective-permute-done.14.refs_0_ = f32[160,256]{1,0:T(8,128)S(1)} collective-permute-done((f32[160,256]{1,0:T(8,128)S(1)}, f32[160,256]{1,0:T(8,128)S(1)}, u32[]{:S(2)}, u32[]{:S(2)}) %collective-permute-start.14) | collective-permute-done | bytes 163872 | tf_op jit(solution)/shard_map/ppermute | solution.py:376
  110.3 1.4 shard_map.72.refs_1_.mine_ref
  111.8 1.6 collective-permute-done.15.refs_0_
  113.4 1.4 shard_map.73.refs_2_.mine_ref
  114.8 1.4 collective-permute-start.17
  116.2 1.6 collective-permute-start.13
  117.8 15.8 %collective-permute-done.13.refs_0_ = f32[128,256]{1,0:T(8,128)S(1)} collective-permute-done((f32[128,256]{1,0:T(8,128)S(1)}, f32[128,256]{1,0:T(8,128)S(1)}, u32[]{:S(2)}, u32[]{:S(2)}) %collective-permute-start.13) | collective-permute-done | bytes 131104 | tf_op jit(solution)/shard_map/ppermute | solution.py:376
  133.6 1.3 shard_map.74.mine_ref
  135.6 2.4 %collective-permute-start.21 = (f32[320,256]{1,0:T(8,128)S(1)}, f32[320,256]{1,0:T(8,128)S(1)}, u32[]{:S(2)}, u32[]{:S(2)}) collective-permute-start(f32[320,256]{1,0:T(8,128)S(1)} %shard_map.75.refs_0_.mine_ref), channel_id=1, source_target_pairs={{0,8},{1,9},{2,10},{3,11},{4,12},{5,13},{6,14},{7,15},{8,0},{9,1},... | collective-permute-start | bytes 983048 | tf_op jit(solution)/shard_map/ppermute | solution.py:376
  138.5 1.6 collective-permute-start.20
  140.1 3.2 %collective-permute-done.16.theirs_ref = f32[128,256]{1,0:T(8,128)S(1)} collective-permute-done((f32[128,256]{1,0:T(8,128)S(1)}, f32[128,256]{1,0:T(8,128)S(1)}, u32[]{:S(2)}, u32[]{:S(2)}) %collective-permute-start.16) | collective-permute-done | bytes 131104 | tf_op jit(solution)/shard_map/ppermute | solution.py:376
  143.9 1.6 collective-permute-start.19
  145.5 2.9 %collective-permute-done.21.theirs_ref = f32[320,256]{1,0:T(8,128)S(1)} collective-permute-done((f32[320,256]{1,0:T(8,128)S(1)}, f32[320,256]{1,0:T(8,128)S(1)}, u32[]{:S(2)}, u32[]{:S(2)}) %collective-permute-start.21) | collective-permute-done | bytes 327712 | tf_op jit(solution)/shard_map/ppermute | solution.py:376
  149.7 1.6 collective-permute-start.24
  151.8 2.0 collective-permute-start.30
  153.9 1.5 collective-permute-start.22
  155.9 20.9 %collective-permute-done.30.refs_2_ = f32[512,256]{1,0:T(8,128)S(1)} collective-permute-done((f32[512,256]{1,0:T(8,128)S(1)}, f32[512,256]{1,0:T(8,128)S(1)}, u32[]{:S(2)}, u32[]{:S(2)}) %collective-permute-start.30) | collective-permute-done | bytes 524320 | tf_op jit(solution)/shard_map/ppermute | solution.py:376
  176.8 1.5 collective-permute-start.28
  178.8 1.5 collective-permute-start.25
  180.6 5.1 %shard_map.81 = (f32[768,256]{1,0:T(8,128)S(1)}, f32[7168,256]{1,0:T(8,128)}) custom-call(s32[22]{0:T(128)S(1)} %fusion.24.core_ref.table_ref, bf16[512,7168]{1,0:T(8,128)(2,1)} %acts_ref.9, f32[640,256]{1,0:T(8,128)S(1)} %shard_map.78.refs_0_, f32[640,256]{1,0:T(8,128)S(1)} %collective-permute-done.24.refs_1_, f32[640,256]{1,0:T(8,128)S(1)} %shard_map.79.refs_0_.refs_2_, ...), custom_call_target="tpu_custom_call" | custom-call | flops 1409286144 | bytes 11010048 | tf_op jit(solution)/shard_map/pallas_call | solution.py:345
  185.8 1.6 collective-permute-done.28.refs_0_
  187.4 3.7 %shard_map.82 = (f32[768,256]{1,0:T(8,128)S(1)}, f32[7168,256]{1,0:T(8,128)}) custom-call(s32[22]{0:T(128)S(1)} %fusion.24.core_ref.table_ref, bf16[512,7168]{1,0:T(8,128)(2,1)} %acts_ref.9, f32[640,256]{1,0:T(8,128)S(1)} %collective-permute-done.28.refs_0_, ...), custom_call_target="tpu_custom_call", output_to_operand_aliasing={{0}: (5, {}), {1}: (6, {})} | custom-call | flops 704643072 | bytes 5505024 | tf_op jit(solution)/shard_map/pallas_call | solution.py:345
  191.0 3.4 %collective-permute-done.27.refs_1_ = f32[640,256]{1,0:T(8,128)S(1)} collective-permute-done((f32[640,256]{1,0:T(8,128)S(1)}, f32[640,256]{1,0:T(8,128)S(1)}, u32[]{:S(2)}, u32[]{:S(2)}) %collective-permute-start.27) | collective-permute-done | bytes 655392 | tf_op jit(solution)/shard_map/ppermute | solution.py:376
  194.4 7.0 %collective-permute-done.25.refs_0_ = f32[640,256]{1,0:T(8,128)S(1)} collective-permute-done((f32[640,256]{1,0:T(8,128)S(1)}, f32[640,256]{1,0:T(8,128)S(1)}, u32[]{:S(2)}, u32[]{:S(2)}) %collective-permute-start.25) | collective-permute-done | bytes 655392 | tf_op jit(solution)/shard_map/ppermute | solution.py:376
  201.4 3.3 %shard_map.83 = (f32[768,256]{1,0:T(8,128)S(1)}, f32[7168,256]{1,0:T(8,128)}) custom-call(s32[22]{0:T(128)S(1)} %fusion.24.core_ref.table_ref, bf16[512,7168]{1,0:T(8,128)(2,1)} %acts_ref.9, f32[640,256]{1,0:T(8,128)S(1)} %collective-permute-done.25.refs_0_, ...), custom_call_target="tpu_custom_call", output_to_operand_aliasing={{0}: (4, {}), {1}: (5, {})} | custom-call | flops 503316480 | bytes 3932160 | tf_op jit(solution)/shard_map/pallas_call | solution.py:345
  204.7 2.2 %shard_map.84 = (f32[768,256]{1,0:T(8,128)S(1)}, f32[7168,256]{1,0:T(8,128)}) custom-call(s32[22]{0:T(128)S(1)} %fusion.24.core_ref.table_ref, bf16[512,7168]{1,0:T(8,128)(2,1)} %acts_ref.9, f32[512,256]{1,0:T(8,128)S(1)} %collective-permute-done.23.refs_0_, f32[768,256]{1,0:T(8,128)S(1)} %get-tuple-element.50.refs_1_, ...), custom_call_target="tpu_custom_call", output_to_operand_aliasing={{0}: (3, {}), {1}: (4, {})} | custom-call | flops 201326592 | bytes 1572864 | tf_op jit(solution)/shard_map/pallas_call | solution.py:345
  207.0 2.3 %collective-permute-done.31.theirs_ref = f32[768,256]{1,0:T(8,128)S(1)} collective-permute-done((f32[768,256]{1,0:T(8,128)S(1)}, f32[768,256]{1,0:T(8,128)S(1)}, u32[]{:S(2)}, u32[]{:S(2)}) %collective-permute-start.31) | collective-permute-done | bytes 786464 | tf_op jit(solution)/shard_map/ppermute | solution.py:409
  209.3 2.0 shard_map.85
  (44 shorter events, 10.1 us)
Async XLA Ops:
  0.6 12.0 %copy-start = (f32[512,256]{1,0:T(8,128)S(1)}, f32[512,256]{1,0:T(8,128)}, u32[]{:S(2)}) copy-start(f32[512,256]{1,0:T(8,128)} %codes_ref.1) | copy-start | bytes 1572868
  10.2 2.4 %collective-permute-start = (f32[768,256]{1,0:T(8,128)S(1)}, f32[768,256]{1,0:T(8,128)S(1)}, u32[]{:S(2)}, u32[]{:S(2)}) collective-permute-start(f32[768,256]{1,0:T(8,128)S(1)} %shard_map.59.mine_ref), channel_id=1, source_target_pairs={{0,1},{1,0},{2,3},{3,2},{4,5},{5,4},{6,7},{7,6},{8,9},{9,8},{10,11... | collective-permute-start | bytes 2359304 | tf_op jit(solution)/shard_map/ppermute | solution.py:409
  14.6 0.8 copy-start.1
  15.4 10.6 %collective-permute-start.2 = (f32[128,256]{1,0:T(8,128)S(1)}, f32[128,256]{1,0:T(8,128)S(1)}, u32[]{:S(2)}, u32[]{:S(2)}) collective-permute-start(f32[128,256]{1,0:T(8,128)S(1)} %get-tuple-element.30.mine_ref), channel_id=1, source_target_pairs={{0,16},{1,17},{2,18},{3,19},{4,20},{5,21},{6,22},{7,23},{8,24},{9,... | collective-permute-start | bytes 393224 | tf_op jit(solution)/shard_map/ppermute | solution.py:376
  22.3 17.8 %collective-permute-start.1 = (f32[1280,256]{1,0:T(8,128)}, f32[1280,256]{1,0:T(8,128)S(1)}, u32[]{:S(2)}, u32[]{:S(2)}) collective-permute-start(f32[1280,256]{1,0:T(8,128)} %fusion.2), channel_id=1, source_target_pairs={{0,2},{1,5},{2,0},{3,7},{4,6},{5,1},{6,4},{7,3},{8,10},{9,13},{10,... | collective-permute-start | bytes 3932168 | tf_op jit(solution)/shard_map/ppermute | solution.py:376
  29.5 33.2 %collective-permute-start.8 = (f32[1280,256]{1,0:T(8,128)}, f32[1280,256]{1,0:T(8,128)}, u32[]{:S(2)}, u32[]{:S(2)}) collective-permute-start(f32[1280,256]{1,0:T(8,128)} %fusion), channel_id=1, source_target_pairs={{0,2},{1,5},{2,0},{3,7},{4,6},{5,1},{6,4},{7,3},{8,10},{9,13},{10,... | collective-permute-start | bytes 3932168 | tf_op jit(solution)/shard_map/ppermute | solution.py:376
  33.7 33.4 %collective-permute-start.7 = (f32[1024,256]{1,0:T(8,128)}, f32[1024,256]{1,0:T(8,128)S(1)}, u32[]{:S(2)}, u32[]{:S(2)}) collective-permute-start(f32[1024,256]{1,0:T(8,128)} %fusion.4), channel_id=1, source_target_pairs={{0,8},{1,9},{2,10},{3,11},{4,12},{5,13},{6,14},{7,15},{8,0},{9,1},... | collective-permute-start | bytes 3145736 | tf_op jit(solution)/shard_map/ppermute | solution.py:376
  40.7 30.0 %collective-permute-start.3 = (f32[768,256]{1,0:T(8,128)S(1)}, f32[768,256]{1,0:T(8,128)}, u32[]{:S(2)}, u32[]{:S(2)}) collective-permute-start(f32[768,256]{1,0:T(8,128)S(1)} %shard_map.62.refs_0_), channel_id=1, source_target_pairs={{0,4},{1,3},{2,6},{3,1},{4,0},{5,7},{6,2},{7,5},{8,12},{9,11},{10,... | collective-permute-start | bytes 2359304 | tf_op jit(solution)/shard_map/ppermute | solution.py:376
  64.1 17.7 %collective-permute-start.10 = (f32[640,256]{1,0:T(8,128)S(1)}, f32[640,256]{1,0:T(8,128)S(1)}, u32[]{:S(2)}, u32[]{:S(2)}) collective-permute-start(f32[640,256]{1,0:T(8,128)S(1)} %shard_map.65.refs_0_), channel_id=1, source_target_pairs={{0,8},{1,9},{2,10},{3,11},{4,12},{5,13},{6,14},{7,15},{8,0},{9,1},... | collective-permute-start | bytes 1966088 | tf_op jit(solution)/shard_map/ppermute | solution.py:376
  67.7 17.7 %collective-permute-start.9 = (f32[512,256]{1,0:T(8,128)S(1)}, f32[512,256]{1,0:T(8,128)S(1)}, u32[]{:S(2)}, u32[]{:S(2)}) collective-permute-start(f32[512,256]{1,0:T(8,128)S(1)} %shard_map.66), channel_id=1, source_target_pairs={{0,2},{1,5},{2,0},{3,7},{4,6},{5,1},{6,4},{7,3},{8,10},{9,13},{10,... | collective-permute-start | bytes 1572872 | tf_op jit(solution)/shard_map/ppermute | solution.py:376
  72.0 17.6 %collective-permute-start.4 = (f32[448,256]{1,0:T(8,128)S(1)}, f32[448,256]{1,0:T(8,128)S(1)}, u32[]{:S(2)}, u32[]{:S(2)}) collective-permute-start(f32[448,256]{1,0:T(8,128)S(1)} %get-tuple-element.33), channel_id=1, source_target_pairs={{0,8},{1,9},{2,10},{3,11},{4,12},{5,13},{6,14},{7,15},{8,0},{9,1},... | collective-permute-start | bytes 1376264 | tf_op jit(solution)/shard_map/ppermute | solution.py:376
  82.5 13.3 %collective-permute-start.12 = (f32[320,256]{1,0:T(8,128)S(1)}, f32[320,256]{1,0:T(8,128)S(1)}, u32[]{:S(2)}, u32[]{:S(2)}) collective-permute-start(f32[320,256]{1,0:T(8,128)S(1)} %get-tuple-element.39), channel_id=1, source_target_pairs={{0,4},{1,3},{2,6},{3,1},{4,0},{5,7},{6,2},{7,5},{8,12},{9,11},{10,... | collective-permute-start | bytes 983048 | tf_op jit(solution)/shard_map/ppermute | solution.py:376
  86.0 13.0 %collective-permute-start.11 = (f32[256,256]{1,0:T(8,128)S(1)}, f32[256,256]{1,0:T(8,128)S(1)}, u32[]{:S(2)}, u32[]{:S(2)}) collective-permute-start(f32[256,256]{1,0:T(8,128)S(1)} %get-tuple-element.38), channel_id=1, source_target_pairs={{0,4},{1,3},{2,6},{3,1},{4,0},{5,7},{6,2},{7,5},{8,12},{9,11},{10,... | collective-permute-start | bytes 786440 | tf_op jit(solution)/shard_map/ppermute | solution.py:376
  90.2 5.0 %collective-permute-start.5 = (f32[128,256]{1,0:T(8,128)S(1)}, f32[128,256]{1,0:T(8,128)S(1)}, u32[]{:S(2)}, u32[]{:S(2)}) collective-permute-start(f32[128,256]{1,0:T(8,128)S(1)} %get-tuple-element.34), channel_id=1, source_target_pairs={{0,2},{1,5},{2,0},{3,7},{4,6},{5,1},{6,4},{7,3},{8,10},{9,13},{10,... | collective-permute-start | bytes 393224 | tf_op jit(solution)/shard_map/ppermute | solution.py:376
  95.3 4.3 %collective-permute-start.6 = (f32[128,256]{1,0:T(8,128)S(1)}, f32[128,256]{1,0:T(8,128)S(1)}, u32[]{:S(2)}, u32[]{:S(2)}) collective-permute-start(f32[128,256]{1,0:T(8,128)S(1)} %add.102.mine_ref), channel_id=1, source_target_pairs={{0,1},{1,0},{2,3},{3,2},{4,5},{5,4},{6,7},{7,6},{8,9},{9,8},{10,11... | collective-permute-start | bytes 393224 | tf_op jit(solution)/shard_map/ppermute | solution.py:409
  95.4 15.0 %collective-permute-start.14 = (f32[160,256]{1,0:T(8,128)S(1)}, f32[160,256]{1,0:T(8,128)S(1)}, u32[]{:S(2)}, u32[]{:S(2)}) collective-permute-start(f32[160,256]{1,0:T(8,128)S(1)} %get-tuple-element.44), channel_id=1, source_target_pairs={{0,16},{1,17},{2,18},{3,19},{4,20},{5,21},{6,22},{7,23},{8,24},{9,... | collective-permute-start | bytes 491528 | tf_op jit(solution)/shard_map/ppermute | solution.py:376
  96.3 17.1 %collective-permute-start.15 = (f32[160,256]{1,0:T(8,128)S(1)}, f32[160,256]{1,0:T(8,128)S(1)}, u32[]{:S(2)}, u32[]{:S(2)}) collective-permute-start(f32[160,256]{1,0:T(8,128)S(1)} %get-tuple-element.45), channel_id=1, source_target_pairs={{0,16},{1,17},{2,18},{3,19},{4,20},{5,21},{6,22},{7,23},{8,24},{9,... | collective-permute-start | bytes 491528 | tf_op jit(solution)/shard_map/ppermute | solution.py:376
  111.7 23.2 %collective-permute-start.18 = (f32[160,256]{1,0:T(8,128)S(1)}, f32[160,256]{1,0:T(8,128)S(1)}, u32[]{:S(2)}, u32[]{:S(2)}) collective-permute-start(f32[160,256]{1,0:T(8,128)S(1)} %shard_map.72.refs_1_.mine_ref), channel_id=1, source_target_pairs={{0,16},{1,17},{2,18},{3,19},{4,20},{5,21},{6,22},{7,23},{8,24},{9,... | collective-permute-start | bytes 491528 | tf_op jit(solution)/shard_map/ppermute | solution.py:376
  114.8 23.2 %collective-permute-start.17 = (f32[160,256]{1,0:T(8,128)S(1)}, f32[160,256]{1,0:T(8,128)S(1)}, u32[]{:S(2)}, u32[]{:S(2)}) collective-permute-start(f32[160,256]{1,0:T(8,128)S(1)} %shard_map.73.refs_2_.mine_ref), channel_id=1, source_target_pairs={{0,16},{1,17},{2,18},{3,19},{4,20},{5,21},{6,22},{7,23},{8,24},{9,... | collective-permute-start | bytes 491528 | tf_op jit(solution)/shard_map/ppermute | solution.py:376
  116.2 17.4 %collective-permute-start.13 = (f32[128,256]{1,0:T(8,128)S(1)}, f32[128,256]{1,0:T(8,128)S(1)}, u32[]{:S(2)}, u32[]{:S(2)}) collective-permute-start(f32[128,256]{1,0:T(8,128)S(1)} %get-tuple-element.43), channel_id=1, source_target_pairs={{0,16},{1,17},{2,18},{3,19},{4,20},{5,21},{6,22},{7,23},{8,24},{9,... | collective-permute-start | bytes 393224 | tf_op jit(solution)/shard_map/ppermute | solution.py:376
  134.9 8.5 %collective-permute-start.16 = (f32[128,256]{1,0:T(8,128)S(1)}, f32[128,256]{1,0:T(8,128)S(1)}, u32[]{:S(2)}, u32[]{:S(2)}) collective-permute-start(f32[128,256]{1,0:T(8,128)S(1)} %shard_map.74.mine_ref), channel_id=1, source_target_pairs={{0,16},{1,17},{2,18},{3,19},{4,20},{5,21},{6,22},{7,23},{8,24},{9,... | collective-permute-start | bytes 393224 | tf_op jit(solution)/shard_map/ppermute | solution.py:376
  135.6 12.8 %collective-permute-start.21 = (f32[320,256]{1,0:T(8,128)S(1)}, f32[320,256]{1,0:T(8,128)S(1)}, u32[]{:S(2)}, u32[]{:S(2)}) collective-permute-start(f32[320,256]{1,0:T(8,128)S(1)} %shard_map.75.refs_0_.mine_ref), channel_id=1, source_target_pairs={{0,8},{1,9},{2,10},{3,11},{4,12},{5,13},{6,14},{7,15},{8,0},{9,1},... | collective-permute-start | bytes 983048 | tf_op jit(solution)/shard_map/ppermute | solution.py:376
  138.5 10.4 %collective-permute-start.20 = (f32[320,256]{1,0:T(8,128)S(1)}, f32[320,256]{1,0:T(8,128)S(1)}, u32[]{:S(2)}, u32[]{:S(2)}) collective-permute-start(f32[320,256]{1,0:T(8,128)S(1)} %shard_map.76.refs_0_.mine_ref), channel_id=1, source_target_pairs={{0,4},{1,3},{2,6},{3,1},{4,0},{5,7},{6,2},{7,5},{8,12},{9,11},{10,... | collective-permute-start | bytes 983048 | tf_op jit(solution)/shard_map/ppermute | solution.py:376
  143.9 7.3 %collective-permute-start.19 = (f32[256,256]{1,0:T(8,128)S(1)}, f32[256,256]{1,0:T(8,128)S(1)}, u32[]{:S(2)}, u32[]{:S(2)}) collective-permute-start(f32[256,256]{1,0:T(8,128)S(1)} %shard_map.77.mine_ref), channel_id=1, source_target_pairs={{0,4},{1,3},{2,6},{3,1},{4,0},{5,7},{6,2},{7,5},{8,12},{9,11},{10,... | collective-permute-start | bytes 786440 | tf_op jit(solution)/shard_map/ppermute | solution.py:376
  149.6 28.7 %collective-permute-start.26 = (f32[640,256]{1,0:T(8,128)S(1)}, f32[640,256]{1,0:T(8,128)S(1)}, u32[]{:S(2)}, u32[]{:S(2)}) collective-permute-start(f32[640,256]{1,0:T(8,128)S(1)} %shard_map.79.refs_0_.refs_2_), channel_id=1, source_target_pairs={{0,8},{1,9},{2,10},{3,11},{4,12},{5,13},{6,14},{7,15},{8,0},{9,1},... | collective-permute-start | bytes 1966088 | tf_op jit(solution)/shard_map/ppermute | solution.py:376
  149.7 29.2 %collective-permute-start.24 = (f32[640,256]{1,0:T(8,128)S(1)}, f32[640,256]{1,0:T(8,128)S(1)}, u32[]{:S(2)}, u32[]{:S(2)}) collective-permute-start(f32[640,256]{1,0:T(8,128)S(1)} %shard_map.78.refs_0_), channel_id=1, source_target_pairs={{0,4},{1,3},{2,6},{3,1},{4,0},{5,7},{6,2},{7,5},{8,12},{9,11},{10,... | collective-permute-start | bytes 1966088 | tf_op jit(solution)/shard_map/ppermute | solution.py:376
  151.8 25.0 %collective-permute-start.30 = (f32[512,256]{1,0:T(8,128)S(1)}, f32[512,256]{1,0:T(8,128)S(1)}, u32[]{:S(2)}, u32[]{:S(2)}) collective-permute-start(f32[512,256]{1,0:T(8,128)S(1)} %shard_map.80.refs_4_), channel_id=1, source_target_pairs={{0,8},{1,9},{2,10},{3,11},{4,12},{5,13},{6,14},{7,15},{8,0},{9,1},... | collective-permute-start | bytes 1572872 | tf_op jit(solution)/shard_map/ppermute | solution.py:376
  153.9 26.5 %collective-permute-start.22 = (f32[512,256]{1,0:T(8,128)S(1)}, f32[512,256]{1,0:T(8,128)S(1)}, u32[]{:S(2)}, u32[]{:S(2)}) collective-permute-start(f32[512,256]{1,0:T(8,128)S(1)} %shard_map.80.refs_4_), channel_id=1, source_target_pairs={{0,2},{1,5},{2,0},{3,7},{4,6},{5,1},{6,4},{7,3},{8,10},{9,13},{10,... | collective-permute-start | bytes 1572872 | tf_op jit(solution)/shard_map/ppermute | solution.py:376
  155.3 30.4 %collective-permute-start.29 = (f32[640,256]{1,0:T(8,128)S(1)}, f32[640,256]{1,0:T(8,128)S(1)}, u32[]{:S(2)}, u32[]{:S(2)}) collective-permute-start(f32[640,256]{1,0:T(8,128)S(1)} %shard_map.79.refs_0_.refs_2_), channel_id=1, source_target_pairs={{0,2},{1,5},{2,0},{3,7},{4,6},{5,1},{6,4},{7,3},{8,10},{9,13},{10,... | collective-permute-start | bytes 1966088 | tf_op jit(solution)/shard_map/ppermute | solution.py:376
  176.8 10.6 %collective-permute-start.28 = (f32[640,256]{1,0:T(8,128)S(1)}, f32[640,256]{1,0:T(8,128)S(1)}, u32[]{:S(2)}, u32[]{:S(2)}) collective-permute-start(f32[640,256]{1,0:T(8,128)S(1)} %shard_map.78.refs_0_), channel_id=1, source_target_pairs={{0,2},{1,5},{2,0},{3,7},{4,6},{5,1},{6,4},{7,3},{8,10},{9,13},{10,... | collective-permute-start | bytes 1966088 | tf_op jit(solution)/shard_map/ppermute | solution.py:376
  178.3 16.1 %collective-permute-start.27 = (f32[640,256]{1,0:T(8,128)S(1)}, f32[640,256]{1,0:T(8,128)S(1)}, u32[]{:S(2)}, u32[]{:S(2)}) collective-permute-start(f32[640,256]{1,0:T(8,128)S(1)} %collective-permute-done.26.refs_3_), channel_id=1, source_target_pairs={{0,2},{1,5},{2,0},{3,7},{4,6},{5,1},{6,4},{7,3},{8,10},{9,13},{10,... | collective-permute-start | bytes 1966088 | tf_op jit(solution)/shard_map/ppermute | solution.py:376
  178.8 22.6 %collective-permute-start.25 = (f32[640,256]{1,0:T(8,128)S(1)}, f32[640,256]{1,0:T(8,128)S(1)}, u32[]{:S(2)}, u32[]{:S(2)}) collective-permute-start(f32[640,256]{1,0:T(8,128)S(1)} %collective-permute-done.24.refs_1_), channel_id=1, source_target_pairs={{0,2},{1,5},{2,0},{3,7},{4,6},{5,1},{6,4},{7,3},{8,10},{9,13},{10,... | collective-permute-start | bytes 1966088 | tf_op jit(solution)/shard_map/ppermute | solution.py:376
  180.3 24.4 %collective-permute-start.23 = (f32[512,256]{1,0:T(8,128)S(1)}, f32[512,256]{1,0:T(8,128)S(1)}, u32[]{:S(2)}, u32[]{:S(2)}) collective-permute-start(f32[512,256]{1,0:T(8,128)S(1)} %collective-permute-done.22.refs_5_), channel_id=1, source_target_pairs={{0,8},{1,9},{2,10},{3,11},{4,12},{5,13},{6,14},{7,15},{8,0},{9,1},... | collective-permute-start | bytes 1572872 | tf_op jit(solution)/shard_map/ppermute | solution.py:376
  204.7 4.6 %copy-start.2 = (f32[512,256]{1,0:T(8,128)S(1)}, f32[512,256]{1,0:T(8,128)}, u32[]{:S(2)}) copy-start(f32[512,256]{1,0:T(8,128)} %copy-done.1) | copy-start | bytes 1572868
  206.9 2.4 %collective-permute-start.31 = (f32[768,256]{1,0:T(8,128)S(1)}, f32[768,256]{1,0:T(8,128)S(1)}, u32[]{:S(2)}, u32[]{:S(2)}) collective-permute-start(f32[768,256]{1,0:T(8,128)S(1)} %get-tuple-element.52.mine_ref), channel_id=1, source_target_pairs={{0,1},{1,0},{2,3},{3,2},{4,5},{5,4},{6,7},{7,6},{8,9},{9,8},{10,11... | collective-permute-start | bytes 2359304 | tf_op jit(solution)/shard_map/ppermute | solution.py:409

commit v6 on v5

--- a/solution.py
+++ b/solution.py
@@ -229,40 +229,63 @@
     return call(relay_kernel, shapes, table, [mine, theirs, low], [])
 
 
-def fold_kernel(at, table_ref, mine_ref, theirs_ref, *refs):
-    rows = mine_ref.shape[0] // 2
-    keep = pl.ds(pl.multiple_of(table_ref[at] * rows, rows), rows)
-    give = pl.ds(pl.multiple_of((1 - table_ref[at]) * rows, rows), rows)
-    refs[-2][...] = mine_ref[give, :] + theirs_ref[give, :]
-    refs[-1][...] = mine_ref[keep, :] + theirs_ref[keep, :]
-
-
-def fold(table, at, mine, theirs, after):
-    half = shape(mine.shape[0] // 2, mine.shape[1])
-    return call(functools.partial(fold_kernel, at), [half, half], table, [mine, theirs], after)
-
-
-def join_kernel(at, table_ref, mine_ref, theirs_ref, *refs):
-    rows = mine_ref.shape[0]
-    refs[-1][pl.ds(pl.multiple_of(table_ref[at] * rows, rows), rows), :] = mine_ref[...]
-    refs[-1][pl.ds(pl.multiple_of((1 - table_ref[at]) * rows, rows), rows), :] = theirs_ref[...]
-
-
-def join(table, at, mine, theirs, after):
-    return call(functools.partial(join_kernel, at), [shape(2 * mine.shape[0], mine.shape[1])], table, [mine, theirs], after)[0]
-
-
-def take_kernel(at, count, table_ref, mine_ref, theirs_ref, *refs):
-    which = 1 - table_ref[at]
-    refs[-1][:count, :] = mine_ref[...] + theirs_ref[pl.ds(pl.multiple_of(which * count, count), count), :]
-    if refs[-1].shape[0] > count:
-        refs[-1][count:, :] = refs[0][...]
-
-
-def take(table, at, mine, theirs, tail, after):
-    count = mine.shape[0]
-    rows = count + sum(value.shape[0] for value in tail)
-    return call(functools.partial(take_kernel, at, count), [shape(rows, mine.shape[1])], table, [mine, theirs, *tail], after)[0]
+def several(kernel, table, groups, outs, after):
+    counts = [len(group) for group in groups]
+    gives = [len(shapes) for shapes in outs]
+
+    def body(table_ref, *refs):
+        ins, results = refs[: sum(counts)], refs[len(refs) - sum(gives) :]
+        for k, (count, give) in enumerate(zip(counts, gives)):
+            kernel(k, table_ref, ins[:count], results[:give])
+            ins, results = ins[count:], results[give:]
+
+    flat = call(body, [one for shapes in outs for one in shapes], table, [value for group in groups for value in group], after)
+    results = []
+    for give in gives:
+        results.append(flat[:give])
+        flat = flat[give:]
+    return results
+
+
+def fold(table, ats, pairs, after):
+    def kernel(k, table_ref, ins, results):
+        rows = ins[0].shape[0] // 2
+        keep = pl.ds(pl.multiple_of(table_ref[ats[k]] * rows, rows), rows)
+        give = pl.ds(pl.multiple_of((1 - table_ref[ats[k]]) * rows, rows), rows)
+        results[0][...] = ins[0][give, :] + ins[1][give, :]
+        results[1][...] = ins[0][keep, :] + ins[1][keep, :]
+
+    return several(kernel, table, pairs, [[shape(mine.shape[0] // 2, mine.shape[1])] * 2 for mine, _ in pairs], after)
+
+
+def join(table, ats, pairs, after):
+    def kernel(k, table_ref, ins, results):
+        rows = ins[0].shape[0]
+        results[0][pl.ds(pl.multiple_of(table_ref[ats[k]] * rows, rows), rows), :] = ins[0][...]
+        results[0][pl.ds(pl.multiple_of((1 - table_ref[ats[k]]) * rows, rows), rows), :] = ins[1][...]
+
+    return several(kernel, table, pairs, [[shape(2 * mine.shape[0], mine.shape[1])] for mine, _ in pairs], after)
+
+
+def take(table, ats, groups, after):
+    def kernel(k, table_ref, ins, results):
+        count = ins[0].shape[0]
+        give = pl.ds(pl.multiple_of((1 - table_ref[ats[k]]) * count, count), count)
+        results[0][:count, :] = ins[0][...] + ins[1][give, :]
+        if len(ins) > 2:
+            results[0][count:, :] = ins[2][...]
+
+    rows = [group[0].shape[0] + sum(value.shape[0] for value in group[2:]) for group in groups]
+    return several(kernel, table, groups, [[shape(count, groups[0][0].shape[1])] for count in rows], after)
+
+
+def solve(table, inverse, pairs, after):
+    def kernel(k, table_ref, ins, results):
+        factor_inv = ins[2][...]
+        results[0][...] = dot(dot(ins[0][...] + ins[1][...], factor_inv, OVER_COLS, HIGHEST), factor_inv, precision=HIGHEST)
+
+    groups = [(mine, theirs, inverse) for mine, theirs in pairs]
+    return several(kernel, table, groups, [[shape(*mine.shape)] for mine, _ in pairs], after)
 
 
 def first_fold_kernel(at, table_ref, mine_ref, theirs_ref, gram_ref, *refs):
@@ -277,12 +300,13 @@
     refs[-1][rows:, :] = gram
 
 
-def first_fold(table, at, mine, theirs, gram):
+def first_fold(table, at, mine, theirs, gram, after):
     half = shape(mine.shape[0] // 2 + gram.shape[0], mine.shape[1])
-    return call(functools.partial(first_fold_kernel, at), [half, half], table, [mine, theirs, gram], [])
-
-
-def split_fold_kernel(at, table_ref, mine_ref, theirs_ref, give_ref, keep_ref, gram_ref):
+    return call(functools.partial(first_fold_kernel, at), [half, half], table, [mine, theirs, gram], after)
+
+
+def split_fold_kernel(at, table_ref, mine_ref, theirs_ref, *refs):
+    give_ref, keep_ref, gram_ref = refs[-3:]
     rows = give_ref.shape[0]
     keep = pl.ds(pl.multiple_of(table_ref[at] * rows, rows), rows)
     give = pl.ds(pl.multiple_of((1 - table_ref[at]) * rows, rows), rows)
@@ -291,20 +315,10 @@
     gram_ref[...] = mine_ref[2 * rows :, :] + theirs_ref[2 * rows :, :]
 
 
-def split_fold(table, at, extra, mine, theirs):
+def split_fold(table, at, extra, mine, theirs, after):
     comp = mine.shape[1]
     half = shape((mine.shape[0] - extra) // 2, comp)
-    return call(functools.partial(split_fold_kernel, at), [half, half, shape(extra, comp)], table, [mine, theirs], [])
-
-
-def rows_kernel(table_ref, inverse_ref, mine_ref, *refs):
-    inverse = inverse_ref[...]
-    cross = mine_ref[...] + refs[0][...]
-    refs[-1][...] = dot(dot(cross, inverse, OVER_COLS, HIGHEST), inverse, precision=HIGHEST)
-
-
-def solve_sum(table, inverse, parts, after):
-    return call(rows_kernel, [shape(*parts[0].shape)], table, [inverse, *parts], after)[0]
+    return call(functools.partial(split_fold_kernel, at), [half, half, shape(extra, comp)], table, [mine, theirs], after)
 
 
 def absorb_kernel(ats, fresh, table_ref, acts_ref, *refs):
@@ -368,6 +382,7 @@
     "B": ("first", "near", "second", "far"),
     "N": ("near", "first", "second", "far"),
 }
+TURNS = (("A",), ("B", "N"))
 SHARES = {"A": 5, "B": 5, "N": 4}
 FIELDS = ("b", "c", "d", "mine", "theirs", "far_mine", "far_theirs")
 
@@ -433,40 +448,44 @@
         return cross_of(starts[name] + a * half + (b if keep else 1 - b) * quarter, quarter, low)
 
     gram, low_later = relay(table, gram, swap(gram, "far"), low)
-    got, keeps, held, last = {}, {}, {}, []
+    got, keeps, held = {}, {}, {}
     for name, order in ORDERS.items():
         got[name] = swap(give_1(name, low if name == "A" else low_later), order[0])
-    for name, order in ORDERS.items():
-        give = take(table, where[name, "b"], own_2(name, False), got[name], [gram] if name == "A" else [], last)
-        held[name], last = swap(give, order[1]), [give]
-        quarter = rows[name] // 4
-        keeps[name] = own_2(name, True) + lax.dynamic_slice_in_dim(got[name], bits[order[1]] * quarter, quarter, 0)
     last = []
-    for name, order in ORDERS.items():
-        if name == "A":
-            give, keep = first_fold(table, where[name, "c"], keeps[name], held[name], gram)
-        else:
-            give, keep = fold(table, where[name, "c"], keeps[name], held[name], last)
-        keeps[name], held[name], last = keep, swap(give, order[2]), [keep]
-    last = []
-    for name, order in ORDERS.items():
-        if name == "A":
-            give, keep, gram = split_fold(table, where[name, "d"], gram.shape[0], keeps[name], held[name])
-            gram = gram + swap(gram, "first")
-        else:
-            give, keep = fold(table, where[name, "d"], keeps[name], held[name], last)
-        held[name], last = (keep, swap(give, order[3])), [keep]
+    for names in TURNS:
+        groups = [[own_2(name, False), got[name]] + ([gram] if name == "A" else []) for name in names]
+        gives = take(table, [where[name, "b"] for name in names], groups, last)
+        for name, (give,) in zip(names, gives):
+            held[name], last = swap(give, ORDERS[name][1]), [give]
+            quarter = rows[name] // 4
+            kept = lax.dynamic_slice_in_dim(got[name], bits[ORDERS[name][1]] * quarter, quarter, 0)
+            keeps[name] = own_2(name, True) + kept
+    for k, field in ((2, "c"), (3, "d")):
+        for names in TURNS:
+            if "A" in names and k == 2:
+                parts = [first_fold(table, where["A", "c"], keeps["A"], held["A"], gram, last)]
+            elif "A" in names:
+                give, keep, gram = split_fold(table, where["A", "d"], gram.shape[0], keeps["A"], held["A"], last)
+                gram = gram + swap(gram, "first")
+                parts = [(give, keep)]
+            else:
+                parts = fold(table, [where[name, field] for name in names], [(keeps[name], held[name]) for name in names], last)
+            for name, (give, keep) in zip(names, parts):
+                keeps[name], held[name], last = keep, swap(give, ORDERS[name][k]), [keep]
 
     inverse = factor_inverse(table, gram, other_core(gram), last)
-    mine = {}
-    for name in held:
-        mine[name] = solve_sum(table, inverse, held[name], list(mine.values()))
+    mine, last = {}, []
+    for names in TURNS:
+        parts = solve(table, inverse, [(keeps[name], held[name]) for name in names], last)
+        for name, (value,) in zip(names, parts):
+            mine[name], last = value, [value]
 
     for k, field in ((3, "d"), (2, "c")):
-        last = []
-        for name, order in ORDERS.items():
-            mine[name] = join(table, where[name, field], mine[name], swap(mine[name], order[k]), last)
-            last = [mine[name]]
+        for names in TURNS:
+            pairs = [(mine[name], swap(mine[name], ORDERS[name][k])) for name in names]
+            parts = join(table, [where[name, field] for name in names], pairs, last)
+            for name, (value,) in zip(names, parts):
+                mine[name], last = value, [value]
     near, far, last = [], [], []
     for name in mine:
         theirs = swap(mine[name], ORDERS[name][1])
@@ -474,7 +493,7 @@
         far += [(swap(mine[name], ORDERS[name][0]), where[name, "far_mine"])]
         last += [(swap(theirs, ORDERS[name][0]), where[name, "far_theirs"])]
     state = None
-    for blocks in (near, far, last[:2], last[2:]):
+    for blocks in (near, far, last[2:], last[:2]):
         state = absorb(table, state, acts, blocks)
     sums, dict_out = state
     return second_update(codes_mid, sums, other_core(sums)), dict_out

time: 212 us -> 212 us (level)
  starting transfers between devices: 38.6 us -> 42.3 us
  Pallas kernels: 51.1 us -> 47.8 us
    ppermute x29, starting transfers between devices: 37.9 us -> 41.6 us  [swap(): return lax.ppermute(value, BOTH, flips(ALONG[along]))]
    pallas_call x19 -> x13, Pallas kernels: 14.9 us -> 11.6 us  [call(): pl.pallas_call(kernel, out_shape=out_shapes, in_specs=[SCALARS] + [WHOLE]...]
  transfers between devices with their start and end apart: 32 -> 32, of which waited for: 17 -> 16; matrix products, arithmetic and copies ran while one was open for 9% -> 7% of each run, Pallas kernels for 17% -> 14%
where the time goes in v6:
time: 212 us; the launch traced here: 211 us
  waiting for transfers between devices  101 us (48%)
  Pallas kernels  47.8 us (23%)
  starting transfers between devices  42.3 us (20%)
  matrix products  17.4 us (8%)
    ppermute x29, waiting for transfers between devices, swap(): return lax.ppermute(value, BOTH, flips(ALONG[along]))  97.6 us
    ppermute x29, starting transfers between devices, swap(): return lax.ppermute(value, BOTH, flips(ALONG[along]))  41.6 us
    dot_general x9, matrix products, dot(): lax.dot_general(left, right, dims, precision=precision, preferred_element...  17.4 us
    pallas_call x4, Pallas kernels, absorb(): pl.pallas_call(functools.partial(absorb_kernel, [at for _, at in blocks],...  14.3 us
    pallas_call x13, Pallas kernels, call(): pl.pallas_call(kernel, out_shape=out_shapes, in_specs=[SCALARS] + [WHOLE]...  11.6 us
    pallas_call x1, Pallas kernels, project(): pl.pallas_call(project_kernel, out_shape=jax.ShapeDtypeStruct((tokens + c...  9.55 us
    pallas_call x1, Pallas kernels, factor_inverse(): pl.pallas_call(halves_kernel, out_shape=jax.ShapeDtypeStruct((comp, comp)...  8.43 us
  transfers between devices with their start and end apart: 32, of which 16 were waited for; matrix products, arithmetic and copies ran while one was open for 7% of the time, Pallas kernels for 14%

profile of v6, /device:TPU:0, one launch (start us, length us, event | category | flops | bytes accessed | tf_op | source)
XLA Modules:
  0.0 211.1 jit_solution(17532383365220389611)
XLA Ops:
  0.6 9.6 %shard_map.59.mine_ref = f32[768,256]{1,0:T(8,128)S(1)} custom-call(bf16[512,7168]{1,0:T(8,128)(2,1)} %acts_ref.9, f32[7168,256]{1,0:T(8,128)} %dict_ref.1), custom_call_target="tpu_custom_call" | custom-call | flops 3758096384 | bytes 14680064 | tf_op jit(solution)/shard_map/pallas_call | solution.py:58
  10.7 0.7 fusion.24.core_ref.table_ref
  11.4 1.2 collective-permute-done.theirs_ref
  12.6 2.0 shard_map.60
  14.6 0.8 copy-done.1
  15.4 2.9 %fusion.2 = f32[1280,256]{1,0:T(8,128)} fusion(bf16[512,256]{1,0:T(8,128)(2,1)S(1)} %get-tuple-element.37.low_ref, bf16[512,7168]{1,0:T(8,128)(2,1)} %acts_ref.9, s32[]{:T(128)S(6)} %select_n.63), kind=kOutput, calls=%fused_computation.2 | convolution fusion | flops 335544320 | bytes 2883588 | tf_op jit(solution)/shard_map/dot_general | solution.py:21
  18.3 2.9 %collective-permute-start.1 = (f32[1280,256]{1,0:T(8,128)}, f32[1280,256]{1,0:T(8,128)S(1)}, u32[]{:S(2)}, u32[]{:S(2)}) collective-permute-start(f32[1280,256]{1,0:T(8,128)} %fusion.2), channel_id=1, source_target_pairs={{0,2},{1,5},{2,0},{3,7},{4,6},{5,1},{6,4},{7,3},{8,10},{9,13},{10,... | collective-permute-start | bytes 3932168 | tf_op jit(solution)/shard_map/ppermute | solution.py:391
  21.2 2.6 %collective-permute-start.2 = (f32[128,256]{1,0:T(8,128)S(1)}, f32[128,256]{1,0:T(8,128)S(1)}, u32[]{:S(2)}, u32[]{:S(2)}) collective-permute-start(f32[128,256]{1,0:T(8,128)S(1)} %get-tuple-element.38.mine_ref), channel_id=1, source_target_pairs={{0,16},{1,17},{2,18},{3,19},{4,20},{5,21},{6,22},{7,23},{8,24},{9,... | collective-permute-start | bytes 393224 | tf_op jit(solution)/shard_map/ppermute | solution.py:391
  23.8 6.4 %collective-permute-done.2.theirs_ref = f32[128,256]{1,0:T(8,128)S(1)} collective-permute-done((f32[128,256]{1,0:T(8,128)S(1)}, f32[128,256]{1,0:T(8,128)S(1)}, u32[]{:S(2)}, u32[]{:S(2)}) %collective-permute-start.2) | collective-permute-done | bytes 131104 | tf_op jit(solution)/shard_map/ppermute | solution.py:391
  30.8 2.9 %fusion = f32[1280,256]{1,0:T(8,128)} fusion(bf16[512,256]{1,0:T(8,128)(2,1)S(1)} %get-tuple-element.40, bf16[512,7168]{1,0:T(8,128)(2,1)} %acts_ref.9, s32[]{:T(128)S(6)} %select_n.68), kind=kOutput, calls=%fused_computation | convolution fusion | flops 335544320 | bytes 2883588 | tf_op jit(solution)/shard_map/dot_general | solution.py:21
  33.7 1.1 collective-permute-start.4
  34.8 2.7 %fusion.4 = f32[1024,256]{1,0:T(8,128)} fusion(bf16[512,256]{1,0:T(8,128)(2,1)S(1)} %get-tuple-element.40, bf16[512,7168]{1,0:T(8,128)(2,1)} %acts_ref.9, s32[]{:T(128)S(6)} %select_n.70), kind=kOutput, calls=%fused_computation.7 | convolution fusion | flops 268435456 | bytes 2359300 | tf_op jit(solution)/shard_map/dot_general | solution.py:21
  37.5 1.1 collective-permute-start.5
  38.6 1.5 fusion.9.refs_0_
  40.1 0.6 shard_map.62.refs_4_
  41.3 1.4 fusion.13.refs_2_
  42.6 1.5 fusion.7.refs_0_
  44.1 16.6 %collective-permute-done.5.refs_3_ = f32[1024,256]{1,0:T(8,128)S(1)} collective-permute-done((f32[1024,256]{1,0:T(8,128)}, f32[1024,256]{1,0:T(8,128)S(1)}, u32[]{:S(2)}, u32[]{:S(2)}) %collective-permute-start.5) | collective-permute-done | bytes 1048608 | tf_op jit(solution)/shard_map/ppermute | solution.py:391
  60.7 1.4 shard_map.63
  62.2 2.2 %collective-permute-start.8 = (f32[512,256]{1,0:T(8,128)S(1)}, f32[512,256]{1,0:T(8,128)S(1)}, u32[]{:S(2)}, u32[]{:S(2)}) collective-permute-start(f32[512,256]{1,0:T(8,128)S(1)} %get-tuple-element.41.refs_0_), channel_id=1, source_target_pairs={{0,2},{1,5},{2,0},{3,7},{4,6},{5,1},{6,4},{7,3},{8,10},{9,13},{10,... | collective-permute-start | bytes 1572872 | tf_op jit(solution)/shard_map/ppermute | solution.py:391
  64.4 1.2 collective-permute-start.7
  65.6 1.5 convolution_add_fusion.1.mine_ref
  67.1 1.2 shard_map.64
  68.3 0.9 collective-permute-start.6
  69.2 1.4 convolution_add_fusion.2.refs_2_
  70.6 1.7 convolution_add_fusion.refs_0_
  72.3 9.8 %collective-permute-done.7.refs_1_ = f32[640,256]{1,0:T(8,128)S(1)} collective-permute-done((f32[640,256]{1,0:T(8,128)S(1)}, f32[640,256]{1,0:T(8,128)S(1)}, u32[]{:S(2)}, u32[]{:S(2)}) %collective-permute-start.7) | collective-permute-done | bytes 655392 | tf_op jit(solution)/shard_map/ppermute | solution.py:391
  82.1 0.7 shard_map.65
  82.8 1.8 collective-permute-start.12
  84.9 4.2 %collective-permute-done.6.theirs_ref = f32[448,256]{1,0:T(8,128)S(1)} collective-permute-done((f32[448,256]{1,0:T(8,128)S(1)}, f32[448,256]{1,0:T(8,128)S(1)}, u32[]{:S(2)}, u32[]{:S(2)}) %collective-permute-start.6) | collective-permute-done | bytes 458784 | tf_op jit(solution)/shard_map/ppermute | solution.py:391
  89.1 0.6 shard_map.66
  89.7 2.8 %collective-permute-start.10 = (f32[128,256]{1,0:T(8,128)S(1)}, f32[128,256]{1,0:T(8,128)S(1)}, u32[]{:S(2)}, u32[]{:S(2)}) collective-permute-start(f32[128,256]{1,0:T(8,128)S(1)} %get-tuple-element.48), channel_id=1, source_target_pairs={{0,2},{1,5},{2,0},{3,7},{4,6},{5,1},{6,4},{7,3},{8,10},{9,13},{10,... | collective-permute-start | bytes 393224 | tf_op jit(solution)/shard_map/ppermute | solution.py:391
  92.5 2.9 %collective-permute-done.10 = f32[128,256]{1,0:T(8,128)S(1)} collective-permute-done((f32[128,256]{1,0:T(8,128)S(1)}, f32[128,256]{1,0:T(8,128)S(1)}, u32[]{:S(2)}, u32[]{:S(2)}) %collective-permute-start.10) | collective-permute-done | bytes 131104 | tf_op jit(solution)/shard_map/ppermute | solution.py:391
  95.6 3.2 %collective-permute-start.9 = (f32[160,256]{1,0:T(8,128)S(1)}, f32[160,256]{1,0:T(8,128)S(1)}, u32[]{:S(2)}, u32[]{:S(2)}) collective-permute-start(f32[160,256]{1,0:T(8,128)S(1)} %get-tuple-element.47), channel_id=1, source_target_pairs={{0,16},{1,17},{2,18},{3,19},{4,20},{5,21},{6,22},{7,23},{8,24},{9,... | collective-permute-start | bytes 491528 | tf_op jit(solution)/shard_map/ppermute | solution.py:391
  98.8 0.6 shard_map.67
  99.5 2.9 %collective-permute-start.15 = (f32[160,256]{1,0:T(8,128)S(1)}, f32[160,256]{1,0:T(8,128)S(1)}, u32[]{:S(2)}, u32[]{:S(2)}) collective-permute-start(f32[160,256]{1,0:T(8,128)S(1)} %get-tuple-element.54), channel_id=1, source_target_pairs={{0,16},{1,17},{2,18},{3,19},{4,20},{5,21},{6,22},{7,23},{8,24},{9,... | collective-permute-start | bytes 491528 | tf_op jit(solution)/shard_map/ppermute | solution.py:391
  102.4 8.4 %shard_map.68.refs_2_.refs_5_ = f32[256,256]{1,0:T(8,128)S(1)} custom-call(s32[22]{0:T(128)S(1)} %fusion.24.core_ref.table_ref, f32[128,256]{1,0:T(8,128)S(1)} %add.120.mine_ref, f32[128,256]{1,0:T(8,128)S(1)} %collective-permute-done.11.theirs_ref, f32[128,256]{1,0:T(8,128)S(1)} %get-tuple-element.52.refs_0_.refs_3_), custom_call_target="tpu_custom_call" | custom-call | flops 10000000000 | bytes 524288 | tf_op jit(solution)/shard_map/pallas_call | solution.py:123
  110.8 2.8 %collective-permute-done.9.refs_1_ = f32[160,256]{1,0:T(8,128)S(1)} collective-permute-done((f32[160,256]{1,0:T(8,128)S(1)}, f32[160,256]{1,0:T(8,128)S(1)}, u32[]{:S(2)}, u32[]{:S(2)}) %collective-permute-start.9) | collective-permute-done | bytes 163872 | tf_op jit(solution)/shard_map/ppermute | solution.py:391
  113.7 1.4 shard_map.69.refs_6_.refs_0_
  115.1 1.3 collective-permute-done.16.refs_4_
  116.5 7.0 %collective-permute-done.15.refs_1_ = f32[160,256]{1,0:T(8,128)S(1)} collective-permute-done((f32[160,256]{1,0:T(8,128)S(1)}, f32[160,256]{1,0:T(8,128)S(1)}, u32[]{:S(2)}, u32[]{:S(2)}) %collective-permute-start.15) | collective-permute-done | bytes 163872 | tf_op jit(solution)/shard_map/ppermute | solution.py:391
  123.5 2.1 %shard_map.70 = (f32[160,256]{1,0:T(8,128)S(1)}, f32[128,256]{1,0:T(8,128)S(1)}) custom-call(s32[22]{0:T(128)S(1)} %fusion.24.core_ref.table_ref, f32[160,256]{1,0:T(8,128)S(1)} %get-tuple-element.53.refs_0_, f32[160,256]{1,0:T(8,128)S(1)} %collective-permute-done.15.refs_1_, f32[256,256]{1,0:T(8,128)S(1)} %shard_map.68.refs_2_.refs_5_, ...), custom_call_target="tpu_custom_call" | custom-call | tf_op jit(solution)/shard_map/pallas_call | solution.py:209
  125.7 2.9 %collective-permute-start.19 = (f32[128,256]{1,0:T(8,128)S(1)}, f32[128,256]{1,0:T(8,128)S(1)}, u32[]{:S(2)}, u32[]{:S(2)}) collective-permute-start(f32[128,256]{1,0:T(8,128)S(1)} %get-tuple-element.56.refs_2_), channel_id=1, source_target_pairs={{0,16},{1,17},{2,18},{3,19},{4,20},{5,21},{6,22},{7,23},{8,24},{9,... | collective-permute-start | bytes 393224 | tf_op jit(solution)/shard_map/ppermute | solution.py:391
  129.2 4.3 %collective-permute-start.17 = (f32[320,256]{1,0:T(8,128)S(1)}, f32[320,256]{1,0:T(8,128)S(1)}, u32[]{:S(2)}, u32[]{:S(2)}) collective-permute-start(f32[320,256]{1,0:T(8,128)S(1)} %shard_map.71.refs_4_.refs_0_), channel_id=1, source_target_pairs={{0,8},{1,9},{2,10},{3,11},{4,12},{5,13},{6,14},{7,15},{8,0},{9,1},... | collective-permute-start | bytes 983048 | tf_op jit(solution)/shard_map/ppermute | solution.py:391
  133.5 8.0 %collective-permute-done.19.refs_3_ = f32[128,256]{1,0:T(8,128)S(1)} collective-permute-done((f32[128,256]{1,0:T(8,128)S(1)}, f32[128,256]{1,0:T(8,128)S(1)}, u32[]{:S(2)}, u32[]{:S(2)}) %collective-permute-start.19) | collective-permute-done | bytes 131104 | tf_op jit(solution)/shard_map/ppermute | solution.py:391
  141.5 0.6 shard_map.72
  142.6 1.7 collective-permute-start.23
  144.2 0.6 shard_map.73.refs_4_.refs_0_
  144.8 7.3 %collective-permute-done.23.refs_3_ = f32[256,256]{1,0:T(8,128)S(1)} collective-permute-done((f32[256,256]{1,0:T(8,128)S(1)}, f32[256,256]{1,0:T(8,128)S(1)}, u32[]{:S(2)}, u32[]{:S(2)}) %collective-permute-start.23) | collective-permute-done | bytes 262176 | tf_op jit(solution)/shard_map/ppermute | solution.py:391
  152.1 0.6 shard_map.74
  153.2 1.9 collective-permute-start.30
  155.2 2.0 collective-permute-start.26
  157.2 21.6 %collective-permute-done.30.refs_2_ = f32[512,256]{1,0:T(8,128)S(1)} collective-permute-done((f32[512,256]{1,0:T(8,128)S(1)}, f32[512,256]{1,0:T(8,128)S(1)}, u32[]{:S(2)}, u32[]{:S(2)}) %collective-permute-start.30) | collective-permute-done | bytes 524320 | tf_op jit(solution)/shard_map/ppermute | solution.py:391
  178.9 1.7 collective-permute-start.28
  180.9 1.7 collective-permute-start.21
  182.9 5.1 %shard_map.75 = (f32[768,256]{1,0:T(8,128)S(1)}, f32[7168,256]{1,0:T(8,128)}) custom-call(s32[22]{0:T(128)S(1)} %fusion.24.core_ref.table_ref, bf16[512,7168]{1,0:T(8,128)(2,1)} %acts_ref.9, f32[640,256]{1,0:T(8,128)S(1)} %shard_map.73.refs_4_.refs_0_, f32[640,256]{1,0:T(8,128)S(1)} %collective-permute-done.20.refs_1_, ...), custom_call_target="tpu_custom_call" | custom-call | flops 1409286144 | bytes 11010048 | tf_op jit(solution)/shard_map/pallas_call | solution.py:359
  188.1 1.4 collective-permute-done.28.refs_0_
  189.4 3.7 %shard_map.76 = (f32[768,256]{1,0:T(8,128)S(1)}, f32[7168,256]{1,0:T(8,128)}) custom-call(s32[22]{0:T(128)S(1)} %fusion.24.core_ref.table_ref, bf16[512,7168]{1,0:T(8,128)(2,1)} %acts_ref.9, f32[640,256]{1,0:T(8,128)S(1)} %collective-permute-done.28.refs_0_, ...), custom_call_target="tpu_custom_call", output_to_operand_aliasing={{0}: (5, {}), {1}: (6, {})} | custom-call | flops 704643072 | bytes 5505024 | tf_op jit(solution)/shard_map/pallas_call | solution.py:359
  193.1 2.2 %shard_map.77 = (f32[768,256]{1,0:T(8,128)S(1)}, f32[7168,256]{1,0:T(8,128)}) custom-call(s32[22]{0:T(128)S(1)} %fusion.24.core_ref.table_ref, bf16[512,7168]{1,0:T(8,128)(2,1)} %acts_ref.9, f32[512,256]{1,0:T(8,128)S(1)} %collective-permute-done.27.refs_0_, f32[768,256]{1,0:T(8,128)S(1)} %get-tuple-element.64.refs_1_, ...), custom_call_target="tpu_custom_call", output_to_operand_aliasing={{0}: (3, {}), {1}: (4, {})} | custom-call | flops 201326592 | bytes 1572864 | tf_op jit(solution)/shard_map/pallas_call | solution.py:359
  195.3 1.1 collective-permute-done.25.refs_1_
  196.5 7.0 %collective-permute-done.21.refs_0_ = f32[640,256]{1,0:T(8,128)S(1)} collective-permute-done((f32[640,256]{1,0:T(8,128)S(1)}, f32[640,256]{1,0:T(8,128)S(1)}, u32[]{:S(2)}, u32[]{:S(2)}) %collective-permute-start.21) | collective-permute-done | bytes 655392 | tf_op jit(solution)/shard_map/ppermute | solution.py:391
  203.5 3.3 %shard_map.78 = (f32[768,256]{1,0:T(8,128)S(1)}, f32[7168,256]{1,0:T(8,128)}) custom-call(s32[22]{0:T(128)S(1)} %fusion.24.core_ref.table_ref, bf16[512,7168]{1,0:T(8,128)(2,1)} %acts_ref.9, f32[640,256]{1,0:T(8,128)S(1)} %collective-permute-done.21.refs_0_, ...), custom_call_target="tpu_custom_call", output_to_operand_aliasing={{0}: (4, {}), {1}: (5, {})} | custom-call | flops 503316480 | bytes 3932160 | tf_op jit(solution)/shard_map/pallas_call | solution.py:359
  206.8 2.3 %collective-permute-done.31.theirs_ref = f32[768,256]{1,0:T(8,128)S(1)} collective-permute-done((f32[768,256]{1,0:T(8,128)S(1)}, f32[768,256]{1,0:T(8,128)S(1)}, u32[]{:S(2)}, u32[]{:S(2)}) %collective-permute-start.31) | collective-permute-done | bytes 786464 | tf_op jit(solution)/shard_map/ppermute | solution.py:424
  209.1 2.0 shard_map.79
  (38 shorter events, 4.5 us)
Async XLA Ops:
  0.6 12.0 %copy-start = (f32[512,256]{1,0:T(8,128)S(1)}, f32[512,256]{1,0:T(8,128)}, u32[]{:S(2)}) copy-start(f32[512,256]{1,0:T(8,128)} %codes_ref.1) | copy-start | bytes 1572868
  10.2 2.4 %collective-permute-start = (f32[768,256]{1,0:T(8,128)S(1)}, f32[768,256]{1,0:T(8,128)S(1)}, u32[]{:S(2)}, u32[]{:S(2)}) collective-permute-start(f32[768,256]{1,0:T(8,128)S(1)} %shard_map.59.mine_ref), channel_id=1, source_target_pairs={{0,1},{1,0},{2,3},{3,2},{4,5},{5,4},{6,7},{7,6},{8,9},{9,8},{10,11... | collective-permute-start | bytes 2359304 | tf_op jit(solution)/shard_map/ppermute | solution.py:424
  14.6 0.8 copy-start.1
  18.3 21.7 %collective-permute-start.1 = (f32[1280,256]{1,0:T(8,128)}, f32[1280,256]{1,0:T(8,128)S(1)}, u32[]{:S(2)}, u32[]{:S(2)}) collective-permute-start(f32[1280,256]{1,0:T(8,128)} %fusion.2), channel_id=1, source_target_pairs={{0,2},{1,5},{2,0},{3,7},{4,6},{5,1},{6,4},{7,3},{8,10},{9,13},{10,... | collective-permute-start | bytes 3932168 | tf_op jit(solution)/shard_map/ppermute | solution.py:391
  21.2 9.0 %collective-permute-start.2 = (f32[128,256]{1,0:T(8,128)S(1)}, f32[128,256]{1,0:T(8,128)S(1)}, u32[]{:S(2)}, u32[]{:S(2)}) collective-permute-start(f32[128,256]{1,0:T(8,128)S(1)} %get-tuple-element.38.mine_ref), channel_id=1, source_target_pairs={{0,16},{1,17},{2,18},{3,19},{4,20},{5,21},{6,22},{7,23},{8,24},{9,... | collective-permute-start | bytes 393224 | tf_op jit(solution)/shard_map/ppermute | solution.py:391
  33.7 27.0 %collective-permute-start.4 = (f32[1280,256]{1,0:T(8,128)}, f32[1280,256]{1,0:T(8,128)}, u32[]{:S(2)}, u32[]{:S(2)}) collective-permute-start(f32[1280,256]{1,0:T(8,128)} %fusion), channel_id=1, source_target_pairs={{0,2},{1,5},{2,0},{3,7},{4,6},{5,1},{6,4},{7,3},{8,10},{9,13},{10,... | collective-permute-start | bytes 3932168 | tf_op jit(solution)/shard_map/ppermute | solution.py:391
  37.5 23.2 %collective-permute-start.5 = (f32[1024,256]{1,0:T(8,128)}, f32[1024,256]{1,0:T(8,128)S(1)}, u32[]{:S(2)}, u32[]{:S(2)}) collective-permute-start(f32[1024,256]{1,0:T(8,128)} %fusion.4), channel_id=1, source_target_pairs={{0,8},{1,9},{2,10},{3,11},{4,12},{5,13},{6,14},{7,15},{8,0},{9,1},... | collective-permute-start | bytes 3145736 | tf_op jit(solution)/shard_map/ppermute | solution.py:391
  40.7 26.4 %collective-permute-start.3 = (f32[768,256]{1,0:T(8,128)S(1)}, f32[768,256]{1,0:T(8,128)}, u32[]{:S(2)}, u32[]{:S(2)}) collective-permute-start(f32[768,256]{1,0:T(8,128)S(1)} %shard_map.62.refs_4_), channel_id=1, source_target_pairs={{0,4},{1,3},{2,6},{3,1},{4,0},{5,7},{6,2},{7,5},{8,12},{9,11},{10,... | collective-permute-start | bytes 2359304 | tf_op jit(solution)/shard_map/ppermute | solution.py:391
  62.2 10.1 %collective-permute-start.8 = (f32[512,256]{1,0:T(8,128)S(1)}, f32[512,256]{1,0:T(8,128)S(1)}, u32[]{:S(2)}, u32[]{:S(2)}) collective-permute-start(f32[512,256]{1,0:T(8,128)S(1)} %get-tuple-element.41.refs_0_), channel_id=1, source_target_pairs={{0,2},{1,5},{2,0},{3,7},{4,6},{5,1},{6,4},{7,3},{8,10},{9,13},{10,... | collective-permute-start | bytes 1572872 | tf_op jit(solution)/shard_map/ppermute | solution.py:391
  64.4 17.7 %collective-permute-start.7 = (f32[640,256]{1,0:T(8,128)S(1)}, f32[640,256]{1,0:T(8,128)S(1)}, u32[]{:S(2)}, u32[]{:S(2)}) collective-permute-start(f32[640,256]{1,0:T(8,128)S(1)} %get-tuple-element.44), channel_id=1, source_target_pairs={{0,8},{1,9},{2,10},{3,11},{4,12},{5,13},{6,14},{7,15},{8,0},{9,1},... | collective-permute-start | bytes 1966088 | tf_op jit(solution)/shard_map/ppermute | solution.py:391
  68.3 20.7 %collective-permute-start.6 = (f32[448,256]{1,0:T(8,128)S(1)}, f32[448,256]{1,0:T(8,128)S(1)}, u32[]{:S(2)}, u32[]{:S(2)}) collective-permute-start(f32[448,256]{1,0:T(8,128)S(1)} %get-tuple-element.43), channel_id=1, source_target_pairs={{0,8},{1,9},{2,10},{3,11},{4,12},{5,13},{6,14},{7,15},{8,0},{9,1},... | collective-permute-start | bytes 1376264 | tf_op jit(solution)/shard_map/ppermute | solution.py:391
  82.8 16.0 %collective-permute-start.12 = (f32[320,256]{1,0:T(8,128)S(1)}, f32[320,256]{1,0:T(8,128)S(1)}, u32[]{:S(2)}, u32[]{:S(2)}) collective-permute-start(f32[320,256]{1,0:T(8,128)S(1)} %get-tuple-element.50), channel_id=1, source_target_pairs={{0,4},{1,3},{2,6},{3,1},{4,0},{5,7},{6,2},{7,5},{8,12},{9,11},{10,... | collective-permute-start | bytes 983048 | tf_op jit(solution)/shard_map/ppermute | solution.py:391
  84.6 14.2 %collective-permute-start.13 = (f32[256,256]{1,0:T(8,128)S(1)}, f32[256,256]{1,0:T(8,128)S(1)}, u32[]{:S(2)}, u32[]{:S(2)}) collective-permute-start(f32[256,256]{1,0:T(8,128)S(1)} %get-tuple-element.51), channel_id=1, source_target_pairs={{0,4},{1,3},{2,6},{3,1},{4,0},{5,7},{6,2},{7,5},{8,12},{9,11},{10,... | collective-permute-start | bytes 786440 | tf_op jit(solution)/shard_map/ppermute | solution.py:391
  89.7 5.8 %collective-permute-start.10 = (f32[128,256]{1,0:T(8,128)S(1)}, f32[128,256]{1,0:T(8,128)S(1)}, u32[]{:S(2)}, u32[]{:S(2)}) collective-permute-start(f32[128,256]{1,0:T(8,128)S(1)} %get-tuple-element.48), channel_id=1, source_target_pairs={{0,2},{1,5},{2,0},{3,7},{4,6},{5,1},{6,4},{7,3},{8,10},{9,13},{10,... | collective-permute-start | bytes 393224 | tf_op jit(solution)/shard_map/ppermute | solution.py:391
  95.5 6.9 %collective-permute-start.11 = (f32[128,256]{1,0:T(8,128)S(1)}, f32[128,256]{1,0:T(8,128)S(1)}, u32[]{:S(2)}, u32[]{:S(2)}) collective-permute-start(f32[128,256]{1,0:T(8,128)S(1)} %add.120.mine_ref), channel_id=1, source_target_pairs={{0,1},{1,0},{2,3},{3,2},{4,5},{5,4},{6,7},{7,6},{8,9},{9,8},{10,11... | collective-permute-start | bytes 393224 | tf_op jit(solution)/shard_map/ppermute | solution.py:424
  95.6 18.1 %collective-permute-start.9 = (f32[160,256]{1,0:T(8,128)S(1)}, f32[160,256]{1,0:T(8,128)S(1)}, u32[]{:S(2)}, u32[]{:S(2)}) collective-permute-start(f32[160,256]{1,0:T(8,128)S(1)} %get-tuple-element.47), channel_id=1, source_target_pairs={{0,16},{1,17},{2,18},{3,19},{4,20},{5,21},{6,22},{7,23},{8,24},{9,... | collective-permute-start | bytes 491528 | tf_op jit(solution)/shard_map/ppermute | solution.py:391
  99.4 17.1 %collective-permute-start.16 = (f32[128,256]{1,0:T(8,128)S(1)}, f32[128,256]{1,0:T(8,128)S(1)}, u32[]{:S(2)}, u32[]{:S(2)}) collective-permute-start(f32[128,256]{1,0:T(8,128)S(1)} %get-tuple-element.55), channel_id=1, source_target_pairs={{0,16},{1,17},{2,18},{3,19},{4,20},{5,21},{6,22},{7,23},{8,24},{9,... | collective-permute-start | bytes 393224 | tf_op jit(solution)/shard_map/ppermute | solution.py:391
  99.5 24.0 %collective-permute-start.15 = (f32[160,256]{1,0:T(8,128)S(1)}, f32[160,256]{1,0:T(8,128)S(1)}, u32[]{:S(2)}, u32[]{:S(2)}) collective-permute-start(f32[160,256]{1,0:T(8,128)S(1)} %get-tuple-element.54), channel_id=1, source_target_pairs={{0,16},{1,17},{2,18},{3,19},{4,20},{5,21},{6,22},{7,23},{8,24},{9,... | collective-permute-start | bytes 491528 | tf_op jit(solution)/shard_map/ppermute | solution.py:391
  115.0 13.6 %collective-permute-start.14 = (f32[160,256]{1,0:T(8,128)S(1)}, f32[160,256]{1,0:T(8,128)S(1)}, u32[]{:S(2)}, u32[]{:S(2)}) collective-permute-start(f32[160,256]{1,0:T(8,128)S(1)} %shard_map.69.refs_6_.refs_0_), channel_id=1, source_target_pairs={{0,16},{1,17},{2,18},{3,19},{4,20},{5,21},{6,22},{7,23},{8,24},{9,... | collective-permute-start | bytes 491528 | tf_op jit(solution)/shard_map/ppermute | solution.py:391
  125.6 15.9 %collective-permute-start.18 = (f32[160,256]{1,0:T(8,128)S(1)}, f32[160,256]{1,0:T(8,128)S(1)}, u32[]{:S(2)}, u32[]{:S(2)}) collective-permute-start(f32[160,256]{1,0:T(8,128)S(1)} %get-tuple-element.57.refs_0_), channel_id=1, source_target_pairs={{0,16},{1,17},{2,18},{3,19},{4,20},{5,21},{6,22},{7,23},{8,24},{9,... | collective-permute-start | bytes 491528 | tf_op jit(solution)/shard_map/ppermute | solution.py:391
  125.7 15.8 %collective-permute-start.19 = (f32[128,256]{1,0:T(8,128)S(1)}, f32[128,256]{1,0:T(8,128)S(1)}, u32[]{:S(2)}, u32[]{:S(2)}) collective-permute-start(f32[128,256]{1,0:T(8,128)S(1)} %get-tuple-element.56.refs_2_), channel_id=1, source_target_pairs={{0,16},{1,17},{2,18},{3,19},{4,20},{5,21},{6,22},{7,23},{8,24},{9,... | collective-permute-start | bytes 393224 | tf_op jit(solution)/shard_map/ppermute | solution.py:391
  129.2 15.0 %collective-permute-start.17 = (f32[320,256]{1,0:T(8,128)S(1)}, f32[320,256]{1,0:T(8,128)S(1)}, u32[]{:S(2)}, u32[]{:S(2)}) collective-permute-start(f32[320,256]{1,0:T(8,128)S(1)} %shard_map.71.refs_4_.refs_0_), channel_id=1, source_target_pairs={{0,8},{1,9},{2,10},{3,11},{4,12},{5,13},{6,14},{7,15},{8,0},{9,1},... | collective-permute-start | bytes 983048 | tf_op jit(solution)/shard_map/ppermute | solution.py:391
  142.1 10.0 %collective-permute-start.22 = (f32[320,256]{1,0:T(8,128)S(1)}, f32[320,256]{1,0:T(8,128)S(1)}, u32[]{:S(2)}, u32[]{:S(2)}) collective-permute-start(f32[320,256]{1,0:T(8,128)S(1)} %get-tuple-element.59.refs_0_), channel_id=1, source_target_pairs={{0,4},{1,3},{2,6},{3,1},{4,0},{5,7},{6,2},{7,5},{8,12},{9,11},{10,... | collective-permute-start | bytes 983048 | tf_op jit(solution)/shard_map/ppermute | solution.py:391
  142.6 9.5 %collective-permute-start.23 = (f32[256,256]{1,0:T(8,128)S(1)}, f32[256,256]{1,0:T(8,128)S(1)}, u32[]{:S(2)}, u32[]{:S(2)}) collective-permute-start(f32[256,256]{1,0:T(8,128)S(1)} %get-tuple-element.58.refs_2_), channel_id=1, source_target_pairs={{0,4},{1,3},{2,6},{3,1},{4,0},{5,7},{6,2},{7,5},{8,12},{9,11},{10,... | collective-permute-start | bytes 786440 | tf_op jit(solution)/shard_map/ppermute | solution.py:391
  152.7 27.9 %collective-permute-start.24 = (f32[640,256]{1,0:T(8,128)S(1)}, f32[640,256]{1,0:T(8,128)S(1)}, u32[]{:S(2)}, u32[]{:S(2)}) collective-permute-start(f32[640,256]{1,0:T(8,128)S(1)} %get-tuple-element.60.refs_2_), channel_id=1, source_target_pairs={{0,8},{1,9},{2,10},{3,11},{4,12},{5,13},{6,14},{7,15},{8,0},{9,1},... | collective-permute-start | bytes 1966088 | tf_op jit(solution)/shard_map/ppermute | solution.py:391
  152.8 28.1 %collective-permute-start.20 = (f32[640,256]{1,0:T(8,128)S(1)}, f32[640,256]{1,0:T(8,128)S(1)}, u32[]{:S(2)}, u32[]{:S(2)}) collective-permute-start(f32[640,256]{1,0:T(8,128)S(1)} %shard_map.73.refs_4_.refs_0_), channel_id=1, source_target_pairs={{0,4},{1,3},{2,6},{3,1},{4,0},{5,7},{6,2},{7,5},{8,12},{9,11},{10,... | collective-permute-start | bytes 1966088 | tf_op jit(solution)/shard_map/ppermute | solution.py:391
  153.2 25.6 %collective-permute-start.30 = (f32[512,256]{1,0:T(8,128)S(1)}, f32[512,256]{1,0:T(8,128)S(1)}, u32[]{:S(2)}, u32[]{:S(2)}) collective-permute-start(f32[512,256]{1,0:T(8,128)S(1)} %get-tuple-element.61.refs_4_), channel_id=1, source_target_pairs={{0,8},{1,9},{2,10},{3,11},{4,12},{5,13},{6,14},{7,15},{8,0},{9,1},... | collective-permute-start | bytes 1572872 | tf_op jit(solution)/shard_map/ppermute | solution.py:391
  155.2 27.5 %collective-permute-start.26 = (f32[512,256]{1,0:T(8,128)S(1)}, f32[512,256]{1,0:T(8,128)S(1)}, u32[]{:S(2)}, u32[]{:S(2)}) collective-permute-start(f32[512,256]{1,0:T(8,128)S(1)} %get-tuple-element.61.refs_4_), channel_id=1, source_target_pairs={{0,2},{1,5},{2,0},{3,7},{4,6},{5,1},{6,4},{7,3},{8,10},{9,13},{10,... | collective-permute-start | bytes 1572872 | tf_op jit(solution)/shard_map/ppermute | solution.py:391
  157.2 30.9 %collective-permute-start.29 = (f32[640,256]{1,0:T(8,128)S(1)}, f32[640,256]{1,0:T(8,128)S(1)}, u32[]{:S(2)}, u32[]{:S(2)}) collective-permute-start(f32[640,256]{1,0:T(8,128)S(1)} %get-tuple-element.60.refs_2_), channel_id=1, source_target_pairs={{0,2},{1,5},{2,0},{3,7},{4,6},{5,1},{6,4},{7,3},{8,10},{9,13},{10,... | collective-permute-start | bytes 1966088 | tf_op jit(solution)/shard_map/ppermute | solution.py:391
  178.9 10.6 %collective-permute-start.28 = (f32[640,256]{1,0:T(8,128)S(1)}, f32[640,256]{1,0:T(8,128)S(1)}, u32[]{:S(2)}, u32[]{:S(2)}) collective-permute-start(f32[640,256]{1,0:T(8,128)S(1)} %shard_map.73.refs_4_.refs_0_), channel_id=1, source_target_pairs={{0,2},{1,5},{2,0},{3,7},{4,6},{5,1},{6,4},{7,3},{8,10},{9,13},{10,... | collective-permute-start | bytes 1966088 | tf_op jit(solution)/shard_map/ppermute | solution.py:391
  180.6 15.9 %collective-permute-start.25 = (f32[640,256]{1,0:T(8,128)S(1)}, f32[640,256]{1,0:T(8,128)S(1)}, u32[]{:S(2)}, u32[]{:S(2)}) collective-permute-start(f32[640,256]{1,0:T(8,128)S(1)} %collective-permute-done.24.refs_3_), channel_id=1, source_target_pairs={{0,2},{1,5},{2,0},{3,7},{4,6},{5,1},{6,4},{7,3},{8,10},{9,13},{10,... | collective-permute-start | bytes 1966088 | tf_op jit(solution)/shard_map/ppermute | solution.py:391
  180.9 22.6 %collective-permute-start.21 = (f32[640,256]{1,0:T(8,128)S(1)}, f32[640,256]{1,0:T(8,128)S(1)}, u32[]{:S(2)}, u32[]{:S(2)}) collective-permute-start(f32[640,256]{1,0:T(8,128)S(1)} %collective-permute-done.20.refs_1_), channel_id=1, source_target_pairs={{0,2},{1,5},{2,0},{3,7},{4,6},{5,1},{6,4},{7,3},{8,10},{9,13},{10,... | collective-permute-start | bytes 1966088 | tf_op jit(solution)/shard_map/ppermute | solution.py:391
  182.6 10.5 %collective-permute-start.27 = (f32[512,256]{1,0:T(8,128)S(1)}, f32[512,256]{1,0:T(8,128)S(1)}, u32[]{:S(2)}, u32[]{:S(2)}) collective-permute-start(f32[512,256]{1,0:T(8,128)S(1)} %collective-permute-done.26.refs_5_), channel_id=1, source_target_pairs={{0,8},{1,9},{2,10},{3,11},{4,12},{5,13},{6,14},{7,15},{8,0},{9,1},... | collective-permute-start | bytes 1572872 | tf_op jit(solution)/shard_map/ppermute | solution.py:391
  203.5 5.6 %copy-start.2 = (f32[512,256]{1,0:T(8,128)S(1)}, f32[512,256]{1,0:T(8,128)}, u32[]{:S(2)}) copy-start(f32[512,256]{1,0:T(8,128)} %copy-done.1) | copy-start | bytes 1572868
  206.8 2.4 %collective-permute-start.31 = (f32[768,256]{1,0:T(8,128)S(1)}, f32[768,256]{1,0:T(8,128)S(1)}, u32[]{:S(2)}, u32[]{:S(2)}) collective-permute-start(f32[768,256]{1,0:T(8,128)S(1)} %get-tuple-element.68.mine_ref), channel_id=1, source_target_pairs={{0,1},{1,0},{2,3},{3,2},{4,5},{5,4},{6,7},{7,6},{8,9},{9,8},{10,11... | collective-permute-start | bytes 2359304 | tf_op jit(solution)/shard_map/ppermute | solution.py:424

commit v7 on v4

--- a/solution.py
+++ b/solution.py
@@ -236,29 +236,55 @@
     return call(functools.partial(first_fold_kernel, at), [half, half], table, [mine, theirs, gram], [])
 
 
-def split_fold_kernel(at, table_ref, mine_ref, theirs_ref, give_ref, keep_ref, gram_ref):
-    rows = give_ref.shape[0]
+def mixed_fold_kernel(at, extra, table_ref, mine_ref, theirs_ref, give_ref, keep_ref):
+    whole = mine_ref.shape[0] - extra
+    rows = whole // 2
     keep = pl.ds(pl.multiple_of(table_ref[at] * rows, rows), rows)
     give = pl.ds(pl.multiple_of((1 - table_ref[at]) * rows, rows), rows)
-    give_ref[...] = mine_ref[give, :] + theirs_ref[give, :]
-    keep_ref[...] = mine_ref[keep, :] + theirs_ref[keep, :]
-    gram_ref[...] = mine_ref[2 * rows :, :] + theirs_ref[2 * rows :, :]
-
-
-def split_fold(table, at, extra, mine, theirs):
-    comp = mine.shape[1]
-    half = shape((mine.shape[0] - extra) // 2, comp)
-    return call(functools.partial(split_fold_kernel, at), [half, half, shape(extra, comp)], table, [mine, theirs], [])
-
-
-def rows_kernel(table_ref, inverse_ref, mine_ref, *refs):
+    gram = mine_ref[whole:, :] + theirs_ref[whole:, :]
+    give_ref[:rows, :] = mine_ref[give, :] + theirs_ref[give, :]
+    give_ref[rows:, :] = gram
+    keep_ref[:rows, :] = mine_ref[keep, :] + theirs_ref[keep, :]
+    keep_ref[rows:, :] = gram
+
+
+def mixed_fold(table, at, extra, mine, theirs):
+    half = shape((mine.shape[0] - extra) // 2 + extra, mine.shape[1])
+    return call(functools.partial(mixed_fold_kernel, at, extra), [half, half], table, [mine, theirs], [])
+
+
+def part_kernel(table_ref, mine_ref, theirs_ref, rows_ref, rest_ref):
+    rows = rows_ref.shape[0]
+    rows_ref[...] = mine_ref[:rows, :] + theirs_ref[:rows, :]
+    rest_ref[...] = mine_ref[rows:, :] + theirs_ref[rows:, :]
+
+
+def part(table, rows, mine, theirs):
+    shapes = [shape(rows, mine.shape[1]), shape(mine.shape[0] - rows, mine.shape[1])]
+    return call(part_kernel, shapes, table, [mine, theirs], [])
+
+
+def join_kernel(at, table_ref, mine_ref, theirs_ref, *refs):
+    rows = mine_ref.shape[0]
+    refs[-1][pl.ds(pl.multiple_of(table_ref[at] * rows, rows), rows), :] = mine_ref[...]
+    refs[-1][pl.ds(pl.multiple_of((1 - table_ref[at]) * rows, rows), rows), :] = theirs_ref[...]
+
+
+def join(table, at, mine, theirs, after):
+    return call(functools.partial(join_kernel, at), [shape(2 * mine.shape[0], mine.shape[1])], table, [mine, theirs], after)[0]
+
+
+def rows_kernel(theirs, table_ref, inverse_ref, mine_ref, *refs):
     inverse = inverse_ref[...]
-    cross = mine_ref[...] + refs[0][...]
+    cross = mine_ref[...]
+    if theirs:
+        cross = cross + refs[0][...]
     refs[-1][...] = dot(dot(cross, inverse, OVER_COLS, HIGHEST), inverse, precision=HIGHEST)
 
 
 def solve_sum(table, inverse, parts, after):
-    return call(rows_kernel, [shape(*parts[0].shape)], table, [inverse, *parts], after)[0]
+    kernel = functools.partial(rows_kernel, len(parts) > 1)
+    return call(kernel, [shape(*parts[0].shape)], table, [inverse, *parts], after)[0]
 
 
 def absorb_kernel(ats, fresh, table_ref, acts_ref, *refs):
@@ -392,15 +418,15 @@
         half = value.shape[0] // 2
         return lax.dynamic_slice_in_dim(value, which * half, half, 0)
 
-    def joined(one, other, which):
-        return jnp.where(which == 0, jnp.concatenate([one, other]), jnp.concatenate([other, one]))
-
-    gram = gram + swap(gram, "far")
     held = {}
     for name, order in ORDERS.items():
-        got = swap(give_1(name), order[0])
+        give = give_1(name)
+        if name == "A":
+            give = jnp.concatenate([give, gram])
+        got = swap(give, order[0])
         give = stage_2(name, got, False)
         if name == "A":
+            gram = gram + got[rows[name] // 2 :]
             give = jnp.concatenate([give, gram])
         held[name] = stage_2(name, got, True), swap(give, order[1])
     for name, (keep, arrived) in held.items():
@@ -414,22 +440,24 @@
     for name, (keep, arrived) in held.items():
         along = ORDERS[name][3]
         if name == "A":
-            give, keep, gram = split_fold(table, where[name, "d"], gram.shape[0], keep, arrived)
-            gram = gram + swap(gram, "first")
+            give, keep = mixed_fold(table, where[name, "d"], gram.shape[0], keep, arrived)
             held[name] = keep, swap(give, along)
         else:
             keep = keep + arrived
             held[name] = part_of(keep, bits[along]), swap(part_of(keep, 1 - bits[along]), along)
 
-    inverse = factor_inverse(table, gram, other_core(gram))
+    a_mine, gram = part(table, rows["A"] // 16, *held["A"])
+    inverse = factor_inverse(table, gram, other_core(gram), [held["N"][0], held["B"][0]])
+    held["A"] = (a_mine,)
     mine = {}
     for name in held:
         mine[name] = solve_sum(table, inverse, held[name], list(mine.values()))
 
-    for k in (3, 2):
-        for name in mine:
-            along = ORDERS[name][k]
-            mine[name] = joined(mine[name], swap(mine[name], along), bits[along])
+    for k, field in ((3, "d"), (2, "c")):
+        last = []
+        for name, order in ORDERS.items():
+            mine[name] = join(table, where[name, field], mine[name], swap(mine[name], order[k]), last)
+            last = [mine[name]]
     near, far, last = [], [], []
     for name in mine:
         theirs = swap(mine[name], ORDERS[name][1])
@@ -437,7 +465,7 @@
         far += [(swap(mine[name], ORDERS[name][0]), where[name, "far_mine"])]
         last += [(swap(theirs, ORDERS[name][0]), where[name, "far_theirs"])]
     state = None
-    for blocks in (near, far, last):
+    for blocks in (near, far, last[2:], last[:2]):
         state = absorb(table, state, acts, blocks)
     sums, dict_out = state
     return second_update(codes_mid, sums, other_core(sums)), dict_out

time: 197 us -> 208 us (1.056)
  waiting for transfers between devices: 91.4 us -> 107 us
  starting transfers between devices: 43.7 us -> 33.9 us
  Pallas kernels: 39.9 us -> 45.8 us
  matrix products: 19.6 us -> 17.3 us
    ppermute x29 -> x27, waiting for transfers between devices: 87.9 us -> 102 us  [swap(): return lax.ppermute(value, BOTH, flips(ALONG[along]))]
    ppermute x29 -> x27, starting transfers between devices: 43.1 us -> 33.2 us  [swap(): return lax.ppermute(value, BOTH, flips(ALONG[along]))]
    pallas_call x5 -> x12, Pallas kernels: 5.29 us -> 9.32 us  [call(): pl.pallas_call(kernel, out_shape=out_shapes, in_specs=[SCALARS] + [WHOLE]...]
    dot_general x9, matrix products: 19.6 us -> 17.3 us  [dot(): lax.dot_general(left, right, dims, precision=precision, preferred_element...]
    pallas_call x3 -> x4, Pallas kernels: 12.7 us -> 14.5 us  [absorb(): pl.pallas_call(functools.partial(absorb_kernel, [at for _, at in blocks],...]
  transfers between devices with their start and end apart: 32 -> 30, of which waited for: 17 -> 14; matrix products, arithmetic and copies ran while one was open for 10% -> 8% of each run, Pallas kernels for 12% -> 14%
where the time goes in v7:
time: 208 us
  waiting for transfers between devices  107 us (51%)
  Pallas kernels  45.8 us (22%)
  starting transfers between devices  33.9 us (16%)
  matrix products  17.3 us (8%)
  other arithmetic  2.19 us (1%)
    ppermute x27, waiting for transfers between devices, swap(): return lax.ppermute(value, BOTH, flips(ALONG[along]))  102 us
    ppermute x27, starting transfers between devices, swap(): return lax.ppermute(value, BOTH, flips(ALONG[along]))  33.2 us
    dot_general x9, matrix products, dot(): lax.dot_general(left, right, dims, precision=precision, preferred_element...  17.3 us
    pallas_call x4, Pallas kernels, absorb(): pl.pallas_call(functools.partial(absorb_kernel, [at for _, at in blocks],...  14.5 us
    pallas_call x1, Pallas kernels, project(): pl.pallas_call(project_kernel, out_shape=jax.ShapeDtypeStruct((tokens + c...  9.55 us
    pallas_call x12, Pallas kernels, call(): pl.pallas_call(kernel, out_shape=out_shapes, in_specs=[SCALARS] + [WHOLE]...  9.32 us
    pallas_call x1, Pallas kernels, factor_inverse(): pl.pallas_call(halves_kernel, out_shape=jax.ShapeDtypeStruct((comp, comp)...  8.43 us
    ppermute x3, waiting for transfers between devices, other_core(): return lax.ppermute(value, 'hid', [(0, 1), (1, 0)])  4.65 us
  transfers between devices with their start and end apart: 30, of which 14 were waited for; matrix products, arithmetic and copies ran while one was open for 8% of the time, Pallas kernels for 14%

profile of v7, /device:TPU:0, one launch (start us, length us, event | category | flops | bytes accessed | tf_op | source)
XLA Modules:
  0.0 207.8 jit_solution(13801386815366983882)
XLA Ops:
  0.6 9.6 %shard_map.59.mine_ref = f32[768,256]{1,0:T(8,128)S(1)} custom-call(bf16[512,7168]{1,0:T(8,128)(2,1)} %acts_ref.9, f32[7168,256]{1,0:T(8,128)} %dict_ref.1), custom_call_target="tpu_custom_call" | custom-call | flops 3758096384 | bytes 14680064 | tf_op jit(solution)/shard_map/pallas_call | solution.py:58
  10.2 0.5 collective-permute-start
  10.7 0.7 fusion.23.core_ref.table_ref
  11.4 1.2 collective-permute-done.theirs_ref
  12.6 2.0 shard_map.60
  14.6 1.7 fusion.6
  16.3 1.1 pad_maximum_fusion
  17.5 2.9 %collective-permute-start.1 = (f32[1152,256]{1,0:T(8,128)}, f32[1152,256]{1,0:T(8,128)}, u32[]{:S(2)}, u32[]{:S(2)}) collective-permute-start(f32[1152,256]{1,0:T(8,128)} %pad_maximum_fusion), channel_id=1, source_target_pairs={{0,2},{1,5},{2,0},{3,7},{4,6},{5,1},{6,4},{7,3},{8,10},{9,13},{10,... | collective-permute-start | bytes 3538952 | tf_op jit(solution)/shard_map/ppermute | solution.py:356
  20.3 2.9 %fusion.2 = f32[1280,256]{1,0:T(8,128)} fusion(bf16[512,256]{1,0:T(8,128)(2,1)S(1)} %get-tuple-element.20, bf16[512,7168]{1,0:T(8,128)(2,1)} %acts_ref.9, s32[]{:T(128)S(6)} %select_n.99), kind=kOutput, calls=%fused_computation.2 | convolution fusion | flops 335544320 | bytes 2883588 | tf_op jit(solution)/shard_map/dot_general | solution.py:21
  23.2 1.6 collective-permute-start.6
  24.8 1.9 fusion
  26.7 0.6 collective-permute-start.9
  27.3 7.5 %collective-permute-done.1 = f32[1152,256]{1,0:T(8,128)} collective-permute-done((f32[1152,256]{1,0:T(8,128)}, f32[1152,256]{1,0:T(8,128)}, u32[]{:S(2)}, u32[]{:S(2)}) %collective-permute-start.1) | collective-permute-done | bytes 1179680 | tf_op jit(solution)/shard_map/ppermute | solution.py:356
  34.8 0.9 slice_add_fusion.gram_ref
  35.7 1.5 convolution_add_fusion.4
  37.3 2.1 %collective-permute-start.2 = (f32[640,256]{1,0:T(8,128)S(1)}, f32[640,256]{1,0:T(8,128)S(1)}, u32[]{:S(2)}, u32[]{:S(2)}) collective-permute-start(f32[640,256]{1,0:T(8,128)S(1)} %pad_maximum_fusion.1), channel_id=1, source_target_pairs={{0,4},{1,3},{2,6},{3,1},{4,0},{5,7},{6,2},{7,5},{8,12},{9,11},{10,... | collective-permute-start | bytes 1966088 | tf_op jit(solution)/shard_map/ppermute | solution.py:356
  39.5 14.7 %collective-permute-done.6 = f32[1280,256]{1,0:T(8,128)} collective-permute-done((f32[1280,256]{1,0:T(8,128)}, f32[1280,256]{1,0:T(8,128)}, u32[]{:S(2)}, u32[]{:S(2)}) %collective-permute-start.6) | collective-permute-done | bytes 1310752 | tf_op jit(solution)/shard_map/ppermute | solution.py:356
  54.1 2.5 %convolution_add_fusion.2 = f32[640,256]{1,0:T(8,128)} fusion(bf16[512,256]{1,0:T(8,128)(2,1)S(1)} %get-tuple-element.20, f32[1280,256]{1,0:T(8,128)} %collective-permute-done.6, s32[]{:T(128)S(6)} %select_n.102, bf16[512,7168]{1,0:T(8,128)(2,1)} %acts_ref.9, s32[]{:T(128)S(6)} %select_n.101), kind=kOutput, calls=%fused_computation.6 | convolution fusion | flops 167936000 | bytes 2228232 | tf_op jit(solution)/shard_map/dot_general | solution.py:21
  56.6 0.9 collective-permute-start.7
  57.5 1.7 convolution_add_fusion
  59.2 2.3 %collective-permute-start.10 = (f32[640,256]{1,0:T(8,128)S(1)}, f32[640,256]{1,0:T(8,128)S(1)}, u32[]{:S(2)}, u32[]{:S(2)}) collective-permute-start(f32[640,256]{1,0:T(8,128)S(1)} %convolution_add_fusion), channel_id=1, source_target_pairs={{0,8},{1,9},{2,10},{3,11},{4,12},{5,13},{6,14},{7,15},{8,0},{9,1},... | collective-permute-start | bytes 1966088 | tf_op jit(solution)/shard_map/ppermute | solution.py:356
  61.4 1.5 convolution_add_fusion.5.mine_ref
  63.0 0.6 shard_map.61
  63.8 3.7 %collective-permute-done.7 = f32[640,256]{1,0:T(8,128)} collective-permute-done((f32[640,256]{1,0:T(8,128)}, f32[640,256]{1,0:T(8,128)}, u32[]{:S(2)}, u32[]{:S(2)}) %collective-permute-start.7) | collective-permute-done | bytes 655392 | tf_op jit(solution)/shard_map/ppermute | solution.py:356
  67.5 1.9 fusion.4
  69.9 7.2 %collective-permute-done.10 = f32[640,256]{1,0:T(8,128)S(1)} collective-permute-done((f32[640,256]{1,0:T(8,128)S(1)}, f32[640,256]{1,0:T(8,128)S(1)}, u32[]{:S(2)}, u32[]{:S(2)}) %collective-permute-start.10) | collective-permute-done | bytes 655392 | tf_op jit(solution)/shard_map/ppermute | solution.py:356
  77.1 1.7 fusion.5
  78.8 1.0 collective-permute-start.11
  79.8 2.6 %collective-permute-done.3.theirs_ref = f32[384,256]{1,0:T(8,128)S(1)} collective-permute-done((f32[384,256]{1,0:T(8,128)S(1)}, f32[384,256]{1,0:T(8,128)S(1)}, u32[]{:S(2)}, u32[]{:S(2)}) %collective-permute-start.3) | collective-permute-done | bytes 393248 | tf_op jit(solution)/shard_map/ppermute | solution.py:356
  82.5 0.6 shard_map.62
  83.1 2.8 %collective-permute-start.4 = (f32[256,256]{1,0:T(8,128)S(1)}, f32[256,256]{1,0:T(8,128)S(1)}, u32[]{:S(2)}, u32[]{:S(2)}) collective-permute-start(f32[256,256]{1,0:T(8,128)S(1)} %get-tuple-element.25), channel_id=1, source_target_pairs={{0,16},{1,17},{2,18},{3,19},{4,20},{5,21},{6,22},{7,23},{8,24},{9,... | collective-permute-start | bytes 786440 | tf_op jit(solution)/shard_map/ppermute | solution.py:356
  86.2 13.2 %collective-permute-done.4.theirs_ref = f32[256,256]{1,0:T(8,128)S(1)} collective-permute-done((f32[256,256]{1,0:T(8,128)S(1)}, f32[256,256]{1,0:T(8,128)S(1)}, u32[]{:S(2)}, u32[]{:S(2)}) %collective-permute-start.4) | collective-permute-done | bytes 262176 | tf_op jit(solution)/shard_map/ppermute | solution.py:356
  99.4 0.6 shard_map.63
  100.2 1.2 collective-permute-done.5.theirs_ref
  101.4 8.4 %shard_map.64.inverse_ref = f32[256,256]{1,0:T(8,128)S(1)} custom-call(s32[19]{0:T(128)S(1)} %fusion.23.core_ref.table_ref, f32[128,256]{1,0:T(8,128)S(1)} %get-tuple-element.26.mine_ref, f32[128,256]{1,0:T(8,128)S(1)} %collective-permute-done.5.theirs_ref, f32[160,256]{1,0:T(8,128)S(1)} %get-tuple-element.37.refs_0_.mine_ref, ...), custom_call_target="tpu_custom_call" | custom-call | flops 10000000000 | bytes 524288 | tf_op jit(solution)/shard_map/pallas_call | solution.py:123
  109.8 1.3 shard_map.65.mine_ref.refs_1_
  111.2 1.4 shard_map.68.mine_ref.refs_2_
  112.6 1.8 collective-permute-start.17
  114.4 1.4 shard_map.71.mine_ref
  115.8 1.2 collective-permute-start.22
  117.0 1.8 collective-permute-start.12
  118.8 17.2 %collective-permute-done.12.theirs_ref = f32[128,256]{1,0:T(8,128)S(1)} collective-permute-done((f32[128,256]{1,0:T(8,128)S(1)}, f32[128,256]{1,0:T(8,128)S(1)}, u32[]{:S(2)}, u32[]{:S(2)}) %collective-permute-start.12) | collective-permute-done | bytes 131104 | tf_op jit(solution)/shard_map/ppermute | solution.py:356
  135.9 0.6 shard_map.66.mine_ref.refs_0_
  136.5 0.6 shard_map.69.mine_ref.refs_0_
  137.1 2.8 %collective-permute-start.18 = (f32[320,256]{1,0:T(8,128)S(1)}, f32[320,256]{1,0:T(8,128)S(1)}, u32[]{:S(2)}, u32[]{:S(2)}) collective-permute-start(f32[320,256]{1,0:T(8,128)S(1)} %shard_map.69.mine_ref.refs_0_), channel_id=1, source_target_pairs={{0,4},{1,3},{2,6},{3,1},{4,0},{5,7},{6,2},{7,5},{8,12},{9,11},{10,... | collective-permute-start | bytes 983048 | tf_op jit(solution)/shard_map/ppermute | solution.py:356
  139.9 0.6 shard_map.72.mine_ref
  140.6 8.6 %collective-permute-done.13.theirs_ref = f32[256,256]{1,0:T(8,128)S(1)} collective-permute-done((f32[256,256]{1,0:T(8,128)S(1)}, f32[256,256]{1,0:T(8,128)S(1)}, u32[]{:S(2)}, u32[]{:S(2)}) %collective-permute-start.13) | collective-permute-done | bytes 262176 | tf_op jit(solution)/shard_map/ppermute | solution.py:356
  149.3 0.6 shard_map.67.refs_0_
  149.8 0.6 shard_map.70.refs_0_.refs_2_
  150.5 0.6 shard_map.73.refs_4_
  151.1 2.3 %collective-permute-start.24 = (f32[640,256]{1,0:T(8,128)S(1)}, f32[640,256]{1,0:T(8,128)S(1)}, u32[]{:S(2)}, u32[]{:S(2)}) collective-permute-start(f32[640,256]{1,0:T(8,128)S(1)} %shard_map.73.refs_4_), channel_id=1, source_target_pairs={{0,2},{1,5},{2,0},{3,7},{4,6},{5,1},{6,4},{7,3},{8,10},{9,13},{10,... | collective-permute-start | bytes 1966088 | tf_op jit(solution)/shard_map/ppermute | solution.py:356
  153.5 2.5 %collective-permute-start.14 = (f32[512,256]{1,0:T(8,128)S(1)}, f32[512,256]{1,0:T(8,128)S(1)}, u32[]{:S(2)}, u32[]{:S(2)}) collective-permute-start(f32[512,256]{1,0:T(8,128)S(1)} %shard_map.67.refs_0_), channel_id=1, source_target_pairs={{0,4},{1,3},{2,6},{3,1},{4,0},{5,7},{6,2},{7,5},{8,12},{9,11},{10,... | collective-permute-start | bytes 1572872 | tf_op jit(solution)/shard_map/ppermute | solution.py:356
  156.0 1.7 collective-permute-start.28
  157.7 15.4 %collective-permute-done.26.refs_0_ = f32[512,256]{1,0:T(8,128)S(1)} collective-permute-done((f32[512,256]{1,0:T(8,128)S(1)}, f32[512,256]{1,0:T(8,128)S(1)}, u32[]{:S(2)}, u32[]{:S(2)}) %collective-permute-start.26) | collective-permute-done | bytes 524320 | tf_op jit(solution)/shard_map/ppermute | solution.py:356
  173.1 1.4 collective-permute-start.27
  175.3 1.7 collective-permute-start.15
  176.9 5.4 %shard_map.74 = (f32[768,256]{1,0:T(8,128)S(1)}, f32[7168,256]{1,0:T(8,128)}) custom-call(s32[19]{0:T(128)S(1)} %fusion.23.core_ref.table_ref, bf16[512,7168]{1,0:T(8,128)(2,1)} %acts_ref.9, f32[512,256]{1,0:T(8,128)S(1)} %shard_map.67.refs_0_, f32[512,256]{1,0:T(8,128)S(1)} %collective-permute-done.14.refs_1_, f32[640,256]{1,0:T(8,128)S(1)} %shard_map.70.refs_0_.refs_2_, ...), custom_call_target="tpu_custom_call" | custom-call | flops 1409286144 | bytes 11010048 | tf_op jit(solution)/shard_map/pallas_call | solution.py:325
  182.3 2.7 %collective-permute-done.28.refs_2_ = f32[640,256]{1,0:T(8,128)S(1)} collective-permute-done((f32[640,256]{1,0:T(8,128)S(1)}, f32[640,256]{1,0:T(8,128)S(1)}, u32[]{:S(2)}, u32[]{:S(2)}) %collective-permute-start.28) | collective-permute-done | bytes 655392 | tf_op jit(solution)/shard_map/ppermute | solution.py:356
  185.0 3.7 %shard_map.75 = (f32[768,256]{1,0:T(8,128)S(1)}, f32[7168,256]{1,0:T(8,128)}) custom-call(s32[19]{0:T(128)S(1)} %fusion.23.core_ref.table_ref, bf16[512,7168]{1,0:T(8,128)(2,1)} %acts_ref.9, f32[512,256]{1,0:T(8,128)S(1)} %collective-permute-done.26.refs_0_, ...), custom_call_target="tpu_custom_call", output_to_operand_aliasing={{0}: (5, {}), {1}: (6, {})} | custom-call | flops 704643072 | bytes 5505024 | tf_op jit(solution)/shard_map/pallas_call | solution.py:325
  188.7 9.2 %collective-permute-done.25.refs_0_ = f32[640,256]{1,0:T(8,128)S(1)} collective-permute-done((f32[640,256]{1,0:T(8,128)S(1)}, f32[640,256]{1,0:T(8,128)S(1)}, u32[]{:S(2)}, u32[]{:S(2)}) %collective-permute-start.25) | collective-permute-done | bytes 655392 | tf_op jit(solution)/shard_map/ppermute | solution.py:356
  197.9 2.4 %shard_map.76 = (f32[768,256]{1,0:T(8,128)S(1)}, f32[7168,256]{1,0:T(8,128)}) custom-call(s32[19]{0:T(128)S(1)} %fusion.23.core_ref.table_ref, bf16[512,7168]{1,0:T(8,128)(2,1)} %acts_ref.9, f32[640,256]{1,0:T(8,128)S(1)} %collective-permute-done.25.refs_0_, f32[768,256]{1,0:T(8,128)S(1)} %get-tuple-element.30.refs_1_, ...), custom_call_target="tpu_custom_call", output_to_operand_aliasing={{0}: (3, {}), {1}: (4, {})} | custom-call | flops 251658240 | bytes 1966080 | tf_op jit(solution)/shard_map/pallas_call | solution.py:325
  200.3 3.2 %shard_map.77 = (f32[768,256]{1,0:T(8,128)S(1)}, f32[7168,256]{1,0:T(8,128)}) custom-call(s32[19]{0:T(128)S(1)} %fusion.23.core_ref.table_ref, bf16[512,7168]{1,0:T(8,128)(2,1)} %acts_ref.9, f32[512,256]{1,0:T(8,128)S(1)} %collective-permute-done.15.refs_0_, ...), custom_call_target="tpu_custom_call", output_to_operand_aliasing={{0}: (4, {}), {1}: (5, {})} | custom-call | flops 452984832 | bytes 3538944 | tf_op jit(solution)/shard_map/pallas_call | solution.py:325
  203.5 2.3 %collective-permute-done.29.theirs_ref = f32[768,256]{1,0:T(8,128)S(1)} collective-permute-done((f32[768,256]{1,0:T(8,128)S(1)}, f32[768,256]{1,0:T(8,128)S(1)}, u32[]{:S(2)}, u32[]{:S(2)}) %collective-permute-start.29) | collective-permute-done | bytes 786464 | tf_op jit(solution)/shard_map/ppermute | solution.py:389
  205.8 2.0 shard_map.78
  (37 shorter events, 2.3 us)
Async XLA Ops:
  0.6 12.0 %copy-start = (f32[512,256]{1,0:T(8,128)S(1)}, f32[512,256]{1,0:T(8,128)}, u32[]{:S(2)}) copy-start(f32[512,256]{1,0:T(8,128)} %codes_ref.1) | copy-start | bytes 1572868
  10.2 2.4 %collective-permute-start = (f32[768,256]{1,0:T(8,128)S(1)}, f32[768,256]{1,0:T(8,128)S(1)}, u32[]{:S(2)}, u32[]{:S(2)}) collective-permute-start(f32[768,256]{1,0:T(8,128)S(1)} %shard_map.59.mine_ref), channel_id=1, source_target_pairs={{0,1},{1,0},{2,3},{3,2},{4,5},{5,4},{6,7},{7,6},{8,9},{9,8},{10,11... | collective-permute-start | bytes 2359304 | tf_op jit(solution)/shard_map/ppermute | solution.py:389
  17.5 17.4 %collective-permute-start.1 = (f32[1152,256]{1,0:T(8,128)}, f32[1152,256]{1,0:T(8,128)}, u32[]{:S(2)}, u32[]{:S(2)}) collective-permute-start(f32[1152,256]{1,0:T(8,128)} %pad_maximum_fusion), channel_id=1, source_target_pairs={{0,2},{1,5},{2,0},{3,7},{4,6},{5,1},{6,4},{7,3},{8,10},{9,13},{10,... | collective-permute-start | bytes 3538952 | tf_op jit(solution)/shard_map/ppermute | solution.py:356
  23.2 30.9 %collective-permute-start.6 = (f32[1280,256]{1,0:T(8,128)}, f32[1280,256]{1,0:T(8,128)}, u32[]{:S(2)}, u32[]{:S(2)}) collective-permute-start(f32[1280,256]{1,0:T(8,128)} %fusion.2), channel_id=1, source_target_pairs={{0,8},{1,9},{2,10},{3,11},{4,12},{5,13},{6,14},{7,15},{8,0},{9,1},... | collective-permute-start | bytes 3932168 | tf_op jit(solution)/shard_map/ppermute | solution.py:356
  26.7 30.8 %collective-permute-start.9 = (f32[1280,256]{1,0:T(8,128)S(1)}, f32[1280,256]{1,0:T(8,128)}, u32[]{:S(2)}, u32[]{:S(2)}) collective-permute-start(f32[1280,256]{1,0:T(8,128)S(1)} %fusion), channel_id=1, source_target_pairs={{0,2},{1,5},{2,0},{3,7},{4,6},{5,1},{6,4},{7,3},{8,10},{9,13},{10,... | collective-permute-start | bytes 3932168 | tf_op jit(solution)/shard_map/ppermute | solution.py:356
  37.3 25.6 %collective-permute-start.2 = (f32[640,256]{1,0:T(8,128)S(1)}, f32[640,256]{1,0:T(8,128)S(1)}, u32[]{:S(2)}, u32[]{:S(2)}) collective-permute-start(f32[640,256]{1,0:T(8,128)S(1)} %pad_maximum_fusion.1), channel_id=1, source_target_pairs={{0,4},{1,3},{2,6},{3,1},{4,0},{5,7},{6,2},{7,5},{8,12},{9,11},{10,... | collective-permute-start | bytes 1966088 | tf_op jit(solution)/shard_map/ppermute | solution.py:356
  56.6 10.9 %collective-permute-start.7 = (f32[640,256]{1,0:T(8,128)}, f32[640,256]{1,0:T(8,128)}, u32[]{:S(2)}, u32[]{:S(2)}) collective-permute-start(f32[640,256]{1,0:T(8,128)} %convolution_add_fusion.2), channel_id=1, source_target_pairs={{0,2},{1,5},{2,0},{3,7},{4,6},{5,1},{6,4},{7,3},{8,10},{9,13},{10,... | collective-permute-start | bytes 1966088 | tf_op jit(solution)/shard_map/ppermute | solution.py:356
  59.2 17.9 %collective-permute-start.10 = (f32[640,256]{1,0:T(8,128)S(1)}, f32[640,256]{1,0:T(8,128)S(1)}, u32[]{:S(2)}, u32[]{:S(2)}) collective-permute-start(f32[640,256]{1,0:T(8,128)S(1)} %convolution_add_fusion), channel_id=1, source_target_pairs={{0,8},{1,9},{2,10},{3,11},{4,12},{5,13},{6,14},{7,15},{8,0},{9,1},... | collective-permute-start | bytes 1966088 | tf_op jit(solution)/shard_map/ppermute | solution.py:356
  63.6 18.8 %collective-permute-start.3 = (f32[384,256]{1,0:T(8,128)S(1)}, f32[384,256]{1,0:T(8,128)S(1)}, u32[]{:S(2)}, u32[]{:S(2)}) collective-permute-start(f32[384,256]{1,0:T(8,128)S(1)} %get-tuple-element.23), channel_id=1, source_target_pairs={{0,8},{1,9},{2,10},{3,11},{4,12},{5,13},{6,14},{7,15},{8,0},{9,1},... | collective-permute-start | bytes 1179656 | tf_op jit(solution)/shard_map/ppermute | solution.py:356
  69.4 16.5 %collective-permute-start.8 = (f32[320,256]{1,0:T(8,128)S(1)}, f32[320,256]{1,0:T(8,128)S(1)}, u32[]{:S(2)}, u32[]{:S(2)}) collective-permute-start(f32[320,256]{1,0:T(8,128)S(1)} %constant_dynamic-slice_fusion.3), channel_id=1, source_target_pairs={{0,4},{1,3},{2,6},{3,1},{4,0},{5,7},{6,2},{7,5},{8,12},{9,11},{10,... | collective-permute-start | bytes 983048 | tf_op jit(solution)/shard_map/ppermute | solution.py:356
  78.8 21.2 %collective-permute-start.11 = (f32[320,256]{1,0:T(8,128)S(1)}, f32[320,256]{1,0:T(8,128)S(1)}, u32[]{:S(2)}, u32[]{:S(2)}) collective-permute-start(f32[320,256]{1,0:T(8,128)S(1)} %constant_dynamic-slice_fusion.5), channel_id=1, source_target_pairs={{0,4},{1,3},{2,6},{3,1},{4,0},{5,7},{6,2},{7,5},{8,12},{9,11},{10,... | collective-permute-start | bytes 983048 | tf_op jit(solution)/shard_map/ppermute | solution.py:356
  83.1 16.3 %collective-permute-start.4 = (f32[256,256]{1,0:T(8,128)S(1)}, f32[256,256]{1,0:T(8,128)S(1)}, u32[]{:S(2)}, u32[]{:S(2)}) collective-permute-start(f32[256,256]{1,0:T(8,128)S(1)} %get-tuple-element.25), channel_id=1, source_target_pairs={{0,16},{1,17},{2,18},{3,19},{4,20},{5,21},{6,22},{7,23},{8,24},{9,... | collective-permute-start | bytes 786440 | tf_op jit(solution)/shard_map/ppermute | solution.py:356
  86.0 28.4 %collective-permute-start.21 = (f32[160,256]{1,0:T(8,128)S(1)}, f32[160,256]{1,0:T(8,128)S(1)}, u32[]{:S(2)}, u32[]{:S(2)}) collective-permute-start(f32[160,256]{1,0:T(8,128)S(1)} %get-tuple-element.36), channel_id=1, source_target_pairs={{0,16},{1,17},{2,18},{3,19},{4,20},{5,21},{6,22},{7,23},{8,24},{9,... | collective-permute-start | bytes 491528 | tf_op jit(solution)/shard_map/ppermute | solution.py:356
  100.0 1.4 collective-permute-start.5
  100.2 11.0 %collective-permute-start.16 = (f32[160,256]{1,0:T(8,128)S(1)}, f32[160,256]{1,0:T(8,128)S(1)}, u32[]{:S(2)}, u32[]{:S(2)}) collective-permute-start(f32[160,256]{1,0:T(8,128)S(1)} %get-tuple-element.38), channel_id=1, source_target_pairs={{0,16},{1,17},{2,18},{3,19},{4,20},{5,21},{6,22},{7,23},{8,24},{9,... | collective-permute-start | bytes 491528 | tf_op jit(solution)/shard_map/ppermute | solution.py:356
  112.6 23.9 %collective-permute-start.17 = (f32[160,256]{1,0:T(8,128)S(1)}, f32[160,256]{1,0:T(8,128)S(1)}, u32[]{:S(2)}, u32[]{:S(2)}) collective-permute-start(f32[160,256]{1,0:T(8,128)S(1)} %shard_map.68.mine_ref.refs_2_), channel_id=1, source_target_pairs={{0,16},{1,17},{2,18},{3,19},{4,20},{5,21},{6,22},{7,23},{8,24},{9,... | collective-permute-start | bytes 491528 | tf_op jit(solution)/shard_map/ppermute | solution.py:356
  115.8 24.1 %collective-permute-start.22 = (f32[160,256]{1,0:T(8,128)S(1)}, f32[160,256]{1,0:T(8,128)S(1)}, u32[]{:S(2)}, u32[]{:S(2)}) collective-permute-start(f32[160,256]{1,0:T(8,128)S(1)} %shard_map.71.mine_ref), channel_id=1, source_target_pairs={{0,16},{1,17},{2,18},{3,19},{4,20},{5,21},{6,22},{7,23},{8,24},{9,... | collective-permute-start | bytes 491528 | tf_op jit(solution)/shard_map/ppermute | solution.py:356
  117.0 18.9 %collective-permute-start.12 = (f32[128,256]{1,0:T(8,128)S(1)}, f32[128,256]{1,0:T(8,128)S(1)}, u32[]{:S(2)}, u32[]{:S(2)}) collective-permute-start(f32[128,256]{1,0:T(8,128)S(1)} %shard_map.65.mine_ref.refs_1_), channel_id=1, source_target_pairs={{0,16},{1,17},{2,18},{3,19},{4,20},{5,21},{6,22},{7,23},{8,24},{9,... | collective-permute-start | bytes 393224 | tf_op jit(solution)/shard_map/ppermute | solution.py:356
  137.1 12.8 %collective-permute-start.18 = (f32[320,256]{1,0:T(8,128)S(1)}, f32[320,256]{1,0:T(8,128)S(1)}, u32[]{:S(2)}, u32[]{:S(2)}) collective-permute-start(f32[320,256]{1,0:T(8,128)S(1)} %shard_map.69.mine_ref.refs_0_), channel_id=1, source_target_pairs={{0,4},{1,3},{2,6},{3,1},{4,0},{5,7},{6,2},{7,5},{8,12},{9,11},{10,... | collective-permute-start | bytes 983048 | tf_op jit(solution)/shard_map/ppermute | solution.py:356
  140.5 10.0 %collective-permute-start.23 = (f32[320,256]{1,0:T(8,128)S(1)}, f32[320,256]{1,0:T(8,128)S(1)}, u32[]{:S(2)}, u32[]{:S(2)}) collective-permute-start(f32[320,256]{1,0:T(8,128)S(1)} %shard_map.72.mine_ref), channel_id=1, source_target_pairs={{0,4},{1,3},{2,6},{3,1},{4,0},{5,7},{6,2},{7,5},{8,12},{9,11},{10,... | collective-permute-start | bytes 983048 | tf_op jit(solution)/shard_map/ppermute | solution.py:356
  140.5 8.7 %collective-permute-start.13 = (f32[256,256]{1,0:T(8,128)S(1)}, f32[256,256]{1,0:T(8,128)S(1)}, u32[]{:S(2)}, u32[]{:S(2)}) collective-permute-start(f32[256,256]{1,0:T(8,128)S(1)} %shard_map.66.mine_ref.refs_0_), channel_id=1, source_target_pairs={{0,8},{1,9},{2,10},{3,11},{4,12},{5,13},{6,14},{7,15},{8,0},{9,1},... | collective-permute-start | bytes 786440 | tf_op jit(solution)/shard_map/ppermute | solution.py:356
  151.1 23.5 %collective-permute-start.24 = (f32[640,256]{1,0:T(8,128)S(1)}, f32[640,256]{1,0:T(8,128)S(1)}, u32[]{:S(2)}, u32[]{:S(2)}) collective-permute-start(f32[640,256]{1,0:T(8,128)S(1)} %shard_map.73.refs_4_), channel_id=1, source_target_pairs={{0,2},{1,5},{2,0},{3,7},{4,6},{5,1},{6,4},{7,3},{8,10},{9,13},{10,... | collective-permute-start | bytes 1966088 | tf_op jit(solution)/shard_map/ppermute | solution.py:356
  153.4 21.6 %collective-permute-start.19 = (f32[640,256]{1,0:T(8,128)S(1)}, f32[640,256]{1,0:T(8,128)S(1)}, u32[]{:S(2)}, u32[]{:S(2)}) collective-permute-start(f32[640,256]{1,0:T(8,128)S(1)} %shard_map.70.refs_0_.refs_2_), channel_id=1, source_target_pairs={{0,8},{1,9},{2,10},{3,11},{4,12},{5,13},{6,14},{7,15},{8,0},{9,1},... | collective-permute-start | bytes 1966088 | tf_op jit(solution)/shard_map/ppermute | solution.py:356
  153.4 19.8 %collective-permute-start.26 = (f32[512,256]{1,0:T(8,128)S(1)}, f32[512,256]{1,0:T(8,128)S(1)}, u32[]{:S(2)}, u32[]{:S(2)}) collective-permute-start(f32[512,256]{1,0:T(8,128)S(1)} %shard_map.67.refs_0_), channel_id=1, source_target_pairs={{0,2},{1,5},{2,0},{3,7},{4,6},{5,1},{6,4},{7,3},{8,10},{9,13},{10,... | collective-permute-start | bytes 1572872 | tf_op jit(solution)/shard_map/ppermute | solution.py:356
  153.5 21.8 %collective-permute-start.14 = (f32[512,256]{1,0:T(8,128)S(1)}, f32[512,256]{1,0:T(8,128)S(1)}, u32[]{:S(2)}, u32[]{:S(2)}) collective-permute-start(f32[512,256]{1,0:T(8,128)S(1)} %shard_map.67.refs_0_), channel_id=1, source_target_pairs={{0,4},{1,3},{2,6},{3,1},{4,0},{5,7},{6,2},{7,5},{8,12},{9,11},{10,... | collective-permute-start | bytes 1572872 | tf_op jit(solution)/shard_map/ppermute | solution.py:356
  156.0 29.0 %collective-permute-start.28 = (f32[640,256]{1,0:T(8,128)S(1)}, f32[640,256]{1,0:T(8,128)S(1)}, u32[]{:S(2)}, u32[]{:S(2)}) collective-permute-start(f32[640,256]{1,0:T(8,128)S(1)} %shard_map.73.refs_4_), channel_id=1, source_target_pairs={{0,8},{1,9},{2,10},{3,11},{4,12},{5,13},{6,14},{7,15},{8,0},{9,1},... | collective-permute-start | bytes 1966088 | tf_op jit(solution)/shard_map/ppermute | solution.py:356
  173.1 11.9 %collective-permute-start.27 = (f32[640,256]{1,0:T(8,128)S(1)}, f32[640,256]{1,0:T(8,128)S(1)}, u32[]{:S(2)}, u32[]{:S(2)}) collective-permute-start(f32[640,256]{1,0:T(8,128)S(1)} %shard_map.70.refs_0_.refs_2_), channel_id=1, source_target_pairs={{0,2},{1,5},{2,0},{3,7},{4,6},{5,1},{6,4},{7,3},{8,10},{9,13},{10,... | collective-permute-start | bytes 1966088 | tf_op jit(solution)/shard_map/ppermute | solution.py:356
  174.6 23.3 %collective-permute-start.25 = (f32[640,256]{1,0:T(8,128)S(1)}, f32[640,256]{1,0:T(8,128)S(1)}, u32[]{:S(2)}, u32[]{:S(2)}) collective-permute-start(f32[640,256]{1,0:T(8,128)S(1)} %collective-permute-done.24.refs_5_), channel_id=1, source_target_pairs={{0,8},{1,9},{2,10},{3,11},{4,12},{5,13},{6,14},{7,15},{8,0},{9,1},... | collective-permute-start | bytes 1966088 | tf_op jit(solution)/shard_map/ppermute | solution.py:356
  174.9 25.4 %collective-permute-start.20 = (f32[640,256]{1,0:T(8,128)S(1)}, f32[640,256]{1,0:T(8,128)S(1)}, u32[]{:S(2)}, u32[]{:S(2)}) collective-permute-start(f32[640,256]{1,0:T(8,128)S(1)} %collective-permute-done.19.refs_3_), channel_id=1, source_target_pairs={{0,2},{1,5},{2,0},{3,7},{4,6},{5,1},{6,4},{7,3},{8,10},{9,13},{10,... | collective-permute-start | bytes 1966088 | tf_op jit(solution)/shard_map/ppermute | solution.py:356
  175.3 25.0 %collective-permute-start.15 = (f32[512,256]{1,0:T(8,128)S(1)}, f32[512,256]{1,0:T(8,128)S(1)}, u32[]{:S(2)}, u32[]{:S(2)}) collective-permute-start(f32[512,256]{1,0:T(8,128)S(1)} %collective-permute-done.14.refs_1_), channel_id=1, source_target_pairs={{0,2},{1,5},{2,0},{3,7},{4,6},{5,1},{6,4},{7,3},{8,10},{9,13},{10,... | collective-permute-start | bytes 1572872 | tf_op jit(solution)/shard_map/ppermute | solution.py:356
  203.5 2.4 %collective-permute-start.29 = (f32[768,256]{1,0:T(8,128)S(1)}, f32[768,256]{1,0:T(8,128)S(1)}, u32[]{:S(2)}, u32[]{:S(2)}) collective-permute-start(f32[768,256]{1,0:T(8,128)S(1)} %get-tuple-element.34.mine_ref), channel_id=1, source_target_pairs={{0,1},{1,0},{2,3},{3,2},{4,5},{5,4},{6,7},{7,6},{8,9},{9,8},{10,11... | collective-permute-start | bytes 2359304 | tf_op jit(solution)/shard_map/ppermute | solution.py:389

commit v8 on v7

--- a/solution.py
+++ b/solution.py
@@ -264,14 +264,27 @@
     return call(part_kernel, shapes, table, [mine, theirs], [])
 
 
-def join_kernel(at, table_ref, mine_ref, theirs_ref, *refs):
-    rows = mine_ref.shape[0]
-    refs[-1][pl.ds(pl.multiple_of(table_ref[at] * rows, rows), rows), :] = mine_ref[...]
-    refs[-1][pl.ds(pl.multiple_of((1 - table_ref[at]) * rows, rows), rows), :] = theirs_ref[...]
-
-
-def join(table, at, mine, theirs, after):
-    return call(functools.partial(join_kernel, at), [shape(2 * mine.shape[0], mine.shape[1])], table, [mine, theirs], after)[0]
+def take_kernel(at, count, table_ref, mine_ref, theirs_ref, *refs):
+    which = 1 - table_ref[at]
+    refs[-1][:count, :] = mine_ref[...] + theirs_ref[pl.ds(pl.multiple_of(which * count, count), count), :]
+    if refs[-1].shape[0] > count:
+        refs[-1][count:, :] = refs[0][...]
+
+
+def take(table, at, mine, theirs, tail, after):
+    count = mine.shape[0]
+    rows = count + sum(value.shape[0] for value in tail)
+    return call(functools.partial(take_kernel, at, count), [shape(rows, mine.shape[1])], table, [mine, theirs, *tail], after)[0]
+
+
+def stack_kernel(table_ref, top_ref, rest_ref, *refs):
+    count = top_ref.shape[0]
+    refs[-1][:count, :] = top_ref[...]
+    refs[-1][count:, :] = rest_ref[...]
+
+
+def stack(table, top, rest, after):
+    return call(stack_kernel, [shape(top.shape[0] + rest.shape[0], top.shape[1])], table, [top, rest], after)[0]
 
 
 def rows_kernel(theirs, table_ref, inverse_ref, mine_ref, *refs):
@@ -345,11 +358,11 @@
 ALONG = {"first": (X, Y), "second": (Y, X), "near": (ZL, ZL), "far": (ZH, ZH)}
 ORDERS = {
     "A": ("first", "second", "near", "far"),
+    "N": ("near", "first", "second", "far"),
     "B": ("first", "near", "second", "far"),
-    "N": ("near", "first", "second", "far"),
 }
-SHARES = {"A": 4, "B": 5, "N": 5}
-FIELDS = ("c", "d", "mine", "theirs", "far_mine", "far_theirs")
+SHARES = {"A": 4, "N": 5, "B": 5}
+FIELDS = ("b", "c", "d", "mine", "theirs", "far_mine", "far_theirs")
 
 
 def swap(value, along):
@@ -370,7 +383,7 @@
                 here, there = start + a * half, start + (1 - a) * half
                 table[t * 2 + core, 0] = core
                 table[t * 2 + core, column : column + len(FIELDS)] = (
-                    c, d,
+                    b, c, d,
                     here + b * quarter, here + (1 - b) * quarter, there + b * quarter, there + (1 - b) * quarter,
                 )
         for k, field in enumerate(FIELDS):
@@ -407,28 +420,31 @@
         half = rows[name] // 2
         return cross_of(starts[name] + (1 - bits[ORDERS[name][0]]) * half, half)
 
-    def stage_2(name, got, keep):
+    def own_2(name, keep):
         half, quarter = rows[name] // 2, rows[name] // 4
         a, b = (bits[along] for along in ORDERS[name][:2])
-        which = b if keep else 1 - b
-        out = cross_of(starts[name] + a * half + which * quarter, quarter)
-        return out + lax.dynamic_slice_in_dim(got, which * quarter, quarter, 0)
+        return cross_of(starts[name] + a * half + (b if keep else 1 - b) * quarter, quarter)
 
     def part_of(value, which):
         half = value.shape[0] // 2
         return lax.dynamic_slice_in_dim(value, which * half, half, 0)
 
-    held = {}
+    def joined(one, other, which):
+        return jnp.where(which == 0, jnp.concatenate([one, other]), jnp.concatenate([other, one]))
+
+    held, last = {}, []
+    first = {name: give_1(name) for name in ORDERS}
+    first["A"] = stack(table, first["A"], gram, [first["N"]])
     for name, order in ORDERS.items():
-        give = give_1(name)
-        if name == "A":
-            give = jnp.concatenate([give, gram])
-        got = swap(give, order[0])
-        give = stage_2(name, got, False)
+        got = swap(first[name], order[0])
+        tail = []
         if name == "A":
             gram = gram + got[rows[name] // 2 :]
-            give = jnp.concatenate([give, gram])
-        held[name] = stage_2(name, got, True), swap(give, order[1])
+            tail = [gram]
+        give = take(table, where[name, "b"], own_2(name, False), got, tail, last)
+        quarter = rows[name] // 4
+        keep = own_2(name, True) + lax.dynamic_slice_in_dim(got, bits[order[1]] * quarter, quarter, 0)
+        held[name], last = (keep, swap(give, order[1])), [give]
     for name, (keep, arrived) in held.items():
         along = ORDERS[name][2]
         if name == "A":
@@ -453,11 +469,10 @@
     for name in held:
         mine[name] = solve_sum(table, inverse, held[name], list(mine.values()))
 
-    for k, field in ((3, "d"), (2, "c")):
-        last = []
-        for name, order in ORDERS.items():
-            mine[name] = join(table, where[name, field], mine[name], swap(mine[name], order[k]), last)
-            last = [mine[name]]
+    for k in (3, 2):
+        for name in mine:
+            along = ORDERS[name][k]
+            mine[name] = joined(mine[name], swap(mine[name], along), bits[along])
     near, far, last = [], [], []
     for name in mine:
         theirs = swap(mine[name], ORDERS[name][1])
@@ -465,7 +480,7 @@
         far += [(swap(mine[name], ORDERS[name][0]), where[name, "far_mine"])]
         last += [(swap(theirs, ORDERS[name][0]), where[name, "far_theirs"])]
     state = None
-    for blocks in (near, far, last[2:], last[:2]):
+    for blocks in (near, far, last[::2], last[1:2]):
         state = absorb(table, state, acts, blocks)
     sums, dict_out = state
     return second_update(codes_mid, sums, other_core(sums)), dict_out

time: 208 us -> 202 us (0.971); the launches traced: 208 us -> 199 us
  waiting for transfers between devices: 107 us -> 96 us
  Pallas kernels: 45.8 us -> 47.9 us
    ppermute x27, waiting for transfers between devices: 102 us -> 91.4 us  [swap(): return lax.ppermute(value, BOTH, flips(ALONG[along]))]
    pallas_call x12 -> x10, Pallas kernels: 9.32 us -> 11.5 us  [call(): pl.pallas_call(kernel, out_shape=out_shapes, in_specs=[SCALARS] + [WHOLE]...]
  transfers between devices with their start and end apart: 30 -> 30, of which waited for: 14 -> 18; matrix products, arithmetic and copies ran while one was open for 8% -> 7% of each run, Pallas kernels for 14% -> 15%
where the time goes in v8:
time: 202 us; the launch traced here: 199 us
  waiting for transfers between devices  96 us (48%)
  Pallas kernels  47.9 us (24%)
  starting transfers between devices  34.2 us (17%)
  matrix products  15.8 us (8%)
  local copies, waits for them, and re-layouts  2.51 us (1%)
    ppermute x27, waiting for transfers between devices, swap(): return lax.ppermute(value, BOTH, flips(ALONG[along]))  91.4 us
    ppermute x27, starting transfers between devices, swap(): return lax.ppermute(value, BOTH, flips(ALONG[along]))  33.5 us
    dot_general x9, matrix products, dot(): lax.dot_general(left, right, dims, precision=precision, preferred_element...  15.8 us
    pallas_call x4, Pallas kernels, absorb(): pl.pallas_call(functools.partial(absorb_kernel, [at for _, at in blocks],...  14.5 us
    pallas_call x10, Pallas kernels, call(): pl.pallas_call(kernel, out_shape=out_shapes, in_specs=[SCALARS] + [WHOLE]...  11.5 us
    pallas_call x1, Pallas kernels, project(): pl.pallas_call(project_kernel, out_shape=jax.ShapeDtypeStruct((tokens + c...  9.5 us
    pallas_call x1, Pallas kernels, factor_inverse(): pl.pallas_call(halves_kernel, out_shape=jax.ShapeDtypeStruct((comp, comp)...  8.43 us
    ppermute x3, waiting for transfers between devices, other_core(): return lax.ppermute(value, 'hid', [(0, 1), (1, 0)])  4.65 us
  transfers between devices with their start and end apart: 30, of which 18 were waited for; matrix products, arithmetic and copies ran while one was open for 7% of the time, Pallas kernels for 15%

profile of v8, /device:TPU:0, one launch (start us, length us, event | category | flops | bytes accessed | tf_op | source)
XLA Modules:
  0.0 198.8 jit_solution(1998184096727024525)
XLA Ops:
  0.6 9.5 %shard_map.59.mine_ref = f32[768,256]{1,0:T(8,128)S(1)} custom-call(bf16[512,7168]{1,0:T(8,128)(2,1)} %acts_ref.9, f32[7168,256]{1,0:T(8,128)} %dict_ref.1), custom_call_target="tpu_custom_call" | custom-call | flops 3758096384 | bytes 14680064 | tf_op jit(solution)/shard_map/pallas_call | solution.py:58
  10.7 0.7 fusion.26.core_ref.table_ref
  11.4 1.2 collective-permute-done.theirs_ref
  12.6 2.0 shard_map.60
  14.6 0.8 copy-done.3
  15.4 1.7 fusion.6.top_ref
  17.0 1.9 fusion.2.refs_0_
  18.9 3.0 %collective-permute-start.6 = (f32[1280,256]{1,0:T(8,128)S(1)}, f32[1280,256]{1,0:T(8,128)S(1)}, u32[]{:S(2)}, u32[]{:S(2)}) collective-permute-start(f32[1280,256]{1,0:T(8,128)S(1)} %fusion.2.refs_0_), channel_id=1, source_target_pairs={{0,8},{1,9},{2,10},{3,11},{4,12},{5,13},{6,14},{7,15},{8,0},{9,1},... | collective-permute-start | bytes 3932168 | tf_op jit(solution)/shard_map/ppermute | solution.py:369
  21.9 1.7 shard_map.61
  23.6 1.5 collective-permute-start.1
  25.1 2.9 %fusion = f32[1280,256]{1,0:T(8,128)} fusion(bf16[512,256]{1,0:T(8,128)(2,1)S(1)} %get-tuple-element.20, bf16[512,7168]{1,0:T(8,128)(2,1)} %acts_ref.9, s32[]{:T(128)S(6)} %select_n.139), kind=kOutput, calls=%fused_computation | convolution fusion | flops 335544320 | bytes 2883588 | tf_op jit(solution)/shard_map/dot_general | solution.py:21
  28.5 1.4 fusion.14.mine_ref
  29.9 1.5 fusion.8.mine_ref
  31.4 1.5 fusion.11.mine_ref
  32.8 7.3 %collective-permute-done.1.theirs_ref = f32[1152,256]{1,0:T(8,128)} collective-permute-done((f32[1152,256]{1,0:T(8,128)}, f32[1152,256]{1,0:T(8,128)}, u32[]{:S(2)}, u32[]{:S(2)}) %collective-permute-start.1) | collective-permute-done | bytes 1179680 | tf_op jit(solution)/shard_map/ppermute | solution.py:369
  40.1 0.9 slice_add_fusion.refs_0_.gram_ref
  41.0 1.4 shard_map.62.refs_0_
  42.4 1.6 collective-permute-start.2
  44.0 7.0 %collective-permute-done.6.theirs_ref = f32[1280,256]{1,0:T(8,128)S(1)} collective-permute-done((f32[1280,256]{1,0:T(8,128)S(1)}, f32[1280,256]{1,0:T(8,128)S(1)}, u32[]{:S(2)}, u32[]{:S(2)}) %collective-permute-start.6) | collective-permute-done | bytes 1310752 | tf_op jit(solution)/shard_map/ppermute | solution.py:369
  51.0 0.6 shard_map.66.refs_0_
  51.6 9.5 %collective-permute-done.9.theirs_ref = f32[1280,256]{1,0:T(8,128)} collective-permute-done((f32[1280,256]{1,0:T(8,128)}, f32[1280,256]{1,0:T(8,128)}, u32[]{:S(2)}, u32[]{:S(2)}) %collective-permute-start.9) | collective-permute-done | bytes 1310752 | tf_op jit(solution)/shard_map/ppermute | solution.py:369
  61.2 1.4 shard_map.67
  62.6 1.9 collective-permute-start.7
  64.6 1.5 convolution_add_fusion.2.mine_ref
  66.1 0.9 copy-done.1
  67.0 1.2 shard_map.63
  68.2 1.6 collective-permute-start.3
  69.9 10.6 %collective-permute-done.10 = f32[640,256]{1,0:T(8,128)} collective-permute-done((f32[640,256]{1,0:T(8,128)S(1)}, f32[640,256]{1,0:T(8,128)}, u32[]{:S(2)}, u32[]{:S(2)}) %collective-permute-start.10) | collective-permute-done | bytes 655392 | tf_op jit(solution)/shard_map/ppermute | solution.py:369
  80.4 1.9 fusion.5
  82.3 1.6 collective-permute-start.11
  83.9 1.7 fusion.4
  86.5 0.6 shard_map.64
  87.1 2.7 %collective-permute-start.4 = (f32[256,256]{1,0:T(8,128)S(1)}, f32[256,256]{1,0:T(8,128)S(1)}, u32[]{:S(2)}, u32[]{:S(2)}) collective-permute-start(f32[256,256]{1,0:T(8,128)S(1)} %get-tuple-element.25), channel_id=1, source_target_pairs={{0,16},{1,17},{2,18},{3,19},{4,20},{5,21},{6,22},{7,23},{8,24},{9,... | collective-permute-start | bytes 786440 | tf_op jit(solution)/shard_map/ppermute | solution.py:369
  89.8 2.4 %collective-permute-start.21 = (f32[160,256]{1,0:T(8,128)S(1)}, f32[160,256]{1,0:T(8,128)S(1)}, u32[]{:S(2)}, u32[]{:S(2)}) collective-permute-start(f32[160,256]{1,0:T(8,128)S(1)} %get-tuple-element.36), channel_id=1, source_target_pairs={{0,16},{1,17},{2,18},{3,19},{4,20},{5,21},{6,22},{7,23},{8,24},{9,... | collective-permute-start | bytes 491528 | tf_op jit(solution)/shard_map/ppermute | solution.py:369
  92.2 11.6 %collective-permute-done.4.theirs_ref = f32[256,256]{1,0:T(8,128)S(1)} collective-permute-done((f32[256,256]{1,0:T(8,128)S(1)}, f32[256,256]{1,0:T(8,128)S(1)}, u32[]{:S(2)}, u32[]{:S(2)}) %collective-permute-start.4) | collective-permute-done | bytes 262176 | tf_op jit(solution)/shard_map/ppermute | solution.py:369
  104.7 1.2 collective-permute-done.5.theirs_ref
  105.8 8.4 %shard_map.68.inverse_ref = f32[256,256]{1,0:T(8,128)S(1)} custom-call(s32[22]{0:T(128)S(1)} %fusion.26.core_ref.table_ref, f32[128,256]{1,0:T(8,128)S(1)} %get-tuple-element.26.mine_ref, f32[128,256]{1,0:T(8,128)S(1)} %collective-permute-done.5.theirs_ref, f32[160,256]{1,0:T(8,128)S(1)} %get-tuple-element.39.refs_0_.mine_ref, ...), custom_call_target="tpu_custom_call" | custom-call | flops 10000000000 | bytes 524288 | tf_op jit(solution)/shard_map/pallas_call | solution.py:123
  114.3 1.3 shard_map.69.refs_1_
  115.7 1.4 shard_map.70.refs_2_
  117.1 1.4 shard_map.71
  118.5 1.8 collective-permute-start.22
  120.2 1.2 collective-permute-start.13
  121.4 12.0 %collective-permute-done.22 = f32[160,256]{1,0:T(8,128)S(1)} collective-permute-done((f32[160,256]{1,0:T(8,128)S(1)}, f32[160,256]{1,0:T(8,128)S(1)}, u32[]{:S(2)}, u32[]{:S(2)}) %collective-permute-start.22) | collective-permute-done | bytes 163872 | tf_op jit(solution)/shard_map/ppermute | solution.py:369
  133.5 1.1 collective-permute-start.23
  134.6 1.6 collective-permute-done.13
  136.2 1.1 collective-permute-start.14
  137.3 4.6 %collective-permute-done.17 = f32[128,256]{1,0:T(8,128)S(1)} collective-permute-done((f32[128,256]{1,0:T(8,128)S(1)}, f32[128,256]{1,0:T(8,128)S(1)}, u32[]{:S(2)}, u32[]{:S(2)}) %collective-permute-start.17) | collective-permute-done | bytes 131104 | tf_op jit(solution)/shard_map/ppermute | solution.py:369
  142.0 2.1 %collective-permute-start.24 = (f32[640,256]{1,0:T(8,128)S(1)}, f32[640,256]{1,0:T(8,128)S(1)}, u32[]{:S(2)}, u32[]{:S(2)}) collective-permute-start(f32[640,256]{1,0:T(8,128)S(1)} %maximum_select_fusion.1.refs_4_), channel_id=1, source_target_pairs={{0,8},{1,9},{2,10},{3,11},{4,12},{5,13},{6,14},{7,15},{8,0},{9,1},... | collective-permute-start | bytes 1966088 | tf_op jit(solution)/shard_map/ppermute | solution.py:369
  144.2 1.0 collective-permute-start.15
  145.3 5.9 %collective-permute-done.18 = f32[256,256]{1,0:T(8,128)S(1)} collective-permute-done((f32[256,256]{1,0:T(8,128)S(1)}, f32[256,256]{1,0:T(8,128)S(1)}, u32[]{:S(2)}, u32[]{:S(2)}) %collective-permute-start.18) | collective-permute-done | bytes 262176 | tf_op jit(solution)/shard_map/ppermute | solution.py:369
  151.2 1.1 collective-permute-start.26
  152.3 1.4 collective-permute-start.19
  153.7 1.1 collective-permute-start.28
  154.8 11.3 %collective-permute-done.26.refs_0_ = f32[512,256]{1,0:T(8,128)S(1)} collective-permute-done((f32[512,256]{1,0:T(8,128)S(1)}, f32[512,256]{1,0:T(8,128)S(1)}, u32[]{:S(2)}, u32[]{:S(2)}) %collective-permute-start.26) | collective-permute-done | bytes 524320 | tf_op jit(solution)/shard_map/ppermute | solution.py:369
  166.1 1.9 collective-permute-start.27
  169.1 1.0 collective-permute-start.20
  170.2 5.4 %shard_map.72 = (f32[768,256]{1,0:T(8,128)S(1)}, f32[7168,256]{1,0:T(8,128)}) custom-call(s32[22]{0:T(128)S(1)} %fusion.26.core_ref.table_ref, bf16[512,7168]{1,0:T(8,128)(2,1)} %acts_ref.9, f32[512,256]{1,0:T(8,128)S(1)} %maximum_select_fusion.2.refs_0_, f32[512,256]{1,0:T(8,128)S(1)} %collective-permute-done.19.refs_1_, ...), custom_call_target="tpu_custom_call" | custom-call | flops 1409286144 | bytes 11010048 | tf_op jit(solution)/shard_map/pallas_call | solution.py:338
  175.6 8.2 %collective-permute-done.27.refs_1_ = f32[640,256]{1,0:T(8,128)S(1)} collective-permute-done((f32[640,256]{1,0:T(8,128)S(1)}, f32[640,256]{1,0:T(8,128)S(1)}, u32[]{:S(2)}, u32[]{:S(2)}) %collective-permute-start.27) | collective-permute-done | bytes 655392 | tf_op jit(solution)/shard_map/ppermute | solution.py:369
  183.8 3.7 %shard_map.73 = (f32[768,256]{1,0:T(8,128)S(1)}, f32[7168,256]{1,0:T(8,128)}) custom-call(s32[22]{0:T(128)S(1)} %fusion.26.core_ref.table_ref, bf16[512,7168]{1,0:T(8,128)(2,1)} %acts_ref.9, f32[512,256]{1,0:T(8,128)S(1)} %collective-permute-done.26.refs_0_, ...), custom_call_target="tpu_custom_call", output_to_operand_aliasing={{0}: (5, {}), {1}: (6, {})} | custom-call | flops 704643072 | bytes 5505024 | tf_op jit(solution)/shard_map/pallas_call | solution.py:338
  187.5 3.2 %shard_map.74 = (f32[768,256]{1,0:T(8,128)S(1)}, f32[7168,256]{1,0:T(8,128)}) custom-call(s32[22]{0:T(128)S(1)} %fusion.26.core_ref.table_ref, bf16[512,7168]{1,0:T(8,128)(2,1)} %acts_ref.9, f32[512,256]{1,0:T(8,128)S(1)} %collective-permute-done.20.refs_0_, ...), custom_call_target="tpu_custom_call", output_to_operand_aliasing={{0}: (4, {}), {1}: (5, {})} | custom-call | flops 452984832 | bytes 3538944 | tf_op jit(solution)/shard_map/pallas_call | solution.py:338
  190.6 1.4 collective-permute-done.16.refs_0_
  192.0 2.4 %shard_map.75 = (f32[768,256]{1,0:T(8,128)S(1)}, f32[7168,256]{1,0:T(8,128)}) custom-call(s32[22]{0:T(128)S(1)} %fusion.26.core_ref.table_ref, bf16[512,7168]{1,0:T(8,128)(2,1)} %acts_ref.9, f32[640,256]{1,0:T(8,128)S(1)} %collective-permute-done.16.refs_0_, f32[768,256]{1,0:T(8,128)S(1)} %get-tuple-element.32.refs_1_, ...), custom_call_target="tpu_custom_call", output_to_operand_aliasing={{0}: (3, {}), {1}: (4, {})} | custom-call | flops 251658240 | bytes 1966080 | tf_op jit(solution)/shard_map/pallas_call | solution.py:338
  194.5 2.3 %collective-permute-done.29.theirs_ref = f32[768,256]{1,0:T(8,128)S(1)} collective-permute-done((f32[768,256]{1,0:T(8,128)S(1)}, f32[768,256]{1,0:T(8,128)S(1)}, u32[]{:S(2)}, u32[]{:S(2)}) %collective-permute-start.29) | collective-permute-done | bytes 786464 | tf_op jit(solution)/shard_map/ppermute | solution.py:402
  196.8 2.0 %shard_map.76 = f32[512,256]{1,0:T(8,128)} custom-call(f32[512,256]{1,0:T(8,128)S(1)} %copy-done.4, f32[768,256]{1,0:T(8,128)S(1)} %get-tuple-element.34.mine_ref, f32[768,256]{1,0:T(8,128)S(1)} %collective-permute-done.29.theirs_ref), custom_call_target="tpu_custom_call" | custom-call | tf_op jit(solution)/shard_map/pallas_call | solution.py:195
  (47 shorter events, 4.6 us)
Async XLA Ops:
  0.6 12.0 %copy-start.2 = (f32[512,256]{1,0:T(8,128)S(1)}, f32[512,256]{1,0:T(8,128)}, u32[]{:S(2)}) copy-start(f32[512,256]{1,0:T(8,128)} %codes_ref.1) | copy-start | bytes 1572868
  10.1 2.4 %collective-permute-start = (f32[768,256]{1,0:T(8,128)S(1)}, f32[768,256]{1,0:T(8,128)S(1)}, u32[]{:S(2)}, u32[]{:S(2)}) collective-permute-start(f32[768,256]{1,0:T(8,128)S(1)} %shard_map.59.mine_ref), channel_id=1, source_target_pairs={{0,1},{1,0},{2,3},{3,2},{4,5},{5,4},{6,7},{7,6},{8,9},{9,8},{10,11... | collective-permute-start | bytes 2359304 | tf_op jit(solution)/shard_map/ppermute | solution.py:402
  14.6 0.8 copy-start.3
  18.9 32.1 %collective-permute-start.6 = (f32[1280,256]{1,0:T(8,128)S(1)}, f32[1280,256]{1,0:T(8,128)S(1)}, u32[]{:S(2)}, u32[]{:S(2)}) collective-permute-start(f32[1280,256]{1,0:T(8,128)S(1)} %fusion.2.refs_0_), channel_id=1, source_target_pairs={{0,8},{1,9},{2,10},{3,11},{4,12},{5,13},{6,14},{7,15},{8,0},{9,1},... | collective-permute-start | bytes 3932168 | tf_op jit(solution)/shard_map/ppermute | solution.py:369
  23.6 16.5 %collective-permute-start.1 = (f32[1152,256]{1,0:T(8,128)}, f32[1152,256]{1,0:T(8,128)}, u32[]{:S(2)}, u32[]{:S(2)}) collective-permute-start(f32[1152,256]{1,0:T(8,128)} %shard_map.61), channel_id=1, source_target_pairs={{0,2},{1,5},{2,0},{3,7},{4,6},{5,1},{6,4},{7,3},{8,10},{9,13},{10,... | collective-permute-start | bytes 3538952 | tf_op jit(solution)/shard_map/ppermute | solution.py:369
  28.0 33.2 %collective-permute-start.9 = (f32[1280,256]{1,0:T(8,128)}, f32[1280,256]{1,0:T(8,128)}, u32[]{:S(2)}, u32[]{:S(2)}) collective-permute-start(f32[1280,256]{1,0:T(8,128)} %fusion), channel_id=1, source_target_pairs={{0,2},{1,5},{2,0},{3,7},{4,6},{5,1},{6,4},{7,3},{8,10},{9,13},{10,... | collective-permute-start | bytes 3932168 | tf_op jit(solution)/shard_map/ppermute | solution.py:369
  41.0 10.6 %copy-start = (f32[128,256]{1,0:T(8,128)}, f32[128,256]{1,0:T(8,128)S(1)}, u32[]{:S(2)}) copy-start(f32[128,256]{1,0:T(8,128)S(1)} %slice_add_fusion.refs_0_.gram_ref) | copy-start | bytes 393220
  42.4 23.7 %collective-permute-start.2 = (f32[640,256]{1,0:T(8,128)S(1)}, f32[640,256]{1,0:T(8,128)}, u32[]{:S(2)}, u32[]{:S(2)}) collective-permute-start(f32[640,256]{1,0:T(8,128)S(1)} %shard_map.62.refs_0_), channel_id=1, source_target_pairs={{0,4},{1,3},{2,6},{3,1},{4,0},{5,7},{6,2},{7,5},{8,12},{9,11},{10,... | collective-permute-start | bytes 1966088 | tf_op jit(solution)/shard_map/ppermute | solution.py:369
  62.6 17.8 %collective-permute-start.10 = (f32[640,256]{1,0:T(8,128)S(1)}, f32[640,256]{1,0:T(8,128)}, u32[]{:S(2)}, u32[]{:S(2)}) collective-permute-start(f32[640,256]{1,0:T(8,128)S(1)} %shard_map.67), channel_id=1, source_target_pairs={{0,8},{1,9},{2,10},{3,11},{4,12},{5,13},{6,14},{7,15},{8,0},{9,1},... | collective-permute-start | bytes 1966088 | tf_op jit(solution)/shard_map/ppermute | solution.py:369
  62.6 21.3 %collective-permute-start.7 = (f32[640,256]{1,0:T(8,128)S(1)}, f32[640,256]{1,0:T(8,128)}, u32[]{:S(2)}, u32[]{:S(2)}) collective-permute-start(f32[640,256]{1,0:T(8,128)S(1)} %shard_map.66.refs_0_), channel_id=1, source_target_pairs={{0,2},{1,5},{2,0},{3,7},{4,6},{5,1},{6,4},{7,3},{8,10},{9,13},{10,... | collective-permute-start | bytes 1966088 | tf_op jit(solution)/shard_map/ppermute | solution.py:369
  66.1 0.9 copy-start.1
  68.2 18.2 %collective-permute-start.3 = (f32[384,256]{1,0:T(8,128)S(1)}, f32[384,256]{1,0:T(8,128)S(1)}, u32[]{:S(2)}, u32[]{:S(2)}) collective-permute-start(f32[384,256]{1,0:T(8,128)S(1)} %get-tuple-element.23), channel_id=1, source_target_pairs={{0,8},{1,9},{2,10},{3,11},{4,12},{5,13},{6,14},{7,15},{8,0},{9,1},... | collective-permute-start | bytes 1179656 | tf_op jit(solution)/shard_map/ppermute | solution.py:369
  82.3 7.4 %collective-permute-start.11 = (f32[320,256]{1,0:T(8,128)S(1)}, f32[320,256]{1,0:T(8,128)S(1)}, u32[]{:S(2)}, u32[]{:S(2)}) collective-permute-start(f32[320,256]{1,0:T(8,128)S(1)} %constant_dynamic-slice_fusion.1), channel_id=1, source_target_pairs={{0,4},{1,3},{2,6},{3,1},{4,0},{5,7},{6,2},{7,5},{8,12},{9,11},{10,... | collective-permute-start | bytes 983048 | tf_op jit(solution)/shard_map/ppermute | solution.py:369
  85.6 18.9 %collective-permute-start.8 = (f32[320,256]{1,0:T(8,128)S(1)}, f32[320,256]{1,0:T(8,128)S(1)}, u32[]{:S(2)}, u32[]{:S(2)}) collective-permute-start(f32[320,256]{1,0:T(8,128)S(1)} %constant_dynamic-slice_fusion.4), channel_id=1, source_target_pairs={{0,4},{1,3},{2,6},{3,1},{4,0},{5,7},{6,2},{7,5},{8,12},{9,11},{10,... | collective-permute-start | bytes 983048 | tf_op jit(solution)/shard_map/ppermute | solution.py:369
  87.1 16.8 %collective-permute-start.4 = (f32[256,256]{1,0:T(8,128)S(1)}, f32[256,256]{1,0:T(8,128)S(1)}, u32[]{:S(2)}, u32[]{:S(2)}) collective-permute-start(f32[256,256]{1,0:T(8,128)S(1)} %get-tuple-element.25), channel_id=1, source_target_pairs={{0,16},{1,17},{2,18},{3,19},{4,20},{5,21},{6,22},{7,23},{8,24},{9,... | collective-permute-start | bytes 786440 | tf_op jit(solution)/shard_map/ppermute | solution.py:369
  89.8 27.3 %collective-permute-start.21 = (f32[160,256]{1,0:T(8,128)S(1)}, f32[160,256]{1,0:T(8,128)S(1)}, u32[]{:S(2)}, u32[]{:S(2)}) collective-permute-start(f32[160,256]{1,0:T(8,128)S(1)} %get-tuple-element.36), channel_id=1, source_target_pairs={{0,16},{1,17},{2,18},{3,19},{4,20},{5,21},{6,22},{7,23},{8,24},{9,... | collective-permute-start | bytes 491528 | tf_op jit(solution)/shard_map/ppermute | solution.py:369
  104.4 1.4 collective-permute-start.5
  104.6 11.1 %collective-permute-start.12 = (f32[160,256]{1,0:T(8,128)S(1)}, f32[160,256]{1,0:T(8,128)S(1)}, u32[]{:S(2)}, u32[]{:S(2)}) collective-permute-start(f32[160,256]{1,0:T(8,128)S(1)} %get-tuple-element.38), channel_id=1, source_target_pairs={{0,16},{1,17},{2,18},{3,19},{4,20},{5,21},{6,22},{7,23},{8,24},{9,... | collective-permute-start | bytes 491528 | tf_op jit(solution)/shard_map/ppermute | solution.py:369
  118.5 15.0 %collective-permute-start.22 = (f32[160,256]{1,0:T(8,128)S(1)}, f32[160,256]{1,0:T(8,128)S(1)}, u32[]{:S(2)}, u32[]{:S(2)}) collective-permute-start(f32[160,256]{1,0:T(8,128)S(1)} %shard_map.71), channel_id=1, source_target_pairs={{0,16},{1,17},{2,18},{3,19},{4,20},{5,21},{6,22},{7,23},{8,24},{9,... | collective-permute-start | bytes 491528 | tf_op jit(solution)/shard_map/ppermute | solution.py:369
  120.2 15.9 %collective-permute-start.13 = (f32[160,256]{1,0:T(8,128)S(1)}, f32[160,256]{1,0:T(8,128)S(1)}, u32[]{:S(2)}, u32[]{:S(2)}) collective-permute-start(f32[160,256]{1,0:T(8,128)S(1)} %shard_map.70.refs_2_), channel_id=1, source_target_pairs={{0,16},{1,17},{2,18},{3,19},{4,20},{5,21},{6,22},{7,23},{8,24},{9,... | collective-permute-start | bytes 491528 | tf_op jit(solution)/shard_map/ppermute | solution.py:369
  133.5 8.4 %collective-permute-start.23 = (f32[320,256]{1,0:T(8,128)S(1)}, f32[320,256]{1,0:T(8,128)S(1)}, u32[]{:S(2)}, u32[]{:S(2)}) collective-permute-start(f32[320,256]{1,0:T(8,128)S(1)} %maximum_select_fusion.4), channel_id=1, source_target_pairs={{0,4},{1,3},{2,6},{3,1},{4,0},{5,7},{6,2},{7,5},{8,12},{9,11},{10,... | collective-permute-start | bytes 983048 | tf_op jit(solution)/shard_map/ppermute | solution.py:369
  134.6 7.2 %collective-permute-start.17 = (f32[128,256]{1,0:T(8,128)S(1)}, f32[128,256]{1,0:T(8,128)S(1)}, u32[]{:S(2)}, u32[]{:S(2)}) collective-permute-start(f32[128,256]{1,0:T(8,128)S(1)} %shard_map.69.refs_1_), channel_id=1, source_target_pairs={{0,16},{1,17},{2,18},{3,19},{4,20},{5,21},{6,22},{7,23},{8,24},{9,... | collective-permute-start | bytes 393224 | tf_op jit(solution)/shard_map/ppermute | solution.py:369
  136.2 8.0 %collective-permute-start.14 = (f32[320,256]{1,0:T(8,128)S(1)}, f32[320,256]{1,0:T(8,128)S(1)}, u32[]{:S(2)}, u32[]{:S(2)}) collective-permute-start(f32[320,256]{1,0:T(8,128)S(1)} %maximum_select_fusion.3), channel_id=1, source_target_pairs={{0,4},{1,3},{2,6},{3,1},{4,0},{5,7},{6,2},{7,5},{8,12},{9,11},{10,... | collective-permute-start | bytes 983048 | tf_op jit(solution)/shard_map/ppermute | solution.py:369
  141.9 9.3 %collective-permute-start.18 = (f32[256,256]{1,0:T(8,128)S(1)}, f32[256,256]{1,0:T(8,128)S(1)}, u32[]{:S(2)}, u32[]{:S(2)}) collective-permute-start(f32[256,256]{1,0:T(8,128)S(1)} %maximum_select_fusion.5), channel_id=1, source_target_pairs={{0,8},{1,9},{2,10},{3,11},{4,12},{5,13},{6,14},{7,15},{8,0},{9,1},... | collective-permute-start | bytes 786440 | tf_op jit(solution)/shard_map/ppermute | solution.py:369
  142.0 26.0 %collective-permute-start.24 = (f32[640,256]{1,0:T(8,128)S(1)}, f32[640,256]{1,0:T(8,128)S(1)}, u32[]{:S(2)}, u32[]{:S(2)}) collective-permute-start(f32[640,256]{1,0:T(8,128)S(1)} %maximum_select_fusion.1.refs_4_), channel_id=1, source_target_pairs={{0,8},{1,9},{2,10},{3,11},{4,12},{5,13},{6,14},{7,15},{8,0},{9,1},... | collective-permute-start | bytes 1966088 | tf_op jit(solution)/shard_map/ppermute | solution.py:369
  144.2 24.3 %collective-permute-start.15 = (f32[640,256]{1,0:T(8,128)S(1)}, f32[640,256]{1,0:T(8,128)S(1)}, u32[]{:S(2)}, u32[]{:S(2)}) collective-permute-start(f32[640,256]{1,0:T(8,128)S(1)} %maximum_select_fusion.refs_2_), channel_id=1, source_target_pairs={{0,2},{1,5},{2,0},{3,7},{4,6},{5,1},{6,4},{7,3},{8,10},{9,13},{10,... | collective-permute-start | bytes 1966088 | tf_op jit(solution)/shard_map/ppermute | solution.py:369
  151.2 14.9 %collective-permute-start.26 = (f32[512,256]{1,0:T(8,128)S(1)}, f32[512,256]{1,0:T(8,128)S(1)}, u32[]{:S(2)}, u32[]{:S(2)}) collective-permute-start(f32[512,256]{1,0:T(8,128)S(1)} %maximum_select_fusion.2.refs_0_), channel_id=1, source_target_pairs={{0,2},{1,5},{2,0},{3,7},{4,6},{5,1},{6,4},{7,3},{8,10},{9,13},{10,... | collective-permute-start | bytes 1572872 | tf_op jit(solution)/shard_map/ppermute | solution.py:369
  152.3 16.8 %collective-permute-start.19 = (f32[512,256]{1,0:T(8,128)S(1)}, f32[512,256]{1,0:T(8,128)S(1)}, u32[]{:S(2)}, u32[]{:S(2)}) collective-permute-start(f32[512,256]{1,0:T(8,128)S(1)} %maximum_select_fusion.2.refs_0_), channel_id=1, source_target_pairs={{0,4},{1,3},{2,6},{3,1},{4,0},{5,7},{6,2},{7,5},{8,12},{9,11},{10,... | collective-permute-start | bytes 1572872 | tf_op jit(solution)/shard_map/ppermute | solution.py:369
  153.7 21.8 %collective-permute-start.28 = (f32[640,256]{1,0:T(8,128)S(1)}, f32[640,256]{1,0:T(8,128)S(1)}, u32[]{:S(2)}, u32[]{:S(2)}) collective-permute-start(f32[640,256]{1,0:T(8,128)S(1)} %maximum_select_fusion.1.refs_4_), channel_id=1, source_target_pairs={{0,2},{1,5},{2,0},{3,7},{4,6},{5,1},{6,4},{7,3},{8,10},{9,13},{10,... | collective-permute-start | bytes 1966088 | tf_op jit(solution)/shard_map/ppermute | solution.py:369
  166.1 17.7 %collective-permute-start.27 = (f32[640,256]{1,0:T(8,128)S(1)}, f32[640,256]{1,0:T(8,128)S(1)}, u32[]{:S(2)}, u32[]{:S(2)}) collective-permute-start(f32[640,256]{1,0:T(8,128)S(1)} %maximum_select_fusion.refs_2_), channel_id=1, source_target_pairs={{0,8},{1,9},{2,10},{3,11},{4,12},{5,13},{6,14},{7,15},{8,0},{9,1},... | collective-permute-start | bytes 1966088 | tf_op jit(solution)/shard_map/ppermute | solution.py:369
  168.0 19.4 %collective-permute-start.25 = (f32[640,256]{1,0:T(8,128)S(1)}, f32[640,256]{1,0:T(8,128)S(1)}, u32[]{:S(2)}, u32[]{:S(2)}) collective-permute-start(f32[640,256]{1,0:T(8,128)S(1)} %collective-permute-done.24.refs_5_), channel_id=1, source_target_pairs={{0,2},{1,5},{2,0},{3,7},{4,6},{5,1},{6,4},{7,3},{8,10},{9,13},{10,... | collective-permute-start | bytes 1966088 | tf_op jit(solution)/shard_map/ppermute | solution.py:369
  168.6 23.5 %collective-permute-start.16 = (f32[640,256]{1,0:T(8,128)S(1)}, f32[640,256]{1,0:T(8,128)S(1)}, u32[]{:S(2)}, u32[]{:S(2)}) collective-permute-start(f32[640,256]{1,0:T(8,128)S(1)} %collective-permute-done.15.refs_3_), channel_id=1, source_target_pairs={{0,8},{1,9},{2,10},{3,11},{4,12},{5,13},{6,14},{7,15},{8,0},{9,1},... | collective-permute-start | bytes 1966088 | tf_op jit(solution)/shard_map/ppermute | solution.py:369
  169.1 18.3 %collective-permute-start.20 = (f32[512,256]{1,0:T(8,128)S(1)}, f32[512,256]{1,0:T(8,128)S(1)}, u32[]{:S(2)}, u32[]{:S(2)}) collective-permute-start(f32[512,256]{1,0:T(8,128)S(1)} %collective-permute-done.19.refs_1_), channel_id=1, source_target_pairs={{0,2},{1,5},{2,0},{3,7},{4,6},{5,1},{6,4},{7,3},{8,10},{9,13},{10,... | collective-permute-start | bytes 1572872 | tf_op jit(solution)/shard_map/ppermute | solution.py:369
  192.0 4.7 %copy-start.4 = (f32[512,256]{1,0:T(8,128)S(1)}, f32[512,256]{1,0:T(8,128)}, u32[]{:S(2)}) copy-start(f32[512,256]{1,0:T(8,128)} %copy-done.3) | copy-start | bytes 1572868
  194.4 2.4 %collective-permute-start.29 = (f32[768,256]{1,0:T(8,128)S(1)}, f32[768,256]{1,0:T(8,128)S(1)}, u32[]{:S(2)}, u32[]{:S(2)}) collective-permute-start(f32[768,256]{1,0:T(8,128)S(1)} %get-tuple-element.34.mine_ref), channel_id=1, source_target_pairs={{0,1},{1,0},{2,3},{3,2},{4,5},{5,4},{6,7},{7,6},{8,9},{9,8},{10,11... | collective-permute-start | bytes 2359304 | tf_op jit(solution)/shard_map/ppermute | solution.py:402

commit v9 on v8

--- a/solution.py
+++ b/solution.py
@@ -357,11 +357,11 @@
 X, Y, ZL, ZH = 1, 2, 4, 8
 ALONG = {"first": (X, Y), "second": (Y, X), "near": (ZL, ZL), "far": (ZH, ZH)}
 ORDERS = {
-    "A": ("first", "second", "near", "far"),
     "N": ("near", "first", "second", "far"),
     "B": ("first", "near", "second", "far"),
+    "A": ("first", "second", "near", "far"),
 }
-SHARES = {"A": 4, "N": 5, "B": 5}
+SHARES = {"N": 5, "B": 5, "A": 4}
 FIELDS = ("b", "c", "d", "mine", "theirs", "far_mine", "far_theirs")
 
 
@@ -480,7 +480,7 @@
         far += [(swap(mine[name], ORDERS[name][0]), where[name, "far_mine"])]
         last += [(swap(theirs, ORDERS[name][0]), where[name, "far_theirs"])]
     state = None
-    for blocks in (near, far, last[::2], last[1:2]):
+    for blocks in (near, far, [last[1], last[2]], [last[0]]):
         state = absorb(table, state, acts, blocks)
     sums, dict_out = state
     return second_update(codes_mid, sums, other_core(sums)), dict_out

time: 202 us -> 196 us (0.970); the launches traced: 199 us -> 195 us
  waiting for transfers between devices: 96 us -> 92.3 us
    ppermute x27, waiting for transfers between devices: 91.4 us -> 87.7 us  [swap(): return lax.ppermute(value, BOTH, flips(ALONG[along]))]
  transfers between devices with their start and end apart: 30 -> 30, of which waited for: 18 -> 16; matrix products, arithmetic and copies ran while one was open for 7% -> 7% of each run, Pallas kernels for 15% -> 15%
where the time goes in v9:
time: 196 us; the launch traced here: 195 us
  waiting for transfers between devices  92.3 us (47%)
  Pallas kernels  48.3 us (25%)
  starting transfers between devices  35.3 us (18%)
  matrix products  15.9 us (8%)
    ppermute x27, waiting for transfers between devices, swap(): return lax.ppermute(value, BOTH, flips(ALONG[along]))  87.7 us
    ppermute x27, starting transfers between devices, swap(): return lax.ppermute(value, BOTH, flips(ALONG[along]))  34.6 us
    dot_general x9, matrix products, dot(): lax.dot_general(left, right, dims, precision=precision, preferred_element...  15.9 us
    pallas_call x4, Pallas kernels, absorb(): pl.pallas_call(functools.partial(absorb_kernel, [at for _, at in blocks],...  14.2 us
    pallas_call x10, Pallas kernels, call(): pl.pallas_call(kernel, out_shape=out_shapes, in_specs=[SCALARS] + [WHOLE]...  12.2 us
    pallas_call x1, Pallas kernels, project(): pl.pallas_call(project_kernel, out_shape=jax.ShapeDtypeStruct((tokens + c...  9.5 us
    pallas_call x1, Pallas kernels, factor_inverse(): pl.pallas_call(halves_kernel, out_shape=jax.ShapeDtypeStruct((comp, comp)...  8.42 us
    ppermute x3, waiting for transfers between devices, other_core(): return lax.ppermute(value, 'hid', [(0, 1), (1, 0)])  4.65 us
  transfers between devices with their start and end apart: 30, of which 16 were waited for; matrix products, arithmetic and copies ran while one was open for 7% of the time, Pallas kernels for 15%

profile of v9, /device:TPU:0, one launch (start us, length us, event | category | flops | bytes accessed | tf_op | source)
XLA Modules:
  0.0 194.9 jit_solution(5981929132573305239)
XLA Ops:
  0.6 9.5 %shard_map.59.mine_ref = f32[768,256]{1,0:T(8,128)S(1)} custom-call(bf16[512,7168]{1,0:T(8,128)(2,1)} %acts_ref.9, f32[7168,256]{1,0:T(8,128)} %dict_ref.1), custom_call_target="tpu_custom_call" | custom-call | flops 3758096384 | bytes 14680064 | tf_op jit(solution)/shard_map/pallas_call | solution.py:58
  10.7 0.7 fusion.26.core_ref.table_ref
  11.4 1.2 collective-permute-done.theirs_ref
  12.6 2.0 %shard_map.60 = (f32[512,256]{1,0:T(8,128)S(1)}, bf16[512,256]{1,0:T(8,128)(2,1)S(1)}, f32[128,256]{1,0:T(8,128)S(1)}) custom-call(s32[22]{0:T(128)S(1)} %fusion.26.core_ref.table_ref, f32[512,256]{1,0:T(8,128)S(1)} %copy-done, f32[768,256]{1,0:T(8,128)S(1)} %shard_map.59.mine_ref, f32[768,256]{1,0:T(8,128)S(1)} %collective-permute-done.theirs_ref), custom_call_target="tpu_custom_call" | custom-call | tf_op jit(solution)/shard_map/pallas_call | solution.py:177
  14.6 1.7 fusion.6.top_ref
  16.3 1.9 fusion.2.refs_0_
  18.2 3.0 %collective-permute-start.3 = (f32[1280,256]{1,0:T(8,128)S(1)}, f32[1280,256]{1,0:T(8,128)}, u32[]{:S(2)}, u32[]{:S(2)}) collective-permute-start(f32[1280,256]{1,0:T(8,128)S(1)} %fusion.2.refs_0_), channel_id=1, source_target_pairs={{0,8},{1,9},{2,10},{3,11},{4,12},{5,13},{6,14},{7,15},{8,0},{9,1},... | collective-permute-start | bytes 3932168 | tf_op jit(solution)/shard_map/ppermute | solution.py:369
  21.2 1.6 shard_map.61
  22.8 1.5 collective-permute-start.1
  24.3 2.9 %fusion = f32[1280,256]{1,0:T(8,128)} fusion(bf16[512,256]{1,0:T(8,128)(2,1)S(1)} %get-tuple-element.20, bf16[512,7168]{1,0:T(8,128)(2,1)} %acts_ref.9, s32[]{:T(128)S(6)} %select_n.133), kind=kOutput, calls=%fused_computation | convolution fusion | flops 335544320 | bytes 2883588 | tf_op jit(solution)/shard_map/dot_general | solution.py:21
  27.3 0.5 collective-permute-start.2
  27.8 1.4 fusion.14.mine_ref
  29.2 1.5 fusion.10.mine_ref
  30.6 1.5 fusion.12.mine_ref
  32.1 7.2 %collective-permute-done.1.theirs_ref = f32[1152,256]{1,0:T(8,128)} collective-permute-done((f32[1152,256]{1,0:T(8,128)}, f32[1152,256]{1,0:T(8,128)}, u32[]{:S(2)}, u32[]{:S(2)}) %collective-permute-start.1) | collective-permute-done | bytes 1179680 | tf_op jit(solution)/shard_map/ppermute | solution.py:369
  39.4 1.0 slice_add_fusion.refs_0_.gram_ref
  40.3 10.0 %collective-permute-done.3.theirs_ref = f32[1280,256]{1,0:T(8,128)} collective-permute-done((f32[1280,256]{1,0:T(8,128)S(1)}, f32[1280,256]{1,0:T(8,128)}, u32[]{:S(2)}, u32[]{:S(2)}) %collective-permute-start.3) | collective-permute-done | bytes 1310752 | tf_op jit(solution)/shard_map/ppermute | solution.py:369
  50.4 1.4 shard_map.62.refs_0_
  51.8 1.5 collective-permute-done.2.theirs_ref
  53.3 0.6 shard_map.63.refs_1_
  53.9 2.2 %shard_map.64 = f32[640,256]{1,0:T(8,128)} custom-call(s32[22]{0:T(128)S(1)} %fusion.26.core_ref.table_ref, f32[512,256]{1,0:T(8,128)S(1)} %fusion.14.mine_ref, f32[1152,256]{1,0:T(8,128)} %collective-permute-done.1.theirs_ref, f32[128,256]{1,0:T(8,128)S(1)} %slice_add_fusion.refs_0_.gram_ref, f32[640,256]{1,0:T(8,128)S(1)} %shard_map.63.refs_1_), custom_call_target="tpu_custom_call" | custom-call | tf_op jit(solution)/shard_map/pallas_call | solution.py:209
  56.1 1.5 collective-permute-start.4
  58.1 1.5 collective-permute-start.8
  59.6 1.5 convolution_add_fusion.2.mine_ref
  61.1 12.2 %collective-permute-done.4.theirs_ref = f32[640,256]{1,0:T(8,128)} collective-permute-done((f32[640,256]{1,0:T(8,128)}, f32[640,256]{1,0:T(8,128)}, u32[]{:S(2)}, u32[]{:S(2)}) %collective-permute-start.4) | collective-permute-done | bytes 655392 | tf_op jit(solution)/shard_map/ppermute | solution.py:369
  73.3 1.2 shard_map.65
  75.0 1.7 fusion.5
  76.7 2.0 %collective-permute-start.11 = (f32[320,256]{1,0:T(8,128)S(1)}, f32[320,256]{1,0:T(8,128)S(1)}, u32[]{:S(2)}, u32[]{:S(2)}) collective-permute-start(f32[320,256]{1,0:T(8,128)S(1)} %constant_dynamic-slice_fusion.1), channel_id=1, source_target_pairs={{0,4},{1,3},{2,6},{3,1},{4,0},{5,7},{6,2},{7,5},{8,12},{9,11},{10,... | collective-permute-start | bytes 983048 | tf_op jit(solution)/shard_map/ppermute | solution.py:369
  78.7 1.9 fusion.4
  80.8 2.7 %collective-permute-done.5.theirs_ref = f32[384,256]{1,0:T(8,128)S(1)} collective-permute-done((f32[384,256]{1,0:T(8,128)S(1)}, f32[384,256]{1,0:T(8,128)S(1)}, u32[]{:S(2)}, u32[]{:S(2)}) %collective-permute-start.5) | collective-permute-done | bytes 393248 | tf_op jit(solution)/shard_map/ppermute | solution.py:369
  83.5 0.6 shard_map.66
  84.1 4.7 %collective-permute-start.6 = (f32[256,256]{1,0:T(8,128)S(1)}, f32[256,256]{1,0:T(8,128)S(1)}, u32[]{:S(2)}, u32[]{:S(2)}) collective-permute-start(f32[256,256]{1,0:T(8,128)S(1)} %get-tuple-element.25), channel_id=1, source_target_pairs={{0,16},{1,17},{2,18},{3,19},{4,20},{5,21},{6,22},{7,23},{8,24},{9,... | collective-permute-start | bytes 786440 | tf_op jit(solution)/shard_map/ppermute | solution.py:369
  89.0 8.6 %collective-permute-done.6.theirs_ref = f32[256,256]{1,0:T(8,128)S(1)} collective-permute-done((f32[256,256]{1,0:T(8,128)S(1)}, f32[256,256]{1,0:T(8,128)S(1)}, u32[]{:S(2)}, u32[]{:S(2)}) %collective-permute-start.6) | collective-permute-done | bytes 262176 | tf_op jit(solution)/shard_map/ppermute | solution.py:369
  97.6 0.6 shard_map.67
  98.5 1.2 collective-permute-done.7.theirs_ref
  99.6 8.4 %shard_map.68.inverse_ref = f32[256,256]{1,0:T(8,128)S(1)} custom-call(s32[22]{0:T(128)S(1)} %fusion.26.core_ref.table_ref, f32[128,256]{1,0:T(8,128)S(1)} %get-tuple-element.26.mine_ref, f32[128,256]{1,0:T(8,128)S(1)} %collective-permute-done.7.theirs_ref, f32[160,256]{1,0:T(8,128)S(1)} %get-tuple-element.39.refs_0_.mine_ref, ...), custom_call_target="tpu_custom_call" | custom-call | flops 10000000000 | bytes 524288 | tf_op jit(solution)/shard_map/pallas_call | solution.py:123
  108.0 1.3 collective-permute-done.12.refs_0_
  109.4 1.4 shard_map.69.refs_1_.refs_0_
  110.8 1.4 shard_map.70.refs_1_
  112.7 2.5 %collective-permute-start.13 = (f32[160,256]{1,0:T(8,128)S(1)}, f32[160,256]{1,0:T(8,128)S(1)}, u32[]{:S(2)}, u32[]{:S(2)}) collective-permute-start(f32[160,256]{1,0:T(8,128)S(1)} %shard_map.69.refs_1_.refs_0_), channel_id=1, source_target_pairs={{0,16},{1,17},{2,18},{3,19},{4,20},{5,21},{6,22},{7,23},{8,24},{9,... | collective-permute-start | bytes 491528 | tf_op jit(solution)/shard_map/ppermute | solution.py:369
  115.2 11.5 %collective-permute-done.18 = f32[160,256]{1,0:T(8,128)S(1)} collective-permute-done((f32[160,256]{1,0:T(8,128)S(1)}, f32[160,256]{1,0:T(8,128)S(1)}, u32[]{:S(2)}, u32[]{:S(2)}) %collective-permute-start.18) | collective-permute-done | bytes 163872 | tf_op jit(solution)/shard_map/ppermute | solution.py:369
  126.7 1.9 collective-permute-start.19
  128.6 1.3 shard_map.71
  130.0 1.7 collective-permute-start.14
  131.8 4.3 %collective-permute-done.22 = f32[128,256]{1,0:T(8,128)S(1)} collective-permute-done((f32[128,256]{1,0:T(8,128)S(1)}, f32[128,256]{1,0:T(8,128)S(1)}, u32[]{:S(2)}, u32[]{:S(2)}) %collective-permute-start.22) | collective-permute-done | bytes 131104 | tf_op jit(solution)/shard_map/ppermute | solution.py:369
  136.3 2.1 %collective-permute-start.20 = (f32[640,256]{1,0:T(8,128)S(1)}, f32[640,256]{1,0:T(8,128)S(1)}, u32[]{:S(2)}, u32[]{:S(2)}) collective-permute-start(f32[640,256]{1,0:T(8,128)S(1)} %maximum_select_fusion.1.refs_2_), channel_id=1, source_target_pairs={{0,8},{1,9},{2,10},{3,11},{4,12},{5,13},{6,14},{7,15},{8,0},{9,1},... | collective-permute-start | bytes 1966088 | tf_op jit(solution)/shard_map/ppermute | solution.py:369
  138.4 1.3 collective-permute-start.15
  139.6 5.8 %collective-permute-done.23 = f32[256,256]{1,0:T(8,128)S(1)} collective-permute-done((f32[256,256]{1,0:T(8,128)S(1)}, f32[256,256]{1,0:T(8,128)S(1)}, u32[]{:S(2)}, u32[]{:S(2)}) %collective-permute-start.23) | collective-permute-done | bytes 262176 | tf_op jit(solution)/shard_map/ppermute | solution.py:369
  145.5 1.3 collective-permute-start.28
  146.7 1.8 collective-permute-start.24
  148.5 1.4 collective-permute-start.27
  149.9 10.3 %collective-permute-done.28.refs_2_ = f32[512,256]{1,0:T(8,128)S(1)} collective-permute-done((f32[512,256]{1,0:T(8,128)S(1)}, f32[512,256]{1,0:T(8,128)S(1)}, u32[]{:S(2)}, u32[]{:S(2)}) %collective-permute-start.28) | collective-permute-done | bytes 524320 | tf_op jit(solution)/shard_map/ppermute | solution.py:369
  160.3 0.8 collective-permute-start.26
  161.1 1.4 collective-permute-start.21
  162.6 0.9 collective-permute-start.16
  163.5 0.8 collective-permute-start.25
  164.3 5.1 %shard_map.72 = (f32[768,256]{1,0:T(8,128)S(1)}, f32[7168,256]{1,0:T(8,128)}) custom-call(s32[22]{0:T(128)S(1)} %fusion.26.core_ref.table_ref, bf16[512,7168]{1,0:T(8,128)(2,1)} %acts_ref.9, f32[640,256]{1,0:T(8,128)S(1)} %maximum_select_fusion.refs_0_, f32[640,256]{1,0:T(8,128)S(1)} %collective-permute-done.15.refs_1_, ...), custom_call_target="tpu_custom_call" | custom-call | flops 1409286144 | bytes 11010048 | tf_op jit(solution)/shard_map/pallas_call | solution.py:338
  169.5 8.5 %collective-permute-done.26.refs_0_ = f32[640,256]{1,0:T(8,128)S(1)} collective-permute-done((f32[640,256]{1,0:T(8,128)S(1)}, f32[640,256]{1,0:T(8,128)S(1)}, u32[]{:S(2)}, u32[]{:S(2)}) %collective-permute-start.26) | collective-permute-done | bytes 655392 | tf_op jit(solution)/shard_map/ppermute | solution.py:369
  177.9 3.7 %shard_map.73 = (f32[768,256]{1,0:T(8,128)S(1)}, f32[7168,256]{1,0:T(8,128)}) custom-call(s32[22]{0:T(128)S(1)} %fusion.26.core_ref.table_ref, bf16[512,7168]{1,0:T(8,128)(2,1)} %acts_ref.9, f32[640,256]{1,0:T(8,128)S(1)} %collective-permute-done.26.refs_0_, ...), custom_call_target="tpu_custom_call", output_to_operand_aliasing={{0}: (5, {}), {1}: (6, {})} | custom-call | flops 704643072 | bytes 5505024 | tf_op jit(solution)/shard_map/pallas_call | solution.py:338
  181.6 3.0 %shard_map.74 = (f32[768,256]{1,0:T(8,128)S(1)}, f32[7168,256]{1,0:T(8,128)}) custom-call(s32[22]{0:T(128)S(1)} %fusion.26.core_ref.table_ref, bf16[512,7168]{1,0:T(8,128)(2,1)} %acts_ref.9, f32[640,256]{1,0:T(8,128)S(1)} %collective-permute-done.21.refs_0_, ...), custom_call_target="tpu_custom_call", output_to_operand_aliasing={{0}: (4, {}), {1}: (5, {})} | custom-call | flops 452984832 | bytes 3538944 | tf_op jit(solution)/shard_map/pallas_call | solution.py:338
  184.6 3.6 %collective-permute-done.16.refs_0_ = f32[640,256]{1,0:T(8,128)S(1)} collective-permute-done((f32[640,256]{1,0:T(8,128)S(1)}, f32[640,256]{1,0:T(8,128)S(1)}, u32[]{:S(2)}, u32[]{:S(2)}) %collective-permute-start.16) | collective-permute-done | bytes 655392 | tf_op jit(solution)/shard_map/ppermute | solution.py:369
  188.2 2.4 %shard_map.75 = (f32[768,256]{1,0:T(8,128)S(1)}, f32[7168,256]{1,0:T(8,128)}) custom-call(s32[22]{0:T(128)S(1)} %fusion.26.core_ref.table_ref, bf16[512,7168]{1,0:T(8,128)(2,1)} %acts_ref.9, f32[640,256]{1,0:T(8,128)S(1)} %collective-permute-done.16.refs_0_, f32[768,256]{1,0:T(8,128)S(1)} %get-tuple-element.32.refs_1_, ...), custom_call_target="tpu_custom_call", output_to_operand_aliasing={{0}: (3, {}), {1}: (4, {})} | custom-call | flops 251658240 | bytes 1966080 | tf_op jit(solution)/shard_map/pallas_call | solution.py:338
  190.7 2.3 %collective-permute-done.29.theirs_ref = f32[768,256]{1,0:T(8,128)S(1)} collective-permute-done((f32[768,256]{1,0:T(8,128)S(1)}, f32[768,256]{1,0:T(8,128)S(1)}, u32[]{:S(2)}, u32[]{:S(2)}) %collective-permute-start.29) | collective-permute-done | bytes 786464 | tf_op jit(solution)/shard_map/ppermute | solution.py:402
  192.9 2.0 %shard_map.76 = f32[512,256]{1,0:T(8,128)} custom-call(f32[512,256]{1,0:T(8,128)S(1)} %get-tuple-element.19.codes_ref, f32[768,256]{1,0:T(8,128)S(1)} %get-tuple-element.34.mine_ref, f32[768,256]{1,0:T(8,128)S(1)} %collective-permute-done.29.theirs_ref), custom_call_target="tpu_custom_call" | custom-call | tf_op jit(solution)/shard_map/pallas_call | solution.py:195
  (41 shorter events, 3.1 us)
Async XLA Ops:
  0.6 12.0 %copy-start = (f32[512,256]{1,0:T(8,128)S(1)}, f32[512,256]{1,0:T(8,128)}, u32[]{:S(2)}) copy-start(f32[512,256]{1,0:T(8,128)} %codes_ref.1) | copy-start | bytes 1572868
  10.1 2.4 %collective-permute-start = (f32[768,256]{1,0:T(8,128)S(1)}, f32[768,256]{1,0:T(8,128)S(1)}, u32[]{:S(2)}, u32[]{:S(2)}) collective-permute-start(f32[768,256]{1,0:T(8,128)S(1)} %shard_map.59.mine_ref), channel_id=1, source_target_pairs={{0,1},{1,0},{2,3},{3,2},{4,5},{5,4},{6,7},{7,6},{8,9},{9,8},{10,11... | collective-permute-start | bytes 2359304 | tf_op jit(solution)/shard_map/ppermute | solution.py:402
  14.6 9.8 %copy-start.1 = (f32[128,256]{1,0:T(8,128)}, f32[128,256]{1,0:T(8,128)S(1)}, u32[]{:S(2)}) copy-start(f32[128,256]{1,0:T(8,128)S(1)} %get-tuple-element.21.rest_ref) | copy-start | bytes 393220
  18.2 32.2 %collective-permute-start.3 = (f32[1280,256]{1,0:T(8,128)S(1)}, f32[1280,256]{1,0:T(8,128)}, u32[]{:S(2)}, u32[]{:S(2)}) collective-permute-start(f32[1280,256]{1,0:T(8,128)S(1)} %fusion.2.refs_0_), channel_id=1, source_target_pairs={{0,8},{1,9},{2,10},{3,11},{4,12},{5,13},{6,14},{7,15},{8,0},{9,1},... | collective-permute-start | bytes 3932168 | tf_op jit(solution)/shard_map/ppermute | solution.py:369
  22.8 16.5 %collective-permute-start.1 = (f32[1152,256]{1,0:T(8,128)}, f32[1152,256]{1,0:T(8,128)}, u32[]{:S(2)}, u32[]{:S(2)}) collective-permute-start(f32[1152,256]{1,0:T(8,128)} %shard_map.61), channel_id=1, source_target_pairs={{0,2},{1,5},{2,0},{3,7},{4,6},{5,1},{6,4},{7,3},{8,10},{9,13},{10,... | collective-permute-start | bytes 3538952 | tf_op jit(solution)/shard_map/ppermute | solution.py:369
  27.3 26.0 %collective-permute-start.2 = (f32[1280,256]{1,0:T(8,128)}, f32[1280,256]{1,0:T(8,128)S(1)}, u32[]{:S(2)}, u32[]{:S(2)}) collective-permute-start(f32[1280,256]{1,0:T(8,128)} %fusion), channel_id=1, source_target_pairs={{0,2},{1,5},{2,0},{3,7},{4,6},{5,1},{6,4},{7,3},{8,10},{9,13},{10,... | collective-permute-start | bytes 3932168 | tf_op jit(solution)/shard_map/ppermute | solution.py:369
  56.1 17.2 %collective-permute-start.4 = (f32[640,256]{1,0:T(8,128)}, f32[640,256]{1,0:T(8,128)}, u32[]{:S(2)}, u32[]{:S(2)}) collective-permute-start(f32[640,256]{1,0:T(8,128)} %shard_map.64), channel_id=1, source_target_pairs={{0,4},{1,3},{2,6},{3,1},{4,0},{5,7},{6,2},{7,5},{8,12},{9,11},{10,... | collective-permute-start | bytes 1966088 | tf_op jit(solution)/shard_map/ppermute | solution.py:369
  57.6 17.4 %collective-permute-start.10 = (f32[640,256]{1,0:T(8,128)S(1)}, f32[640,256]{1,0:T(8,128)}, u32[]{:S(2)}, u32[]{:S(2)}) collective-permute-start(f32[640,256]{1,0:T(8,128)S(1)} %shard_map.63.refs_1_), channel_id=1, source_target_pairs={{0,8},{1,9},{2,10},{3,11},{4,12},{5,13},{6,14},{7,15},{8,0},{9,1},... | collective-permute-start | bytes 1966088 | tf_op jit(solution)/shard_map/ppermute | solution.py:369
  58.1 20.6 %collective-permute-start.8 = (f32[640,256]{1,0:T(8,128)S(1)}, f32[640,256]{1,0:T(8,128)}, u32[]{:S(2)}, u32[]{:S(2)}) collective-permute-start(f32[640,256]{1,0:T(8,128)S(1)} %shard_map.62.refs_0_), channel_id=1, source_target_pairs={{0,2},{1,5},{2,0},{3,7},{4,6},{5,1},{6,4},{7,3},{8,10},{9,13},{10,... | collective-permute-start | bytes 1966088 | tf_op jit(solution)/shard_map/ppermute | solution.py:369
  74.5 9.0 %collective-permute-start.5 = (f32[384,256]{1,0:T(8,128)S(1)}, f32[384,256]{1,0:T(8,128)S(1)}, u32[]{:S(2)}, u32[]{:S(2)}) collective-permute-start(f32[384,256]{1,0:T(8,128)S(1)} %get-tuple-element.23), channel_id=1, source_target_pairs={{0,8},{1,9},{2,10},{3,11},{4,12},{5,13},{6,14},{7,15},{8,0},{9,1},... | collective-permute-start | bytes 1179656 | tf_op jit(solution)/shard_map/ppermute | solution.py:369
  76.7 12.1 %collective-permute-start.11 = (f32[320,256]{1,0:T(8,128)S(1)}, f32[320,256]{1,0:T(8,128)S(1)}, u32[]{:S(2)}, u32[]{:S(2)}) collective-permute-start(f32[320,256]{1,0:T(8,128)S(1)} %constant_dynamic-slice_fusion.1), channel_id=1, source_target_pairs={{0,4},{1,3},{2,6},{3,1},{4,0},{5,7},{6,2},{7,5},{8,12},{9,11},{10,... | collective-permute-start | bytes 983048 | tf_op jit(solution)/shard_map/ppermute | solution.py:369
  80.6 17.7 %collective-permute-start.9 = (f32[320,256]{1,0:T(8,128)S(1)}, f32[320,256]{1,0:T(8,128)S(1)}, u32[]{:S(2)}, u32[]{:S(2)}) collective-permute-start(f32[320,256]{1,0:T(8,128)S(1)} %constant_dynamic-slice_fusion.3), channel_id=1, source_target_pairs={{0,4},{1,3},{2,6},{3,1},{4,0},{5,7},{6,2},{7,5},{8,12},{9,11},{10,... | collective-permute-start | bytes 983048 | tf_op jit(solution)/shard_map/ppermute | solution.py:369
  84.1 13.5 %collective-permute-start.6 = (f32[256,256]{1,0:T(8,128)S(1)}, f32[256,256]{1,0:T(8,128)S(1)}, u32[]{:S(2)}, u32[]{:S(2)}) collective-permute-start(f32[256,256]{1,0:T(8,128)S(1)} %get-tuple-element.25), channel_id=1, source_target_pairs={{0,16},{1,17},{2,18},{3,19},{4,20},{5,21},{6,22},{7,23},{8,24},{9,... | collective-permute-start | bytes 786440 | tf_op jit(solution)/shard_map/ppermute | solution.py:369
  88.9 21.9 %collective-permute-start.17 = (f32[160,256]{1,0:T(8,128)S(1)}, f32[160,256]{1,0:T(8,128)S(1)}, u32[]{:S(2)}, u32[]{:S(2)}) collective-permute-start(f32[160,256]{1,0:T(8,128)S(1)} %get-tuple-element.36), channel_id=1, source_target_pairs={{0,16},{1,17},{2,18},{3,19},{4,20},{5,21},{6,22},{7,23},{8,24},{9,... | collective-permute-start | bytes 491528 | tf_op jit(solution)/shard_map/ppermute | solution.py:369
  98.2 1.4 collective-permute-start.7
  98.4 11.0 %collective-permute-start.12 = (f32[160,256]{1,0:T(8,128)S(1)}, f32[160,256]{1,0:T(8,128)S(1)}, u32[]{:S(2)}, u32[]{:S(2)}) collective-permute-start(f32[160,256]{1,0:T(8,128)S(1)} %get-tuple-element.38), channel_id=1, source_target_pairs={{0,16},{1,17},{2,18},{3,19},{4,20},{5,21},{6,22},{7,23},{8,24},{9,... | collective-permute-start | bytes 491528 | tf_op jit(solution)/shard_map/ppermute | solution.py:369
  112.2 14.5 %collective-permute-start.18 = (f32[160,256]{1,0:T(8,128)S(1)}, f32[160,256]{1,0:T(8,128)S(1)}, u32[]{:S(2)}, u32[]{:S(2)}) collective-permute-start(f32[160,256]{1,0:T(8,128)S(1)} %shard_map.70.refs_1_), channel_id=1, source_target_pairs={{0,16},{1,17},{2,18},{3,19},{4,20},{5,21},{6,22},{7,23},{8,24},{9,... | collective-permute-start | bytes 491528 | tf_op jit(solution)/shard_map/ppermute | solution.py:369
  112.7 17.3 %collective-permute-start.13 = (f32[160,256]{1,0:T(8,128)S(1)}, f32[160,256]{1,0:T(8,128)S(1)}, u32[]{:S(2)}, u32[]{:S(2)}) collective-permute-start(f32[160,256]{1,0:T(8,128)S(1)} %shard_map.69.refs_1_.refs_0_), channel_id=1, source_target_pairs={{0,16},{1,17},{2,18},{3,19},{4,20},{5,21},{6,22},{7,23},{8,24},{9,... | collective-permute-start | bytes 491528 | tf_op jit(solution)/shard_map/ppermute | solution.py:369
  126.7 9.5 %collective-permute-start.19 = (f32[320,256]{1,0:T(8,128)S(1)}, f32[320,256]{1,0:T(8,128)S(1)}, u32[]{:S(2)}, u32[]{:S(2)}) collective-permute-start(f32[320,256]{1,0:T(8,128)S(1)} %maximum_select_fusion.4), channel_id=1, source_target_pairs={{0,4},{1,3},{2,6},{3,1},{4,0},{5,7},{6,2},{7,5},{8,12},{9,11},{10,... | collective-permute-start | bytes 983048 | tf_op jit(solution)/shard_map/ppermute | solution.py:369
  129.9 6.2 %collective-permute-start.22 = (f32[128,256]{1,0:T(8,128)S(1)}, f32[128,256]{1,0:T(8,128)S(1)}, u32[]{:S(2)}, u32[]{:S(2)}) collective-permute-start(f32[128,256]{1,0:T(8,128)S(1)} %shard_map.71), channel_id=1, source_target_pairs={{0,16},{1,17},{2,18},{3,19},{4,20},{5,21},{6,22},{7,23},{8,24},{9,... | collective-permute-start | bytes 393224 | tf_op jit(solution)/shard_map/ppermute | solution.py:369
  130.0 8.3 %collective-permute-start.14 = (f32[320,256]{1,0:T(8,128)S(1)}, f32[320,256]{1,0:T(8,128)S(1)}, u32[]{:S(2)}, u32[]{:S(2)}) collective-permute-start(f32[320,256]{1,0:T(8,128)S(1)} %maximum_select_fusion.3), channel_id=1, source_target_pairs={{0,4},{1,3},{2,6},{3,1},{4,0},{5,7},{6,2},{7,5},{8,12},{9,11},{10,... | collective-permute-start | bytes 983048 | tf_op jit(solution)/shard_map/ppermute | solution.py:369
  136.1 9.3 %collective-permute-start.23 = (f32[256,256]{1,0:T(8,128)S(1)}, f32[256,256]{1,0:T(8,128)S(1)}, u32[]{:S(2)}, u32[]{:S(2)}) collective-permute-start(f32[256,256]{1,0:T(8,128)S(1)} %maximum_select_fusion.5), channel_id=1, source_target_pairs={{0,8},{1,9},{2,10},{3,11},{4,12},{5,13},{6,14},{7,15},{8,0},{9,1},... | collective-permute-start | bytes 786440 | tf_op jit(solution)/shard_map/ppermute | solution.py:369
  136.3 24.9 %collective-permute-start.20 = (f32[640,256]{1,0:T(8,128)S(1)}, f32[640,256]{1,0:T(8,128)S(1)}, u32[]{:S(2)}, u32[]{:S(2)}) collective-permute-start(f32[640,256]{1,0:T(8,128)S(1)} %maximum_select_fusion.1.refs_2_), channel_id=1, source_target_pairs={{0,8},{1,9},{2,10},{3,11},{4,12},{5,13},{6,14},{7,15},{8,0},{9,1},... | collective-permute-start | bytes 1966088 | tf_op jit(solution)/shard_map/ppermute | solution.py:369
  138.4 24.2 %collective-permute-start.15 = (f32[640,256]{1,0:T(8,128)S(1)}, f32[640,256]{1,0:T(8,128)S(1)}, u32[]{:S(2)}, u32[]{:S(2)}) collective-permute-start(f32[640,256]{1,0:T(8,128)S(1)} %maximum_select_fusion.refs_0_), channel_id=1, source_target_pairs={{0,2},{1,5},{2,0},{3,7},{4,6},{5,1},{6,4},{7,3},{8,10},{9,13},{10,... | collective-permute-start | bytes 1966088 | tf_op jit(solution)/shard_map/ppermute | solution.py:369
  145.5 14.8 %collective-permute-start.28 = (f32[512,256]{1,0:T(8,128)S(1)}, f32[512,256]{1,0:T(8,128)S(1)}, u32[]{:S(2)}, u32[]{:S(2)}) collective-permute-start(f32[512,256]{1,0:T(8,128)S(1)} %maximum_select_fusion.2.refs_4_), channel_id=1, source_target_pairs={{0,2},{1,5},{2,0},{3,7},{4,6},{5,1},{6,4},{7,3},{8,10},{9,13},{10,... | collective-permute-start | bytes 1572872 | tf_op jit(solution)/shard_map/ppermute | solution.py:369
  146.7 16.8 %collective-permute-start.24 = (f32[512,256]{1,0:T(8,128)S(1)}, f32[512,256]{1,0:T(8,128)S(1)}, u32[]{:S(2)}, u32[]{:S(2)}) collective-permute-start(f32[512,256]{1,0:T(8,128)S(1)} %maximum_select_fusion.2.refs_4_), channel_id=1, source_target_pairs={{0,4},{1,3},{2,6},{3,1},{4,0},{5,7},{6,2},{7,5},{8,12},{9,11},{10,... | collective-permute-start | bytes 1572872 | tf_op jit(solution)/shard_map/ppermute | solution.py:369
  148.5 21.0 %collective-permute-start.27 = (f32[640,256]{1,0:T(8,128)S(1)}, f32[640,256]{1,0:T(8,128)S(1)}, u32[]{:S(2)}, u32[]{:S(2)}) collective-permute-start(f32[640,256]{1,0:T(8,128)S(1)} %maximum_select_fusion.1.refs_2_), channel_id=1, source_target_pairs={{0,2},{1,5},{2,0},{3,7},{4,6},{5,1},{6,4},{7,3},{8,10},{9,13},{10,... | collective-permute-start | bytes 1966088 | tf_op jit(solution)/shard_map/ppermute | solution.py:369
  160.3 17.7 %collective-permute-start.26 = (f32[640,256]{1,0:T(8,128)S(1)}, f32[640,256]{1,0:T(8,128)S(1)}, u32[]{:S(2)}, u32[]{:S(2)}) collective-permute-start(f32[640,256]{1,0:T(8,128)S(1)} %maximum_select_fusion.refs_0_), channel_id=1, source_target_pairs={{0,8},{1,9},{2,10},{3,11},{4,12},{5,13},{6,14},{7,15},{8,0},{9,1},... | collective-permute-start | bytes 1966088 | tf_op jit(solution)/shard_map/ppermute | solution.py:369
  161.1 20.5 %collective-permute-start.21 = (f32[640,256]{1,0:T(8,128)S(1)}, f32[640,256]{1,0:T(8,128)S(1)}, u32[]{:S(2)}, u32[]{:S(2)}) collective-permute-start(f32[640,256]{1,0:T(8,128)S(1)} %collective-permute-done.20.refs_3_), channel_id=1, source_target_pairs={{0,2},{1,5},{2,0},{3,7},{4,6},{5,1},{6,4},{7,3},{8,10},{9,13},{10,... | collective-permute-start | bytes 1966088 | tf_op jit(solution)/shard_map/ppermute | solution.py:369
  162.6 25.6 %collective-permute-start.16 = (f32[640,256]{1,0:T(8,128)S(1)}, f32[640,256]{1,0:T(8,128)S(1)}, u32[]{:S(2)}, u32[]{:S(2)}) collective-permute-start(f32[640,256]{1,0:T(8,128)S(1)} %collective-permute-done.15.refs_1_), channel_id=1, source_target_pairs={{0,8},{1,9},{2,10},{3,11},{4,12},{5,13},{6,14},{7,15},{8,0},{9,1},... | collective-permute-start | bytes 1966088 | tf_op jit(solution)/shard_map/ppermute | solution.py:369
  163.5 18.1 %collective-permute-start.25 = (f32[512,256]{1,0:T(8,128)S(1)}, f32[512,256]{1,0:T(8,128)S(1)}, u32[]{:S(2)}, u32[]{:S(2)}) collective-permute-start(f32[512,256]{1,0:T(8,128)S(1)} %collective-permute-done.24.refs_5_), channel_id=1, source_target_pairs={{0,2},{1,5},{2,0},{3,7},{4,6},{5,1},{6,4},{7,3},{8,10},{9,13},{10,... | collective-permute-start | bytes 1572872 | tf_op jit(solution)/shard_map/ppermute | solution.py:369
  190.6 2.4 %collective-permute-start.29 = (f32[768,256]{1,0:T(8,128)S(1)}, f32[768,256]{1,0:T(8,128)S(1)}, u32[]{:S(2)}, u32[]{:S(2)}) collective-permute-start(f32[768,256]{1,0:T(8,128)S(1)} %get-tuple-element.34.mine_ref), channel_id=1, source_target_pairs={{0,1},{1,0},{2,3},{3,2},{4,5},{5,4},{6,7},{7,6},{8,9},{9,8},{10,11... | collective-permute-start | bytes 2359304 | tf_op jit(solution)/shard_map/ppermute | solution.py:402

commit v10 on v9

--- a/solution.py
+++ b/solution.py
@@ -236,32 +236,19 @@
     return call(functools.partial(first_fold_kernel, at), [half, half], table, [mine, theirs, gram], [])
 
 
-def mixed_fold_kernel(at, extra, table_ref, mine_ref, theirs_ref, give_ref, keep_ref):
-    whole = mine_ref.shape[0] - extra
-    rows = whole // 2
+def split_fold_kernel(at, table_ref, mine_ref, theirs_ref, give_ref, keep_ref, gram_ref):
+    rows = give_ref.shape[0]
     keep = pl.ds(pl.multiple_of(table_ref[at] * rows, rows), rows)
     give = pl.ds(pl.multiple_of((1 - table_ref[at]) * rows, rows), rows)
-    gram = mine_ref[whole:, :] + theirs_ref[whole:, :]
-    give_ref[:rows, :] = mine_ref[give, :] + theirs_ref[give, :]
-    give_ref[rows:, :] = gram
-    keep_ref[:rows, :] = mine_ref[keep, :] + theirs_ref[keep, :]
-    keep_ref[rows:, :] = gram
-
-
-def mixed_fold(table, at, extra, mine, theirs):
-    half = shape((mine.shape[0] - extra) // 2 + extra, mine.shape[1])
-    return call(functools.partial(mixed_fold_kernel, at, extra), [half, half], table, [mine, theirs], [])
-
-
-def part_kernel(table_ref, mine_ref, theirs_ref, rows_ref, rest_ref):
-    rows = rows_ref.shape[0]
-    rows_ref[...] = mine_ref[:rows, :] + theirs_ref[:rows, :]
-    rest_ref[...] = mine_ref[rows:, :] + theirs_ref[rows:, :]
-
-
-def part(table, rows, mine, theirs):
-    shapes = [shape(rows, mine.shape[1]), shape(mine.shape[0] - rows, mine.shape[1])]
-    return call(part_kernel, shapes, table, [mine, theirs], [])
+    give_ref[...] = mine_ref[give, :] + theirs_ref[give, :]
+    keep_ref[...] = mine_ref[keep, :] + theirs_ref[keep, :]
+    gram_ref[...] = mine_ref[2 * rows :, :] + theirs_ref[2 * rows :, :]
+
+
+def split_fold(table, at, extra, mine, theirs):
+    comp = mine.shape[1]
+    half = shape((mine.shape[0] - extra) // 2, comp)
+    return call(functools.partial(split_fold_kernel, at), [half, half, shape(extra, comp)], table, [mine, theirs], [])
 
 
 def take_kernel(at, count, table_ref, mine_ref, theirs_ref, *refs):
@@ -287,17 +274,14 @@
     return call(stack_kernel, [shape(top.shape[0] + rest.shape[0], top.shape[1])], table, [top, rest], after)[0]
 
 
-def rows_kernel(theirs, table_ref, inverse_ref, mine_ref, *refs):
+def rows_kernel(table_ref, inverse_ref, mine_ref, *refs):
     inverse = inverse_ref[...]
-    cross = mine_ref[...]
-    if theirs:
-        cross = cross + refs[0][...]
+    cross = mine_ref[...] + refs[0][...]
     refs[-1][...] = dot(dot(cross, inverse, OVER_COLS, HIGHEST), inverse, precision=HIGHEST)
 
 
 def solve_sum(table, inverse, parts, after):
-    kernel = functools.partial(rows_kernel, len(parts) > 1)
-    return call(kernel, [shape(*parts[0].shape)], table, [inverse, *parts], after)[0]
+    return call(rows_kernel, [shape(*parts[0].shape)], table, [inverse, *parts], after)[0]
 
 
 def absorb_kernel(ats, fresh, table_ref, acts_ref, *refs):
@@ -318,8 +302,12 @@
         outs[k].start()
     proj, gram = (0.0, 0.0) if fresh else (sums_ref[:tokens, :], sums_ref[tokens:, :])
     for k, value in enumerate(values):
-        high = value[...].astype(bf16)
-        gram = gram + dot(high.T, high)
+        block = value[...]
+        high = block.astype(bf16)
+        low = (block - high.astype(f32)).astype(bf16)
+        turned = high.T
+        cross = dot(turned, low)
+        gram = gram + (dot(turned, high) + (cross + cross.T))
         ins[k].wait()
         proj = proj + dot(buffers[k][...], high)
     out_ref[:tokens, :] = proj
@@ -456,15 +444,14 @@
     for name, (keep, arrived) in held.items():
         along = ORDERS[name][3]
         if name == "A":
-            give, keep = mixed_fold(table, where[name, "d"], gram.shape[0], keep, arrived)
+            give, keep, gram = split_fold(table, where[name, "d"], gram.shape[0], keep, arrived)
+            gram = gram + swap(gram, along)
             held[name] = keep, swap(give, along)
         else:
             keep = keep + arrived
             held[name] = part_of(keep, bits[along]), swap(part_of(keep, 1 - bits[along]), along)
 
-    a_mine, gram = part(table, rows["A"] // 16, *held["A"])
     inverse = factor_inverse(table, gram, other_core(gram), [held["N"][0], held["B"][0]])
-    held["A"] = (a_mine,)
     mine = {}
     for name in held:
         mine[name] = solve_sum(table, inverse, held[name], list(mine.values()))

time: 196 us -> 196 us (level)
    ppermute x27 -> x28, starting transfers between devices: 34.6 us -> 35.9 us  [swap(): return lax.ppermute(value, BOTH, flips(ALONG[along]))]
    pallas_call x10 -> x9, Pallas kernels: 12.2 us -> 11.7 us  [call(): pl.pallas_call(kernel, out_shape=out_shapes, in_specs=[SCALARS] + [WHOLE]...]
    ppermute x27 -> x28, waiting for transfers between devices: 87.7 us -> 88 us  [swap(): return lax.ppermute(value, BOTH, flips(ALONG[along]))]
  transfers between devices with their start and end apart: 30 -> 31, of which waited for: 16 -> 15; matrix products, arithmetic and copies ran while one was open for 7% -> 7% of each run, Pallas kernels for 15% -> 15%
where the time goes in v10:
time: 196 us; the launch traced here: 195 us
  waiting for transfers between devices  91.5 us (47%)
  Pallas kernels  48.3 us (25%)
  starting transfers between devices  36.6 us (19%)
  matrix products  15.9 us (8%)
    ppermute x28, waiting for transfers between devices, swap(): return lax.ppermute(value, BOTH, flips(ALONG[along]))  88 us
    ppermute x28, starting transfers between devices, swap(): return lax.ppermute(value, BOTH, flips(ALONG[along]))  35.9 us
    dot_general x9, matrix products, dot(): lax.dot_general(left, right, dims, precision=precision, preferred_element...  15.9 us
    pallas_call x4, Pallas kernels, absorb(): pl.pallas_call(functools.partial(absorb_kernel, [at for _, at in blocks],...  14.8 us
    pallas_call x9, Pallas kernels, call(): pl.pallas_call(kernel, out_shape=out_shapes, in_specs=[SCALARS] + [WHOLE]...  11.7 us
    pallas_call x1, Pallas kernels, project(): pl.pallas_call(project_kernel, out_shape=jax.ShapeDtypeStruct((tokens + c...  9.5 us
    pallas_call x1, Pallas kernels, factor_inverse(): pl.pallas_call(halves_kernel, out_shape=jax.ShapeDtypeStruct((comp, comp)...  8.43 us
  transfers between devices with their start and end apart: 31, of which 15 were waited for; matrix products, arithmetic and copies ran while one was open for 7% of the time, Pallas kernels for 15%

profile of v10, /device:TPU:0, one launch (start us, length us, event | category | flops | bytes accessed | tf_op | source)
XLA Modules:
  0.0 195.4 jit_solution(17967388131344600083)
XLA Ops:
  0.6 9.5 %shard_map.59.mine_ref = f32[768,256]{1,0:T(8,128)S(1)} custom-call(bf16[512,7168]{1,0:T(8,128)(2,1)} %acts_ref.9, f32[7168,256]{1,0:T(8,128)} %dict_ref.1), custom_call_target="tpu_custom_call" | custom-call | flops 3758096384 | bytes 14680064 | tf_op jit(solution)/shard_map/pallas_call | solution.py:58
  10.7 0.7 fusion.26.core_ref.table_ref
  11.4 1.2 collective-permute-done.theirs_ref
  12.6 2.0 %shard_map.60 = (f32[512,256]{1,0:T(8,128)S(1)}, bf16[512,256]{1,0:T(8,128)(2,1)S(1)}, f32[128,256]{1,0:T(8,128)S(1)}) custom-call(s32[22]{0:T(128)S(1)} %fusion.26.core_ref.table_ref, f32[512,256]{1,0:T(8,128)S(1)} %copy-done, f32[768,256]{1,0:T(8,128)S(1)} %shard_map.59.mine_ref, f32[768,256]{1,0:T(8,128)S(1)} %collective-permute-done.theirs_ref), custom_call_target="tpu_custom_call" | custom-call | tf_op jit(solution)/shard_map/pallas_call | solution.py:177
  14.6 1.7 fusion.6.top_ref
  16.3 1.9 fusion.2.refs_0_
  18.2 3.0 %collective-permute-start.3 = (f32[1280,256]{1,0:T(8,128)S(1)}, f32[1280,256]{1,0:T(8,128)}, u32[]{:S(2)}, u32[]{:S(2)}) collective-permute-start(f32[1280,256]{1,0:T(8,128)S(1)} %fusion.2.refs_0_), channel_id=1, source_target_pairs={{0,8},{1,9},{2,10},{3,11},{4,12},{5,13},{6,14},{7,15},{8,0},{9,1},... | collective-permute-start | bytes 3932168 | tf_op jit(solution)/shard_map/ppermute | solution.py:357
  21.2 1.6 shard_map.61
  22.8 1.5 collective-permute-start.1
  24.3 2.9 %fusion = f32[1280,256]{1,0:T(8,128)} fusion(bf16[512,256]{1,0:T(8,128)(2,1)S(1)} %get-tuple-element.19, bf16[512,7168]{1,0:T(8,128)(2,1)} %acts_ref.9, s32[]{:T(128)S(6)} %select_n.133), kind=kOutput, calls=%fused_computation | convolution fusion | flops 335544320 | bytes 2883588 | tf_op jit(solution)/shard_map/dot_general | solution.py:21
  27.3 0.5 collective-permute-start.2
  27.8 1.4 fusion.14.mine_ref
  29.2 1.5 fusion.10.mine_ref
  30.6 1.5 fusion.12.mine_ref
  32.1 7.2 %collective-permute-done.1.theirs_ref = f32[1152,256]{1,0:T(8,128)} collective-permute-done((f32[1152,256]{1,0:T(8,128)}, f32[1152,256]{1,0:T(8,128)}, u32[]{:S(2)}, u32[]{:S(2)}) %collective-permute-start.1) | collective-permute-done | bytes 1179680 | tf_op jit(solution)/shard_map/ppermute | solution.py:357
  39.4 1.0 slice_add_fusion.refs_0_.gram_ref
  40.3 10.0 %collective-permute-done.3.theirs_ref = f32[1280,256]{1,0:T(8,128)} collective-permute-done((f32[1280,256]{1,0:T(8,128)S(1)}, f32[1280,256]{1,0:T(8,128)}, u32[]{:S(2)}, u32[]{:S(2)}) %collective-permute-start.3) | collective-permute-done | bytes 1310752 | tf_op jit(solution)/shard_map/ppermute | solution.py:357
  50.4 1.4 shard_map.62.refs_0_
  51.8 1.5 collective-permute-done.2.theirs_ref
  53.3 0.6 shard_map.63.refs_1_
  53.9 2.2 %shard_map.64 = f32[640,256]{1,0:T(8,128)} custom-call(s32[22]{0:T(128)S(1)} %fusion.26.core_ref.table_ref, f32[512,256]{1,0:T(8,128)S(1)} %fusion.14.mine_ref, f32[1152,256]{1,0:T(8,128)} %collective-permute-done.1.theirs_ref, f32[128,256]{1,0:T(8,128)S(1)} %slice_add_fusion.refs_0_.gram_ref, f32[640,256]{1,0:T(8,128)S(1)} %shard_map.63.refs_1_), custom_call_target="tpu_custom_call" | custom-call | tf_op jit(solution)/shard_map/pallas_call | solution.py:209
  56.1 1.5 collective-permute-start.4
  58.1 1.5 collective-permute-start.8
  59.6 1.5 convolution_add_fusion.2.mine_ref
  61.1 12.2 %collective-permute-done.4.theirs_ref = f32[640,256]{1,0:T(8,128)} collective-permute-done((f32[640,256]{1,0:T(8,128)}, f32[640,256]{1,0:T(8,128)}, u32[]{:S(2)}, u32[]{:S(2)}) %collective-permute-start.4) | collective-permute-done | bytes 655392 | tf_op jit(solution)/shard_map/ppermute | solution.py:357
  73.3 1.2 shard_map.65
  75.0 1.7 fusion.5
  76.7 2.0 %collective-permute-start.11 = (f32[320,256]{1,0:T(8,128)S(1)}, f32[320,256]{1,0:T(8,128)S(1)}, u32[]{:S(2)}, u32[]{:S(2)}) collective-permute-start(f32[320,256]{1,0:T(8,128)S(1)} %constant_dynamic-slice_fusion.1), channel_id=1, source_target_pairs={{0,4},{1,3},{2,6},{3,1},{4,0},{5,7},{6,2},{7,5},{8,12},{9,11},{10,... | collective-permute-start | bytes 983048 | tf_op jit(solution)/shard_map/ppermute | solution.py:357
  78.7 1.9 fusion.4
  80.8 2.7 %collective-permute-done.5.theirs_ref = f32[384,256]{1,0:T(8,128)S(1)} collective-permute-done((f32[384,256]{1,0:T(8,128)S(1)}, f32[384,256]{1,0:T(8,128)S(1)}, u32[]{:S(2)}, u32[]{:S(2)}) %collective-permute-start.5) | collective-permute-done | bytes 393248 | tf_op jit(solution)/shard_map/ppermute | solution.py:357
  83.5 0.6 shard_map.66
  84.1 4.6 %collective-permute-start.6 = (f32[128,256]{1,0:T(8,128)S(1)}, f32[128,256]{1,0:T(8,128)S(1)}, u32[]{:S(2)}, u32[]{:S(2)}) collective-permute-start(f32[128,256]{1,0:T(8,128)S(1)} %get-tuple-element.23), channel_id=1, source_target_pairs={{0,16},{1,17},{2,18},{3,19},{4,20},{5,21},{6,22},{7,23},{8,24},{9,... | collective-permute-start | bytes 393224 | tf_op jit(solution)/shard_map/ppermute | solution.py:357
  88.9 3.2 %collective-permute-done.6 = f32[128,256]{1,0:T(8,128)S(1)} collective-permute-done((f32[128,256]{1,0:T(8,128)S(1)}, f32[128,256]{1,0:T(8,128)S(1)}, u32[]{:S(2)}, u32[]{:S(2)}) %collective-permute-start.6) | collective-permute-done | bytes 131104 | tf_op jit(solution)/shard_map/ppermute | solution.py:357
  92.3 2.7 %collective-permute-start.12 = (f32[160,256]{1,0:T(8,128)S(1)}, f32[160,256]{1,0:T(8,128)S(1)}, u32[]{:S(2)}, u32[]{:S(2)}) collective-permute-start(f32[160,256]{1,0:T(8,128)S(1)} %get-tuple-element.36), channel_id=1, source_target_pairs={{0,16},{1,17},{2,18},{3,19},{4,20},{5,21},{6,22},{7,23},{8,24},{9,... | collective-permute-start | bytes 491528 | tf_op jit(solution)/shard_map/ppermute | solution.py:357
  95.0 8.4 %shard_map.67.inverse_ref = f32[256,256]{1,0:T(8,128)S(1)} custom-call(s32[22]{0:T(128)S(1)} %fusion.26.core_ref.table_ref, f32[128,256]{1,0:T(8,128)S(1)} %add.145.mine_ref, f32[128,256]{1,0:T(8,128)S(1)} %collective-permute-done.7.theirs_ref, f32[160,256]{1,0:T(8,128)S(1)} %get-tuple-element.37.refs_0_.mine_ref, ...), custom_call_target="tpu_custom_call" | custom-call | flops 10000000000 | bytes 524288 | tf_op jit(solution)/shard_map/pallas_call | solution.py:123
  103.4 1.4 shard_map.68.refs_1_
  104.8 1.4 shard_map.69.refs_2_
  106.2 1.2 collective-permute-start.18
  107.4 1.8 collective-permute-start.13
  109.2 1.2 collective-permute-start.22
  110.4 11.9 %collective-permute-done.18 = f32[160,256]{1,0:T(8,128)S(1)} collective-permute-done((f32[160,256]{1,0:T(8,128)S(1)}, f32[160,256]{1,0:T(8,128)S(1)}, u32[]{:S(2)}, u32[]{:S(2)}) %collective-permute-start.18) | collective-permute-done | bytes 163872 | tf_op jit(solution)/shard_map/ppermute | solution.py:357
  122.3 1.1 collective-permute-start.19
  123.4 5.1 %collective-permute-done.22.refs_0_ = f32[128,256]{1,0:T(8,128)S(1)} collective-permute-done((f32[128,256]{1,0:T(8,128)S(1)}, f32[128,256]{1,0:T(8,128)S(1)}, u32[]{:S(2)}, u32[]{:S(2)}) %collective-permute-start.22) | collective-permute-done | bytes 131104 | tf_op jit(solution)/shard_map/ppermute | solution.py:357
  128.5 1.3 shard_map.70
  130.0 1.1 collective-permute-start.14
  131.1 7.2 %collective-permute-done.23 = f32[128,256]{1,0:T(8,128)S(1)} collective-permute-done((f32[128,256]{1,0:T(8,128)S(1)}, f32[128,256]{1,0:T(8,128)S(1)}, u32[]{:S(2)}, u32[]{:S(2)}) %collective-permute-start.23) | collective-permute-done | bytes 131104 | tf_op jit(solution)/shard_map/ppermute | solution.py:357
  138.4 2.1 %collective-permute-start.20 = (f32[640,256]{1,0:T(8,128)S(1)}, f32[640,256]{1,0:T(8,128)S(1)}, u32[]{:S(2)}, u32[]{:S(2)}) collective-permute-start(f32[640,256]{1,0:T(8,128)S(1)} %maximum_select_fusion.1.refs_2_), channel_id=1, source_target_pairs={{0,8},{1,9},{2,10},{3,11},{4,12},{5,13},{6,14},{7,15},{8,0},{9,1},... | collective-permute-start | bytes 1966088 | tf_op jit(solution)/shard_map/ppermute | solution.py:357
  140.6 1.5 collective-permute-start.15
  142.1 5.4 %collective-permute-done.24 = f32[256,256]{1,0:T(8,128)S(1)} collective-permute-done((f32[256,256]{1,0:T(8,128)S(1)}, f32[256,256]{1,0:T(8,128)S(1)}, u32[]{:S(2)}, u32[]{:S(2)}) %collective-permute-start.24) | collective-permute-done | bytes 262176 | tf_op jit(solution)/shard_map/ppermute | solution.py:357
  147.6 1.5 collective-permute-start.29
  149.1 1.0 collective-permute-start.25
  150.1 0.6 collective-permute-start.28
  150.7 11.7 %collective-permute-done.29.refs_2_ = f32[512,256]{1,0:T(8,128)S(1)} collective-permute-done((f32[512,256]{1,0:T(8,128)S(1)}, f32[512,256]{1,0:T(8,128)S(1)}, u32[]{:S(2)}, u32[]{:S(2)}) %collective-permute-start.29) | collective-permute-done | bytes 524320 | tf_op jit(solution)/shard_map/ppermute | solution.py:357
  162.5 1.5 collective-permute-start.21
  163.9 2.0 %collective-permute-start.16 = (f32[640,256]{1,0:T(8,128)S(1)}, f32[640,256]{1,0:T(8,128)S(1)}, u32[]{:S(2)}, u32[]{:S(2)}) collective-permute-start(f32[640,256]{1,0:T(8,128)S(1)} %collective-permute-done.15.refs_1_), channel_id=1, source_target_pairs={{0,8},{1,9},{2,10},{3,11},{4,12},{5,13},{6,14},{7,15},{8,0},{9,1},... | collective-permute-start | bytes 1966088 | tf_op jit(solution)/shard_map/ppermute | solution.py:357
  165.9 0.6 collective-permute-start.26
  166.5 5.6 %shard_map.71 = (f32[768,256]{1,0:T(8,128)S(1)}, f32[7168,256]{1,0:T(8,128)}) custom-call(s32[22]{0:T(128)S(1)} %fusion.26.core_ref.table_ref, bf16[512,7168]{1,0:T(8,128)(2,1)} %acts_ref.9, f32[640,256]{1,0:T(8,128)S(1)} %maximum_select_fusion.refs_0_, f32[640,256]{1,0:T(8,128)S(1)} %collective-permute-done.15.refs_1_, ...), custom_call_target="tpu_custom_call" | custom-call | flops 1409286144 | bytes 11010048 | tf_op jit(solution)/shard_map/pallas_call | solution.py:326
  172.1 8.0 %collective-permute-done.27.refs_0_ = f32[640,256]{1,0:T(8,128)S(1)} collective-permute-done((f32[640,256]{1,0:T(8,128)S(1)}, f32[640,256]{1,0:T(8,128)S(1)}, u32[]{:S(2)}, u32[]{:S(2)}) %collective-permute-start.27) | collective-permute-done | bytes 655392 | tf_op jit(solution)/shard_map/ppermute | solution.py:357
  180.1 3.8 %shard_map.72 = (f32[768,256]{1,0:T(8,128)S(1)}, f32[7168,256]{1,0:T(8,128)}) custom-call(s32[22]{0:T(128)S(1)} %fusion.26.core_ref.table_ref, bf16[512,7168]{1,0:T(8,128)(2,1)} %acts_ref.9, f32[640,256]{1,0:T(8,128)S(1)} %collective-permute-done.27.refs_0_, ...), custom_call_target="tpu_custom_call", output_to_operand_aliasing={{0}: (5, {}), {1}: (6, {})} | custom-call | flops 704643072 | bytes 5505024 | tf_op jit(solution)/shard_map/pallas_call | solution.py:326
  183.9 3.0 %shard_map.73 = (f32[768,256]{1,0:T(8,128)S(1)}, f32[7168,256]{1,0:T(8,128)}) custom-call(s32[22]{0:T(128)S(1)} %fusion.26.core_ref.table_ref, bf16[512,7168]{1,0:T(8,128)(2,1)} %acts_ref.9, f32[640,256]{1,0:T(8,128)S(1)} %collective-permute-done.21.refs_0_, ...), custom_call_target="tpu_custom_call", output_to_operand_aliasing={{0}: (4, {}), {1}: (5, {})} | custom-call | flops 452984832 | bytes 3538944 | tf_op jit(solution)/shard_map/pallas_call | solution.py:326
  187.0 1.8 collective-permute-done.16.refs_0_
  188.7 2.3 %shard_map.74 = (f32[768,256]{1,0:T(8,128)S(1)}, f32[7168,256]{1,0:T(8,128)}) custom-call(s32[22]{0:T(128)S(1)} %fusion.26.core_ref.table_ref, bf16[512,7168]{1,0:T(8,128)(2,1)} %acts_ref.9, f32[640,256]{1,0:T(8,128)S(1)} %collective-permute-done.16.refs_0_, f32[768,256]{1,0:T(8,128)S(1)} %get-tuple-element.30.refs_1_, ...), custom_call_target="tpu_custom_call", output_to_operand_aliasing={{0}: (3, {}), {1}: (4, {})} | custom-call | flops 251658240 | bytes 1966080 | tf_op jit(solution)/shard_map/pallas_call | solution.py:326
  191.2 2.3 %collective-permute-done.30.theirs_ref = f32[768,256]{1,0:T(8,128)S(1)} collective-permute-done((f32[768,256]{1,0:T(8,128)S(1)}, f32[768,256]{1,0:T(8,128)S(1)}, u32[]{:S(2)}, u32[]{:S(2)}) %collective-permute-start.30) | collective-permute-done | bytes 786464 | tf_op jit(solution)/shard_map/ppermute | solution.py:390
  193.4 2.0 %shard_map.75 = f32[512,256]{1,0:T(8,128)} custom-call(f32[512,256]{1,0:T(8,128)S(1)} %get-tuple-element.18.codes_ref, f32[768,256]{1,0:T(8,128)S(1)} %get-tuple-element.32.mine_ref, f32[768,256]{1,0:T(8,128)S(1)} %collective-permute-done.30.theirs_ref), custom_call_target="tpu_custom_call" | custom-call | tf_op jit(solution)/shard_map/pallas_call | solution.py:195
  (43 shorter events, 2.6 us)
Async XLA Ops:
  0.6 12.0 %copy-start = (f32[512,256]{1,0:T(8,128)S(1)}, f32[512,256]{1,0:T(8,128)}, u32[]{:S(2)}) copy-start(f32[512,256]{1,0:T(8,128)} %codes_ref.1) | copy-start | bytes 1572868
  10.1 2.4 %collective-permute-start = (f32[768,256]{1,0:T(8,128)S(1)}, f32[768,256]{1,0:T(8,128)S(1)}, u32[]{:S(2)}, u32[]{:S(2)}) collective-permute-start(f32[768,256]{1,0:T(8,128)S(1)} %shard_map.59.mine_ref), channel_id=1, source_target_pairs={{0,1},{1,0},{2,3},{3,2},{4,5},{5,4},{6,7},{7,6},{8,9},{9,8},{10,11... | collective-permute-start | bytes 2359304 | tf_op jit(solution)/shard_map/ppermute | solution.py:390
  14.6 9.8 %copy-start.1 = (f32[128,256]{1,0:T(8,128)}, f32[128,256]{1,0:T(8,128)S(1)}, u32[]{:S(2)}) copy-start(f32[128,256]{1,0:T(8,128)S(1)} %get-tuple-element.20.rest_ref) | copy-start | bytes 393220
  18.2 32.2 %collective-permute-start.3 = (f32[1280,256]{1,0:T(8,128)S(1)}, f32[1280,256]{1,0:T(8,128)}, u32[]{:S(2)}, u32[]{:S(2)}) collective-permute-start(f32[1280,256]{1,0:T(8,128)S(1)} %fusion.2.refs_0_), channel_id=1, source_target_pairs={{0,8},{1,9},{2,10},{3,11},{4,12},{5,13},{6,14},{7,15},{8,0},{9,1},... | collective-permute-start | bytes 3932168 | tf_op jit(solution)/shard_map/ppermute | solution.py:357
  22.8 16.5 %collective-permute-start.1 = (f32[1152,256]{1,0:T(8,128)}, f32[1152,256]{1,0:T(8,128)}, u32[]{:S(2)}, u32[]{:S(2)}) collective-permute-start(f32[1152,256]{1,0:T(8,128)} %shard_map.61), channel_id=1, source_target_pairs={{0,2},{1,5},{2,0},{3,7},{4,6},{5,1},{6,4},{7,3},{8,10},{9,13},{10,... | collective-permute-start | bytes 3538952 | tf_op jit(solution)/shard_map/ppermute | solution.py:357
  27.3 26.0 %collective-permute-start.2 = (f32[1280,256]{1,0:T(8,128)}, f32[1280,256]{1,0:T(8,128)S(1)}, u32[]{:S(2)}, u32[]{:S(2)}) collective-permute-start(f32[1280,256]{1,0:T(8,128)} %fusion), channel_id=1, source_target_pairs={{0,2},{1,5},{2,0},{3,7},{4,6},{5,1},{6,4},{7,3},{8,10},{9,13},{10,... | collective-permute-start | bytes 3932168 | tf_op jit(solution)/shard_map/ppermute | solution.py:357
  56.1 17.2 %collective-permute-start.4 = (f32[640,256]{1,0:T(8,128)}, f32[640,256]{1,0:T(8,128)}, u32[]{:S(2)}, u32[]{:S(2)}) collective-permute-start(f32[640,256]{1,0:T(8,128)} %shard_map.64), channel_id=1, source_target_pairs={{0,4},{1,3},{2,6},{3,1},{4,0},{5,7},{6,2},{7,5},{8,12},{9,11},{10,... | collective-permute-start | bytes 1966088 | tf_op jit(solution)/shard_map/ppermute | solution.py:357
  57.6 17.4 %collective-permute-start.10 = (f32[640,256]{1,0:T(8,128)S(1)}, f32[640,256]{1,0:T(8,128)}, u32[]{:S(2)}, u32[]{:S(2)}) collective-permute-start(f32[640,256]{1,0:T(8,128)S(1)} %shard_map.63.refs_1_), channel_id=1, source_target_pairs={{0,8},{1,9},{2,10},{3,11},{4,12},{5,13},{6,14},{7,15},{8,0},{9,1},... | collective-permute-start | bytes 1966088 | tf_op jit(solution)/shard_map/ppermute | solution.py:357
  58.1 20.6 %collective-permute-start.8 = (f32[640,256]{1,0:T(8,128)S(1)}, f32[640,256]{1,0:T(8,128)}, u32[]{:S(2)}, u32[]{:S(2)}) collective-permute-start(f32[640,256]{1,0:T(8,128)S(1)} %shard_map.62.refs_0_), channel_id=1, source_target_pairs={{0,2},{1,5},{2,0},{3,7},{4,6},{5,1},{6,4},{7,3},{8,10},{9,13},{10,... | collective-permute-start | bytes 1966088 | tf_op jit(solution)/shard_map/ppermute | solution.py:357
  74.5 9.0 %collective-permute-start.5 = (f32[384,256]{1,0:T(8,128)S(1)}, f32[384,256]{1,0:T(8,128)S(1)}, u32[]{:S(2)}, u32[]{:S(2)}) collective-permute-start(f32[384,256]{1,0:T(8,128)S(1)} %get-tuple-element.22), channel_id=1, source_target_pairs={{0,8},{1,9},{2,10},{3,11},{4,12},{5,13},{6,14},{7,15},{8,0},{9,1},... | collective-permute-start | bytes 1179656 | tf_op jit(solution)/shard_map/ppermute | solution.py:357
  76.7 12.0 %collective-permute-start.11 = (f32[320,256]{1,0:T(8,128)S(1)}, f32[320,256]{1,0:T(8,128)S(1)}, u32[]{:S(2)}, u32[]{:S(2)}) collective-permute-start(f32[320,256]{1,0:T(8,128)S(1)} %constant_dynamic-slice_fusion.1), channel_id=1, source_target_pairs={{0,4},{1,3},{2,6},{3,1},{4,0},{5,7},{6,2},{7,5},{8,12},{9,11},{10,... | collective-permute-start | bytes 983048 | tf_op jit(solution)/shard_map/ppermute | solution.py:357
  80.6 11.6 %collective-permute-start.9 = (f32[320,256]{1,0:T(8,128)S(1)}, f32[320,256]{1,0:T(8,128)S(1)}, u32[]{:S(2)}, u32[]{:S(2)}) collective-permute-start(f32[320,256]{1,0:T(8,128)S(1)} %constant_dynamic-slice_fusion.3), channel_id=1, source_target_pairs={{0,4},{1,3},{2,6},{3,1},{4,0},{5,7},{6,2},{7,5},{8,12},{9,11},{10,... | collective-permute-start | bytes 983048 | tf_op jit(solution)/shard_map/ppermute | solution.py:357
  84.1 7.9 %collective-permute-start.6 = (f32[128,256]{1,0:T(8,128)S(1)}, f32[128,256]{1,0:T(8,128)S(1)}, u32[]{:S(2)}, u32[]{:S(2)}) collective-permute-start(f32[128,256]{1,0:T(8,128)S(1)} %get-tuple-element.23), channel_id=1, source_target_pairs={{0,16},{1,17},{2,18},{3,19},{4,20},{5,21},{6,22},{7,23},{8,24},{9,... | collective-permute-start | bytes 393224 | tf_op jit(solution)/shard_map/ppermute | solution.py:357
  88.8 16.0 %collective-permute-start.17 = (f32[160,256]{1,0:T(8,128)S(1)}, f32[160,256]{1,0:T(8,128)S(1)}, u32[]{:S(2)}, u32[]{:S(2)}) collective-permute-start(f32[160,256]{1,0:T(8,128)S(1)} %get-tuple-element.34), channel_id=1, source_target_pairs={{0,16},{1,17},{2,18},{3,19},{4,20},{5,21},{6,22},{7,23},{8,24},{9,... | collective-permute-start | bytes 491528 | tf_op jit(solution)/shard_map/ppermute | solution.py:357
  92.1 2.9 %collective-permute-start.7 = (f32[128,256]{1,0:T(8,128)S(1)}, f32[128,256]{1,0:T(8,128)S(1)}, u32[]{:S(2)}, u32[]{:S(2)}) collective-permute-start(f32[128,256]{1,0:T(8,128)S(1)} %add.145.mine_ref), channel_id=1, source_target_pairs={{0,1},{1,0},{2,3},{3,2},{4,5},{5,4},{6,7},{7,6},{8,9},{9,8},{10,11... | collective-permute-start | bytes 393224 | tf_op jit(solution)/shard_map/ppermute | solution.py:390
  92.3 11.1 %collective-permute-start.12 = (f32[160,256]{1,0:T(8,128)S(1)}, f32[160,256]{1,0:T(8,128)S(1)}, u32[]{:S(2)}, u32[]{:S(2)}) collective-permute-start(f32[160,256]{1,0:T(8,128)S(1)} %get-tuple-element.36), channel_id=1, source_target_pairs={{0,16},{1,17},{2,18},{3,19},{4,20},{5,21},{6,22},{7,23},{8,24},{9,... | collective-permute-start | bytes 491528 | tf_op jit(solution)/shard_map/ppermute | solution.py:357
  106.2 16.1 %collective-permute-start.18 = (f32[160,256]{1,0:T(8,128)S(1)}, f32[160,256]{1,0:T(8,128)S(1)}, u32[]{:S(2)}, u32[]{:S(2)}) collective-permute-start(f32[160,256]{1,0:T(8,128)S(1)} %shard_map.69.refs_2_), channel_id=1, source_target_pairs={{0,16},{1,17},{2,18},{3,19},{4,20},{5,21},{6,22},{7,23},{8,24},{9,... | collective-permute-start | bytes 491528 | tf_op jit(solution)/shard_map/ppermute | solution.py:357
  107.4 22.5 %collective-permute-start.13 = (f32[160,256]{1,0:T(8,128)S(1)}, f32[160,256]{1,0:T(8,128)S(1)}, u32[]{:S(2)}, u32[]{:S(2)}) collective-permute-start(f32[160,256]{1,0:T(8,128)S(1)} %shard_map.68.refs_1_), channel_id=1, source_target_pairs={{0,16},{1,17},{2,18},{3,19},{4,20},{5,21},{6,22},{7,23},{8,24},{9,... | collective-permute-start | bytes 491528 | tf_op jit(solution)/shard_map/ppermute | solution.py:357
  109.2 19.3 %collective-permute-start.22 = (f32[128,256]{1,0:T(8,128)S(1)}, f32[128,256]{1,0:T(8,128)S(1)}, u32[]{:S(2)}, u32[]{:S(2)}) collective-permute-start(f32[128,256]{1,0:T(8,128)S(1)} %get-tuple-element.25), channel_id=1, source_target_pairs={{0,16},{1,17},{2,18},{3,19},{4,20},{5,21},{6,22},{7,23},{8,24},{9,... | collective-permute-start | bytes 393224 | tf_op jit(solution)/shard_map/ppermute | solution.py:357
  122.3 16.1 %collective-permute-start.19 = (f32[320,256]{1,0:T(8,128)S(1)}, f32[320,256]{1,0:T(8,128)S(1)}, u32[]{:S(2)}, u32[]{:S(2)}) collective-permute-start(f32[320,256]{1,0:T(8,128)S(1)} %maximum_select_fusion.4), channel_id=1, source_target_pairs={{0,4},{1,3},{2,6},{3,1},{4,0},{5,7},{6,2},{7,5},{8,12},{9,11},{10,... | collective-permute-start | bytes 983048 | tf_op jit(solution)/shard_map/ppermute | solution.py:357
  129.8 8.4 %collective-permute-start.23 = (f32[128,256]{1,0:T(8,128)S(1)}, f32[128,256]{1,0:T(8,128)S(1)}, u32[]{:S(2)}, u32[]{:S(2)}) collective-permute-start(f32[128,256]{1,0:T(8,128)S(1)} %shard_map.70), channel_id=1, source_target_pairs={{0,16},{1,17},{2,18},{3,19},{4,20},{5,21},{6,22},{7,23},{8,24},{9,... | collective-permute-start | bytes 393224 | tf_op jit(solution)/shard_map/ppermute | solution.py:357
  130.0 10.5 %collective-permute-start.14 = (f32[320,256]{1,0:T(8,128)S(1)}, f32[320,256]{1,0:T(8,128)S(1)}, u32[]{:S(2)}, u32[]{:S(2)}) collective-permute-start(f32[320,256]{1,0:T(8,128)S(1)} %maximum_select_fusion.3), channel_id=1, source_target_pairs={{0,4},{1,3},{2,6},{3,1},{4,0},{5,7},{6,2},{7,5},{8,12},{9,11},{10,... | collective-permute-start | bytes 983048 | tf_op jit(solution)/shard_map/ppermute | solution.py:357
  138.3 9.2 %collective-permute-start.24 = (f32[256,256]{1,0:T(8,128)S(1)}, f32[256,256]{1,0:T(8,128)S(1)}, u32[]{:S(2)}, u32[]{:S(2)}) collective-permute-start(f32[256,256]{1,0:T(8,128)S(1)} %maximum_select_fusion.5), channel_id=1, source_target_pairs={{0,8},{1,9},{2,10},{3,11},{4,12},{5,13},{6,14},{7,15},{8,0},{9,1},... | collective-permute-start | bytes 786440 | tf_op jit(solution)/shard_map/ppermute | solution.py:357
  138.4 24.0 %collective-permute-start.20 = (f32[640,256]{1,0:T(8,128)S(1)}, f32[640,256]{1,0:T(8,128)S(1)}, u32[]{:S(2)}, u32[]{:S(2)}) collective-permute-start(f32[640,256]{1,0:T(8,128)S(1)} %maximum_select_fusion.1.refs_2_), channel_id=1, source_target_pairs={{0,8},{1,9},{2,10},{3,11},{4,12},{5,13},{6,14},{7,15},{8,0},{9,1},... | collective-permute-start | bytes 1966088 | tf_op jit(solution)/shard_map/ppermute | solution.py:357
  140.6 23.4 %collective-permute-start.15 = (f32[640,256]{1,0:T(8,128)S(1)}, f32[640,256]{1,0:T(8,128)S(1)}, u32[]{:S(2)}, u32[]{:S(2)}) collective-permute-start(f32[640,256]{1,0:T(8,128)S(1)} %maximum_select_fusion.refs_0_), channel_id=1, source_target_pairs={{0,2},{1,5},{2,0},{3,7},{4,6},{5,1},{6,4},{7,3},{8,10},{9,13},{10,... | collective-permute-start | bytes 1966088 | tf_op jit(solution)/shard_map/ppermute | solution.py:357
  147.6 14.9 %collective-permute-start.29 = (f32[512,256]{1,0:T(8,128)S(1)}, f32[512,256]{1,0:T(8,128)S(1)}, u32[]{:S(2)}, u32[]{:S(2)}) collective-permute-start(f32[512,256]{1,0:T(8,128)S(1)} %maximum_select_fusion.2.refs_4_), channel_id=1, source_target_pairs={{0,2},{1,5},{2,0},{3,7},{4,6},{5,1},{6,4},{7,3},{8,10},{9,13},{10,... | collective-permute-start | bytes 1572872 | tf_op jit(solution)/shard_map/ppermute | solution.py:357
  149.1 16.9 %collective-permute-start.25 = (f32[512,256]{1,0:T(8,128)S(1)}, f32[512,256]{1,0:T(8,128)S(1)}, u32[]{:S(2)}, u32[]{:S(2)}) collective-permute-start(f32[512,256]{1,0:T(8,128)S(1)} %maximum_select_fusion.2.refs_4_), channel_id=1, source_target_pairs={{0,4},{1,3},{2,6},{3,1},{4,0},{5,7},{6,2},{7,5},{8,12},{9,11},{10,... | collective-permute-start | bytes 1572872 | tf_op jit(solution)/shard_map/ppermute | solution.py:357
  150.1 22.1 %collective-permute-start.28 = (f32[640,256]{1,0:T(8,128)S(1)}, f32[640,256]{1,0:T(8,128)S(1)}, u32[]{:S(2)}, u32[]{:S(2)}) collective-permute-start(f32[640,256]{1,0:T(8,128)S(1)} %maximum_select_fusion.1.refs_2_), channel_id=1, source_target_pairs={{0,2},{1,5},{2,0},{3,7},{4,6},{5,1},{6,4},{7,3},{8,10},{9,13},{10,... | collective-permute-start | bytes 1966088 | tf_op jit(solution)/shard_map/ppermute | solution.py:357
  162.4 17.7 %collective-permute-start.27 = (f32[640,256]{1,0:T(8,128)S(1)}, f32[640,256]{1,0:T(8,128)S(1)}, u32[]{:S(2)}, u32[]{:S(2)}) collective-permute-start(f32[640,256]{1,0:T(8,128)S(1)} %maximum_select_fusion.refs_0_), channel_id=1, source_target_pairs={{0,8},{1,9},{2,10},{3,11},{4,12},{5,13},{6,14},{7,15},{8,0},{9,1},... | collective-permute-start | bytes 1966088 | tf_op jit(solution)/shard_map/ppermute | solution.py:357
  162.5 21.4 %collective-permute-start.21 = (f32[640,256]{1,0:T(8,128)S(1)}, f32[640,256]{1,0:T(8,128)S(1)}, u32[]{:S(2)}, u32[]{:S(2)}) collective-permute-start(f32[640,256]{1,0:T(8,128)S(1)} %collective-permute-done.20.refs_3_), channel_id=1, source_target_pairs={{0,2},{1,5},{2,0},{3,7},{4,6},{5,1},{6,4},{7,3},{8,10},{9,13},{10,... | collective-permute-start | bytes 1966088 | tf_op jit(solution)/shard_map/ppermute | solution.py:357
  163.9 24.8 %collective-permute-start.16 = (f32[640,256]{1,0:T(8,128)S(1)}, f32[640,256]{1,0:T(8,128)S(1)}, u32[]{:S(2)}, u32[]{:S(2)}) collective-permute-start(f32[640,256]{1,0:T(8,128)S(1)} %collective-permute-done.15.refs_1_), channel_id=1, source_target_pairs={{0,8},{1,9},{2,10},{3,11},{4,12},{5,13},{6,14},{7,15},{8,0},{9,1},... | collective-permute-start | bytes 1966088 | tf_op jit(solution)/shard_map/ppermute | solution.py:357
  165.9 17.9 %collective-permute-start.26 = (f32[512,256]{1,0:T(8,128)S(1)}, f32[512,256]{1,0:T(8,128)S(1)}, u32[]{:S(2)}, u32[]{:S(2)}) collective-permute-start(f32[512,256]{1,0:T(8,128)S(1)} %collective-permute-done.25.refs_5_), channel_id=1, source_target_pairs={{0,2},{1,5},{2,0},{3,7},{4,6},{5,1},{6,4},{7,3},{8,10},{9,13},{10,... | collective-permute-start | bytes 1572872 | tf_op jit(solution)/shard_map/ppermute | solution.py:357
  191.1 2.4 %collective-permute-start.30 = (f32[768,256]{1,0:T(8,128)S(1)}, f32[768,256]{1,0:T(8,128)S(1)}, u32[]{:S(2)}, u32[]{:S(2)}) collective-permute-start(f32[768,256]{1,0:T(8,128)S(1)} %get-tuple-element.32.mine_ref), channel_id=1, source_target_pairs={{0,1},{1,0},{2,3},{3,2},{4,5},{5,4},{6,7},{7,6},{8,9},{9,8},{10,11... | collective-permute-start | bytes 2359304 | tf_op jit(solution)/shard_map/ppermute | solution.py:390

commit v11 on v10

--- a/solution.py
+++ b/solution.py
@@ -154,10 +154,19 @@
     return refine(codes_mid, proj_two, gram_new), dict_out
 
 
-def update(codes, sums, tokens, precision=HIGHEST):
+def halves(value):
+    high = value.astype(bf16)
+    return high, (value - high.astype(f32)).astype(bf16)
+
+
+def update(codes, sums, tokens):
     proj, gram = sums[:tokens], sums[tokens:]
-    numer = jnp.maximum(proj, 0.0) + dot(codes, jnp.maximum(-gram, 0.0), precision=precision)
-    denom = jnp.maximum(-proj, 0.0) + dot(codes, jnp.maximum(gram, 0.0), precision=precision)
+    comp = gram.shape[1]
+    high, low = halves(codes)
+    gram_high, gram_low = halves(jnp.concatenate([jnp.maximum(-gram, 0.0), jnp.maximum(gram, 0.0)], axis=1))
+    both = dot(high, gram_high) + (dot(high, gram_low) + dot(low, gram_high))
+    numer = jnp.maximum(proj, 0.0) + both[:, :comp]
+    denom = jnp.maximum(-proj, 0.0) + both[:, comp:]
     return codes * jnp.sqrt(numer / jnp.maximum(denom, floor_value))
 
 

time: 196 us -> 195 us (level)
  no operation moved by 1% of the time
where the time goes in v11:
time: 195 us
  waiting for transfers between devices  91.5 us (47%)
  Pallas kernels  47.4 us (24%)
  starting transfers between devices  36.6 us (19%)
  matrix products  15.9 us (8%)
    ppermute x28, waiting for transfers between devices, swap(): return lax.ppermute(value, BOTH, flips(ALONG[along]))  88 us
    ppermute x28, starting transfers between devices, swap(): return lax.ppermute(value, BOTH, flips(ALONG[along]))  35.9 us
    dot_general x9, matrix products, dot(): lax.dot_general(left, right, dims, precision=precision, preferred_element...  15.9 us
    pallas_call x4, Pallas kernels, absorb(): pl.pallas_call(functools.partial(absorb_kernel, [at for _, at in blocks],...  14.8 us
    pallas_call x9, Pallas kernels, call(): pl.pallas_call(kernel, out_shape=out_shapes, in_specs=[SCALARS] + [WHOLE]...  11.7 us
    pallas_call x1, Pallas kernels, project(): pl.pallas_call(project_kernel, out_shape=jax.ShapeDtypeStruct((tokens + c...  9.5 us
    pallas_call x1, Pallas kernels, factor_inverse(): pl.pallas_call(halves_kernel, out_shape=jax.ShapeDtypeStruct((comp, comp)...  8.43 us
  transfers between devices with their start and end apart: 31, of which 15 were waited for; matrix products, arithmetic and copies ran while one was open for 7% of the time, Pallas kernels for 15%

profile of v11, /device:TPU:0, one launch (start us, length us, event | category | flops | bytes accessed | tf_op | source)
XLA Modules:
  0.0 194.5 jit_solution(8825907556196691621)
XLA Ops:
  0.6 9.5 %shard_map.59.mine_ref = f32[768,256]{1,0:T(8,128)S(1)} custom-call(bf16[512,7168]{1,0:T(8,128)(2,1)} %acts_ref.9, f32[7168,256]{1,0:T(8,128)} %dict_ref.1), custom_call_target="tpu_custom_call" | custom-call | flops 3758096384 | bytes 14680064 | tf_op jit(solution)/shard_map/pallas_call | solution.py:58
  10.7 0.7 fusion.26.core_ref.table_ref
  11.4 1.2 collective-permute-done.theirs_ref
  12.6 1.5 shard_map.60
  14.1 1.7 fusion.6.top_ref
  15.9 1.9 fusion.2.refs_0_
  17.8 3.0 %collective-permute-start.3 = (f32[1280,256]{1,0:T(8,128)S(1)}, f32[1280,256]{1,0:T(8,128)}, u32[]{:S(2)}, u32[]{:S(2)}) collective-permute-start(f32[1280,256]{1,0:T(8,128)S(1)} %fusion.2.refs_0_), channel_id=1, source_target_pairs={{0,8},{1,9},{2,10},{3,11},{4,12},{5,13},{6,14},{7,15},{8,0},{9,1},... | collective-permute-start | bytes 3932168 | tf_op jit(solution)/shard_map/ppermute | solution.py:366
  20.8 1.6 shard_map.61
  22.4 1.5 collective-permute-start.1
  23.9 2.9 %fusion = f32[1280,256]{1,0:T(8,128)} fusion(bf16[512,256]{1,0:T(8,128)(2,1)S(1)} %get-tuple-element.19, bf16[512,7168]{1,0:T(8,128)(2,1)} %acts_ref.9, s32[]{:T(128)S(6)} %select_n.133), kind=kOutput, calls=%fused_computation | convolution fusion | flops 335544320 | bytes 2883588 | tf_op jit(solution)/shard_map/dot_general | solution.py:21
  26.8 0.5 collective-permute-start.2
  27.4 1.4 fusion.14.mine_ref
  28.7 1.5 fusion.10.mine_ref
  30.2 1.5 fusion.12.mine_ref
  31.7 7.2 %collective-permute-done.1.theirs_ref = f32[1152,256]{1,0:T(8,128)} collective-permute-done((f32[1152,256]{1,0:T(8,128)}, f32[1152,256]{1,0:T(8,128)}, u32[]{:S(2)}, u32[]{:S(2)}) %collective-permute-start.1) | collective-permute-done | bytes 1179680 | tf_op jit(solution)/shard_map/ppermute | solution.py:366
  38.9 1.0 slice_add_fusion.refs_0_.gram_ref
  39.9 10.0 %collective-permute-done.3.theirs_ref = f32[1280,256]{1,0:T(8,128)} collective-permute-done((f32[1280,256]{1,0:T(8,128)S(1)}, f32[1280,256]{1,0:T(8,128)}, u32[]{:S(2)}, u32[]{:S(2)}) %collective-permute-start.3) | collective-permute-done | bytes 1310752 | tf_op jit(solution)/shard_map/ppermute | solution.py:366
  49.9 1.4 shard_map.62.refs_0_
  51.3 1.5 collective-permute-done.2.theirs_ref
  52.9 0.6 shard_map.63.refs_1_
  53.5 2.2 %shard_map.64 = f32[640,256]{1,0:T(8,128)} custom-call(s32[22]{0:T(128)S(1)} %fusion.26.core_ref.table_ref, f32[512,256]{1,0:T(8,128)S(1)} %fusion.14.mine_ref, f32[1152,256]{1,0:T(8,128)} %collective-permute-done.1.theirs_ref, f32[128,256]{1,0:T(8,128)S(1)} %slice_add_fusion.refs_0_.gram_ref, f32[640,256]{1,0:T(8,128)S(1)} %shard_map.63.refs_1_), custom_call_target="tpu_custom_call" | custom-call | tf_op jit(solution)/shard_map/pallas_call | solution.py:218
  55.7 1.5 collective-permute-start.4
  57.6 1.5 collective-permute-start.8
  59.1 1.5 convolution_add_fusion.2.mine_ref
  60.7 12.2 %collective-permute-done.4.theirs_ref = f32[640,256]{1,0:T(8,128)} collective-permute-done((f32[640,256]{1,0:T(8,128)}, f32[640,256]{1,0:T(8,128)}, u32[]{:S(2)}, u32[]{:S(2)}) %collective-permute-start.4) | collective-permute-done | bytes 655392 | tf_op jit(solution)/shard_map/ppermute | solution.py:366
  72.9 1.2 shard_map.65
  74.0 0.5 collective-permute-start.5
  74.6 1.7 fusion.5
  76.3 2.0 %collective-permute-start.11 = (f32[320,256]{1,0:T(8,128)S(1)}, f32[320,256]{1,0:T(8,128)S(1)}, u32[]{:S(2)}, u32[]{:S(2)}) collective-permute-start(f32[320,256]{1,0:T(8,128)S(1)} %constant_dynamic-slice_fusion.1), channel_id=1, source_target_pairs={{0,4},{1,3},{2,6},{3,1},{4,0},{5,7},{6,2},{7,5},{8,12},{9,11},{10,... | collective-permute-start | bytes 983048 | tf_op jit(solution)/shard_map/ppermute | solution.py:366
  78.3 1.9 fusion.4
  80.3 2.7 %collective-permute-done.5.theirs_ref = f32[384,256]{1,0:T(8,128)S(1)} collective-permute-done((f32[384,256]{1,0:T(8,128)S(1)}, f32[384,256]{1,0:T(8,128)S(1)}, u32[]{:S(2)}, u32[]{:S(2)}) %collective-permute-start.5) | collective-permute-done | bytes 393248 | tf_op jit(solution)/shard_map/ppermute | solution.py:366
  83.1 0.6 shard_map.66
  83.6 4.6 %collective-permute-start.6 = (f32[128,256]{1,0:T(8,128)S(1)}, f32[128,256]{1,0:T(8,128)S(1)}, u32[]{:S(2)}, u32[]{:S(2)}) collective-permute-start(f32[128,256]{1,0:T(8,128)S(1)} %get-tuple-element.23), channel_id=1, source_target_pairs={{0,16},{1,17},{2,18},{3,19},{4,20},{5,21},{6,22},{7,23},{8,24},{9,... | collective-permute-start | bytes 393224 | tf_op jit(solution)/shard_map/ppermute | solution.py:366
  88.5 3.2 %collective-permute-done.6 = f32[128,256]{1,0:T(8,128)S(1)} collective-permute-done((f32[128,256]{1,0:T(8,128)S(1)}, f32[128,256]{1,0:T(8,128)S(1)}, u32[]{:S(2)}, u32[]{:S(2)}) %collective-permute-start.6) | collective-permute-done | bytes 131104 | tf_op jit(solution)/shard_map/ppermute | solution.py:366
  91.8 2.7 %collective-permute-start.12 = (f32[160,256]{1,0:T(8,128)S(1)}, f32[160,256]{1,0:T(8,128)S(1)}, u32[]{:S(2)}, u32[]{:S(2)}) collective-permute-start(f32[160,256]{1,0:T(8,128)S(1)} %get-tuple-element.36), channel_id=1, source_target_pairs={{0,16},{1,17},{2,18},{3,19},{4,20},{5,21},{6,22},{7,23},{8,24},{9,... | collective-permute-start | bytes 491528 | tf_op jit(solution)/shard_map/ppermute | solution.py:366
  94.5 8.4 %shard_map.67.inverse_ref = f32[256,256]{1,0:T(8,128)S(1)} custom-call(s32[22]{0:T(128)S(1)} %fusion.26.core_ref.table_ref, f32[128,256]{1,0:T(8,128)S(1)} %add.145.mine_ref, f32[128,256]{1,0:T(8,128)S(1)} %collective-permute-done.7.theirs_ref, f32[160,256]{1,0:T(8,128)S(1)} %get-tuple-element.37.refs_0_.mine_ref, ...), custom_call_target="tpu_custom_call" | custom-call | flops 10000000000 | bytes 524288 | tf_op jit(solution)/shard_map/pallas_call | solution.py:123
  103.0 1.4 shard_map.68.refs_1_
  104.4 1.4 shard_map.69.refs_2_
  105.8 1.2 collective-permute-start.18
  107.0 1.8 collective-permute-start.13
  108.8 1.2 collective-permute-start.22
  109.9 11.9 %collective-permute-done.18 = f32[160,256]{1,0:T(8,128)S(1)} collective-permute-done((f32[160,256]{1,0:T(8,128)S(1)}, f32[160,256]{1,0:T(8,128)S(1)}, u32[]{:S(2)}, u32[]{:S(2)}) %collective-permute-start.18) | collective-permute-done | bytes 163872 | tf_op jit(solution)/shard_map/ppermute | solution.py:366
  121.9 1.1 collective-permute-start.19
  123.0 5.1 %collective-permute-done.22.refs_0_ = f32[128,256]{1,0:T(8,128)S(1)} collective-permute-done((f32[128,256]{1,0:T(8,128)S(1)}, f32[128,256]{1,0:T(8,128)S(1)}, u32[]{:S(2)}, u32[]{:S(2)}) %collective-permute-start.22) | collective-permute-done | bytes 131104 | tf_op jit(solution)/shard_map/ppermute | solution.py:366
  128.1 1.3 shard_map.70
  129.5 1.1 collective-permute-start.14
  130.6 7.2 %collective-permute-done.23 = f32[128,256]{1,0:T(8,128)S(1)} collective-permute-done((f32[128,256]{1,0:T(8,128)S(1)}, f32[128,256]{1,0:T(8,128)S(1)}, u32[]{:S(2)}, u32[]{:S(2)}) %collective-permute-start.23) | collective-permute-done | bytes 131104 | tf_op jit(solution)/shard_map/ppermute | solution.py:366
  138.0 2.1 %collective-permute-start.20 = (f32[640,256]{1,0:T(8,128)S(1)}, f32[640,256]{1,0:T(8,128)S(1)}, u32[]{:S(2)}, u32[]{:S(2)}) collective-permute-start(f32[640,256]{1,0:T(8,128)S(1)} %maximum_select_fusion.1.refs_2_), channel_id=1, source_target_pairs={{0,8},{1,9},{2,10},{3,11},{4,12},{5,13},{6,14},{7,15},{8,0},{9,1},... | collective-permute-start | bytes 1966088 | tf_op jit(solution)/shard_map/ppermute | solution.py:366
  140.1 1.6 collective-permute-start.15
  141.7 5.4 %collective-permute-done.24 = f32[256,256]{1,0:T(8,128)S(1)} collective-permute-done((f32[256,256]{1,0:T(8,128)S(1)}, f32[256,256]{1,0:T(8,128)S(1)}, u32[]{:S(2)}, u32[]{:S(2)}) %collective-permute-start.24) | collective-permute-done | bytes 262176 | tf_op jit(solution)/shard_map/ppermute | solution.py:366
  147.1 1.6 collective-permute-start.29
  148.7 0.9 collective-permute-start.25
  149.6 0.6 collective-permute-start.28
  150.2 11.8 %collective-permute-done.29.refs_2_ = f32[512,256]{1,0:T(8,128)S(1)} collective-permute-done((f32[512,256]{1,0:T(8,128)S(1)}, f32[512,256]{1,0:T(8,128)S(1)}, u32[]{:S(2)}, u32[]{:S(2)}) %collective-permute-start.29) | collective-permute-done | bytes 524320 | tf_op jit(solution)/shard_map/ppermute | solution.py:366
  162.0 1.5 collective-permute-start.21
  163.6 2.0 %collective-permute-start.16 = (f32[640,256]{1,0:T(8,128)S(1)}, f32[640,256]{1,0:T(8,128)S(1)}, u32[]{:S(2)}, u32[]{:S(2)}) collective-permute-start(f32[640,256]{1,0:T(8,128)S(1)} %collective-permute-done.15.refs_1_), channel_id=1, source_target_pairs={{0,8},{1,9},{2,10},{3,11},{4,12},{5,13},{6,14},{7,15},{8,0},{9,1},... | collective-permute-start | bytes 1966088 | tf_op jit(solution)/shard_map/ppermute | solution.py:366
  166.1 5.6 %shard_map.71 = (f32[768,256]{1,0:T(8,128)S(1)}, f32[7168,256]{1,0:T(8,128)}) custom-call(s32[22]{0:T(128)S(1)} %fusion.26.core_ref.table_ref, bf16[512,7168]{1,0:T(8,128)(2,1)} %acts_ref.9, f32[640,256]{1,0:T(8,128)S(1)} %maximum_select_fusion.refs_0_, f32[640,256]{1,0:T(8,128)S(1)} %collective-permute-done.15.refs_1_, ...), custom_call_target="tpu_custom_call" | custom-call | flops 1409286144 | bytes 11010048 | tf_op jit(solution)/shard_map/pallas_call | solution.py:335
  171.7 8.0 %collective-permute-done.27.refs_0_ = f32[640,256]{1,0:T(8,128)S(1)} collective-permute-done((f32[640,256]{1,0:T(8,128)S(1)}, f32[640,256]{1,0:T(8,128)S(1)}, u32[]{:S(2)}, u32[]{:S(2)}) %collective-permute-start.27) | collective-permute-done | bytes 655392 | tf_op jit(solution)/shard_map/ppermute | solution.py:366
  179.7 3.8 %shard_map.72 = (f32[768,256]{1,0:T(8,128)S(1)}, f32[7168,256]{1,0:T(8,128)}) custom-call(s32[22]{0:T(128)S(1)} %fusion.26.core_ref.table_ref, bf16[512,7168]{1,0:T(8,128)(2,1)} %acts_ref.9, f32[640,256]{1,0:T(8,128)S(1)} %collective-permute-done.27.refs_0_, ...), custom_call_target="tpu_custom_call", output_to_operand_aliasing={{0}: (5, {}), {1}: (6, {})} | custom-call | flops 704643072 | bytes 5505024 | tf_op jit(solution)/shard_map/pallas_call | solution.py:335
  183.5 3.0 %shard_map.73 = (f32[768,256]{1,0:T(8,128)S(1)}, f32[7168,256]{1,0:T(8,128)}) custom-call(s32[22]{0:T(128)S(1)} %fusion.26.core_ref.table_ref, bf16[512,7168]{1,0:T(8,128)(2,1)} %acts_ref.9, f32[640,256]{1,0:T(8,128)S(1)} %collective-permute-done.21.refs_0_, ...), custom_call_target="tpu_custom_call", output_to_operand_aliasing={{0}: (4, {}), {1}: (5, {})} | custom-call | flops 452984832 | bytes 3538944 | tf_op jit(solution)/shard_map/pallas_call | solution.py:335
  186.5 1.8 collective-permute-done.16.refs_0_
  188.3 2.3 %shard_map.74 = (f32[768,256]{1,0:T(8,128)S(1)}, f32[7168,256]{1,0:T(8,128)}) custom-call(s32[22]{0:T(128)S(1)} %fusion.26.core_ref.table_ref, bf16[512,7168]{1,0:T(8,128)(2,1)} %acts_ref.9, f32[640,256]{1,0:T(8,128)S(1)} %collective-permute-done.16.refs_0_, f32[768,256]{1,0:T(8,128)S(1)} %get-tuple-element.30.refs_1_, ...), custom_call_target="tpu_custom_call", output_to_operand_aliasing={{0}: (3, {}), {1}: (4, {})} | custom-call | flops 251658240 | bytes 1966080 | tf_op jit(solution)/shard_map/pallas_call | solution.py:335
  190.7 2.3 %collective-permute-done.30.theirs_ref = f32[768,256]{1,0:T(8,128)S(1)} collective-permute-done((f32[768,256]{1,0:T(8,128)S(1)}, f32[768,256]{1,0:T(8,128)S(1)}, u32[]{:S(2)}, u32[]{:S(2)}) %collective-permute-start.30) | collective-permute-done | bytes 786464 | tf_op jit(solution)/shard_map/ppermute | solution.py:399
  193.0 1.6 shard_map.75
  (43 shorter events, 2.6 us)
Async XLA Ops:
  0.6 12.0 %copy-start = (f32[512,256]{1,0:T(8,128)S(1)}, f32[512,256]{1,0:T(8,128)}, u32[]{:S(2)}) copy-start(f32[512,256]{1,0:T(8,128)} %codes_ref.1) | copy-start | bytes 1572868
  10.1 2.4 %collective-permute-start = (f32[768,256]{1,0:T(8,128)S(1)}, f32[768,256]{1,0:T(8,128)S(1)}, u32[]{:S(2)}, u32[]{:S(2)}) collective-permute-start(f32[768,256]{1,0:T(8,128)S(1)} %shard_map.59.mine_ref), channel_id=1, source_target_pairs={{0,1},{1,0},{2,3},{3,2},{4,5},{5,4},{6,7},{7,6},{8,9},{9,8},{10,11... | collective-permute-start | bytes 2359304 | tf_op jit(solution)/shard_map/ppermute | solution.py:399
  14.1 9.8 %copy-start.1 = (f32[128,256]{1,0:T(8,128)}, f32[128,256]{1,0:T(8,128)S(1)}, u32[]{:S(2)}) copy-start(f32[128,256]{1,0:T(8,128)S(1)} %get-tuple-element.20.rest_ref) | copy-start | bytes 393220
  17.8 32.2 %collective-permute-start.3 = (f32[1280,256]{1,0:T(8,128)S(1)}, f32[1280,256]{1,0:T(8,128)}, u32[]{:S(2)}, u32[]{:S(2)}) collective-permute-start(f32[1280,256]{1,0:T(8,128)S(1)} %fusion.2.refs_0_), channel_id=1, source_target_pairs={{0,8},{1,9},{2,10},{3,11},{4,12},{5,13},{6,14},{7,15},{8,0},{9,1},... | collective-permute-start | bytes 3932168 | tf_op jit(solution)/shard_map/ppermute | solution.py:366
  22.4 16.5 %collective-permute-start.1 = (f32[1152,256]{1,0:T(8,128)}, f32[1152,256]{1,0:T(8,128)}, u32[]{:S(2)}, u32[]{:S(2)}) collective-permute-start(f32[1152,256]{1,0:T(8,128)} %shard_map.61), channel_id=1, source_target_pairs={{0,2},{1,5},{2,0},{3,7},{4,6},{5,1},{6,4},{7,3},{8,10},{9,13},{10,... | collective-permute-start | bytes 3538952 | tf_op jit(solution)/shard_map/ppermute | solution.py:366
  26.8 26.0 %collective-permute-start.2 = (f32[1280,256]{1,0:T(8,128)}, f32[1280,256]{1,0:T(8,128)S(1)}, u32[]{:S(2)}, u32[]{:S(2)}) collective-permute-start(f32[1280,256]{1,0:T(8,128)} %fusion), channel_id=1, source_target_pairs={{0,2},{1,5},{2,0},{3,7},{4,6},{5,1},{6,4},{7,3},{8,10},{9,13},{10,... | collective-permute-start | bytes 3932168 | tf_op jit(solution)/shard_map/ppermute | solution.py:366
  55.7 17.2 %collective-permute-start.4 = (f32[640,256]{1,0:T(8,128)}, f32[640,256]{1,0:T(8,128)}, u32[]{:S(2)}, u32[]{:S(2)}) collective-permute-start(f32[640,256]{1,0:T(8,128)} %shard_map.64), channel_id=1, source_target_pairs={{0,4},{1,3},{2,6},{3,1},{4,0},{5,7},{6,2},{7,5},{8,12},{9,11},{10,... | collective-permute-start | bytes 1966088 | tf_op jit(solution)/shard_map/ppermute | solution.py:366
  57.2 17.4 %collective-permute-start.10 = (f32[640,256]{1,0:T(8,128)S(1)}, f32[640,256]{1,0:T(8,128)}, u32[]{:S(2)}, u32[]{:S(2)}) collective-permute-start(f32[640,256]{1,0:T(8,128)S(1)} %shard_map.63.refs_1_), channel_id=1, source_target_pairs={{0,8},{1,9},{2,10},{3,11},{4,12},{5,13},{6,14},{7,15},{8,0},{9,1},... | collective-permute-start | bytes 1966088 | tf_op jit(solution)/shard_map/ppermute | solution.py:366
  57.6 20.6 %collective-permute-start.8 = (f32[640,256]{1,0:T(8,128)S(1)}, f32[640,256]{1,0:T(8,128)}, u32[]{:S(2)}, u32[]{:S(2)}) collective-permute-start(f32[640,256]{1,0:T(8,128)S(1)} %shard_map.62.refs_0_), channel_id=1, source_target_pairs={{0,2},{1,5},{2,0},{3,7},{4,6},{5,1},{6,4},{7,3},{8,10},{9,13},{10,... | collective-permute-start | bytes 1966088 | tf_op jit(solution)/shard_map/ppermute | solution.py:366
  74.0 9.0 %collective-permute-start.5 = (f32[384,256]{1,0:T(8,128)S(1)}, f32[384,256]{1,0:T(8,128)S(1)}, u32[]{:S(2)}, u32[]{:S(2)}) collective-permute-start(f32[384,256]{1,0:T(8,128)S(1)} %get-tuple-element.22), channel_id=1, source_target_pairs={{0,8},{1,9},{2,10},{3,11},{4,12},{5,13},{6,14},{7,15},{8,0},{9,1},... | collective-permute-start | bytes 1179656 | tf_op jit(solution)/shard_map/ppermute | solution.py:366
  76.3 12.0 %collective-permute-start.11 = (f32[320,256]{1,0:T(8,128)S(1)}, f32[320,256]{1,0:T(8,128)S(1)}, u32[]{:S(2)}, u32[]{:S(2)}) collective-permute-start(f32[320,256]{1,0:T(8,128)S(1)} %constant_dynamic-slice_fusion.1), channel_id=1, source_target_pairs={{0,4},{1,3},{2,6},{3,1},{4,0},{5,7},{6,2},{7,5},{8,12},{9,11},{10,... | collective-permute-start | bytes 983048 | tf_op jit(solution)/shard_map/ppermute | solution.py:366
  80.2 11.6 %collective-permute-start.9 = (f32[320,256]{1,0:T(8,128)S(1)}, f32[320,256]{1,0:T(8,128)S(1)}, u32[]{:S(2)}, u32[]{:S(2)}) collective-permute-start(f32[320,256]{1,0:T(8,128)S(1)} %constant_dynamic-slice_fusion.3), channel_id=1, source_target_pairs={{0,4},{1,3},{2,6},{3,1},{4,0},{5,7},{6,2},{7,5},{8,12},{9,11},{10,... | collective-permute-start | bytes 983048 | tf_op jit(solution)/shard_map/ppermute | solution.py:366
  83.6 8.0 %collective-permute-start.6 = (f32[128,256]{1,0:T(8,128)S(1)}, f32[128,256]{1,0:T(8,128)S(1)}, u32[]{:S(2)}, u32[]{:S(2)}) collective-permute-start(f32[128,256]{1,0:T(8,128)S(1)} %get-tuple-element.23), channel_id=1, source_target_pairs={{0,16},{1,17},{2,18},{3,19},{4,20},{5,21},{6,22},{7,23},{8,24},{9,... | collective-permute-start | bytes 393224 | tf_op jit(solution)/shard_map/ppermute | solution.py:366
  88.4 16.0 %collective-permute-start.17 = (f32[160,256]{1,0:T(8,128)S(1)}, f32[160,256]{1,0:T(8,128)S(1)}, u32[]{:S(2)}, u32[]{:S(2)}) collective-permute-start(f32[160,256]{1,0:T(8,128)S(1)} %get-tuple-element.34), channel_id=1, source_target_pairs={{0,16},{1,17},{2,18},{3,19},{4,20},{5,21},{6,22},{7,23},{8,24},{9,... | collective-permute-start | bytes 491528 | tf_op jit(solution)/shard_map/ppermute | solution.py:366
  91.6 2.9 %collective-permute-start.7 = (f32[128,256]{1,0:T(8,128)S(1)}, f32[128,256]{1,0:T(8,128)S(1)}, u32[]{:S(2)}, u32[]{:S(2)}) collective-permute-start(f32[128,256]{1,0:T(8,128)S(1)} %add.145.mine_ref), channel_id=1, source_target_pairs={{0,1},{1,0},{2,3},{3,2},{4,5},{5,4},{6,7},{7,6},{8,9},{9,8},{10,11... | collective-permute-start | bytes 393224 | tf_op jit(solution)/shard_map/ppermute | solution.py:399
  91.8 11.1 %collective-permute-start.12 = (f32[160,256]{1,0:T(8,128)S(1)}, f32[160,256]{1,0:T(8,128)S(1)}, u32[]{:S(2)}, u32[]{:S(2)}) collective-permute-start(f32[160,256]{1,0:T(8,128)S(1)} %get-tuple-element.36), channel_id=1, source_target_pairs={{0,16},{1,17},{2,18},{3,19},{4,20},{5,21},{6,22},{7,23},{8,24},{9,... | collective-permute-start | bytes 491528 | tf_op jit(solution)/shard_map/ppermute | solution.py:366
  105.8 16.1 %collective-permute-start.18 = (f32[160,256]{1,0:T(8,128)S(1)}, f32[160,256]{1,0:T(8,128)S(1)}, u32[]{:S(2)}, u32[]{:S(2)}) collective-permute-start(f32[160,256]{1,0:T(8,128)S(1)} %shard_map.69.refs_2_), channel_id=1, source_target_pairs={{0,16},{1,17},{2,18},{3,19},{4,20},{5,21},{6,22},{7,23},{8,24},{9,... | collective-permute-start | bytes 491528 | tf_op jit(solution)/shard_map/ppermute | solution.py:366
  107.0 22.5 %collective-permute-start.13 = (f32[160,256]{1,0:T(8,128)S(1)}, f32[160,256]{1,0:T(8,128)S(1)}, u32[]{:S(2)}, u32[]{:S(2)}) collective-permute-start(f32[160,256]{1,0:T(8,128)S(1)} %shard_map.68.refs_1_), channel_id=1, source_target_pairs={{0,16},{1,17},{2,18},{3,19},{4,20},{5,21},{6,22},{7,23},{8,24},{9,... | collective-permute-start | bytes 491528 | tf_op jit(solution)/shard_map/ppermute | solution.py:366
  108.8 19.3 %collective-permute-start.22 = (f32[128,256]{1,0:T(8,128)S(1)}, f32[128,256]{1,0:T(8,128)S(1)}, u32[]{:S(2)}, u32[]{:S(2)}) collective-permute-start(f32[128,256]{1,0:T(8,128)S(1)} %get-tuple-element.25), channel_id=1, source_target_pairs={{0,16},{1,17},{2,18},{3,19},{4,20},{5,21},{6,22},{7,23},{8,24},{9,... | collective-permute-start | bytes 393224 | tf_op jit(solution)/shard_map/ppermute | solution.py:366
  121.9 16.1 %collective-permute-start.19 = (f32[320,256]{1,0:T(8,128)S(1)}, f32[320,256]{1,0:T(8,128)S(1)}, u32[]{:S(2)}, u32[]{:S(2)}) collective-permute-start(f32[320,256]{1,0:T(8,128)S(1)} %maximum_select_fusion.4), channel_id=1, source_target_pairs={{0,4},{1,3},{2,6},{3,1},{4,0},{5,7},{6,2},{7,5},{8,12},{9,11},{10,... | collective-permute-start | bytes 983048 | tf_op jit(solution)/shard_map/ppermute | solution.py:366
  129.4 8.4 %collective-permute-start.23 = (f32[128,256]{1,0:T(8,128)S(1)}, f32[128,256]{1,0:T(8,128)S(1)}, u32[]{:S(2)}, u32[]{:S(2)}) collective-permute-start(f32[128,256]{1,0:T(8,128)S(1)} %shard_map.70), channel_id=1, source_target_pairs={{0,16},{1,17},{2,18},{3,19},{4,20},{5,21},{6,22},{7,23},{8,24},{9,... | collective-permute-start | bytes 393224 | tf_op jit(solution)/shard_map/ppermute | solution.py:366
  129.5 10.5 %collective-permute-start.14 = (f32[320,256]{1,0:T(8,128)S(1)}, f32[320,256]{1,0:T(8,128)S(1)}, u32[]{:S(2)}, u32[]{:S(2)}) collective-permute-start(f32[320,256]{1,0:T(8,128)S(1)} %maximum_select_fusion.3), channel_id=1, source_target_pairs={{0,4},{1,3},{2,6},{3,1},{4,0},{5,7},{6,2},{7,5},{8,12},{9,11},{10,... | collective-permute-start | bytes 983048 | tf_op jit(solution)/shard_map/ppermute | solution.py:366
  137.8 9.2 %collective-permute-start.24 = (f32[256,256]{1,0:T(8,128)S(1)}, f32[256,256]{1,0:T(8,128)S(1)}, u32[]{:S(2)}, u32[]{:S(2)}) collective-permute-start(f32[256,256]{1,0:T(8,128)S(1)} %maximum_select_fusion.5), channel_id=1, source_target_pairs={{0,8},{1,9},{2,10},{3,11},{4,12},{5,13},{6,14},{7,15},{8,0},{9,1},... | collective-permute-start | bytes 786440 | tf_op jit(solution)/shard_map/ppermute | solution.py:366
  138.0 24.0 %collective-permute-start.20 = (f32[640,256]{1,0:T(8,128)S(1)}, f32[640,256]{1,0:T(8,128)S(1)}, u32[]{:S(2)}, u32[]{:S(2)}) collective-permute-start(f32[640,256]{1,0:T(8,128)S(1)} %maximum_select_fusion.1.refs_2_), channel_id=1, source_target_pairs={{0,8},{1,9},{2,10},{3,11},{4,12},{5,13},{6,14},{7,15},{8,0},{9,1},... | collective-permute-start | bytes 1966088 | tf_op jit(solution)/shard_map/ppermute | solution.py:366
  140.1 23.4 %collective-permute-start.15 = (f32[640,256]{1,0:T(8,128)S(1)}, f32[640,256]{1,0:T(8,128)S(1)}, u32[]{:S(2)}, u32[]{:S(2)}) collective-permute-start(f32[640,256]{1,0:T(8,128)S(1)} %maximum_select_fusion.refs_0_), channel_id=1, source_target_pairs={{0,2},{1,5},{2,0},{3,7},{4,6},{5,1},{6,4},{7,3},{8,10},{9,13},{10,... | collective-permute-start | bytes 1966088 | tf_op jit(solution)/shard_map/ppermute | solution.py:366
  147.1 14.9 %collective-permute-start.29 = (f32[512,256]{1,0:T(8,128)S(1)}, f32[512,256]{1,0:T(8,128)S(1)}, u32[]{:S(2)}, u32[]{:S(2)}) collective-permute-start(f32[512,256]{1,0:T(8,128)S(1)} %maximum_select_fusion.2.refs_4_), channel_id=1, source_target_pairs={{0,2},{1,5},{2,0},{3,7},{4,6},{5,1},{6,4},{7,3},{8,10},{9,13},{10,... | collective-permute-start | bytes 1572872 | tf_op jit(solution)/shard_map/ppermute | solution.py:366
  148.7 16.9 %collective-permute-start.25 = (f32[512,256]{1,0:T(8,128)S(1)}, f32[512,256]{1,0:T(8,128)S(1)}, u32[]{:S(2)}, u32[]{:S(2)}) collective-permute-start(f32[512,256]{1,0:T(8,128)S(1)} %maximum_select_fusion.2.refs_4_), channel_id=1, source_target_pairs={{0,4},{1,3},{2,6},{3,1},{4,0},{5,7},{6,2},{7,5},{8,12},{9,11},{10,... | collective-permute-start | bytes 1572872 | tf_op jit(solution)/shard_map/ppermute | solution.py:366
  149.6 22.1 %collective-permute-start.28 = (f32[640,256]{1,0:T(8,128)S(1)}, f32[640,256]{1,0:T(8,128)S(1)}, u32[]{:S(2)}, u32[]{:S(2)}) collective-permute-start(f32[640,256]{1,0:T(8,128)S(1)} %maximum_select_fusion.1.refs_2_), channel_id=1, source_target_pairs={{0,2},{1,5},{2,0},{3,7},{4,6},{5,1},{6,4},{7,3},{8,10},{9,13},{10,... | collective-permute-start | bytes 1966088 | tf_op jit(solution)/shard_map/ppermute | solution.py:366
  162.0 17.7 %collective-permute-start.27 = (f32[640,256]{1,0:T(8,128)S(1)}, f32[640,256]{1,0:T(8,128)S(1)}, u32[]{:S(2)}, u32[]{:S(2)}) collective-permute-start(f32[640,256]{1,0:T(8,128)S(1)} %maximum_select_fusion.refs_0_), channel_id=1, source_target_pairs={{0,8},{1,9},{2,10},{3,11},{4,12},{5,13},{6,14},{7,15},{8,0},{9,1},... | collective-permute-start | bytes 1966088 | tf_op jit(solution)/shard_map/ppermute | solution.py:366
  162.0 21.4 %collective-permute-start.21 = (f32[640,256]{1,0:T(8,128)S(1)}, f32[640,256]{1,0:T(8,128)S(1)}, u32[]{:S(2)}, u32[]{:S(2)}) collective-permute-start(f32[640,256]{1,0:T(8,128)S(1)} %collective-permute-done.20.refs_3_), channel_id=1, source_target_pairs={{0,2},{1,5},{2,0},{3,7},{4,6},{5,1},{6,4},{7,3},{8,10},{9,13},{10,... | collective-permute-start | bytes 1966088 | tf_op jit(solution)/shard_map/ppermute | solution.py:366
  163.6 24.7 %collective-permute-start.16 = (f32[640,256]{1,0:T(8,128)S(1)}, f32[640,256]{1,0:T(8,128)S(1)}, u32[]{:S(2)}, u32[]{:S(2)}) collective-permute-start(f32[640,256]{1,0:T(8,128)S(1)} %collective-permute-done.15.refs_1_), channel_id=1, source_target_pairs={{0,8},{1,9},{2,10},{3,11},{4,12},{5,13},{6,14},{7,15},{8,0},{9,1},... | collective-permute-start | bytes 1966088 | tf_op jit(solution)/shard_map/ppermute | solution.py:366
  165.6 17.9 %collective-permute-start.26 = (f32[512,256]{1,0:T(8,128)S(1)}, f32[512,256]{1,0:T(8,128)S(1)}, u32[]{:S(2)}, u32[]{:S(2)}) collective-permute-start(f32[512,256]{1,0:T(8,128)S(1)} %collective-permute-done.25.refs_5_), channel_id=1, source_target_pairs={{0,2},{1,5},{2,0},{3,7},{4,6},{5,1},{6,4},{7,3},{8,10},{9,13},{10,... | collective-permute-start | bytes 1572872 | tf_op jit(solution)/shard_map/ppermute | solution.py:366
  190.6 2.4 %collective-permute-start.30 = (f32[768,256]{1,0:T(8,128)S(1)}, f32[768,256]{1,0:T(8,128)S(1)}, u32[]{:S(2)}, u32[]{:S(2)}) collective-permute-start(f32[768,256]{1,0:T(8,128)S(1)} %get-tuple-element.32.mine_ref), channel_id=1, source_target_pairs={{0,1},{1,0},{2,3},{3,2},{4,5},{5,4},{6,7},{7,6},{8,9},{9,8},{10,11... | collective-permute-start | bytes 2359304 | tf_op jit(solution)/shard_map/ppermute | solution.py:399
